TPU v7x, 32 devices: a whole 2x2x4 slice. The times are simulated.
32 devices in a mesh: seq: 16 (over z, y, x), tp: 2 (over core).
Axes of the slice: x: 2, y: 2, z: 4, core: 2. Of those that a mesh axis runs over, the one named last changes fastest.
Arguments:
- tokens: bfloat16 [2048, 2048], P('seq'), may hold values from -6 to 6
- attn_gain: bfloat16 [2048], P('seq'), may hold values from 0.099609375 to 1.8984375
- q_gain: bfloat16 [1024], P('seq'), may hold values from 0.099609375 to 1.8984375
- w_qdown: bfloat16 [2048, 1024], P('seq'), may hold values from -0.125 to 0.125
- w_qup: bfloat16 [1024, 4096], P('seq', 'tp'), may hold values from -0.1875 to 0.1875
- w_kv: bfloat16 [2048, 512], P('seq'), may hold values from -0.125 to 0.125
- w_out: bfloat16 [4096, 2048], P('tp', 'seq'), may hold values from -2 to 2
- mlp_gain: bfloat16 [2048], P('seq'), may hold values from 0.099609375 to 1.8984375
- w_gate: bfloat16 [2048, 5632], P('seq', 'tp'), may hold values from -0.125 to 0.125
- w_up: bfloat16 [2048, 5632], P('seq', 'tp'), may hold values from -0.125 to 0.125
- w_down: bfloat16 [5632, 2048], P('tp', 'seq'), may hold values from -0.078125 to 0.078125
- cotangent: bfloat16 [2048, 2048], P('seq'), may hold values from -6 to 6
- seq_lengths: int32 [4], replicated, may hold values from 64 to 1152, as said below
- block_slots: int32 [32], replicated, may hold values from 0 to 31, as said below
Outputs:
- layer_out: bfloat16 [2048, 2048], P('seq')
- token_grad: bfloat16 [2048, 2048], P('seq')
- attn_gain_grad: float32 [2048], P('seq')
- q_gain_grad: float32 [1024], P('seq')
- w_qdown_grad: float32 [2048, 1024], P('seq')
- w_qup_grad: float32 [1024, 4096], P('seq', 'tp')
- w_kv_grad: float32 [2048, 512], P('seq')
- w_out_grad: float32 [4096, 2048], P('tp', 'seq')
- mlp_gain_grad: float32 [2048], P('seq')
- w_gate_grad: float32 [2048, 5632], P('seq', 'tp')
- w_up_grad: float32 [2048, 5632], P('seq', 'tp')
- w_down_grad: float32 [5632, 2048], P('tp', 'seq')
Inputs may be any that keep to these rules, and one draw needn't show every extreme that they name: `seq_lengths`: the 4 lengths sum to 2048; either the first or the last sequence has exactly 1152 tokens, and the other lengths are shorter. `block_slots`: every block appears once; the slots 2 i and 2 i + 1 hold blocks c and 31 - c for some c below 16.
All inputs are finite; a program needn't handle non-finite values.
Results may differ from a plain program's by a relative error of at most 0.023.
Values may be sent and summed in bfloat16 or wider, within the bound.
No kernel may reach another device: no remote copies, remote signals or barrier semaphores. Data moves between devices by JAX's collectives and lax.ppermute only.
A program may use at most 256 MiB of HBM per device.

v0:
```python
import math

import jax
import jax.numpy as jnp
from jax import lax
from jax.sharding import PartitionSpec as P

EPSILON = 1e-06
ROPE_BASE = 10000.0
MASKED = -1e30


def layout(seq_lengths, block_slots, block_rows):
    slot_count = block_slots.shape[0]
    natural = jnp.repeat(block_slots, block_rows) * block_rows + jnp.tile(
        jnp.arange(block_rows, dtype=jnp.int32), slot_count
    )
    bounds = jnp.cumsum(seq_lengths)
    starts = bounds - seq_lengths
    member = (natural[:, None] >= starts[None, :]) & (natural[:, None] < bounds[None, :])
    numbers = jnp.arange(seq_lengths.shape[0], dtype=jnp.int32)
    doc_ids = jnp.sum(jnp.where(member, numbers[None, :], 0), axis=1)
    offset = jnp.sum(jnp.where(member, starts[None, :], 0), axis=1)
    return (natural, doc_ids, natural - offset)


def angles(position, width):
    half_width = width // 2
    frequency = jnp.exp(
        jnp.arange(half_width, dtype=jnp.float32) * (-math.log(ROPE_BASE) / half_width)
    )
    phase_angle = position.astype(jnp.float32)[:, None] * frequency[None, :]
    return (jnp.cos(phase_angle), jnp.sin(phase_angle))


def rotate(vector, cosine, sine_table):
    half_width = vector.shape[-1] // 2
    front_half = vector[..., :half_width]
    back_half = vector[..., half_width:]
    return jnp.concatenate(
        [
            front_half * cosine - back_half * sine_table,
            back_half * cosine + front_half * sine_table,
        ],
        axis=-1,
    )


def unrotate(vector, cosine, sine_table):
    half_width = vector.shape[-1] // 2
    front_half = vector[..., :half_width]
    back_half = vector[..., half_width:]
    return jnp.concatenate(
        [
            front_half * cosine + back_half * sine_table,
            back_half * cosine - front_half * sine_table,
        ],
        axis=-1,
    )


def inverse_rms(vector):
    return lax.rsqrt(jnp.mean(vector * vector, axis=-1, keepdims=True) + EPSILON)


def norm_back(scaled_grad, normed, inverse):
    return inverse * (scaled_grad - normed * jnp.mean(scaled_grad * normed, axis=-1, keepdims=True))


def matmul(left, right):
    return jnp.dot(left, right, preferred_element_type=jnp.float32)


def contract_rows(left, right):
    return lax.dot_general(
        left, right, (((0,), (0,)), ((), ())), preferred_element_type=jnp.float32
    )


def times_transposed(left, right):
    return lax.dot_general(
        left, right, (((1,), (1,)), ((), ())), preferred_element_type=jnp.float32
    )


def local(
    tokens,
    attn_gain,
    q_gain,
    w_qdown,
    w_qup,
    w_kv,
    w_out,
    mlp_gain,
    w_gate,
    w_up,
    w_down,
    cotangent,
    seq_lengths,
    block_slots,
):
    tok_dev = tokens.shape[0]
    block_rows = tok_dev // 2
    device_index = lax.axis_index("seq")
    natural, doc_ids, position = layout(seq_lengths, block_slots, block_rows)
    q_natural = lax.dynamic_slice_in_dim(natural, device_index * tok_dev, tok_dev)
    q_doc = lax.dynamic_slice_in_dim(doc_ids, device_index * tok_dev, tok_dev)
    q_position = lax.dynamic_slice_in_dim(position, device_index * tok_dev, tok_dev)
    (
        gain_attn,
        gain_query,
        full_qdown,
        full_qup,
        full_kv,
        full_out,
        gain_mlp,
        full_gate,
        full_up,
        full_down,
    ) = (
        lax.all_gather(attn_gain, "seq", axis=0, tiled=True),
        lax.all_gather(q_gain, "seq", axis=0, tiled=True),
        lax.all_gather(w_qdown, "seq", axis=0, tiled=True),
        lax.all_gather(w_qup, "seq", axis=0, tiled=True),
        lax.all_gather(w_kv, "seq", axis=0, tiled=True),
        lax.all_gather(w_out, "seq", axis=1, tiled=True),
        lax.all_gather(mlp_gain, "seq", axis=0, tiled=True),
        lax.all_gather(w_gate, "seq", axis=0, tiled=True),
        lax.all_gather(w_up, "seq", axis=0, tiled=True),
        lax.all_gather(w_down, "seq", axis=1, tiled=True),
    )
    gain_attn = gain_attn.astype(jnp.float32)
    gain_query = gain_query.astype(jnp.float32)
    gain_mlp = gain_mlp.astype(jnp.float32)
    head_dim = full_kv.shape[1] // 2
    head_count = full_qup.shape[1] // head_dim
    score_scale = head_dim ** (-0.5)
    cosine, sine_table = angles(q_position, head_dim)
    inputs = tokens.astype(jnp.float32)
    x_inverse = inverse_rms(inputs)
    x_hat = inputs * x_inverse
    x_norm = (x_hat * gain_attn).astype(jnp.bfloat16)
    q_lat = matmul(x_norm, full_qdown)
    lat_inverse = inverse_rms(q_lat)
    lat_hat = q_lat * lat_inverse
    q_norm = (lat_hat * gain_query).astype(jnp.bfloat16)
    q_pre = matmul(q_norm, full_qup).reshape(tok_dev, head_count, head_dim)
    queries = rotate(q_pre, cosine[:, None, :], sine_table[:, None, :]).astype(jnp.bfloat16)
    kv_pre = matmul(x_norm, full_kv)
    kv_local = jnp.concatenate(
        [rotate(kv_pre[:, :head_dim], cosine, sine_table), kv_pre[:, head_dim:]], axis=1
    ).astype(jnp.bfloat16)

    def scores_of(key_piece, first_row):
        row_count = key_piece.shape[0]
        k_natural = lax.dynamic_slice_in_dim(natural, first_row, row_count)
        k_doc = lax.dynamic_slice_in_dim(doc_ids, first_row, row_count)
        allowed = (q_doc[:, None] == k_doc[None, :]) & (k_natural[None, :] <= q_natural[:, None])
        scores = (
            jnp.einsum(
                "qhd,kd->hqk", queries, key_piece[:, :head_dim], preferred_element_type=jnp.float32
            )
            * score_scale
        )
        return (scores, allowed)

    key_piece = lax.all_gather(kv_local, "seq", axis=0, tiled=True)
    running_max = jnp.full((head_count, tok_dev), MASKED, jnp.float32)
    scores, allowed = scores_of(key_piece, jnp.int32(0))
    new_max = jnp.maximum(running_max, jnp.max(jnp.where(allowed[None], scores, MASKED), axis=-1))
    exp_terms = jnp.where(allowed[None], jnp.exp(scores - new_max[..., None]), 0.0)
    row_total = jnp.sum(exp_terms, axis=-1)
    weighted = jnp.einsum(
        "hqk,kd->qhd",
        exp_terms.astype(jnp.bfloat16),
        key_piece[:, head_dim:],
        preferred_element_type=jnp.float32,
    )
    running_max, row_total, weighted = (new_max, row_total, weighted)
    log_total = running_max + jnp.log(row_total)
    attn_mix = weighted / jnp.transpose(row_total)[:, :, None]
    o_low = attn_mix.astype(jnp.bfloat16).reshape(tok_dev, head_count * head_dim)
    attn_branch = lax.psum(matmul(o_low, full_out).astype(jnp.bfloat16), "tp").astype(jnp.float32)
    hidden = inputs + attn_branch
    h_inverse = inverse_rms(hidden)
    h_hat = hidden * h_inverse
    h_norm = (h_hat * gain_mlp).astype(jnp.bfloat16)
    gate_act = matmul(h_norm, full_gate)
    up_proj = matmul(h_norm, full_up)
    sigmoid_gate = jax.nn.sigmoid(gate_act)
    silu_gate = gate_act * sigmoid_gate
    hidden_act = (silu_gate * up_proj).astype(jnp.bfloat16)
    mlp_branch = lax.psum(matmul(hidden_act, full_down).astype(jnp.bfloat16), "tp").astype(
        jnp.float32
    )
    layer_out = (hidden + mlp_branch).astype(jnp.bfloat16)
    out_grad = cotangent.astype(jnp.float32)
    grad_down = contract_rows(hidden_act, cotangent)
    d_act = times_transposed(cotangent, full_down)
    d_gate = (d_act * up_proj * sigmoid_gate * (1.0 + gate_act * (1.0 - sigmoid_gate))).astype(
        jnp.bfloat16
    )
    d_up = (d_act * silu_gate).astype(jnp.bfloat16)
    grad_gate = contract_rows(h_norm, d_gate)
    grad_up = contract_rows(h_norm, d_up)
    d_hnorm = lax.psum(
        (times_transposed(d_gate, full_gate) + times_transposed(d_up, full_up)).astype(
            jnp.bfloat16
        ),
        "tp",
    ).astype(jnp.float32)
    grad_mlp_gain = jnp.sum(d_hnorm * h_hat, axis=0)
    d_hidden = out_grad + norm_back(d_hnorm * gain_mlp, h_hat, h_inverse)
    d_attn = d_hidden.astype(jnp.bfloat16)
    grad_out = contract_rows(o_low, d_attn)
    d_o = (
        times_transposed(d_attn, full_out)
        .astype(jnp.bfloat16)
        .reshape(tok_dev, head_count, head_dim)
    )
    row_delta = jnp.transpose(jnp.sum(d_o.astype(jnp.float32) * attn_mix, axis=-1))
    kv_whole = lax.all_gather(kv_local, "seq", axis=0, tiled=True)
    key_block = math.gcd(kv_whole.shape[0], 1024)

    def back_step(step_index, state_carry):
        d_query, d_keys = state_carry
        first_row = step_index * key_block
        key_piece = lax.dynamic_slice_in_dim(kv_whole, first_row, key_block)
        scores, allowed = scores_of(key_piece, first_row)
        probs = jnp.where(allowed[None], jnp.exp(scores - log_total[..., None]), 0.0)
        d_value = jnp.einsum(
            "hqk,qhd->kd", probs.astype(jnp.bfloat16), d_o, preferred_element_type=jnp.float32
        )
        d_probs = jnp.einsum(
            "qhd,kd->hqk", d_o, key_piece[:, head_dim:], preferred_element_type=jnp.float32
        )
        d_scores = (probs * (d_probs - row_delta[..., None])).astype(jnp.bfloat16)
        d_query = (
            d_query
            + jnp.einsum(
                "hqk,kd->qhd", d_scores, key_piece[:, :head_dim], preferred_element_type=jnp.float32
            )
            * score_scale
        )
        d_key = (
            jnp.einsum("hqk,qhd->kd", d_scores, queries, preferred_element_type=jnp.float32)
            * score_scale
        )
        d_keys = lax.dynamic_update_slice_in_dim(
            d_keys, jnp.concatenate([d_key, d_value], axis=1), first_row, 0
        )
        return (d_query, d_keys)

    back_start = (
        jnp.zeros((tok_dev, head_count, head_dim), jnp.float32),
        jnp.zeros((kv_whole.shape[0], 2 * head_dim), jnp.float32),
    )
    d_query, d_keys = lax.fori_loop(0, kv_whole.shape[0] // key_block, back_step, back_start)
    d_kv_part = lax.psum_scatter(d_keys, "seq", scatter_dimension=0, tiled=True)
    d_qpre = (
        unrotate(d_query, cosine[:, None, :], sine_table[:, None, :])
        .astype(jnp.bfloat16)
        .reshape(tok_dev, head_count * head_dim)
    )
    grad_qup = contract_rows(q_norm, d_qpre)
    d_qnorm, d_kv = (
        lax.psum(times_transposed(d_qpre, full_qup).astype(jnp.bfloat16), "tp").astype(jnp.float32),
        lax.psum(d_kv_part.astype(jnp.bfloat16), "tp").astype(jnp.float32),
    )
    grad_q_gain = jnp.sum(d_qnorm * lat_hat, axis=0)
    d_lat = norm_back(d_qnorm * gain_query, lat_hat, lat_inverse).astype(jnp.bfloat16)
    d_kvpre = jnp.concatenate(
        [unrotate(d_kv[:, :head_dim], cosine, sine_table), d_kv[:, head_dim:]], axis=1
    ).astype(jnp.bfloat16)
    grad_qdown = contract_rows(x_norm, d_lat)
    grad_kv = contract_rows(x_norm, d_kvpre)
    d_xnorm = times_transposed(d_lat, full_qdown) + times_transposed(d_kvpre, full_kv)
    grad_attn_gain = jnp.sum(d_xnorm * x_hat, axis=0)
    token_grad = (d_hidden + norm_back(d_xnorm * gain_attn, x_hat, x_inverse)).astype(jnp.bfloat16)
    (
        attn_gain_part,
        q_gain_part,
        qdown_part,
        qup_part,
        kv_part,
        out_part,
        mlp_gain_part,
        gate_part,
        up_part,
        down_part,
    ) = (
        lax.psum_scatter(grad_attn_gain, "seq", scatter_dimension=0, tiled=True),
        lax.psum_scatter(grad_q_gain, "seq", scatter_dimension=0, tiled=True),
        lax.psum_scatter(grad_qdown, "seq", scatter_dimension=0, tiled=True),
        lax.psum_scatter(grad_qup, "seq", scatter_dimension=0, tiled=True),
        lax.psum_scatter(grad_kv, "seq", scatter_dimension=0, tiled=True),
        lax.psum_scatter(grad_out, "seq", scatter_dimension=1, tiled=True),
        lax.psum_scatter(grad_mlp_gain, "seq", scatter_dimension=0, tiled=True),
        lax.psum_scatter(grad_gate, "seq", scatter_dimension=0, tiled=True),
        lax.psum_scatter(grad_up, "seq", scatter_dimension=0, tiled=True),
        lax.psum_scatter(grad_down, "seq", scatter_dimension=1, tiled=True),
    )
    return (
        layer_out,
        token_grad,
        attn_gain_part,
        q_gain_part,
        qdown_part,
        qup_part,
        kv_part,
        out_part,
        mlp_gain_part,
        gate_part,
        up_part,
        down_part,
    )


def solution(mesh):
    in_specs = (
        P("seq", None),
        P("seq"),
        P("seq"),
        P("seq", None),
        P("seq", "tp"),
        P("seq", None),
        P("tp", "seq"),
        P("seq"),
        P("seq", "tp"),
        P("seq", "tp"),
        P("tp", "seq"),
        P("seq", None),
        P(),
        P(),
    )
    out_specs = (
        P("seq", None),
        P("seq", None),
        P("seq"),
        P("seq"),
        P("seq", None),
        P("seq", "tp"),
        P("seq", None),
        P("tp", "seq"),
        P("seq"),
        P("seq", "tp"),
        P("seq", "tp"),
        P("tp", "seq"),
    )
    return jax.shard_map(local, mesh=mesh, in_specs=in_specs, out_specs=out_specs, check_vma=False)
```

profile of v0, /device:TPU:0, one launch (start us, length us, event | category | flops | bytes accessed | tf_op | source)
XLA Modules:
  0.0 3416.4 jit_solution(8796281800278769453)
XLA Ops:
  11.1 42.4 %all-gather = bf16[16,1,128]{2,1,0:T(2,128)(2,1)S(1)} all-gather(bf16[1,1,128]{2,1,0:T(2,128)(2,1)} %bitcast.179), channel_id=1, replica_groups=mesh['seq'=16,'tp'=2] {'seq'}, dimensions={0}, use_global_device_ids=true | all-gather | bytes 4352 | tf_op jit(solution)/shard_map/all_gather | solution.py:121
  55.7 18.6 all-gather.11.cloned.1.call-done
  79.8 40.1 %all-reduce = bf16[1024]{0:T(1024)(128)(2,1)S(1)} all-reduce(bf16[1024]{0:T(1024)(128)(2,1)S(1)} %dynamic-update-slice), channel_id=1, replica_groups=mesh['seq'=16,'tp'=2] {'seq'}, use_global_device_ids=true, to_apply=%add | all-reduce | flops 1024 | bytes 4096
  121.3 30.6 all-gather.15.cloned.1.call-done
  155.0 74.4 %all-gather.17.cloned.1.call-done = bf16[1024,2048]{1,0:T(8,128)(2,1)} async-done(((bf16[64,2048]{1,0:T(8,128)(2,1)}), bf16[1024,2048]{1,0:T(8,128)(2,1)}) %all-gather.17.cloned.1.call-update) | async-done | bytes 4194320 | tf_op jit(solution)/shard_map/all_gather | solution.py:124
  233.0 58.9 %all-gather.13.cloned.1.call-done = bf16[2048,512]{1,0:T(8,128)(2,1)} async-done(((bf16[128,512]{1,0:T(8,128)(2,1)}), bf16[2048,512]{1,0:T(8,128)(2,1)}) %all-gather.13.cloned.1.call-update) | async-done | bytes 2097168 | tf_op jit(solution)/shard_map/all_gather | solution.py:167
  300.7 134.8 %all-gather.19.cloned.1.call-done = bf16[2048,2048]{1,0:T(8,128)(2,1)} async-done(((bf16[2048,128]{1,0:T(8,128)(2,1)}), bf16[2048,2048]{1,0:T(8,128)(2,1)}) %all-gather.19.cloned.1.call-update) | async-done | bytes 8388624 | tf_op jit(solution)/shard_map/all_gather | solution.py:126
  443.3 38.2 %all-gather.1 = bf16[16,1,128]{2,1,0:T(2,128)(2,1)S(1)} all-gather(bf16[1,1,128]{2,1,0:T(2,128)(2,1)S(1)} %bitcast.180), channel_id=1, replica_groups=mesh['seq'=16,'tp'=2] {'seq'}, dimensions={0}, use_global_device_ids=true | all-gather | bytes 4352 | tf_op jit(solution)/shard_map/all_gather | solution.py:127
  484.2 120.5 %all-gather.21.cloned.1.call-done = bf16[2048,2816]{1,0:T(8,128)(2,1)} async-done(((bf16[128,2816]{1,0:T(8,128)(2,1)}), bf16[2048,2816]{1,0:T(8,128)(2,1)}) %all-gather.21.cloned.1.call-update) | async-done | bytes 11534352 | tf_op jit(solution)/shard_map/all_gather | solution.py:128
  610.6 137.5 %all-gather.23.cloned.1.call-done = bf16[2048,2816]{1,0:T(8,128)(2,1)} async-done(((bf16[128,2816]{1,0:T(8,128)(2,1)}), bf16[2048,2816]{1,0:T(8,128)(2,1)}) %all-gather.23.cloned.1.call-update) | async-done | bytes 11534352 | tf_op jit(solution)/shard_map/all_gather | solution.py:129
  748.1 7.0 fusion.104
  755.2 176.8 %all-gather.25.cloned.1.call-done = bf16[2816,2048]{1,0:T(8,128)(2,1)} async-done(((bf16[2816,128]{1,0:T(8,128)(2,1)}), bf16[2816,2048]{1,0:T(8,128)(2,1)}) %all-gather.25.cloned.1.call-update) | async-done | bytes 11534352 | tf_op jit(solution)/shard_map/all_gather | solution.py:130
  932.0 9.8 multiply_convert_fusion
  941.8 8.6 fusion.105
  958.0 14.1 all-reduce.12.cloned.1.call-done
  974.3 6.5 convolution_convert_fusion
  985.8 41.0 %while.16 = (s32[]{:T(128)}, f32[128,8,256]{0,2,1:T(8,128)S(1)}, f32[2048,512]{1,0:T(8,128)}, bf16[2048,512]{1,0:T(8,128)(2,1)}, s32[128]{0:T(128)S(1)}, /*index...) while((s32[]{:T(128)}, f32[128,8,256]{0,2,1:T(8,128)S(1)}, ...), condition=%wide.region_14.15_spmd.clone, body=%wide.region_13.14_spmd.clone.sunk | while | flops 2696806400 | bytes 73307472 | solution.py:258
  1028.0 6.7 convolution_convert_fusion.2
  1040.0 83.4 %reduce-scatter.9.cloned.1.call-done = f32[128,512]{1,0:T(8,128)} async-done(((f32[2048,512]{1,0:T(8,128)}), f32[128,512]{1,0:T(8,128)}) %reduce-scatter.9.cloned.1.call-update) | async-done | bytes 262160 | tf_op jit(solution)/shard_map/reduce_scatter | solution.py:259
  1129.9 15.6 all-reduce.14.cloned.1.call-done
  1157.9 8.4 fusion.64
  1167.5 9.5 fusion.107
  1178.1 9.5 fusion.108
  1188.7 9.4 fusion.109
  1205.3 78.0 %all-reduce.4 = (f32[2048]{0:T(1024)S(1)}, f32[1024]{0:T(1024)S(1)}, f32[2048]{0:T(1024)S(1)}) all-reduce(f32[2048]{0:T(1024)S(1)} %get-tuple-element.303, f32[1024]{0:T(1024)S(1)} %get-tuple-element.305, f32[2048]{0:T(1024)S(1)} %copy-done.34), channel_id=3, replica_groups=mesh['seq'=16,'tp'=2] {'seq'}, use_global_device_ids=true, to_apply=%region_21.22.clone | all-reduce | flops 5120 | bytes 40960
  1288.0 42.1 %reduce-scatter.13.cloned.1.call-done = f32[64,2048]{1,0:T(8,128)} async-done(((f32[1024,2048]{1,0:T(8,128)}), f32[64,2048]{1,0:T(8,128)}) %reduce-scatter.13.cloned.1.call-update) | async-done | bytes 524304 | tf_op jit(solution)/shard_map/reduce_scatter | solution.py:295
  1330.1 100.4 %reduce-scatter.15.cloned.1.call-done = f32[128,512]{1,0:T(8,128)} async-done(((f32[2048,512]{1,0:T(8,128)}), f32[128,512]{1,0:T(8,128)}) %reduce-scatter.15.cloned.1.call-update) | async-done | bytes 262160 | tf_op jit(solution)/shard_map/reduce_scatter | solution.py:296
  1430.5 180.3 %reduce-scatter.11.cloned.1.call-done = f32[128,1024]{1,0:T(8,128)} async-done(((f32[2048,1024]{1,0:T(8,128)}), f32[128,1024]{1,0:T(8,128)}) %reduce-scatter.11.cloned.1.call-update) | async-done | bytes 524304 | tf_op jit(solution)/shard_map/reduce_scatter | solution.py:294
  1610.8 351.6 %reduce-scatter.17.cloned.1.call-done = f32[2048,128]{1,0:T(8,128)} async-done(((f32[2048,2048]{1,0:T(8,128)}), f32[2048,128]{1,0:T(8,128)}) %reduce-scatter.17.cloned.1.call-update) | async-done | bytes 1048592 | tf_op jit(solution)/shard_map/reduce_scatter | solution.py:297
  1962.4 481.5 %reduce-scatter.19.cloned.1.call-done = f32[128,2816]{1,0:T(8,128)} async-done(((f32[2048,2816]{1,0:T(8,128)}), f32[128,2816]{1,0:T(8,128)}) %reduce-scatter.19.cloned.1.call-update) | async-done | bytes 1441808 | tf_op jit(solution)/shard_map/reduce_scatter | solution.py:299
  2444.0 482.7 %reduce-scatter.21.cloned.1.call-done = f32[128,2816]{1,0:T(8,128)} async-done(((f32[2048,2816]{1,0:T(8,128)}), f32[128,2816]{1,0:T(8,128)}) %reduce-scatter.21.cloned.1.call-update) | async-done | bytes 1441808 | tf_op jit(solution)/shard_map/reduce_scatter | solution.py:300
  2926.6 482.8 %reduce-scatter.23.cloned.1.call-done = f32[2816,128]{1,0:T(8,128)} async-done(((f32[2816,2048]{1,0:T(8,128)}), f32[2816,128]{1,0:T(8,128)}) %reduce-scatter.23.cloned.1.call-update) | async-done | bytes 1441808 | tf_op jit(solution)/shard_map/reduce_scatter | solution.py:301
  (255 shorter events, 138.2 us)
Async XLA Ops:
  7.2 144.7 %copy-start.3 = (bf16[128,2048]{1,0:T(8,128)(2,1)S(1)}, bf16[128,2048]{1,0:T(8,128)(2,1)}, u32[]{:S(2)}) copy-start(bf16[128,2048]{1,0:T(8,128)(2,1)} %param.16) | copy-start | bytes 1572868
  7.2 67.1 %all-gather.11.cloned.1.call-start = ((), (), s32[]{:S(2)}) async-start(), calls=%async_computation.8 | async-start | bytes 2228224 | tf_op jit(solution)/shard_map/all_gather | solution.py:125
  7.9 144.0 %all-gather.15.cloned.1.call-start = ((), (), s32[]{:S(2)}) async-start(), calls=%async_computation.10 | async-start | bytes 4456448 | tf_op jit(solution)/shard_map/all_gather | solution.py:123
  8.7 220.7 %all-gather.17.cloned.1.call-start = ((), (), s32[]{:S(2)}) async-start(), calls=%async_computation.11 | async-start | bytes 4456448 | tf_op jit(solution)/shard_map/all_gather | solution.py:124
  9.4 282.5 %all-gather.13.cloned.1.call-start = ((), (), s32[]{:S(2)}) async-start(), calls=%async_computation.9 | async-start | bytes 2228224 | tf_op jit(solution)/shard_map/all_gather | solution.py:167
  10.3 111.0 %copy-start.30 = (s32[2048]{0:T(1024)}, s32[2048]{0:T(1024)S(1)}, u32[]{:S(2)}) copy-start(s32[2048]{0:T(1024)S(1)} %add.149) | copy-start | bytes 24580
  55.7 99.2 %copy-start.37 = (f32[128]{0:T(128)}, f32[128]{0:T(128)S(1)}, u32[]{:S(2)}) copy-start(f32[128]{0:T(128)S(1)} %add_rsqrt_fusion.2) | copy-start | bytes 1540
  77.6 357.9 %all-gather.19.cloned.1.call-start = ((), (), s32[]{:S(2)}) async-start(), calls=%async_computation.12 | async-start | bytes 8912896 | tf_op jit(solution)/shard_map/all_gather | solution.py:126
  78.2 403.3 %all-reduce.10.cloned.1.call-start = ((), (), s32[]{:S(2)}) async-start(), calls=%async_computation.13 | async-start | bytes 1048576 | tf_op jit(solution)/shard_map/psum | solution.py:183
  119.9 112.5 %copy-start.28 = (f32[1024]{0:T(1024)}, f32[1024]{0:T(1024)S(1)}, u32[]{:S(2)}) copy-start(f32[1024]{0:T(1024)S(1)} %convert_element_type.116) | copy-start | bytes 12292
  300.7 140.3 %copy-start.17 = (bf16[128,8,256]{0,2,1:T(8,128)(2,1)}, bf16[128,8,256]{0,2,1:T(8,128)(2,1)S(1)}, u32[]{:S(2)}) copy-start(bf16[128,8,256]{0,2,1:T(8,128)(2,1)S(1)} %get-tuple-element.366) | copy-start | bytes 1572868
  441.1 163.6 %all-gather.21.cloned.1.call-start = ((), (), s32[]{:S(2)}) async-start(), calls=%async_computation.14 | async-start | bytes 12255232 | tf_op jit(solution)/shard_map/all_gather | solution.py:128
  441.8 306.3 %all-gather.23.cloned.1.call-start = ((), (), s32[]{:S(2)}) async-start(), calls=%async_computation.15 | async-start | bytes 12255232 | tf_op jit(solution)/shard_map/all_gather | solution.py:129
  442.6 489.4 %all-gather.25.cloned.1.call-start = ((), (), s32[]{:S(2)}) async-start(), calls=%async_computation.16 | async-start | bytes 12255232 | tf_op jit(solution)/shard_map/all_gather | solution.py:130
  443.3 528.8 %all-reduce.12.cloned.1.call-start = ((), (), s32[]{:S(2)}) async-start(), calls=%async_computation.17 | async-start | bytes 1048576 | tf_op jit(solution)/shard_map/psum | solution.py:206
  482.9 121.8 %copy-start.43 = (f32[128]{0:T(128)}, f32[128]{0:T(128)S(1)}, u32[]{:S(2)}) copy-start(f32[128]{0:T(128)S(1)} %add_rsqrt_fusion) | copy-start | bytes 1540
  484.1 264.0 %copy-start.5 = (bf16[128,2048]{1,0:T(8,128)(2,1)}, bf16[128,2048]{1,0:T(8,128)(2,1)S(1)}, u32[]{:S(2)}) copy-start(bf16[128,2048]{1,0:T(8,128)(2,1)S(1)} %multiply_convert_fusion.3) | copy-start | bytes 1572868
  610.6 321.4 %copy-start.11 = (bf16[128,2048]{1,0:T(8,128)(2,1)S(1)}, bf16[128,2048]{1,0:T(8,128)(2,1)}, u32[]{:S(2)}) copy-start(bf16[128,2048]{1,0:T(8,128)(2,1)} %param.27) | copy-start | bytes 1572868
  955.1 168.3 %reduce-scatter.9.cloned.1.call-start = ((), (), s32[]{:S(2)}) async-start(), calls=%async_computation.18 | async-start | bytes 4456448 | tf_op jit(solution)/shard_map/reduce_scatter | solution.py:259
  974.3 182.2 %copy-start.47 = (f32[128]{0:T(128)}, f32[128]{0:T(128)S(1)}, u32[]{:S(2)}) copy-start(f32[128]{0:T(128)S(1)} %broadcast_multiply_fusion.3) | copy-start | bytes 1540
  1026.9 118.6 %all-reduce.14.cloned.1.call-start = ((), (), s32[]{:S(2)}) async-start(), calls=%async_computation.26 | async-start | bytes 1835008 | tf_op jit(solution)/shard_map/psum | solution.py:193
  1035.2 89.9 %copy-start.10 = (f32[128,1024]{1,0:T(8,128)S(1)}, f32[128,1024]{1,0:T(8,128)}, u32[]{:S(2)}) copy-start(f32[128,1024]{1,0:T(8,128)} %copy-done.9) | copy-start | bytes 1572868
  1035.2 89.9 %copy-start.29 = (f32[1024]{0:T(1024)S(1)}, f32[1024]{0:T(1024)}, u32[]{:S(2)}) copy-start(f32[1024]{0:T(1024)} %copy-done.28) | copy-start | bytes 12292
  1035.2 89.9 %copy-start.46 = (f32[128]{0:T(128)S(1)}, f32[128]{0:T(128)}, u32[]{:S(2)}) copy-start(f32[128]{0:T(128)} %copy-done.45) | copy-start | bytes 1540
  1125.0 205.1 %reduce-scatter.13.cloned.1.call-start = ((), (), s32[]{:S(2)}) async-start(), calls=%async_computation.20 | async-start | bytes 8912896 | tf_op jit(solution)/shard_map/reduce_scatter | solution.py:295
  1129.8 300.7 %reduce-scatter.15.cloned.1.call-start = ((), (), s32[]{:S(2)}) async-start(), calls=%async_computation.21 | async-start | bytes 4456448 | tf_op jit(solution)/shard_map/reduce_scatter | solution.py:296
  1150.5 460.4 %reduce-scatter.11.cloned.1.call-start = ((), (), s32[]{:S(2)}) async-start(), calls=%async_computation.19 | async-start | bytes 8912896 | tf_op jit(solution)/shard_map/reduce_scatter | solution.py:294
  1156.4 806.1 %reduce-scatter.17.cloned.1.call-start = ((), (), s32[]{:S(2)}) async-start(), calls=%async_computation.22 | async-start | bytes 17825792 | tf_op jit(solution)/shard_map/reduce_scatter | solution.py:297
  1166.3 1277.7 %reduce-scatter.19.cloned.1.call-start = ((), (), s32[]{:S(2)}) async-start(), calls=%async_computation.23 | async-start | bytes 24510464 | tf_op jit(solution)/shard_map/reduce_scatter | solution.py:299
  1177.0 1749.6 %reduce-scatter.21.cloned.1.call-start = ((), (), s32[]{:S(2)}) async-start(), calls=%async_computation.24 | async-start | bytes 24510464 | tf_op jit(solution)/shard_map/reduce_scatter | solution.py:300
  1187.6 2221.8 %reduce-scatter.23.cloned.1.call-start = ((), (), s32[]{:S(2)}) async-start(), calls=%async_computation.25 | async-start | bytes 24510464 | tf_op jit(solution)/shard_map/reduce_scatter | solution.py:301
  1199.5 85.5 %copy-start.27 = (bf16[128,2048]{1,0:T(8,128)(2,1)S(1)}, bf16[128,2048]{1,0:T(8,128)(2,1)}, u32[]{:S(2)}) copy-start(bf16[128,2048]{1,0:T(8,128)(2,1)} %get-tuple-element.336) | copy-start | bytes 1572868
  (49 other events, 952.9 us)
Sparse Core Ops, SparseCore 0:
  10.8 63.4 all-gather.10
  77.1 74.7 all-gather.14
  154.7 74.6 all-gather.16
  232.6 59.2 all-gather.12
  294.5 140.9 all-gather.18
  441.2 16.9 all-reduce.9
  461.2 143.3 all-gather.20
  607.8 140.3 all-gather.22
  751.2 180.7 all-gather.24
  955.2 16.9 all-reduce.11
  1027.0 96.3 reduce-scatter.8
  1126.3 19.1 all-reduce.13
  1148.5 181.6 reduce-scatter.12
  1333.0 97.5 reduce-scatter.14
  1433.3 177.4 reduce-scatter.10
  1613.6 348.7 reduce-scatter.16
  1965.3 478.6 reduce-scatter.18
  2446.8 479.7 reduce-scatter.20
  2929.6 479.7 reduce-scatter.22
where the time goes:
time: 3430 us; the launch traced here: 3420 us
  waiting for transfers between devices  2990 us (87%)
  blocking collectives  199 us (6%)
  matrix products  156 us (5%)
    reduce_scatter x1, waiting for transfers between devices, local(): lax.psum_scatter(grad_down, 'seq', scatter_dimension=1, tiled=True)  483 us
    reduce_scatter x1, waiting for transfers between devices, local(): lax.psum_scatter(grad_up, 'seq', scatter_dimension=0, tiled=True)  483 us
    reduce_scatter x1, waiting for transfers between devices, local(): lax.psum_scatter(grad_gate, 'seq', scatter_dimension=0, tiled=True)  482 us
    reduce_scatter x1, waiting for transfers between devices, local(): lax.psum_scatter(grad_out, 'seq', scatter_dimension=1, tiled=True)  352 us
    reduce_scatter x1, waiting for transfers between devices, local(): lax.psum_scatter(grad_qdown, 'seq', scatter_dimension=0, tiled=True)  180 us
    all_gather x1, waiting for transfers between devices, local(): lax.all_gather(w_down, 'seq', axis=1, tiled=True)  177 us
    all_gather x1, waiting for transfers between devices, local(): lax.all_gather(w_up, 'seq', axis=0, tiled=True)  138 us
    all_gather x1, waiting for transfers between devices, local(): lax.all_gather(w_out, 'seq', axis=1, tiled=True)  135 us
  transfers between devices with their start and end apart: 19, of which 18 were waited for; matrix products, arithmetic and copies ran while one was open for 3% of the time, Pallas kernels for 0%

commit v1 on v0

v1 whole, which is shorter than its diff:
```python
import functools
import math

import jax
import jax.numpy as jnp
from jax import lax
from jax.experimental import pallas as pl
from jax.experimental.pallas import tpu as pltpu
from jax.sharding import PartitionSpec as P

EPSILON = 1e-06
ROPE_BASE = 10000.0
MASKED = -1e30
HEAD = 256
SQUARE = 4
VMEM_LIMIT = 56 * 1024 * 1024
BF16 = jnp.bfloat16
F32 = jnp.float32


def matmul(left, right):
    return jnp.dot(left, right, preferred_element_type=F32)


def contract_rows(left, right):
    return lax.dot_general(left, right, (((0,), (0,)), ((), ())), preferred_element_type=F32)


def times_transposed(left, right):
    return lax.dot_general(left, right, (((1,), (1,)), ((), ())), preferred_element_type=F32)


def inverse_rms(vector):
    return lax.rsqrt(jnp.mean(vector * vector, axis=-1, keepdims=True) + EPSILON)


def norm_back(scaled_grad, normed, inverse):
    return inverse * (scaled_grad - normed * jnp.mean(scaled_grad * normed, axis=-1, keepdims=True))


def angles(position):
    half = HEAD // 2
    frequency = jnp.exp(jnp.arange(half, dtype=F32) * (-math.log(ROPE_BASE) / half))
    phase = position.astype(F32)[:, None] * frequency[None, :]
    return jnp.cos(phase), jnp.sin(phase)


def rotate(vector, cosine, sine):
    half = HEAD // 2
    front, back = vector[:, :half], vector[:, half:]
    return jnp.concatenate([front * cosine - back * sine, back * cosine + front * sine], axis=1)


def unrotate(vector, cosine, sine):
    return rotate(vector, cosine, -sine)


def masked_scores(q, k, row_natural, row_start, key_natural):
    scores = times_transposed(q, k)
    allowed = (key_natural <= row_natural) & (key_natural >= row_start)
    return scores, allowed


def attend_kernel(q_ref, natural_ref, start_ref, kv_ref, keys_ref, o_ref, lse_ref):
    scores, allowed = masked_scores(
        q_ref[...], kv_ref[:, :HEAD], natural_ref[...], start_ref[...], keys_ref[...]
    )
    scores = jnp.where(allowed, scores, MASKED)
    top = jnp.max(scores, axis=-1, keepdims=True)
    terms = jnp.exp(scores - top)
    total = jnp.sum(terms, axis=-1, keepdims=True)
    o_ref[...] = matmul(terms.astype(BF16), kv_ref[:, HEAD:]) / total
    lse_ref[...] = top + jnp.log(total)


def attend(q, natural, start, kv, keys, block):
    rows, count = q.shape[0], kv.shape[0]
    row = lambda width: pl.BlockSpec((block, width), lambda i: (i, 0))
    whole = lambda shape: pl.BlockSpec(shape, lambda i: (0, 0))
    return pl.pallas_call(
        attend_kernel,
        grid=(rows // block,),
        in_specs=[row(HEAD), row(1), row(1), whole((count, 2 * HEAD)), whole((1, count))],
        out_specs=[row(HEAD), row(1)],
        out_shape=[
            jax.ShapeDtypeStruct((rows, HEAD), F32),
            jax.ShapeDtypeStruct((rows, 1), F32),
        ],
        compiler_params=pltpu.CompilerParams(vmem_limit_bytes=VMEM_LIMIT),
        cost_estimate=pl.CostEstimate(
            flops=4 * rows * count * HEAD, bytes_accessed=4 * count * HEAD, transcendentals=rows * count
        ),
        name="attend",
    )(q, natural, start, kv, keys)


def attend_back_kernel(
    q_ref, natural_ref, start_ref, kv_ref, keys_ref, o_ref, lse_ref, do_ref, dq_ref, dkv_ref
):
    scores, allowed = masked_scores(
        q_ref[...], kv_ref[:, :HEAD], natural_ref[...], start_ref[...], keys_ref[...]
    )
    probs = jnp.exp(jnp.where(allowed, scores - lse_ref[...], MASKED))
    d_o = do_ref[...]
    delta = jnp.sum(d_o.astype(F32) * o_ref[...], axis=-1, keepdims=True)
    d_probs = times_transposed(d_o, kv_ref[:, HEAD:])
    d_scores = (probs * (d_probs - delta)).astype(BF16)
    dq_ref[...] = matmul(d_scores, kv_ref[:, :HEAD]) * HEAD**-0.5

    @pl.when(pl.program_id(0) == 0)
    def _():
        dkv_ref[...] = jnp.zeros_like(dkv_ref)

    dkv_ref[:, :HEAD] += contract_rows(d_scores, q_ref[...])
    dkv_ref[:, HEAD:] += contract_rows(probs.astype(BF16), d_o)


def attend_back(q, natural, start, kv, keys, o, lse, d_o, block):
    rows, count = q.shape[0], kv.shape[0]
    row = lambda width: pl.BlockSpec((block, width), lambda i: (i, 0))
    whole = lambda shape: pl.BlockSpec(shape, lambda i: (0, 0))
    return pl.pallas_call(
        attend_back_kernel,
        grid=(rows // block,),
        in_specs=[
            row(HEAD),
            row(1),
            row(1),
            whole((count, 2 * HEAD)),
            whole((1, count)),
            row(HEAD),
            row(1),
            row(HEAD),
        ],
        out_specs=[row(HEAD), whole((count, 2 * HEAD))],
        out_shape=[
            jax.ShapeDtypeStruct((rows, HEAD), F32),
            jax.ShapeDtypeStruct((count, 2 * HEAD), F32),
        ],
        compiler_params=pltpu.CompilerParams(vmem_limit_bytes=VMEM_LIMIT),
        cost_estimate=pl.CostEstimate(
            flops=10 * rows * count * HEAD, bytes_accessed=12 * count * HEAD, transcendentals=rows * count
        ),
        name="attend_back",
    )(q, natural, start, kv, keys, o, lse, d_o)


def local(
    chips,
    tokens,
    attn_gain,
    q_gain,
    w_qdown,
    w_qup,
    w_kv,
    w_out,
    mlp_gain,
    w_gate,
    w_up,
    w_down,
    cotangent,
    seq_lengths,
    block_slots,
):
    layers = chips // SQUARE
    rows, width = tokens.shape[0] // 2, tokens.shape[1]
    lanes = width // chips
    rank = w_qdown.shape[1]
    rank_rows = w_qup.shape[0]
    heads_half = w_qup.shape[1] // HEAD
    heads = 2 * heads_half
    sharing = chips // heads
    units = w_gate.shape[1] // chips
    squares = range(SQUARE // sharing)
    half = HEAD // 2
    place = lax.axis_index("seq")
    core = lax.axis_index("tp")
    layer, corner = place // SQUARE, place % SQUARE
    first = core == 0

    def across(value):
        return lax.ppermute(value, "tp", [(0, 1), (1, 0)])

    def along(value, step):
        pairs = [
            (z * SQUARE + c, (z + step) % layers * SQUARE + c)
            for z in range(layers)
            for c in range(SQUARE)
        ]
        return lax.ppermute(value, "seq", pairs)

    def within(value, flip):
        return lax.ppermute(value, "seq", [(i, i ^ flip) for i in range(chips)])

    def gather(value, flips=range(SQUARE)):
        column = jnp.stack([value] + [along(value, k) for k in range(1, layers)])
        return [column if m == 0 else within(column, m) for m in flips]

    def scatter(pieces):
        total = sum(
            (piece if m == 0 else within(piece, m)).astype(F32) for m, piece in enumerate(pieces)
        )
        low = total.astype(BF16)
        return total[0] + sum(along(low[k], -k).astype(F32) for k in range(1, layers))

    def own(pair_value):
        return lax.dynamic_slice_in_dim(pair_value, core * rows, rows, 0)

    def others(pair_value):
        return lax.dynamic_slice_in_dim(pair_value, (1 - core) * rows, rows, 0)

    def both(mine, theirs, axis=0):
        return jnp.concatenate(
            [jnp.where(first, mine, theirs), jnp.where(first, theirs, mine)], axis=axis
        )

    def half_of(value, which, axis):
        size = value.shape[axis] // 2
        low_half = lax.slice_in_dim(value, 0, size, axis=axis)
        high_half = lax.slice_in_dim(value, size, 2 * size, axis=axis)
        return jnp.where(which == 0, low_half, high_half)

    bounds = jnp.cumsum(seq_lengths)
    starts = bounds - seq_lengths

    def layout(blocks):
        natural = (blocks[:, None] * rows + jnp.arange(rows, dtype=jnp.int32)[None, :]).reshape(-1)
        member = (natural[:, None] >= starts[None, :]) & (natural[:, None] < bounds[None, :])
        return natural, jnp.sum(jnp.where(member, starts[None, :], 0), axis=1)

    back_steps = jnp.arange(layers, dtype=jnp.int32)
    owners = jnp.concatenate(
        [((layer - back_steps) % layers) * SQUARE + (corner ^ m) for m in range(SQUARE)]
    )
    row_natural, row_start = layout(block_slots[2 * owners + core])
    far_natural, _ = layout(block_slots[2 * owners + 1 - core])
    key_natural = jnp.concatenate([row_natural, far_natural])[None, :]
    row_cos, row_sin = angles(row_natural - row_start)
    own_cos, own_sin = row_cos[:rows], row_sin[:rows]
    live = len(squares) * layers * rows
    q_cos, q_sin = row_cos[:live], row_sin[:live]
    q_natural, q_start = row_natural[:live, None], row_start[:live, None]

    gain_rows = attn_gain.astype(F32)[:, None]
    down = jnp.concatenate([w_qdown, w_kv], axis=1)
    down_scaled = (down.astype(F32) * gain_rows).astype(BF16)
    columns = down.shape[1] // 2
    down_own = half_of(down_scaled, core, 1)

    def put(parts, indices):
        stacked = jnp.zeros((len(parts),) + parts[0].shape, parts[0].dtype)
        for part, index in zip(parts, indices):
            stacked = lax.dynamic_update_index_in_dim(stacked, part, index, 0)
        return stacked

    down_line = put(
        [down_own] + [along(down_own, k) for k in range(1, layers)],
        [(layer - k) % layers for k in range(layers)],
    )
    down_full = put(
        [down_line] + [within(down_line, m) for m in range(1, SQUARE)],
        [corner ^ m for m in range(SQUARE)],
    ).reshape(width, columns)

    def to_placed(value):
        shaped = value.reshape(value.shape[0], layers, SQUARE, lanes)
        return jnp.swapaxes(shaped, 1, 2).reshape(value.shape[0], width)

    def from_placed(value):
        shaped = value.reshape(value.shape[0], SQUARE, layers, lanes)
        return jnp.swapaxes(shaped, 1, 2).reshape(value.shape[0], width)

    inputs = tokens.astype(F32)
    x_inverse = inverse_rms(inputs)
    x_hat = inputs * x_inverse
    x_low = to_placed(x_hat.astype(BF16))

    q_gain_rows = q_gain.astype(F32)[:, None]
    mlp_gain_rows = mlp_gain.astype(F32)[:, None]
    gate_up = jnp.concatenate([w_gate, w_up], axis=1)
    gate_up_scaled = (gate_up.astype(F32) * mlp_gain_rows).astype(BF16).T
    mlp_out = jnp.concatenate([gate_up_scaled, w_down]).reshape(3, chips, units, lanes)
    mlp_out = jnp.swapaxes(mlp_out, 0, 1).reshape(chips, 3 * units, lanes)

    qup_scaled = (w_qup.astype(F32) * q_gain_rows).astype(BF16)
    qup_heads = qup_scaled.reshape(rank_rows, heads_half, 2, half)
    qup_heads = jnp.transpose(qup_heads, (2, 1, 0, 3))
    out_heads = jnp.swapaxes(w_out.reshape(heads_half, 2, half, lanes), 0, 1)

    def of_core(value, which):
        return lax.dynamic_index_in_dim(value, which, 0, keepdims=False)

    qup_mine = both(of_core(qup_heads, core), across(of_core(qup_heads, 1 - core)))
    out_mine = both(of_core(out_heads, core), across(of_core(out_heads, 1 - core)))
    attn_out = jnp.concatenate(
        [qup_mine.reshape(heads, -1, lanes), out_mine.reshape(heads, -1, lanes)], axis=1
    )
    attn_out = jnp.repeat(attn_out, sharing, axis=0)

    def exchange(value):
        return lax.all_to_all(value, "seq", 0, 0, tiled=True)

    attn_in = exchange(attn_out)
    qup_size = rank_rows * half // lanes
    qup_half = attn_in[:, :qup_size].reshape(rank, half)
    out_half = jnp.swapaxes(attn_in[:, qup_size:], 0, 1).reshape(half, width)
    qup_head = both(qup_half, across(qup_half), axis=1)
    out_head = both(out_half, across(out_half), axis=0)

    mlp_in = jnp.swapaxes(exchange(mlp_out), 0, 1).reshape(3, units, width)
    mlp_far = across(mlp_in)
    gate_up_units = jnp.concatenate([mlp_in[0], mlp_far[0], mlp_in[1], mlp_far[1]])
    down_units = jnp.concatenate([mlp_in[2], mlp_far[2]])

    cot_own = own(cotangent)
    cot_pieces = gather(cot_own)

    part = matmul(x_low, down_full)
    mine, theirs = own(part), across(others(part))
    projected = both(mine, theirs, axis=1)
    q_lat, kv_pre = projected[:, :rank], projected[:, rank:]
    lat_inverse = inverse_rms(q_lat)
    lat_hat = q_lat * lat_inverse
    kv_own = jnp.concatenate([rotate(kv_pre[:, :HEAD], own_cos, own_sin), kv_pre[:, HEAD:]], axis=1)
    latent_pieces = gather(jnp.concatenate([lat_hat, kv_own], axis=1).astype(BF16))
    lat_all = jnp.concatenate([latent_pieces[m][..., :rank] for m in squares]).reshape(live, rank)
    kv_near = jnp.concatenate([piece[..., rank:] for piece in latent_pieces])
    kv_near = kv_near.reshape(-1, 2 * HEAD)
    kv_all = jnp.concatenate([kv_near, across(kv_near)])

    queries = rotate(matmul(lat_all, qup_head), q_cos, q_sin).astype(BF16)
    queries = queries * jnp.asarray(HEAD**-0.5, BF16)
    block = max(64, min(256, 256 * 2048 // kv_all.shape[0]))
    attn_mix, log_total = attend(queries, q_natural, q_start, kv_all, key_natural, block)
    o_low = attn_mix.astype(BF16)

    def cut(value):
        return value.reshape(len(squares), layers, rows, value.shape[-1])

    attn_pieces = cut(matmul(o_low, out_head).astype(BF16))
    hidden = own(inputs) + scatter([attn_pieces[m] for m in squares])
    h_inverse = inverse_rms(hidden)
    h_hat = hidden * h_inverse

    piece_rows = layers * rows
    h_pieces = [piece.reshape(piece_rows, width) for piece in gather(h_hat.astype(BF16))]
    cot_pieces = [piece.reshape(piece_rows, width) for piece in cot_pieces]
    chip_units = 2 * units
    mlp_parts, d_h_parts, act_parts, d_gate_up_parts = [], [], [], []
    for h_piece, cot_piece in zip(h_pieces, cot_pieces):
        d_act = times_transposed(cot_piece, down_units)
        both_act = times_transposed(h_piece, gate_up_units)
        gate_act, up_proj = both_act[:, :chip_units], both_act[:, chip_units:]
        sigmoid_gate = jax.nn.sigmoid(gate_act)
        silu_gate = gate_act * sigmoid_gate
        act = (silu_gate * up_proj).astype(BF16)
        d_gate = d_act * up_proj * sigmoid_gate * (1.0 + gate_act * (1.0 - sigmoid_gate))
        d_up = d_act * silu_gate
        d_gate_up = jnp.concatenate([d_gate, d_up], axis=1).astype(BF16)
        d_h_parts.append(matmul(d_gate_up, gate_up_units).astype(BF16).reshape(layers, rows, width))
        mlp_parts.append(matmul(act, down_units).astype(BF16).reshape(layers, rows, width))
        act_parts.append(act)
        d_gate_up_parts.append(d_gate_up)
    d_hscaled = scatter(d_h_parts)
    layer_own = (hidden + scatter(mlp_parts)).astype(BF16)
    layer_out = both(layer_own, across(layer_own))

    out_grad = cot_own.astype(F32)
    d_hidden = out_grad + norm_back(d_hscaled, h_hat, h_inverse)
    d_attn = d_hidden.astype(BF16)
    d_attn_pieces = gather(d_attn, squares)

    h_all, cot_all = jnp.concatenate(h_pieces), jnp.concatenate(cot_pieces)
    grad_gate_up = contract_rows(jnp.concatenate(d_gate_up_parts), h_all)
    grad_down = contract_rows(jnp.concatenate(act_parts), cot_all)
    mlp_grads = jnp.concatenate([grad_gate_up, grad_down]).reshape(3, 2, units, width)
    mlp_sum = mlp_grads[:, 0] + across(mlp_grads[:, 1].astype(BF16)).astype(F32)
    mlp_sum = mlp_sum.astype(BF16).reshape(3 * units, chips, lanes)
    mlp_back = exchange(jnp.swapaxes(mlp_sum, 0, 1))
    mlp_back = jnp.swapaxes(mlp_back.reshape(chips, 3, units, lanes), 0, 1).astype(F32)
    mlp_back = mlp_back.reshape(3, chips * units, lanes)
    gate_up_back = mlp_back[:2].reshape(2 * chips * units, lanes).T
    gate_up_grad = gate_up_back * mlp_gain_rows
    mlp_gain_part = jnp.sum(gate_up_back * gate_up.astype(F32), axis=1)
    gate_part = gate_up_grad[:, : chips * units]
    up_part = gate_up_grad[:, chips * units :]
    down_part = mlp_back[2]

    d_attn_all = jnp.concatenate(d_attn_pieces).reshape(live, width)
    grad_out = contract_rows(o_low, d_attn_all)
    d_o = times_transposed(d_attn_all, out_head).astype(BF16)
    d_query, d_kv = attend_back(
        queries, q_natural, q_start, kv_all, key_natural, attn_mix, log_total, d_o, block
    )
    d_qpre = unrotate(d_query, q_cos, q_sin).astype(BF16)
    grad_qup = contract_rows(lat_all, d_qpre)
    d_lat_pieces = cut(times_transposed(d_qpre, qup_head).astype(BF16))
    near = SQUARE * layers * rows
    d_kv_near = d_kv[:near] + across(d_kv[near:].astype(BF16)).astype(F32)
    d_kv_pieces = d_kv_near.astype(BF16).reshape(SQUARE, layers, rows, 2 * HEAD)
    if len(squares) == SQUARE:
        d_latent = scatter(
            [jnp.concatenate([d_lat_pieces[m], d_kv_pieces[m]], axis=-1) for m in squares]
        )
        d_lat_scaled, d_kv_own = d_latent[:, :rank], d_latent[:, rank:]
    else:
        d_lat_scaled = scatter([d_lat_pieces[m] for m in squares])
        d_kv_own = scatter([d_kv_pieces[m] for m in range(SQUARE)])
    d_lat = norm_back(d_lat_scaled, lat_hat, lat_inverse)
    d_kvpre = jnp.concatenate([unrotate(d_kv_own[:, :HEAD], own_cos, own_sin), d_kv_own[:, HEAD:]], axis=1)
    d_down = jnp.concatenate([d_lat, d_kvpre], axis=1).astype(BF16)

    d_columns = both(half_of(d_down, core, 1), across(half_of(d_down, 1 - core, 1)))
    d_x_part = times_transposed(d_columns, down_full)
    d_xscaled = from_placed(own(d_x_part) + across(others(d_x_part)))
    x_hat_own, x_inverse_own = own(x_hat), own(x_inverse)
    token_own = (d_hidden + norm_back(d_xscaled, x_hat_own, x_inverse_own)).astype(BF16)
    token_grad = both(token_own, across(token_own))

    grad_down_in = contract_rows(x_low, d_columns).astype(BF16)
    grad_down_in = grad_down_in.reshape(SQUARE, layers, lanes, columns)
    down_pieces = [lax.dynamic_index_in_dim(grad_down_in, corner ^ m, 0, keepdims=False) for m in range(SQUARE)]
    total = sum(
        (piece if m == 0 else within(piece, m)).astype(F32) for m, piece in enumerate(down_pieces)
    )
    low = total.astype(BF16)

    def level(value, k):
        return lax.dynamic_index_in_dim(value, (layer - k) % layers, 0, keepdims=False)

    down_half = level(total, 0) + sum(along(level(low, k), -k).astype(F32) for k in range(1, layers))
    down_sum = both(down_half, across(down_half), axis=1)
    attn_gain_part = jnp.sum(down_sum * down.astype(F32), axis=1)
    down_grad = down_sum * gain_rows
    qdown_part, kv_part = down_grad[:, :rank], down_grad[:, rank:]

    qup_sum = half_of(grad_qup, core, 1) + across(half_of(grad_qup, 1 - core, 1).astype(BF16)).astype(F32)
    out_sum = half_of(grad_out, core, 0) + across(half_of(grad_out, 1 - core, 0).astype(BF16)).astype(F32)
    qup_send = qup_sum.astype(BF16).reshape(chips, -1, lanes)
    out_send = jnp.swapaxes(out_sum.astype(BF16).reshape(half, chips, lanes), 0, 1)
    attn_back = exchange(jnp.concatenate([qup_send, out_send], axis=1))
    attn_back = attn_back.reshape(heads, sharing, -1, lanes)
    if sharing > 1:
        attn_back = jnp.sum(attn_back.astype(F32), axis=1).astype(BF16)
    attn_back = attn_back.reshape(2, heads_half, -1, lanes)
    attn_near, attn_far = of_core(attn_back, core), across(of_core(attn_back, 1 - core))
    attn_grads = jnp.stack([jnp.where(first, attn_near, attn_far), jnp.where(first, attn_far, attn_near)])
    attn_grads = attn_grads.astype(F32)
    qup_back = attn_grads[:, :, :qup_size].reshape(2, heads_half, rank_rows, half)
    qup_back = jnp.transpose(qup_back, (2, 1, 0, 3)).reshape(rank_rows, heads_half * HEAD)
    out_part = jnp.swapaxes(attn_grads[:, :, qup_size:], 0, 1).reshape(heads_half * HEAD, lanes)
    qup_part = qup_back * q_gain_rows
    q_gain_half = jnp.sum(qup_back * w_qup.astype(F32), axis=1)
    gain_parts = jnp.concatenate([q_gain_half, mlp_gain_part])
    gain_parts = gain_parts + across(gain_parts)
    q_gain_part, mlp_gain_part = gain_parts[:rank_rows], gain_parts[rank_rows:]
    return (
        layer_out,
        token_grad,
        attn_gain_part,
        q_gain_part,
        qdown_part,
        qup_part,
        kv_part,
        out_part,
        mlp_gain_part,
        gate_part,
        up_part,
        down_part,
    )


def solution(mesh):
    in_specs = (
        P("seq", None),
        P("seq"),
        P("seq"),
        P("seq", None),
        P("seq", "tp"),
        P("seq", None),
        P("tp", "seq"),
        P("seq"),
        P("seq", "tp"),
        P("seq", "tp"),
        P("tp", "seq"),
        P("seq", None),
        P(),
        P(),
    )
    out_specs = (
        P("seq", None),
        P("seq", None),
        P("seq"),
        P("seq"),
        P("seq", None),
        P("seq", "tp"),
        P("seq", None),
        P("tp", "seq"),
        P("seq"),
        P("seq", "tp"),
        P("seq", "tp"),
        P("tp", "seq"),
    )
    body = functools.partial(local, mesh.shape["seq"])
    return jax.shard_map(body, mesh=mesh, in_specs=in_specs, out_specs=out_specs, check_vma=False)
```

time: 3430 us -> 785 us (0.23)
  waiting for transfers between devices: 2990 us -> 436 us
  blocking collectives: 199 us -> 0 us
  matrix products: 156 us -> 35.8 us
  starting transfers between devices: 1.4 us -> 113 us
  local copies, waits for them, and re-layouts: 27.6 us -> 89.1 us
  other arithmetic: 23.5 us -> 71.4 us
    reduce_scatter x8 -> x0, waiting for transfers between devices: 2200 us -> none  [the longest x1 483 us: local(): lax.psum_scatter(grad_down, 'seq', scatter_dimension=1, tiled=True)]
    all_gather x8 -> x0, waiting for transfers between devices: 752 us -> none  [the longest x1 177 us: local(): lax.all_gather(w_down, 'seq', axis=1, tiled=True)]
    ppermute x0 -> x78, waiting for transfers between devices: none -> 421 us  [the longest x30 297 us: within(): return lax.ppermute(value, 'seq', [(i, i ^ flip) for i in range(chips)])]
    unnamed x2 -> x0, blocking collectives: 118 us -> none
    ppermute x0 -> x78, starting transfers between devices: none -> 93 us  [the longest x30 53.5 us: along(): return lax.ppermute(value, 'seq', pairs)]
    all_gather x2 -> x0, blocking collectives: 80.6 us -> none  [the longest x1 42.4 us: local(): lax.all_gather(attn_gain, 'seq', axis=0, tiled=True)]
    dot_general x19 -> x11, matrix products: 67.7 us -> 11.9 us  [matmul(): return jnp.dot(left, right, preferred_element_type=F32)]
    dot_general x7 -> x5, matrix products: 48.9 us -> 11.2 us  [contract_rows(): lax.dot_general(left, right, (((0,), (0,)), ((), ())), preferred_element_...]
  transfers between devices with their start and end apart: 19 -> 82, of which waited for: 18 -> 40; matrix products, arithmetic and copies ran while one was open for 3% -> 22% of each run, Pallas kernels for 0% -> 1%
where the time goes in v1:
time: 785 us; the launch traced here: 774 us
  waiting for transfers between devices  436 us (56%)
  starting transfers between devices  113 us (14%)
  local copies, waits for them, and re-layouts  89.1 us (11%)
  other arithmetic  71.4 us (9%)
  matrix products  35.8 us (5%)
  Pallas kernels  24.9 us (3%)
    ppermute x30, waiting for transfers between devices, within(): return lax.ppermute(value, 'seq', [(i, i ^ flip) for i in range(chips)])  297 us
    ppermute x30, waiting for transfers between devices, along(): return lax.ppermute(value, 'seq', pairs)  122 us
    ppermute x30, starting transfers between devices, along(): return lax.ppermute(value, 'seq', pairs)  53.5 us
    ppermute x30, starting transfers between devices, within(): return lax.ppermute(value, 'seq', [(i, i ^ flip) for i in range(chips)])  36.1 us
    all_to_all x4, starting transfers between devices, exchange(): return lax.all_to_all(value, 'seq', 0, 0, tiled=True)  20 us
    unnamed x182, local copies, waits for them, and re-layouts  17.3 us
  transfers between devices with their start and end apart: 82, of which 40 were waited for; matrix products, arithmetic and copies ran while one was open for 22% of the time, Pallas kernels for 1%

profile of v1, /device:TPU:0, one launch (start us, length us, event | category | flops | bytes accessed | tf_op | source)
XLA Modules:
  0.0 773.8 jit_solution(9608001964330875155)
XLA Ops:
  43.8 9.7 %collective-permute-done.3 = bf16[4,128,768]{2,1,0:T(8,128)(2,1)} collective-permute-done((bf16[4,128,768]{2,1,0:T(8,128)(2,1)}, bf16[4,128,768]{2,1,0:T(8,128)(2,1)}, u32[]{:S(2)}, u32[]{:S(2)}) %collective-permute-start.3) | collective-permute-done | bytes 786464 | tf_op jit(solution)/shard_map/ppermute | solution.py:193
  54.7 16.0 %collective-permute-done.4 = bf16[4,128,768]{2,1,0:T(8,128)(2,1)} collective-permute-done((bf16[4,128,768]{2,1,0:T(8,128)(2,1)}, bf16[4,128,768]{2,1,0:T(8,128)(2,1)}, u32[]{:S(2)}, u32[]{:S(2)}) %collective-permute-start.4) | collective-permute-done | bytes 786464 | tf_op jit(solution)/shard_map/ppermute | solution.py:193
  86.3 13.0 %collective-permute-done.9 = bf16[64,1536]{1,0:T(8,128)(2,1)S(1)} collective-permute-done((bf16[64,1536]{1,0:T(8,128)(2,1)S(1)}, bf16[64,1536]{1,0:T(8,128)(2,1)S(1)}, u32[]{:S(2)}, u32[]{:S(2)}) %collective-permute-start.9) | collective-permute-done | bytes 196640 | tf_op jit(solution)/shard_map/ppermute | solution.py:190
  99.3 17.9 %collective-permute-done.8 = bf16[64,1536]{1,0:T(8,128)(2,1)S(1)} collective-permute-done((bf16[64,1536]{1,0:T(8,128)(2,1)S(1)}, bf16[64,1536]{1,0:T(8,128)(2,1)S(1)}, u32[]{:S(2)}, u32[]{:S(2)}) %collective-permute-start.8) | collective-permute-done | bytes 196640 | tf_op jit(solution)/shard_map/ppermute | solution.py:190
  133.3 9.2 %collective-permute-done.12 = bf16[4,64,1536]{2,1,0:T(8,128)(2,1)} collective-permute-done((bf16[4,64,1536]{2,1,0:T(8,128)(2,1)}, bf16[4,64,1536]{2,1,0:T(8,128)(2,1)}, u32[]{:S(2)}, u32[]{:S(2)}) %collective-permute-start.12) | collective-permute-done | bytes 786464 | tf_op jit(solution)/shard_map/ppermute | solution.py:193
  143.5 26.7 %collective-permute-done.11 = bf16[4,64,1536]{2,1,0:T(8,128)(2,1)} collective-permute-done((bf16[4,64,1536]{2,1,0:T(8,128)(2,1)}, bf16[4,64,1536]{2,1,0:T(8,128)(2,1)}, u32[]{:S(2)}, u32[]{:S(2)}) %collective-permute-start.11) | collective-permute-done | bytes 786464 | tf_op jit(solution)/shard_map/ppermute | solution.py:193
  187.6 9.8 %attend.1 = (f32[1024,256]{1,0:T(8,128)}, f32[1024,1]{1,0:T(8,128)}) custom-call(bf16[1024,256]{1,0:T(8,128)(2,1)} %maximum_multiply_fusion.q_ref, s32[1024,1]{1,0:T(8,128)} %add.546.natural_ref, s32[1024,1]{1,0:T(8,128)} %copy.294.start_ref, bf16[2048,512]{1,0:T(8,128)(2,1)} %pad_maximum_fusion.4.kv_ref, s32[1,2048]{1,0:T(1,128)} %bitcast.379), custom_call_target="tpu_custom_call" | custom-call | flops 2147483648 | bytes 2097152 | tf_op jit(solution)/shard_map/attend/pallas_call | solution.py:80
  206.4 9.5 %collective-permute-done.40 = bf16[64,2048]{1,0:T(8,128)(2,1)} collective-permute-done((bf16[64,2048]{1,0:T(8,128)(2,1)}, bf16[64,2048]{1,0:T(8,128)(2,1)}, u32[]{:S(2)}, u32[]{:S(2)}) %collective-permute-start.40) | collective-permute-done | bytes 262176 | tf_op jit(solution)/shard_map/ppermute | solution.py:190
  220.5 9.5 %collective-permute-done.39 = bf16[64,2048]{1,0:T(8,128)(2,1)} collective-permute-done((bf16[64,2048]{1,0:T(8,128)(2,1)}, bf16[64,2048]{1,0:T(8,128)(2,1)}, u32[]{:S(2)}, u32[]{:S(2)}) %collective-permute-start.39) | collective-permute-done | bytes 262176 | tf_op jit(solution)/shard_map/ppermute | solution.py:190
  241.7 10.0 %collective-permute-done.19 = bf16[4,64,2048]{2,1,0:T(8,128)(2,1)} collective-permute-done((bf16[4,64,2048]{2,1,0:T(8,128)(2,1)}, bf16[4,64,2048]{2,1,0:T(8,128)(2,1)}, u32[]{:S(2)}, u32[]{:S(2)}) %collective-permute-start.19) | collective-permute-done | bytes 1048608 | tf_op jit(solution)/shard_map/ppermute | solution.py:193
  265.9 10.3 %collective-permute-done.22 = bf16[64,2048]{1,0:T(8,128)(2,1)S(1)} collective-permute-done((bf16[64,2048]{1,0:T(8,128)(2,1)S(1)}, bf16[64,2048]{1,0:T(8,128)(2,1)S(1)}, u32[]{:S(2)}, u32[]{:S(2)}) %collective-permute-start.22) | collective-permute-done | bytes 262176 | tf_op jit(solution)/shard_map/ppermute | solution.py:190
  288.7 16.9 %collective-permute-done.25 = bf16[64,2048]{1,0:T(8,128)(2,1)S(1)} collective-permute-done((bf16[64,2048]{1,0:T(8,128)(2,1)S(1)}, bf16[64,2048]{1,0:T(8,128)(2,1)S(1)}, u32[]{:S(2)}, u32[]{:S(2)}) %collective-permute-start.25) | collective-permute-done | bytes 262176 | tf_op jit(solution)/shard_map/ppermute | solution.py:190
  310.7 40.3 %collective-permute-done.32 = bf16[4,64,2048]{2,1,0:T(8,128)(2,1)S(1)} collective-permute-done((bf16[4,64,2048]{2,1,0:T(8,128)(2,1)S(1)}, bf16[4,64,2048]{2,1,0:T(8,128)(2,1)S(1)}, u32[]{:S(2)}, u32[]{:S(2)}) %collective-permute-start.32) | collective-permute-done | bytes 1048608 | tf_op jit(solution)/shard_map/ppermute | solution.py:193
  362.1 15.1 %collective-permute-done.28 = bf16[4,64,2048]{2,1,0:T(8,128)(2,1)S(1)} collective-permute-done((bf16[4,64,2048]{2,1,0:T(8,128)(2,1)S(1)}, bf16[4,64,2048]{2,1,0:T(8,128)(2,1)S(1)}, u32[]{:S(2)}, u32[]{:S(2)}) %collective-permute-start.28) | collective-permute-done | bytes 1048608 | tf_op jit(solution)/shard_map/ppermute | solution.py:193
  401.9 8.7 %collective-permute-done.44 = bf16[4,64,2048]{2,1,0:T(8,128)(2,1)S(1)} collective-permute-done((bf16[4,64,2048]{2,1,0:T(8,128)(2,1)S(1)}, bf16[4,64,2048]{2,1,0:T(8,128)(2,1)S(1)}, u32[]{:S(2)}, u32[]{:S(2)}) %collective-permute-start.44) | collective-permute-done | bytes 1048608 | tf_op jit(solution)/shard_map/ppermute | solution.py:193
  410.6 11.5 %collective-permute-done.42 = bf16[4,64,2048]{2,1,0:T(8,128)(2,1)S(1)} collective-permute-done((bf16[4,64,2048]{2,1,0:T(8,128)(2,1)}, bf16[4,64,2048]{2,1,0:T(8,128)(2,1)S(1)}, u32[]{:S(2)}, u32[]{:S(2)}) %collective-permute-start.42) | collective-permute-done | bytes 1048608 | tf_op jit(solution)/shard_map/ppermute | solution.py:193
  429.2 17.7 %collective-permute-done.33 = bf16[4,64,2048]{2,1,0:T(8,128)(2,1)S(1)} collective-permute-done((bf16[4,64,2048]{2,1,0:T(8,128)(2,1)S(1)}, bf16[4,64,2048]{2,1,0:T(8,128)(2,1)S(1)}, u32[]{:S(2)}, u32[]{:S(2)}) %collective-permute-start.33) | collective-permute-done | bytes 1048608 | tf_op jit(solution)/shard_map/ppermute | solution.py:193
  450.6 13.6 %collective-permute-done.29 = bf16[4,64,2048]{2,1,0:T(8,128)(2,1)S(1)} collective-permute-done((bf16[4,64,2048]{2,1,0:T(8,128)(2,1)S(1)}, bf16[4,64,2048]{2,1,0:T(8,128)(2,1)S(1)}, u32[]{:S(2)}, u32[]{:S(2)}) %collective-permute-start.29) | collective-permute-done | bytes 1048608 | tf_op jit(solution)/shard_map/ppermute | solution.py:193
  470.9 6.7 pad_maximum_fusion
  478.5 7.5 collective-permute-done.35
  502.4 8.8 %collective-permute-done.51 = bf16[64,2048]{1,0:T(8,128)(2,1)S(1)} collective-permute-done((bf16[64,2048]{1,0:T(8,128)(2,1)S(1)}, bf16[64,2048]{1,0:T(8,128)(2,1)S(1)}, u32[]{:S(2)}, u32[]{:S(2)}) %collective-permute-start.51) | collective-permute-done | bytes 262176 | tf_op jit(solution)/shard_map/ppermute | solution.py:190
  519.7 18.3 %collective-permute-done.53 = bf16[4,64,2048]{2,1,0:T(8,128)(2,1)S(1)} collective-permute-done((bf16[4,64,2048]{2,1,0:T(8,128)(2,1)S(1)}, bf16[4,64,2048]{2,1,0:T(8,128)(2,1)S(1)}, u32[]{:S(2)}, u32[]{:S(2)}) %collective-permute-start.53) | collective-permute-done | bytes 1048608 | tf_op jit(solution)/shard_map/ppermute | solution.py:193
  538.1 20.9 %collective-permute-done.54 = bf16[4,64,2048]{2,1,0:T(8,128)(2,1)S(1)} collective-permute-done((bf16[4,64,2048]{2,1,0:T(8,128)(2,1)S(1)}, bf16[4,64,2048]{2,1,0:T(8,128)(2,1)S(1)}, u32[]{:S(2)}, u32[]{:S(2)}) %collective-permute-start.54) | collective-permute-done | bytes 1048608 | tf_op jit(solution)/shard_map/ppermute | solution.py:193
  561.3 15.1 %attend_back.1 = (f32[1024,256]{1,0:T(8,128)}, f32[2048,512]{1,0:T(8,128)}) custom-call(bf16[1024,256]{1,0:T(8,128)(2,1)} %maximum_multiply_fusion.q_ref, s32[1024,1]{1,0:T(8,128)} %add.546.natural_ref, s32[1024,1]{1,0:T(8,128)} %copy.294.start_ref, bf16[2048,512]{1,0:T(8,128)(2,1)} %pad_maximum_fusion.4.kv_ref, s32[1,2048]{1,0:T(1,128)} %bitcast.380, ...), custom_call_target="tpu_custom_call" | custom-call | flops 5368709120 | bytes 6291456 | tf_op jit(solution)/shard_map/attend_back/pallas_call | solution.py:122
  592.6 15.8 %collective-permute-done.59 = bf16[4,64,1536]{2,1,0:T(8,128)(2,1)S(1)} collective-permute-done((bf16[4,64,1536]{2,1,0:T(8,128)(2,1)S(1)}, bf16[4,64,1536]{2,1,0:T(8,128)(2,1)S(1)}, u32[]{:S(2)}, u32[]{:S(2)}) %collective-permute-start.59) | collective-permute-done | bytes 786464 | tf_op jit(solution)/shard_map/ppermute | solution.py:193
  608.4 16.4 %collective-permute-done.58 = bf16[4,64,1536]{2,1,0:T(8,128)(2,1)S(1)} collective-permute-done((bf16[4,64,1536]{2,1,0:T(8,128)(2,1)S(1)}, bf16[4,64,1536]{2,1,0:T(8,128)(2,1)S(1)}, u32[]{:S(2)}, u32[]{:S(2)}) %collective-permute-start.58) | collective-permute-done | bytes 786464 | tf_op jit(solution)/shard_map/ppermute | solution.py:193
  641.4 8.0 %collective-permute-done.61 = bf16[64,1536]{1,0:T(8,128)(2,1)} collective-permute-done((bf16[64,1536]{1,0:T(8,128)(2,1)}, bf16[64,1536]{1,0:T(8,128)(2,1)}, u32[]{:S(2)}, u32[]{:S(2)}) %collective-permute-start.61) | collective-permute-done | bytes 196640 | tf_op jit(solution)/shard_map/ppermute | solution.py:190
  652.7 15.1 %all-to-all-done.2 = bf16[16,192,128]{2,1,0:T(8,128)(2,1)} async-done(((bf16[16,192,128]{2,1,0:T(8,128)(2,1)}), bf16[16,192,128]{2,1,0:T(8,128)(2,1)}, u32[]{:S(2)}, u32[]{:S(2)}) %all-to-all-start.2) | async-done | bytes 786464 | tf_op jit(solution)/shard_map/all_to_all | solution.py:301
  667.8 6.5 all-to-all-start.3
  701.2 23.7 %collective-permute-done.68 = bf16[4,128,768]{2,1,0:T(8,128)(2,1)} collective-permute-done((bf16[4,128,768]{2,1,0:T(8,128)(2,1)}, bf16[4,128,768]{2,1,0:T(8,128)(2,1)}, u32[]{:S(2)}, u32[]{:S(2)}) %collective-permute-start.68) | collective-permute-done | bytes 786464 | tf_op jit(solution)/shard_map/ppermute | solution.py:193
  724.9 8.5 %collective-permute-done.67 = bf16[4,128,768]{2,1,0:T(8,128)(2,1)} collective-permute-done((bf16[4,128,768]{2,1,0:T(8,128)(2,1)}, bf16[4,128,768]{2,1,0:T(8,128)(2,1)}, u32[]{:S(2)}, u32[]{:S(2)}) %collective-permute-start.67) | collective-permute-done | bytes 786464 | tf_op jit(solution)/shard_map/ppermute | solution.py:193
  751.7 7.3 collective-permute-done.70
  (514 shorter events, 326.9 us)
Async XLA Ops:
  12.6 61.5 %collective-permute-start.14 = (bf16[8,128,128]{2,1,0:T(8,128)(2,1)}, bf16[8,128,128]{2,1,0:T(8,128)(2,1)S(1)}, u32[]{:S(2)}, u32[]{:S(2)}) collective-permute-start(bf16[8,128,128]{2,1,0:T(8,128)(2,1)} %dynamic-slice_bitcast_fusion.4), channel_id=1, source_target_pairs={{0,1},{1,0},{2,3},{3,2},{4,5},{5,4},{6,7},{7,6},{8,9},{9,8},{10,11... | collective-permute-start | bytes 786440 | tf_op jit(solution)/shard_map/ppermute | solution.py:182
  34.3 36.4 %collective-permute-start.4 = (bf16[4,128,768]{2,1,0:T(8,128)(2,1)}, bf16[4,128,768]{2,1,0:T(8,128)(2,1)}, u32[]{:S(2)}, u32[]{:S(2)}) collective-permute-start(bf16[4,128,768]{2,1,0:T(8,128)(2,1)} %bitcast_dynamic-update-slice_fusion.4), channel_id=1, source_target_pairs={{0,4},{2,6},{4,0},{6,2},{8,12},{10,14},{12,8},{14,10},{16,20},{18,... | collective-permute-start | bytes 2359304 | tf_op jit(solution)/shard_map/ppermute | solution.py:193
  75.1 50.6 %all-to-all-start = ((bf16[16,192,128]{2,1,0:T(8,128)(2,1)}), bf16[16,192,128]{2,1,0:T(8,128)(2,1)}, u32[]{:S(2)}, u32[]{:S(2)}) async-start(bf16[16,192,128]{2,1,0:T(8,128)(2,1)} %maximum_maximum_fusion), calls=%async_computation | async-start | bytes 1572864 | tf_op jit(solution)/shard_map/all_to_all | solution.py:301
  120.6 49.5 %collective-permute-start.11 = (bf16[4,64,1536]{2,1,0:T(8,128)(2,1)}, bf16[4,64,1536]{2,1,0:T(8,128)(2,1)}, u32[]{:S(2)}, u32[]{:S(2)}) collective-permute-start(bf16[4,64,1536]{2,1,0:T(8,128)(2,1)} %pad_maximum_fusion.12), channel_id=1, source_target_pairs={{0,4},{2,6},{4,0},{6,2},{8,12},{10,14},{12,8},{14,10},{16,20},{18,... | collective-permute-start | bytes 2359304 | tf_op jit(solution)/shard_map/ppermute | solution.py:193
  121.0 54.2 %collective-permute-start.10 = (bf16[4,64,1536]{2,1,0:T(8,128)(2,1)}, bf16[4,64,1536]{2,1,0:T(8,128)(2,1)}, u32[]{:S(2)}, u32[]{:S(2)}) collective-permute-start(bf16[4,64,1536]{2,1,0:T(8,128)(2,1)} %pad_maximum_fusion.12), channel_id=1, source_target_pairs={{0,2},{2,0},{4,6},{6,4},{8,10},{10,8},{12,14},{14,12},{16,18},{18,... | collective-permute-start | bytes 2359304 | tf_op jit(solution)/shard_map/ppermute | solution.py:193
  125.7 107.9 %all-to-all-start.1 = ((bf16[16,528,128]{2,1,0:T(8,128)(2,1)}), bf16[16,528,128]{2,1,0:T(8,128)(2,1)}, u32[]{:S(2)}, u32[]{:S(2)}) async-start(bf16[16,528,128]{2,1,0:T(8,128)(2,1)} %bitcast.328), calls=%async_computation.1 | async-start | bytes 4325376 | tf_op jit(solution)/shard_map/all_to_all | solution.py:301
  132.6 52.0 %collective-permute-start.17 = (bf16[128,2048]{1,0:T(8,128)(2,1)S(1)}, bf16[128,2048]{1,0:T(8,128)(2,1)S(1)}, u32[]{:S(2)}, u32[]{:S(2)}) collective-permute-start(bf16[128,2048]{1,0:T(8,128)(2,1)S(1)} %copy_bitcast_fusion.4), channel_id=1, source_target_pairs={{0,1},{1,0},{2,3},{3,2},{4,5},{5,4},{6,7},{7,6},{8,9},{9,8},{10,11... | collective-permute-start | bytes 1572872 | tf_op jit(solution)/shard_map/ppermute | solution.py:182
  202.2 39.6 %collective-permute-start.20 = (bf16[4,64,2048]{2,1,0:T(8,128)(2,1)}, bf16[4,64,2048]{2,1,0:T(8,128)(2,1)}, u32[]{:S(2)}, u32[]{:S(2)}) collective-permute-start(bf16[4,64,2048]{2,1,0:T(8,128)(2,1)} %bitcast.45), channel_id=1, source_target_pairs={{0,6},{2,4},{4,2},{6,0},{8,14},{10,12},{12,10},{14,8},{16,22},{18,... | collective-permute-start | bytes 3145736 | tf_op jit(solution)/shard_map/ppermute | solution.py:193
  204.3 47.4 %collective-permute-start.19 = (bf16[4,64,2048]{2,1,0:T(8,128)(2,1)}, bf16[4,64,2048]{2,1,0:T(8,128)(2,1)}, u32[]{:S(2)}, u32[]{:S(2)}) collective-permute-start(bf16[4,64,2048]{2,1,0:T(8,128)(2,1)} %bitcast.44), channel_id=1, source_target_pairs={{0,4},{2,6},{4,0},{6,2},{8,12},{10,14},{12,8},{14,10},{16,20},{18,... | collective-permute-start | bytes 3145736 | tf_op jit(solution)/shard_map/ppermute | solution.py:193
  204.7 47.0 %collective-permute-start.18 = (bf16[4,64,2048]{2,1,0:T(8,128)(2,1)}, bf16[4,64,2048]{2,1,0:T(8,128)(2,1)}, u32[]{:S(2)}, u32[]{:S(2)}) collective-permute-start(bf16[4,64,2048]{2,1,0:T(8,128)(2,1)} %bitcast.43), channel_id=1, source_target_pairs={{0,2},{2,0},{4,6},{6,4},{8,10},{10,8},{12,14},{14,12},{16,18},{18,... | collective-permute-start | bytes 3145736 | tf_op jit(solution)/shard_map/ppermute | solution.py:193
  232.2 121.5 %collective-permute-start.45 = (bf16[4,64,2048]{2,1,0:T(8,128)(2,1)}, bf16[4,64,2048]{2,1,0:T(8,128)(2,1)}, u32[]{:S(2)}, u32[]{:S(2)}) collective-permute-start(bf16[4,64,2048]{2,1,0:T(8,128)(2,1)} %pad_maximum_fusion.10), channel_id=1, source_target_pairs={{0,6},{2,4},{4,2},{6,0},{8,14},{10,12},{12,10},{14,8},{16,22},{18,... | collective-permute-start | bytes 3145736 | tf_op jit(solution)/shard_map/ppermute | solution.py:193
  241.7 65.9 %collective-permute-start.27 = (bf16[3,176,2048]{2,1,0:T(8,128)(2,1)}, bf16[3,176,2048]{2,1,0:T(8,128)(2,1)S(1)}, u32[]{:S(2)}, u32[]{:S(2)}) collective-permute-start(bf16[3,176,2048]{2,1,0:T(8,128)(2,1)} %reshape.481), channel_id=1, source_target_pairs={{0,1},{1,0},{2,3},{3,2},{4,5},{5,4},{6,7},{7,6},{8,9},{9,8},{10,11... | collective-permute-start | bytes 6488072 | tf_op jit(solution)/shard_map/ppermute | solution.py:182
  287.8 72.4 %collective-permute-start.43 = (bf16[4,64,2048]{2,1,0:T(8,128)(2,1)}, bf16[4,64,2048]{2,1,0:T(8,128)(2,1)S(1)}, u32[]{:S(2)}, u32[]{:S(2)}) collective-permute-start(bf16[4,64,2048]{2,1,0:T(8,128)(2,1)} %pad_maximum_fusion.10), channel_id=1, source_target_pairs={{0,4},{2,6},{4,0},{6,2},{8,12},{10,14},{12,8},{14,10},{16,20},{18,... | collective-permute-start | bytes 3145736 | tf_op jit(solution)/shard_map/ppermute | solution.py:193
  305.6 72.5 %collective-permute-start.41 = (bf16[4,64,2048]{2,1,0:T(8,128)(2,1)}, bf16[4,64,2048]{2,1,0:T(8,128)(2,1)S(1)}, u32[]{:S(2)}, u32[]{:S(2)}) collective-permute-start(bf16[4,64,2048]{2,1,0:T(8,128)(2,1)} %pad_maximum_fusion.10), channel_id=1, source_target_pairs={{0,2},{2,0},{4,6},{6,4},{8,10},{10,8},{12,14},{14,12},{16,18},{18,... | collective-permute-start | bytes 3145736 | tf_op jit(solution)/shard_map/ppermute | solution.py:193
  306.4 44.7 %collective-permute-start.32 = (bf16[4,64,2048]{2,1,0:T(8,128)(2,1)S(1)}, bf16[4,64,2048]{2,1,0:T(8,128)(2,1)S(1)}, u32[]{:S(2)}, u32[]{:S(2)}) collective-permute-start(bf16[4,64,2048]{2,1,0:T(8,128)(2,1)S(1)} %pad_maximum_fusion.9), channel_id=1, source_target_pairs={{0,6},{2,4},{4,2},{6,0},{8,14},{10,12},{12,10},{14,8},{16,22},{18,... | collective-permute-start | bytes 3145736 | tf_op jit(solution)/shard_map/ppermute | solution.py:193
  307.6 51.7 %collective-permute-start.30 = (bf16[4,64,2048]{2,1,0:T(8,128)(2,1)S(1)}, bf16[4,64,2048]{2,1,0:T(8,128)(2,1)S(1)}, u32[]{:S(2)}, u32[]{:S(2)}) collective-permute-start(bf16[4,64,2048]{2,1,0:T(8,128)(2,1)S(1)} %pad_maximum_fusion.9), channel_id=1, source_target_pairs={{0,4},{2,6},{4,0},{6,2},{8,12},{10,14},{12,8},{14,10},{16,20},{18,... | collective-permute-start | bytes 3145736 | tf_op jit(solution)/shard_map/ppermute | solution.py:193
  356.6 45.3 %collective-permute-start.46 = (bf16[4,64,2048]{2,1,0:T(8,128)(2,1)S(1)}, bf16[4,64,2048]{2,1,0:T(8,128)(2,1)S(1)}, u32[]{:S(2)}, u32[]{:S(2)}) collective-permute-start(bf16[4,64,2048]{2,1,0:T(8,128)(2,1)S(1)} %bitcast.392), channel_id=1, source_target_pairs={{0,6},{2,4},{4,2},{6,0},{8,14},{10,12},{12,10},{14,8},{16,22},{18,... | collective-permute-start | bytes 3145736 | tf_op jit(solution)/shard_map/ppermute | solution.py:193
  362.0 48.6 %collective-permute-start.44 = (bf16[4,64,2048]{2,1,0:T(8,128)(2,1)S(1)}, bf16[4,64,2048]{2,1,0:T(8,128)(2,1)S(1)}, u32[]{:S(2)}, u32[]{:S(2)}) collective-permute-start(bf16[4,64,2048]{2,1,0:T(8,128)(2,1)S(1)} %bitcast.393), channel_id=1, source_target_pairs={{0,4},{2,6},{4,0},{6,2},{8,12},{10,14},{12,8},{14,10},{16,20},{18,... | collective-permute-start | bytes 3145736 | tf_op jit(solution)/shard_map/ppermute | solution.py:193
  380.7 41.4 %collective-permute-start.42 = (bf16[4,64,2048]{2,1,0:T(8,128)(2,1)}, bf16[4,64,2048]{2,1,0:T(8,128)(2,1)S(1)}, u32[]{:S(2)}, u32[]{:S(2)}) collective-permute-start(bf16[4,64,2048]{2,1,0:T(8,128)(2,1)} %bitcast.81), channel_id=1, source_target_pairs={{0,2},{2,0},{4,6},{6,4},{8,10},{10,8},{12,14},{14,12},{16,18},{18,... | collective-permute-start | bytes 3145736 | tf_op jit(solution)/shard_map/ppermute | solution.py:193
  384.1 62.8 %collective-permute-start.33 = (bf16[4,64,2048]{2,1,0:T(8,128)(2,1)S(1)}, bf16[4,64,2048]{2,1,0:T(8,128)(2,1)S(1)}, u32[]{:S(2)}, u32[]{:S(2)}) collective-permute-start(bf16[4,64,2048]{2,1,0:T(8,128)(2,1)S(1)} %bitcast.357), channel_id=1, source_target_pairs={{0,6},{2,4},{4,2},{6,0},{8,14},{10,12},{12,10},{14,8},{16,22},{18,... | collective-permute-start | bytes 3145736 | tf_op jit(solution)/shard_map/ppermute | solution.py:193
  387.6 63.0 %collective-permute-start.31 = (bf16[4,64,2048]{2,1,0:T(8,128)(2,1)S(1)}, bf16[4,64,2048]{2,1,0:T(8,128)(2,1)S(1)}, u32[]{:S(2)}, u32[]{:S(2)}) collective-permute-start(bf16[4,64,2048]{2,1,0:T(8,128)(2,1)S(1)} %bitcast.355), channel_id=1, source_target_pairs={{0,4},{2,6},{4,0},{6,2},{8,12},{10,14},{12,8},{14,10},{16,20},{18,... | collective-permute-start | bytes 3145736 | tf_op jit(solution)/shard_map/ppermute | solution.py:193
  401.9 62.2 %collective-permute-start.29 = (bf16[4,64,2048]{2,1,0:T(8,128)(2,1)S(1)}, bf16[4,64,2048]{2,1,0:T(8,128)(2,1)S(1)}, u32[]{:S(2)}, u32[]{:S(2)}) collective-permute-start(bf16[4,64,2048]{2,1,0:T(8,128)(2,1)S(1)} %bitcast.356), channel_id=1, source_target_pairs={{0,2},{2,0},{4,6},{6,4},{8,10},{10,8},{12,14},{14,12},{16,18},{18,... | collective-permute-start | bytes 3145736 | tf_op jit(solution)/shard_map/ppermute | solution.py:193
  425.1 42.0 %collective-permute-start.49 = (bf16[64,2048]{1,0:T(8,128)(2,1)S(1)}, bf16[64,2048]{1,0:T(8,128)(2,1)}, u32[]{:S(2)}, u32[]{:S(2)}) collective-permute-start(bf16[64,2048]{1,0:T(8,128)(2,1)S(1)} %get-tuple-element.155), channel_id=1, source_target_pairs={{0,8},{2,10},{4,12},{6,14},{8,16},{10,18},{12,20},{14,22},{16,24},... | collective-permute-start | bytes 786440 | tf_op jit(solution)/shard_map/ppermute | solution.py:190
  429.2 48.4 %collective-permute-start.48 = (bf16[64,2048]{1,0:T(8,128)(2,1)}, bf16[64,2048]{1,0:T(8,128)(2,1)}, u32[]{:S(2)}, u32[]{:S(2)}) collective-permute-start(bf16[64,2048]{1,0:T(8,128)(2,1)} %get-tuple-element.156), channel_id=1, source_target_pairs={{0,16},{2,18},{4,20},{6,22},{8,24},{10,26},{12,28},{14,30},{16,0},... | collective-permute-start | bytes 786440 | tf_op jit(solution)/shard_map/ppermute | solution.py:190
  512.0 47.0 %collective-permute-start.54 = (bf16[4,64,2048]{2,1,0:T(8,128)(2,1)S(1)}, bf16[4,64,2048]{2,1,0:T(8,128)(2,1)S(1)}, u32[]{:S(2)}, u32[]{:S(2)}) collective-permute-start(bf16[4,64,2048]{2,1,0:T(8,128)(2,1)S(1)} %pad_maximum_fusion.11), channel_id=1, source_target_pairs={{0,4},{2,6},{4,0},{6,2},{8,12},{10,14},{12,8},{14,10},{16,20},{18,... | collective-permute-start | bytes 3145736 | tf_op jit(solution)/shard_map/ppermute | solution.py:193
  512.8 46.3 %collective-permute-start.55 = (bf16[4,64,2048]{2,1,0:T(8,128)(2,1)S(1)}, bf16[4,64,2048]{2,1,0:T(8,128)(2,1)S(1)}, u32[]{:S(2)}, u32[]{:S(2)}) collective-permute-start(bf16[4,64,2048]{2,1,0:T(8,128)(2,1)S(1)} %pad_maximum_fusion.11), channel_id=1, source_target_pairs={{0,6},{2,4},{4,2},{6,0},{8,14},{10,12},{12,10},{14,8},{16,22},{18,... | collective-permute-start | bytes 3145736 | tf_op jit(solution)/shard_map/ppermute | solution.py:193
  588.5 36.2 %collective-permute-start.58 = (bf16[4,64,1536]{2,1,0:T(8,128)(2,1)S(1)}, bf16[4,64,1536]{2,1,0:T(8,128)(2,1)S(1)}, u32[]{:S(2)}, u32[]{:S(2)}) collective-permute-start(bf16[4,64,1536]{2,1,0:T(8,128)(2,1)S(1)} %pad_maximum_fusion.14), channel_id=1, source_target_pairs={{0,4},{2,6},{4,0},{6,2},{8,12},{10,14},{12,8},{14,10},{16,20},{18,... | collective-permute-start | bytes 2359304 | tf_op jit(solution)/shard_map/ppermute | solution.py:193
  591.1 44.7 %collective-permute-start.74 = (bf16[128,2048]{1,0:T(8,128)(2,1)S(1)}, bf16[128,2048]{1,0:T(8,128)(2,1)S(1)}, u32[]{:S(2)}, u32[]{:S(2)}) collective-permute-start(bf16[128,2048]{1,0:T(8,128)(2,1)S(1)} %select_convert_fusion), channel_id=1, source_target_pairs={{0,1},{1,0},{2,3},{3,2},{4,5},{5,4},{6,7},{7,6},{8,9},{9,8},{10,11... | collective-permute-start | bytes 1572872 | tf_op jit(solution)/shard_map/ppermute | solution.py:182
  667.8 95.4 %all-to-all-start.3 = ((bf16[16,528,128]{2,1,0:T(8,128)(2,1)}), bf16[16,528,128]{2,1,0:T(8,128)(2,1)}, u32[]{:S(2)}, u32[]{:S(2)}) async-start(bf16[16,528,128]{2,1,0:T(8,128)(2,1)} %copy.312), calls=%async_computation.3 | async-start | bytes 4325376 | tf_op jit(solution)/shard_map/all_to_all | solution.py:301
  680.6 44.3 %collective-permute-start.68 = (bf16[4,128,768]{2,1,0:T(8,128)(2,1)}, bf16[4,128,768]{2,1,0:T(8,128)(2,1)}, u32[]{:S(2)}, u32[]{:S(2)}) collective-permute-start(bf16[4,128,768]{2,1,0:T(8,128)(2,1)} %get-tuple-element.116), channel_id=1, source_target_pairs={{0,6},{2,4},{4,2},{6,0},{8,14},{10,12},{12,10},{14,8},{16,22},{18,... | collective-permute-start | bytes 2359304 | tf_op jit(solution)/shard_map/ppermute | solution.py:193
  683.5 49.9 %collective-permute-start.67 = (bf16[4,128,768]{2,1,0:T(8,128)(2,1)}, bf16[4,128,768]{2,1,0:T(8,128)(2,1)}, u32[]{:S(2)}, u32[]{:S(2)}) collective-permute-start(bf16[4,128,768]{2,1,0:T(8,128)(2,1)} %get-tuple-element.117), channel_id=1, source_target_pairs={{0,4},{2,6},{4,0},{6,2},{8,12},{10,14},{12,8},{14,10},{16,20},{18,... | collective-permute-start | bytes 2359304 | tf_op jit(solution)/shard_map/ppermute | solution.py:193
  684.1 55.8 %collective-permute-start.66 = (bf16[4,128,768]{2,1,0:T(8,128)(2,1)}, bf16[4,128,768]{2,1,0:T(8,128)(2,1)}, u32[]{:S(2)}, u32[]{:S(2)}) collective-permute-start(bf16[4,128,768]{2,1,0:T(8,128)(2,1)} %get-tuple-element.115), channel_id=1, source_target_pairs={{0,2},{2,0},{4,6},{6,4},{8,10},{10,8},{12,14},{14,12},{16,18},{18,... | collective-permute-start | bytes 2359304 | tf_op jit(solution)/shard_map/ppermute | solution.py:193
  (135 other events, 1724.0 us)

commit v2 on v1

v2 whole, which is shorter than its diff:
```python
import functools
import math

import jax
import jax.numpy as jnp
from jax import lax
from jax.experimental import pallas as pl
from jax.experimental.pallas import tpu as pltpu
from jax.sharding import PartitionSpec as P

EPSILON = 1e-06
ROPE_BASE = 10000.0
MASKED = -1e30
HEAD = 256
SQUARE = 4
VMEM_LIMIT = 56 * 1024 * 1024
BF16 = jnp.bfloat16
F32 = jnp.float32


def matmul(left, right):
    return jnp.dot(left, right, preferred_element_type=F32)


def contract_rows(left, right):
    return lax.dot_general(left, right, (((0,), (0,)), ((), ())), preferred_element_type=F32)


def times_transposed(left, right):
    return lax.dot_general(left, right, (((1,), (1,)), ((), ())), preferred_element_type=F32)


def inverse_rms(vector):
    return lax.rsqrt(jnp.mean(vector * vector, axis=-1, keepdims=True) + EPSILON)


def norm_back(scaled_grad, normed, inverse):
    return inverse * (scaled_grad - normed * jnp.mean(scaled_grad * normed, axis=-1, keepdims=True))


def angles(position):
    half = HEAD // 2
    frequency = jnp.exp(jnp.arange(half, dtype=F32) * (-math.log(ROPE_BASE) / half))
    phase = position.astype(F32)[:, None] * frequency[None, :]
    return jnp.cos(phase), jnp.sin(phase)


def rotate(vector, cosine, sine):
    half = HEAD // 2
    front, back = vector[:, :half], vector[:, half:]
    return jnp.concatenate([front * cosine - back * sine, back * cosine + front * sine], axis=1)


def unrotate(vector, cosine, sine):
    return rotate(vector, cosine, -sine)


def attend_kernel(
    lat_ref,
    wq_ref,
    cos_ref,
    sin_ref,
    natural_ref,
    start_ref,
    kv_ref,
    keys_ref,
    out_ref,
    q_ref,
    o_ref,
    lse_ref,
    part_ref,
    part_sum,
):
    head, heads = pl.program_id(1), pl.num_programs(1)
    q_pre = matmul(lat_ref[...], wq_ref[...])
    q = (rotate(q_pre, cos_ref[...], sin_ref[...]).astype(BF16).astype(F32) * HEAD**-0.5).astype(BF16)
    q_ref[...] = q
    scores = times_transposed(q, kv_ref[:, :HEAD])
    keys = keys_ref[...]
    allowed = (keys <= natural_ref[...]) & (keys >= start_ref[...])
    scores = jnp.where(allowed, scores, MASKED)
    top = jnp.max(scores, axis=-1, keepdims=True)
    terms = jnp.exp(scores - top)
    total = jnp.sum(terms, axis=-1, keepdims=True)
    mix = matmul(terms.astype(BF16), kv_ref[:, HEAD:]) / total
    o_ref[...] = mix
    lse_ref[0] = top + jnp.log(total)
    share = matmul(mix.astype(BF16), out_ref[...])

    @pl.when(head == 0)
    def _():
        part_sum[...] = share

    @pl.when(head > 0)
    def _():
        part_sum[...] += share

    @pl.when(head == heads - 1)
    def _():
        part_ref[...] = part_sum[...].astype(BF16)


def attend(lat, wq, cosine, sine, natural, start, kv, keys, out_proj, block):
    rows, rank = lat.shape
    count, width = kv.shape[0], out_proj.shape[1]
    heads = wq.shape[1] // HEAD
    row = lambda size: pl.BlockSpec((block, size), lambda i, h: (i, 0))
    whole = lambda shape: pl.BlockSpec(shape, lambda i, h: (0, 0))
    row_head = pl.BlockSpec((block, HEAD), lambda i, h: (i, h))
    half = HEAD // 2
    return pl.pallas_call(
        attend_kernel,
        grid=(rows // block, heads),
        in_specs=[
            row(rank),
            pl.BlockSpec((rank, HEAD), lambda i, h: (0, h)),
            row(half),
            row(half),
            row(1),
            row(1),
            whole((count, 2 * HEAD)),
            whole((1, count)),
            pl.BlockSpec((HEAD, width), lambda i, h: (h, 0)),
        ],
        out_specs=[
            row_head,
            row_head,
            pl.BlockSpec((1, block, 1), lambda i, h: (h, i, 0)),
            row(width),
        ],
        out_shape=[
            jax.ShapeDtypeStruct((rows, heads * HEAD), BF16),
            jax.ShapeDtypeStruct((rows, heads * HEAD), F32),
            jax.ShapeDtypeStruct((heads, rows, 1), F32),
            jax.ShapeDtypeStruct((rows, width), BF16),
        ],
        scratch_shapes=[pltpu.VMEM((block, width), F32)],
        compiler_params=pltpu.CompilerParams(vmem_limit_bytes=VMEM_LIMIT),
        cost_estimate=pl.CostEstimate(
            flops=2 * rows * heads * HEAD * (2 * count + rank + width),
            bytes_accessed=4 * count * HEAD + 2 * heads * HEAD * (rank + width),
            transcendentals=rows * heads * count,
        ),
        name="attend",
    )(lat, wq, cosine, sine, natural, start, kv, keys, out_proj)


def attend_back_kernel(
    lat_ref,
    wq_ref,
    cos_ref,
    sin_ref,
    natural_ref,
    start_ref,
    kv_ref,
    keys_ref,
    out_ref,
    q_ref,
    o_ref,
    lse_ref,
    d_attn_ref,
    grad_q_ref,
    grad_out_ref,
    d_lat_ref,
    dot_ref,
    near_ref,
    far_ref,
    grad_q_sum,
    grad_out_sum,
    d_lat_sum,
    d_kv_sum,
):
    step, steps = pl.program_id(0), pl.num_programs(0)
    head, heads = pl.program_id(1), pl.num_programs(1)
    d_attn, mix, q = d_attn_ref[...], o_ref[...], q_ref[...]
    keys = keys_ref[...]
    allowed = (keys <= natural_ref[...]) & (keys >= start_ref[...])

    @pl.when(step == 0)
    def _():
        grad_q_sum[...] = jnp.zeros_like(grad_q_sum)
        grad_out_sum[...] = jnp.zeros_like(grad_out_sum)

    @pl.when(head == 0)
    def _():
        d_lat_sum[...] = jnp.zeros_like(d_lat_sum)

    @pl.when((step == 0) & (head == 0))
    def _():
        d_kv_sum[...] = jnp.zeros_like(d_kv_sum)

    grad_out_sum[...] += contract_rows(mix.astype(BF16), d_attn)
    d_o = times_transposed(d_attn, out_ref[...]).astype(BF16)
    delta = jnp.sum(d_o.astype(F32) * mix, axis=-1, keepdims=True)
    scores = times_transposed(q, kv_ref[:, :HEAD])
    probs = jnp.exp(jnp.where(allowed, scores - lse_ref[0], MASKED))
    d_probs = times_transposed(d_o, kv_ref[:, HEAD:])
    d_scores = (probs * (d_probs - delta)).astype(BF16)
    d_query = matmul(d_scores, kv_ref[:, :HEAD]) * HEAD**-0.5
    d_kv_sum[:, :HEAD] += contract_rows(d_scores, q)
    d_kv_sum[:, HEAD:] += contract_rows(probs.astype(BF16), d_o)
    d_qpre = unrotate(d_query, cos_ref[...], sin_ref[...]).astype(BF16)
    grad_q_sum[...] += contract_rows(lat_ref[...], d_qpre)
    d_lat_sum[...] += times_transposed(d_qpre, wq_ref[...])

    @pl.when(step == steps - 1)
    def _():
        grad_q_ref[...] = grad_q_sum[...].astype(BF16)
        grad_out_ref[...] = grad_out_sum[...].astype(BF16)

    @pl.when(head == heads - 1)
    def _():
        d_lat = d_lat_sum[...]
        d_lat_ref[...] = d_lat.astype(BF16)
        dot = jnp.sum(d_lat * lat_ref[...].astype(F32), axis=-1, keepdims=True)
        dot_ref[...] = jnp.broadcast_to(dot, dot_ref.shape).astype(BF16)

    @pl.when((step == steps - 1) & (head == heads - 1))
    def _():
        size = near_ref.shape[0]
        near_ref[...] = d_kv_sum[:size, :]
        far_ref[...] = d_kv_sum[size:, :].astype(BF16)


def attend_back(lat, wq, cosine, sine, natural, start, kv, keys, out_proj, q, o, lse, d_attn, block):
    rows, rank = lat.shape
    count, width = kv.shape[0], out_proj.shape[1]
    heads = wq.shape[1] // HEAD
    row = lambda size: pl.BlockSpec((block, size), lambda i, h: (i, 0))
    whole = lambda shape: pl.BlockSpec(shape, lambda i, h: (0, 0))
    row_head = pl.BlockSpec((block, HEAD), lambda i, h: (i, h))
    half = HEAD // 2
    wq_spec = pl.BlockSpec((rank, HEAD), lambda i, h: (0, h))
    out_spec = pl.BlockSpec((HEAD, width), lambda i, h: (h, 0))
    return pl.pallas_call(
        attend_back_kernel,
        grid=(rows // block, heads),
        in_specs=[
            row(rank),
            wq_spec,
            row(half),
            row(half),
            row(1),
            row(1),
            whole((count, 2 * HEAD)),
            whole((1, count)),
            out_spec,
            row_head,
            row_head,
            pl.BlockSpec((1, block, 1), lambda i, h: (h, i, 0)),
            row(width),
        ],
        out_specs=[
            wq_spec,
            out_spec,
            row(rank),
            row(128),
            whole((count // 2, 2 * HEAD)),
            whole((count // 2, 2 * HEAD)),
        ],
        out_shape=[
            jax.ShapeDtypeStruct((rank, heads * HEAD), BF16),
            jax.ShapeDtypeStruct((heads * HEAD, width), BF16),
            jax.ShapeDtypeStruct((rows, rank), BF16),
            jax.ShapeDtypeStruct((rows, 128), BF16),
            jax.ShapeDtypeStruct((count // 2, 2 * HEAD), F32),
            jax.ShapeDtypeStruct((count // 2, 2 * HEAD), BF16),
        ],
        scratch_shapes=[
            pltpu.VMEM((rank, HEAD), F32),
            pltpu.VMEM((HEAD, width), F32),
            pltpu.VMEM((block, rank), F32),
            pltpu.VMEM((count, 2 * HEAD), F32),
        ],
        compiler_params=pltpu.CompilerParams(vmem_limit_bytes=VMEM_LIMIT),
        cost_estimate=pl.CostEstimate(
            flops=2 * rows * heads * HEAD * (5 * count + 2 * rank + 2 * width),
            bytes_accessed=12 * count * HEAD + 4 * heads * HEAD * (rank + width),
            transcendentals=rows * heads * count,
        ),
        name="attend_back",
    )(lat, wq, cosine, sine, natural, start, kv, keys, out_proj, q, o, lse, d_attn)


def mlp_kernel(
    h_ref, cot_ref, near_ref, far_ref, d_h_ref, out_ref, act_near_ref, act_far_ref, weights, d_h_sum, out_sum, sems
):
    copies = [
        pltpu.make_async_copy(source, weights.at[i], sems.at[i])
        for i, source in enumerate((near_ref, far_ref))
    ]
    for copy in copies:
        copy.start()
    size = weights.shape[-1]
    for i, acts in enumerate((act_near_ref, act_far_ref)):
        copies[i].wait()

        def product(value_ref, kind):
            return sum(
                times_transposed(value_ref[:, q * size : (q + 1) * size], weights[i, q, kind])
                for q in range(SQUARE)
            )

        gate_act, up_proj, d_act = product(h_ref, 0), product(h_ref, 1), product(cot_ref, 2)
        sigmoid_gate = 1.0 / (1.0 + jnp.exp(-gate_act))
        silu_gate = gate_act * sigmoid_gate
        d_gate = d_act * up_proj * sigmoid_gate * (1.0 + gate_act * (1.0 - sigmoid_gate))
        acts[0] = d_gate.astype(BF16)
        acts[1] = (d_act * silu_gate).astype(BF16)
        acts[2] = (silu_gate * up_proj).astype(BF16)
        for q in range(SQUARE):
            here = slice(q * size, (q + 1) * size)
            d_h = matmul(acts[0], weights[i, q, 0]) + matmul(acts[1], weights[i, q, 1])
            out = matmul(acts[2], weights[i, q, 2])
            if i == 0:
                d_h_sum[:, here] = d_h
                out_sum[:, here] = out
            else:
                d_h_ref[:, here] = (d_h_sum[:, here] + d_h).astype(BF16)
                out_ref[:, here] = (out_sum[:, here] + out).astype(BF16)


def mlp(h, cot, near, far):
    rows, width = h.shape
    units = near.shape[2]
    vmem = pl.BlockSpec(memory_space=pltpu.VMEM)
    hbm = pl.BlockSpec(memory_space=pl.ANY)
    low = jax.ShapeDtypeStruct((rows, width), BF16)
    acts = jax.ShapeDtypeStruct((3, rows, units), BF16)
    return pl.pallas_call(
        mlp_kernel,
        in_specs=[vmem, vmem, hbm, hbm],
        out_specs=[vmem] * 4,
        out_shape=[low, low, acts, acts],
        scratch_shapes=[
            pltpu.VMEM((2,) + near.shape, BF16),
            pltpu.VMEM((rows, width), F32),
            pltpu.VMEM((rows, width), F32),
            pltpu.SemaphoreType.DMA((2,)),
        ],
        compiler_params=pltpu.CompilerParams(vmem_limit_bytes=VMEM_LIMIT),
        cost_estimate=pl.CostEstimate(
            flops=24 * rows * width * units,
            bytes_accessed=4 * near.size + 8 * rows * width,
            transcendentals=2 * rows * units,
        ),
        name="mlp",
    )(h, cot, near, far)


def unit_grads_kernel(acts_ref, h_ref, cot_ref, *refs):
    grads_ref = refs[-1]

    def store(value):
        grad = contract_rows(acts_ref[0], value)
        if len(refs) > 1:
            grad = grad + refs[0][0, 0].astype(F32)
        grads_ref[0, 0] = grad.astype(BF16)

    @pl.when(pl.program_id(1) < 2)
    def _():
        store(h_ref[...])

    @pl.when(pl.program_id(1) == 2)
    def _():
        store(cot_ref[...])


def unit_grads(acts, h, cot, *more):
    rows, width = h.shape
    units, size = acts.shape[2], width // SQUARE
    column = pl.BlockSpec((rows, size), lambda q, kind: (0, q))
    grads = pl.BlockSpec((1, 1, units, size), lambda q, kind: (q, kind, 0, 0))
    return pl.pallas_call(
        unit_grads_kernel,
        grid=(SQUARE, 3),
        in_specs=[pl.BlockSpec((1, rows, units), lambda q, kind: (kind, 0, 0)), column, column]
        + [grads] * len(more),
        out_specs=grads,
        out_shape=jax.ShapeDtypeStruct((SQUARE, 3, units, size), BF16),
        compiler_params=pltpu.CompilerParams(vmem_limit_bytes=VMEM_LIMIT),
        cost_estimate=pl.CostEstimate(
            flops=6 * rows * width * units, bytes_accessed=6 * width * units, transcendentals=0
        ),
        name="unit_grads",
    )(acts, h, cot, *more)


def local(
    chips,
    tokens,
    attn_gain,
    q_gain,
    w_qdown,
    w_qup,
    w_kv,
    w_out,
    mlp_gain,
    w_gate,
    w_up,
    w_down,
    cotangent,
    seq_lengths,
    block_slots,
):
    layers = chips // SQUARE
    rows, width = tokens.shape[0] // 2, tokens.shape[1]
    line_rows = layers * rows
    lanes = width // chips
    rank = w_qdown.shape[1]
    rank_rows = w_qup.shape[0]
    heads_half = w_qup.shape[1] // HEAD
    heads = 2 * heads_half
    heads_here = heads // layers
    units = w_gate.shape[1] // layers
    half = HEAD // 2
    place = lax.axis_index("seq")
    core = lax.axis_index("tp")
    layer, corner = place // SQUARE, place % SQUARE
    first = core == 0
    lines = [[z * SQUARE + c for z in range(layers)] for c in range(SQUARE)]
    square_groups = [[z * SQUARE + c for c in range(SQUARE)] for z in range(layers)]

    def across(value):
        return lax.ppermute(value, "tp", [(0, 1), (1, 0)])

    def along(value, step):
        pairs = [
            (z * SQUARE + c, (z + step) % layers * SQUARE + c)
            for z in range(layers)
            for c in range(SQUARE)
        ]
        return lax.ppermute(value, "seq", pairs)

    def within(value, flip):
        return lax.ppermute(value, "seq", [(i, i ^ flip) for i in range(chips)])

    def exchange(value):
        return lax.all_to_all(value, "seq", 0, 0, axis_index_groups=lines, tiled=True)

    def line_gather(value):
        return jnp.concatenate([value] + [along(value, k) for k in range(1, layers)])

    def line_scatter(value):
        blocks = value.reshape(layers, rows, value.shape[1])
        return blocks[0].astype(F32) + sum(
            along(blocks[k], -k).astype(F32) for k in range(1, layers)
        )

    def put(parts, indices):
        stacked = jnp.zeros((len(parts),) + parts[0].shape, parts[0].dtype)
        for part, index in zip(parts, indices):
            stacked = lax.dynamic_update_index_in_dim(stacked, part, index, 0)
        return stacked

    def square_gather(value):
        size = value.shape[0] // 2
        one, two = within(value, 1), within(value, 2)
        three = jnp.concatenate([within(one[:size], 2), within(two[size:], 1)])
        return put([value, one, two, three], [corner ^ m for m in range(SQUARE)])

    def square_scatter(value):
        size = value.shape[1] // 2
        piece = lambda m: lax.dynamic_index_in_dim(value, corner ^ m, 0, keepdims=False)
        pieces = [piece(m) for m in range(SQUARE)]
        sums = []
        for here, near, next_one in ((slice(0, size), 1, 2), (slice(size, None), 2, 1)):
            sent = jnp.stack([pieces[near][here], pieces[3][here]])
            got = within(sent, near)
            mine = pieces[0][here].astype(F32) + got[0].astype(F32)
            other = pieces[next_one][here].astype(F32) + got[1].astype(F32)
            sums.append(mine + within(other.astype(BF16), next_one).astype(F32))
        return jnp.concatenate(sums)

    def own(pair_value):
        return lax.dynamic_slice_in_dim(pair_value, core * rows, rows, 0)

    def both(mine, theirs, axis=0):
        return jnp.concatenate(
            [jnp.where(first, mine, theirs), jnp.where(first, theirs, mine)], axis=axis
        )

    def of_core(value, which):
        return lax.dynamic_index_in_dim(value, which, 0, keepdims=False)

    def block_of(value, index, size):
        return lax.dynamic_slice_in_dim(value, index * size, size, 1)

    def to_placed(value):
        shaped = value.reshape(value.shape[0], layers, SQUARE, lanes)
        return jnp.swapaxes(shaped, 1, 2).reshape(value.shape[0], width)

    def from_placed(value):
        shaped = value.reshape(value.shape[0], SQUARE, layers, lanes)
        return jnp.swapaxes(shaped, 1, 2).reshape(value.shape[0], width)

    inputs = to_placed(own(tokens).astype(F32))
    x_inverse = inverse_rms(inputs)
    x_hat = inputs * x_inverse
    x_all = line_gather(x_hat.astype(BF16))

    gain_rows = attn_gain.astype(F32)[:, None]
    down = jnp.concatenate([w_qdown, w_kv], axis=1)
    rank_share, kv_share = rank // layers, 2 * HEAD // layers
    share = rank_share + kv_share

    def shares(value):
        lat = value[:, :rank].reshape(-1, layers, rank_share)
        kv = value[:, rank:].reshape(-1, layers, kv_share)
        return jnp.swapaxes(jnp.concatenate([lat, kv], axis=2), 0, 1)

    def unshares(value):
        value = jnp.swapaxes(value, 0, 1)
        count = value.shape[0]
        lat = value[:, :, :rank_share].reshape(count, rank)
        return jnp.concatenate([lat, value[:, :, rank_share:].reshape(count, 2 * HEAD)], axis=1)

    down_scaled = (down.astype(F32) * gain_rows).astype(BF16)
    down_half = lax.dynamic_slice_in_dim(down_scaled, core * (lanes // 2), lanes // 2, 0)
    down_near = square_gather(exchange(shares(down_half))).reshape(SQUARE, layers, lanes // 2, share)
    down_here = both(down_near, across(down_near), axis=2).reshape(width, share)

    q_gain_rows = q_gain.astype(F32)[:, None]
    qup_scaled = (w_qup.astype(F32) * q_gain_rows).astype(BF16)
    qup_heads = qup_scaled.reshape(rank_rows, heads_half, 2, half)
    qup_heads = jnp.transpose(qup_heads, (2, 1, 0, 3))
    out_heads = jnp.swapaxes(w_out.reshape(heads_half, 2, half, lanes), 0, 1)
    qup_mine = both(of_core(qup_heads, core), across(of_core(qup_heads, 1 - core)))
    out_mine = both(of_core(out_heads, core), across(of_core(out_heads, 1 - core)))
    attn_send = jnp.concatenate(
        [qup_mine.reshape(layers, -1, lanes), out_mine.reshape(layers, -1, lanes)], axis=1
    )
    qup_size = heads_here * rank_rows * half // lanes
    attn_in = square_gather(exchange(attn_send))
    qup_half = attn_in[:, :, :qup_size].reshape(SQUARE, layers, heads_here, rank_rows, half)
    qup_half = jnp.transpose(qup_half, (1, 0, 3, 2, 4)).reshape(rank, heads_here, half)
    out_half = attn_in[:, :, qup_size:].reshape(SQUARE, layers, heads_here, half, lanes)
    out_half = jnp.transpose(out_half, (2, 3, 0, 1, 4)).reshape(heads_here, half, width)
    qup_here = both(qup_half, across(qup_half), axis=2).reshape(rank, heads_here * HEAD)
    out_here = both(out_half, across(out_half), axis=1).reshape(heads_here * HEAD, width)

    mlp_gain_rows = mlp_gain.astype(F32)[:, None]
    gate_up = jnp.concatenate([w_gate, w_up], axis=1)
    gate_up_scaled = (gate_up.astype(F32) * mlp_gain_rows).astype(BF16).T
    mlp_send = jnp.concatenate([gate_up_scaled, w_down]).reshape(3, layers, units, lanes)
    mlp_send = jnp.swapaxes(mlp_send, 0, 1).reshape(layers, 3 * units, lanes)
    mlp_block = jnp.swapaxes(exchange(mlp_send), 0, 1).reshape(3 * units, layers * lanes)
    mlp_near = lax.all_gather(mlp_block, "seq", axis_index_groups=square_groups)
    mlp_near = mlp_near.reshape(SQUARE, 3, units, layers * lanes)
    mlp_far = across(mlp_near)
    cot_own = to_placed(own(cotangent))
    cot_all = line_gather(cot_own)

    bounds = jnp.cumsum(seq_lengths)
    starts = bounds - seq_lengths

    def layout(blocks):
        natural = (blocks[:, None] * rows + jnp.arange(rows, dtype=jnp.int32)[None, :]).reshape(-1)
        member = (natural[:, None] >= starts[None, :]) & (natural[:, None] < bounds[None, :])
        return natural, jnp.sum(jnp.where(member, starts[None, :], 0), axis=1)

    back_steps = jnp.arange(layers, dtype=jnp.int32)
    owners = jnp.concatenate(
        [((layer - back_steps) % layers) * SQUARE + (corner ^ m) for m in range(SQUARE)]
    )
    near_natural, near_start = layout(block_slots[2 * owners + core])
    far_natural, _ = layout(block_slots[2 * owners + 1 - core])
    key_natural = jnp.concatenate([near_natural, far_natural])[None, :]
    row_natural, row_start = near_natural[:line_rows], near_start[:line_rows]
    cosine, sine = angles(row_natural - row_start)
    row_natural, row_start = row_natural[:, None], row_start[:, None]

    part = matmul(x_all, down_here).astype(BF16)

    def rolled(value, step):
        return jnp.roll(value.reshape(layers, rows, value.shape[1]), step, axis=0).reshape(value.shape)

    parts = jnp.stack([part] + [rolled(along(part, k), k) for k in range(1, layers)])
    parts = jnp.stack([of_core(parts, (layer - z) % layers) for z in range(layers)])
    projected = unshares(parts).astype(F32)
    q_lat, kv_pre = projected[:, :rank], projected[:, rank:]
    lat_inverse = inverse_rms(q_lat)
    lat_hat = q_lat * lat_inverse
    lat_low = lat_hat.astype(BF16)
    kv_line = jnp.concatenate([rotate(kv_pre[:, :HEAD], cosine, sine), kv_pre[:, HEAD:]], axis=1)
    kv_line = kv_line.astype(BF16)
    kv_near = jnp.concatenate([kv_line] + [within(kv_line, m) for m in range(1, SQUARE)])
    kv_all = jnp.concatenate([kv_near, across(kv_near)])

    block = max(64, min(line_rows, 256 * 2048 // kv_all.shape[0]))
    queries, attn_mix, log_total, attn_part = attend(
        lat_low, qup_here, cosine, sine, row_natural, row_start, kv_all, key_natural, out_here, block
    )
    hidden = inputs + line_scatter(attn_part)
    h_inverse = inverse_rms(hidden)
    h_hat = hidden * h_inverse
    h_all = line_gather(h_hat.astype(BF16))

    d_h_part, mlp_part, acts_near, acts_far = mlp(h_all, cot_all, mlp_near, mlp_far)
    d_hscaled = line_scatter(d_h_part)
    d_hidden = cot_own.astype(F32) + norm_back(d_hscaled, h_hat, h_inverse)
    d_attn_all = line_gather(d_hidden.astype(BF16))
    layer_own = from_placed((hidden + line_scatter(mlp_part)).astype(BF16))
    layer_out = both(layer_own, across(layer_own))

    grads_far = unit_grads(acts_far, h_all, cot_all)
    grads_near = unit_grads(acts_near, h_all, cot_all, across(grads_far))
    mlp_back = lax.psum_scatter(
        grads_near.reshape(SQUARE, 3 * units, layers * lanes), "seq", axis_index_groups=square_groups
    )
    mlp_back = jnp.swapaxes(mlp_back.reshape(3 * units, layers, lanes), 0, 1)
    mlp_back = exchange(mlp_back).reshape(layers, 3, units, lanes)
    mlp_back = jnp.swapaxes(mlp_back, 0, 1).astype(F32).reshape(3, layers * units, lanes)
    gate_up_back = mlp_back[:2].reshape(2 * layers * units, lanes).T
    gate_up_grad = gate_up_back * mlp_gain_rows
    mlp_gain_part = jnp.sum(gate_up_back * gate_up.astype(F32), axis=1)
    gate_part = gate_up_grad[:, : layers * units]
    up_part = gate_up_grad[:, layers * units :]
    down_part = mlp_back[2]

    grad_qup, grad_out, d_lat_part, dot_part, d_kv_near, d_kv_far = attend_back(
        lat_low,
        qup_here,
        cosine,
        sine,
        row_natural,
        row_start,
        kv_all,
        key_natural,
        out_here,
        queries,
        attn_mix,
        log_total,
        d_attn_all,
        block,
    )
    d_kv_low = (d_kv_near + across(d_kv_far).astype(F32)).astype(BF16)
    d_kv_low = d_kv_low.reshape(SQUARE, line_rows, 2 * HEAD)
    d_kv_line = d_kv_low[0].astype(F32) + sum(
        within(d_kv_low[m], m).astype(F32) for m in range(1, SQUARE)
    )
    d_kv_line = jnp.concatenate(
        [unrotate(d_kv_line[:, :HEAD], cosine, sine), d_kv_line[:, HEAD:]], axis=1
    ).astype(BF16)

    def columns_for(where):
        return jnp.concatenate(
            [block_of(d_lat_part, where, rank_share), block_of(d_kv_line, where, kv_share), dot_part],
            axis=1,
        )

    d_share = columns_for(layer).astype(F32) + sum(
        rolled(along(columns_for((layer - k) % layers), -k), -k).astype(F32)
        for k in range(1, layers)
    )
    dot = d_share[:, share : share + 1] / rank
    d_lat = lat_inverse * (d_share[:, :rank_share] - block_of(lat_hat, layer, rank_share) * dot)
    d_down = jnp.concatenate([d_lat, d_share[:, rank_share:share]], axis=1).astype(BF16)

    d_xscaled = line_scatter(times_transposed(d_down, down_here).astype(BF16))
    token_own = from_placed((d_hidden + norm_back(d_xscaled, x_hat, x_inverse)).astype(BF16))
    token_grad = both(token_own, across(token_own))
    grad_down = contract_rows(x_all, d_down).reshape(SQUARE, layers, 2, lanes // 2, share)
    grad_down = jnp.transpose(grad_down, (2, 0, 1, 3, 4))
    grad_down = of_core(grad_down, core) + across(of_core(grad_down, 1 - core).astype(BF16)).astype(F32)
    down_back = square_scatter(grad_down.astype(BF16)).astype(BF16)
    down_back = unshares(exchange(down_back)).astype(F32)
    down_sum = both(down_back, across(down_back))
    attn_gain_part = jnp.sum(down_sum * down.astype(F32), axis=1)
    down_grad = down_sum * gain_rows
    qdown_part, kv_part = down_grad[:, :rank], down_grad[:, rank:]

    grad_qup = grad_qup.reshape(layers, SQUARE, rank_rows, heads_here, 2, half)
    grad_qup = jnp.transpose(grad_qup, (4, 1, 0, 3, 2, 5)).reshape(2, SQUARE, layers, -1, lanes)
    grad_out = grad_out.reshape(heads_here, 2, half, SQUARE, layers, lanes)
    grad_out = jnp.transpose(grad_out, (1, 3, 4, 0, 2, 5)).reshape(2, SQUARE, layers, -1, lanes)
    attn_grads = jnp.concatenate([grad_qup, grad_out], axis=3)
    attn_sum = of_core(attn_grads, core).astype(F32) + across(of_core(attn_grads, 1 - core)).astype(F32)
    attn_back = exchange(square_scatter(attn_sum.astype(BF16)).astype(BF16))
    qup_back = attn_back[:, :qup_size].reshape(2, heads_half, rank_rows, half)
    out_back = attn_back[:, qup_size:].reshape(2, heads_half, half, lanes)
    qup_back = both(of_core(qup_back, core)[None], across(of_core(qup_back, 1 - core))[None])
    out_back = both(of_core(out_back, core)[None], across(of_core(out_back, 1 - core))[None])
    qup_back = jnp.transpose(qup_back, (2, 1, 0, 3)).reshape(rank_rows, heads_half * HEAD).astype(F32)
    out_part = jnp.swapaxes(out_back, 0, 1).reshape(heads_half * HEAD, lanes).astype(F32)
    qup_part = qup_back * q_gain_rows
    q_gain_half = jnp.sum(qup_back * w_qup.astype(F32), axis=1)
    gain_parts = jnp.concatenate([q_gain_half, mlp_gain_part])
    gain_parts = gain_parts + across(gain_parts)
    q_gain_part, mlp_gain_part = gain_parts[:rank_rows], gain_parts[rank_rows:]
    return (
        layer_out,
        token_grad,
        attn_gain_part,
        q_gain_part,
        qdown_part,
        qup_part,
        kv_part,
        out_part,
        mlp_gain_part,
        gate_part,
        up_part,
        down_part,
    )


def solution(mesh):
    in_specs = (
        P("seq", None),
        P("seq"),
        P("seq"),
        P("seq", None),
        P("seq", "tp"),
        P("seq", None),
        P("tp", "seq"),
        P("seq"),
        P("seq", "tp"),
        P("seq", "tp"),
        P("tp", "seq"),
        P("seq", None),
        P(),
        P(),
    )
    out_specs = (
        P("seq", None),
        P("seq", None),
        P("seq"),
        P("seq"),
        P("seq", None),
        P("seq", "tp"),
        P("seq", None),
        P("tp", "seq"),
        P("seq"),
        P("seq", "tp"),
        P("seq", "tp"),
        P("tp", "seq"),
    )
    body = functools.partial(local, mesh.shape["seq"])
    return jax.shard_map(body, mesh=mesh, in_specs=in_specs, out_specs=out_specs, check_vma=False)
```

time: 785 us -> 717 us (0.913)
  waiting for transfers between devices: 436 us -> 281 us
  blocking collectives: 0 us -> 55.8 us
  Pallas kernels: 24.9 us -> 77.8 us
  matrix products: 35.8 us -> 5.14 us
  between operations: 3.13 us -> 15.9 us
  other arithmetic: 71.4 us -> 59.7 us
  local copies, waits for them, and re-layouts: 89.1 us -> 97.4 us
    ppermute x30 -> x22, waiting for transfers between devices: 297 us -> 51.2 us  [within(): return lax.ppermute(value, 'seq', [(i, i ^ flip) for i in range(chips)])]
    all_to_all x4 -> x5, waiting for transfers between devices: 15.1 us -> 82.7 us  [exchange(): lax.all_to_all(value, 'seq', 0, 0, axis_index_groups=lines, tiled=True)]
    all_to_all x0 -> x1, blocking collectives: none -> 55.8 us  [exchange(): lax.all_to_all(value, 'seq', 0, 0, axis_index_groups=lines, tiled=True)]
    pallas_call x2 -> x5, Pallas kernels: 24.9 us -> 77.8 us  [the longest x2 25.5 us: unit_grads(): pl.pallas_call(unit_grads_kernel, grid=(SQUARE, 3), in_specs=[pl.BlockSpe...]
    all_gather x0 -> x1, waiting for transfers between devices: none -> 20 us  [local(): mlp_near = lax.all_gather(mlp_block, 'seq', axis_index_groups=square_groups)]
    reshape x3 -> x15, local copies, waits for them, and re-layouts: 7.9 us -> 25.2 us  [the longest x2 13.2 us: local(): grad_out = grad_out.reshape(heads_here, 2, half, SQUARE, layers, lanes)]
    ppermute x18 -> x17, waiting for transfers between devices: 1.71 us -> 13.9 us  [across(): return lax.ppermute(value, 'tp', [(0, 1), (1, 0)])]
    dot_general x11 -> x1, matrix products: 12.8 us -> 0.75 us  [times_transposed(): lax.dot_general(left, right, (((1,), (1,)), ((), ())), preferred_element_...]
  transfers between devices with their start and end apart: 82 -> 76, of which waited for: 40 -> 33; matrix products, arithmetic and copies ran while one was open for 22% -> 19% of each run, Pallas kernels for 1% -> 5%
where the time goes in v2:
time: 717 us; the launch traced here: 706 us
  waiting for transfers between devices  281 us (39%)
  starting transfers between devices  113 us (16%)
  local copies, waits for them, and re-layouts  97.4 us (14%)
  Pallas kernels  77.8 us (11%)
  other arithmetic  59.7 us (8%)
  blocking collectives  55.8 us (8%)
  between operations  15.9 us (2%)
    ppermute x30, waiting for transfers between devices, along(): return lax.ppermute(value, 'seq', pairs)  113 us
    all_to_all x5, waiting for transfers between devices, exchange(): lax.all_to_all(value, 'seq', 0, 0, axis_index_groups=lines, tiled=True)  82.7 us
    ppermute x30, starting transfers between devices, along(): return lax.ppermute(value, 'seq', pairs)  64.9 us
    all_to_all x1, blocking collectives, exchange(): lax.all_to_all(value, 'seq', 0, 0, axis_index_groups=lines, tiled=True)  55.8 us
    ppermute x22, waiting for transfers between devices, within(): return lax.ppermute(value, 'seq', [(i, i ^ flip) for i in range(chips)])  51.2 us
    pallas_call x2, Pallas kernels, unit_grads(): pl.pallas_call(unit_grads_kernel, grid=(SQUARE, 3), in_specs=[pl.BlockSpe...  25.5 us
    ppermute x22, starting transfers between devices, within(): return lax.ppermute(value, 'seq', [(i, i ^ flip) for i in range(chips)])  25.4 us
    all_to_all x5, starting transfers between devices, exchange(): lax.all_to_all(value, 'seq', 0, 0, axis_index_groups=lines, tiled=True)  20.3 us
  transfers between devices with their start and end apart: 76, of which 33 were waited for; matrix products, arithmetic and copies ran while one was open for 19% of the time, Pallas kernels for 5%

profile of v2, /device:TPU:0, one launch (start us, length us, event | category | flops | bytes accessed | tf_op | source)
XLA Modules:
  0.0 705.8 jit_solution(14853139073207933126)
XLA Ops:
  11.6 6.3 pad_maximum_fusion.1
  18.1 55.8 %all_to_all.30 = bf16[4,2112,128]{2,1,0:T(8,128)(2,1)} all-to-all(bf16[4,2112,128]{2,1,0:T(8,128)(2,1)S(1)} %bitcast.220), channel_id=1, replica_groups={{0,8,16,24},{2,10,18,26},{4,12,20,28},{6,14,22,30},{1,9,17,25},{3,11,19..., dimensions={0} | all-to-all | bytes 4325376 | tf_op jit(solution)/shard_map/all_to_all | solution.py:439
  94.7 12.5 %all-to-all-done = bf16[4,64,384]{2,1,0:T(8,128)(2,1)S(1)} async-done(((bf16[4,64,384]{2,1,0:T(8,128)(2,1)}), bf16[4,64,384]{2,1,0:T(8,128)(2,1)S(1)}, u32[]{:S(2)}, u32[]{:S(2)}) %all-to-all-start) | async-done | bytes 196640 | tf_op jit(solution)/shard_map/all_to_all | solution.py:439
  110.4 7.5 %collective-permute-done.3 = bf16[4,64,384]{2,1,0:T(8,128)(2,1)S(1)} collective-permute-done((bf16[4,64,384]{2,1,0:T(8,128)(2,1)S(1)}, bf16[4,64,384]{2,1,0:T(8,128)(2,1)S(1)}, u32[]{:S(2)}, u32[]{:S(2)}) %collective-permute-start.3) | collective-permute-done | bytes 196640 | tf_op jit(solution)/shard_map/ppermute | solution.py:436
  141.0 18.9 %all-to-all-done.1 = bf16[4,768,128]{2,1,0:T(8,128)(2,1)S(1)} async-done(((bf16[4,768,128]{2,1,0:T(8,128)(2,1)}), bf16[4,768,128]{2,1,0:T(8,128)(2,1)S(1)}, u32[]{:S(2)}, u32[]{:S(2)}) %all-to-all-start.1) | async-done | bytes 786464 | tf_op jit(solution)/shard_map/all_to_all | solution.py:439
  165.7 20.0 %all-gather.2.cloned.1.call-done = bf16[4,2112,512]{2,1,0:T(8,128)(2,1)} async-done(((bf16[1,2112,512]{2,1,0:T(8,128)(2,1)}), bf16[4,2112,512]{2,1,0:T(8,128)(2,1)}) %all-gather.2.cloned.1.call-update) | async-done | bytes 8650768 | tf_op jit(solution)/shard_map/all_gather | solution.py:548
  207.3 5.9 collective-permute-done.16
  244.7 14.5 %attend.1 = (bf16[256,1024]{1,0:T(8,128)(2,1)}, f32[256,1024]{1,0:T(8,128)}, f32[4,256,1]{2,1,0:T(8,128)}, bf16[256,2048]{1,0:T(8,128)(2,1)}) custom-call(bf16[256,1024]{1,0:T(8,128)(2,1)} %get-tuple-element.109.lat_ref, bf16[1024,1024]{1,0:T(8,128)(2,1)} %bitcast.234, f32[256,128]{1,0:T(8,128)} %get-tuple-element.200.cos_ref, ...), custom_call_target="tpu_custom_call" | custom-call | flops 3758096384 | bytes 8388608 | tf_op jit(solution)/shard_map/attend/pallas_call | solution.py:111
  273.5 18.6 %collective-permute-done.24 = bf16[64,2048]{1,0:T(8,128)(2,1)S(1)} collective-permute-done((bf16[64,2048]{1,0:T(8,128)(2,1)S(1)}, bf16[64,2048]{1,0:T(8,128)(2,1)S(1)}, u32[]{:S(2)}, u32[]{:S(2)}) %collective-permute-start.24) | collective-permute-done | bytes 262176 | tf_op jit(solution)/shard_map/ppermute | solution.py:433
  293.4 6.1 collective-permute-start.26
  306.4 13.7 %collective-permute-done.27 = bf16[64,2048]{1,0:T(8,128)(2,1)S(1)} collective-permute-done((bf16[64,2048]{1,0:T(8,128)(2,1)S(1)}, bf16[64,2048]{1,0:T(8,128)(2,1)S(1)}, u32[]{:S(2)}, u32[]{:S(2)}) %collective-permute-start.27) | collective-permute-done | bytes 262176 | tf_op jit(solution)/shard_map/ppermute | solution.py:433
  321.3 18.1 %mlp.1 = (bf16[256,2048]{1,0:T(8,128)(2,1)}, bf16[256,2048]{1,0:T(8,128)(2,1)}, bf16[3,256,704]{2,1,0:T(8,128)(2,1)}, bf16[3,256,704]{2,1,0:T(8,128)(2,1)}) custom-call(bf16[256,2048]{1,0:T(8,128)(2,1)} %pad_maximum_fusion.6.h_ref, bf16[256,2048]{1,0:T(8,128)(2,1)} %copy-done.9, bf16[4,3,704,512]{3,2,1,0:T(8,128)(2,1)} %bitcast.269, ...), custom_call_target="tpu_custom_call" | custom-call | flops 8858370048 | bytes 21495808 | tf_op jit(solution)/shard_map/mlp/pallas_call | solution.py:330
  339.3 11.7 %unit_grads.2 = bf16[4,3,704,512]{3,2,1,0:T(8,128)(2,1)} custom-call(bf16[3,256,704]{2,1,0:T(8,128)(2,1)} %get-tuple-element.39.acts_ref, bf16[256,2048]{1,0:T(8,128)(2,1)} %pad_maximum_fusion.6.h_ref, bf16[256,2048]{1,0:T(8,128)(2,1)} %copy-done.9), custom_call_target="tpu_custom_call" | custom-call | flops 2214592512 | bytes 8650752 | tf_op jit(solution)/shard_map/unit_grads/pallas_call | solution.py:374
  351.1 13.9 %collective-permute-done.66.refs_0_ = bf16[4,3,704,512]{3,2,1,0:T(8,128)(2,1)} collective-permute-done((bf16[4,3,704,512]{3,2,1,0:T(8,128)(2,1)}, bf16[4,3,704,512]{3,2,1,0:T(8,128)(2,1)}, u32[]{:S(2)}, u32[]{:S(2)}) %collective-permute-start.66) | collective-permute-done | bytes 8650784 | tf_op jit(solution)/shard_map/ppermute | solution.py:425
  364.9 13.8 %unit_grads.3 = bf16[4,3,704,512]{3,2,1,0:T(8,128)(2,1)} custom-call(bf16[3,256,704]{2,1,0:T(8,128)(2,1)} %get-tuple-element.38.acts_ref, bf16[256,2048]{1,0:T(8,128)(2,1)} %pad_maximum_fusion.6.h_ref, bf16[256,2048]{1,0:T(8,128)(2,1)} %copy-done.9, bf16[4,3,704,512]{3,2,1,0:T(8,128)(2,1)} %collective-permute-done.66.refs_0_), custom_call_target="tpu_custom_call" | custom-call | flops 2214592512 | bytes 8650752 | tf_op jit(solution)/shard_map/unit_grads/pallas_call | solution.py:374
  380.0 8.6 %collective-permute-start.37 = (bf16[64,2048]{1,0:T(8,128)(2,1)S(1)}, bf16[64,2048]{1,0:T(8,128)(2,1)S(1)}, u32[]{:S(2)}, u32[]{:S(2)}) collective-permute-start(bf16[64,2048]{1,0:T(8,128)(2,1)S(1)} %get-tuple-element.135), channel_id=1, source_target_pairs={{0,24},{2,26},{4,28},{6,30},{8,0},{10,2},{12,4},{14,6},{16,8},{18,... | collective-permute-start | bytes 786440 | tf_op jit(solution)/shard_map/ppermute | solution.py:433
  395.4 15.9 %collective-permute-done.38 = bf16[64,2048]{1,0:T(8,128)(2,1)S(1)} collective-permute-done((bf16[64,2048]{1,0:T(8,128)(2,1)S(1)}, bf16[64,2048]{1,0:T(8,128)(2,1)S(1)}, u32[]{:S(2)}, u32[]{:S(2)}) %collective-permute-start.38) | collective-permute-done | bytes 262176 | tf_op jit(solution)/shard_map/ppermute | solution.py:433
  412.3 20.7 %collective-permute-done.34 = bf16[64,2048]{1,0:T(8,128)(2,1)S(1)} collective-permute-done((bf16[64,2048]{1,0:T(8,128)(2,1)S(1)}, bf16[64,2048]{1,0:T(8,128)(2,1)S(1)}, u32[]{:S(2)}, u32[]{:S(2)}) %collective-permute-start.34) | collective-permute-done | bytes 262176 | tf_op jit(solution)/shard_map/ppermute | solution.py:433
  441.1 4.8 collective-permute-done.40
  445.9 9.5 %collective-permute-done.41 = bf16[64,2048]{1,0:T(8,128)(2,1)S(1)} collective-permute-done((bf16[64,2048]{1,0:T(8,128)(2,1)S(1)}, bf16[64,2048]{1,0:T(8,128)(2,1)S(1)}, u32[]{:S(2)}, u32[]{:S(2)}) %collective-permute-start.41) | collective-permute-done | bytes 262176 | tf_op jit(solution)/shard_map/ppermute | solution.py:433
  456.4 19.8 %attend_back.1 = (bf16[1024,1024]{1,0:T(8,128)(2,1)}, bf16[1024,2048]{1,0:T(8,128)(2,1)}, bf16[256,1024]{1,0:T(8,128)(2,1)}, bf16[256,128]{1,0:T(8,128)(2,1)}, f...) custom-call(bf16[256,1024]{1,0:T(8,128)(2,1)} %get-tuple-element.109.lat_ref, bf16[1024,1024]{1,0:T(8,128)(2,1)} %bitcast.235, ...), custom_call_target="tpu_custom_call" | custom-call | flops 8589934592 | bytes 18874368 | tf_op jit(solution)/shard_map/attend_back/pallas_call | solution.py:235
  476.4 7.7 %reshape.499 = bf16[4,2,128,4,4,128]{5,4,3,2,1,0:T(4,128)(2,1)} reshape(bf16[1024,2048]{1,0:T(8,128)(2,1)} %get-tuple-element.37) | data formatting | bytes 8388608 | tf_op jit(solution)/shard_map/reshape | solution.py:675
  484.1 5.4 copy.197
  505.7 5.2 collective-permute-done.45
  511.9 5.9 collective-permute-start.49
  520.7 6.4 collective-permute-done.49
  531.1 11.6 %collective-permute-done.48 = bf16[256,512]{1,0:T(8,128)(2,1)S(1)} collective-permute-done((bf16[256,512]{1,0:T(8,128)(2,1)S(1)}, bf16[256,512]{1,0:T(8,128)(2,1)S(1)}, u32[]{:S(2)}, u32[]{:S(2)}) %collective-permute-start.48) | collective-permute-done | bytes 262176 | tf_op jit(solution)/shard_map/ppermute | solution.py:433
  565.6 18.5 %collective-permute-done.57 = bf16[2,2,64,384]{3,2,1,0:T(8,128)(2,1)S(1)} collective-permute-done((bf16[2,2,64,384]{3,2,1,0:T(8,128)(2,1)S(1)}, bf16[2,2,64,384]{3,2,1,0:T(8,128)(2,1)S(1)}, u32[]{:S(2)}, u32[]{:S(2)}) %collective-permute-start.57) | collective-permute-done | bytes 196640 | tf_op jit(solution)/shard_map/ppermute | solution.py:436
  592.5 5.2 all-to-all-start.3
  602.6 13.8 %all-to-all-done.3 = bf16[4,64,384]{2,1,0:T(8,128)(2,1)} async-done(((bf16[4,64,384]{2,1,0:T(8,128)(2,1)}), bf16[4,64,384]{2,1,0:T(8,128)(2,1)}, u32[]{:S(2)}, u32[]{:S(2)}) %all-to-all-start.3) | async-done | bytes 196640 | tf_op jit(solution)/shard_map/all_to_all | solution.py:439
  631.8 6.5 all-to-all-done.4
  659.6 30.9 %all-to-all-done.5 = bf16[4,2112,128]{2,1,0:T(8,128)(2,1)S(1)} async-done(((bf16[4,2112,128]{2,1,0:T(8,128)(2,1)}), bf16[4,2112,128]{2,1,0:T(8,128)(2,1)S(1)}, u32[]{:S(2)}, u32[]{:S(2)}) %all-to-all-start.5) | async-done | bytes 2162720 | tf_op jit(solution)/shard_map/all_to_all | solution.py:439
  (452 shorter events, 256.0 us)
Async XLA Ops:
  7.2 178.5 %all-gather.2.cloned.1.call-start = ((), (), s32[]{:S(2)}) async-start(), calls=%async_computation.7 | async-start | bytes 10813440 | tf_op jit(solution)/shard_map/all_gather | solution.py:548
  83.4 49.0 %collective-permute-start = (bf16[64,2048]{1,0:T(8,128)(2,1)}, bf16[64,2048]{1,0:T(8,128)(2,1)}, u32[]{:S(2)}, u32[]{:S(2)}) collective-permute-start(bf16[64,2048]{1,0:T(8,128)(2,1)} %multiply_convert_fusion.1), channel_id=1, source_target_pairs={{0,8},{2,10},{4,12},{6,14},{8,16},{10,18},{12,20},{14,22},{16,24},... | collective-permute-start | bytes 786440 | tf_op jit(solution)/shard_map/ppermute | solution.py:433
  83.8 48.7 %collective-permute-start.1 = (bf16[64,2048]{1,0:T(8,128)(2,1)}, bf16[64,2048]{1,0:T(8,128)(2,1)}, u32[]{:S(2)}, u32[]{:S(2)}) collective-permute-start(bf16[64,2048]{1,0:T(8,128)(2,1)} %multiply_convert_fusion.1), channel_id=1, source_target_pairs={{0,16},{2,18},{4,20},{6,22},{8,24},{10,26},{12,28},{14,30},{16,0},... | collective-permute-start | bytes 786440 | tf_op jit(solution)/shard_map/ppermute | solution.py:433
  87.3 37.0 %collective-permute-start.12 = (bf16[8,128,128]{2,1,0:T(8,128)(2,1)}, bf16[8,128,128]{2,1,0:T(8,128)(2,1)}, u32[]{:S(2)}, u32[]{:S(2)}) collective-permute-start(bf16[8,128,128]{2,1,0:T(8,128)(2,1)} %dynamic-slice_bitcast_fusion.1), channel_id=1, source_target_pairs={{0,1},{1,0},{2,3},{3,2},{4,5},{5,4},{6,7},{7,6},{8,9},{9,8},{10,11... | collective-permute-start | bytes 786440 | tf_op jit(solution)/shard_map/ppermute | solution.py:425
  126.5 33.4 %all-to-all-start.1 = ((bf16[4,768,128]{2,1,0:T(8,128)(2,1)}), bf16[4,768,128]{2,1,0:T(8,128)(2,1)S(1)}, u32[]{:S(2)}, u32[]{:S(2)}) async-start(bf16[4,768,128]{2,1,0:T(8,128)(2,1)} %pad_maximum_fusion.9), calls=%async_computation.1 | async-start | bytes 1572864 | tf_op jit(solution)/shard_map/all_to_all | solution.py:439
  130.0 496.4 %reduce-scatter.4.cloned.1.call-start = ((), (), s32[]{:S(2)}) async-start(), calls=%async_computation.8 | async-start | bytes 10813440
  135.0 30.6 %collective-permute-start.8 = (bf16[256,384]{1,0:T(8,128)(2,1)S(1)}, bf16[256,384]{1,0:T(8,128)(2,1)S(1)}, u32[]{:S(2)}, u32[]{:S(2)}) collective-permute-start(bf16[256,384]{1,0:T(8,128)(2,1)S(1)} %convolution_convert_fusion.1), channel_id=1, source_target_pairs={{0,8},{2,10},{4,12},{6,14},{8,16},{10,18},{12,20},{14,22},{16,24},... | collective-permute-start | bytes 589832 | tf_op jit(solution)/shard_map/ppermute | solution.py:433
  137.0 28.7 %collective-permute-start.9 = (bf16[256,384]{1,0:T(8,128)(2,1)S(1)}, bf16[256,384]{1,0:T(8,128)(2,1)S(1)}, u32[]{:S(2)}, u32[]{:S(2)}) collective-permute-start(bf16[256,384]{1,0:T(8,128)(2,1)S(1)} %convolution_convert_fusion.1), channel_id=1, source_target_pairs={{0,16},{2,18},{4,20},{6,22},{8,24},{10,26},{12,28},{14,30},{16,0},... | collective-permute-start | bytes 589832 | tf_op jit(solution)/shard_map/ppermute | solution.py:433
  139.3 46.4 %collective-permute-start.10 = (bf16[256,384]{1,0:T(8,128)(2,1)S(1)}, bf16[256,384]{1,0:T(8,128)(2,1)S(1)}, u32[]{:S(2)}, u32[]{:S(2)}) collective-permute-start(bf16[256,384]{1,0:T(8,128)(2,1)S(1)} %convolution_convert_fusion.1), channel_id=1, source_target_pairs={{0,24},{2,26},{4,28},{6,30},{8,0},{10,2},{12,4},{14,6},{16,8},{18,... | collective-permute-start | bytes 589832 | tf_op jit(solution)/shard_map/ppermute | solution.py:433
  159.9 30.7 %collective-permute-start.13 = (bf16[4,768,128]{2,1,0:T(8,128)(2,1)S(1)}, bf16[4,768,128]{2,1,0:T(8,128)(2,1)}, u32[]{:S(2)}, u32[]{:S(2)}) collective-permute-start(bf16[4,768,128]{2,1,0:T(8,128)(2,1)S(1)} %all-to-all-done.1), channel_id=1, source_target_pairs={{0,2},{2,0},{4,6},{6,4},{8,10},{10,8},{12,14},{14,12},{16,18},{18,... | collective-permute-start | bytes 2359304 | tf_op jit(solution)/shard_map/ppermute | solution.py:436
  161.0 35.1 %collective-permute-start.14 = (bf16[4,768,128]{2,1,0:T(8,128)(2,1)S(1)}, bf16[4,768,128]{2,1,0:T(8,128)(2,1)}, u32[]{:S(2)}, u32[]{:S(2)}) collective-permute-start(bf16[4,768,128]{2,1,0:T(8,128)(2,1)S(1)} %all-to-all-done.1), channel_id=1, source_target_pairs={{0,4},{2,6},{4,0},{6,2},{8,12},{10,14},{12,8},{14,10},{16,20},{18,... | collective-permute-start | bytes 2359304 | tf_op jit(solution)/shard_map/ppermute | solution.py:436
  185.7 135.6 %collective-permute-start.32 = (bf16[4,3,704,512]{3,2,1,0:T(8,128)(2,1)}, bf16[4,3,704,512]{3,2,1,0:T(8,128)(2,1)}, u32[]{:S(2)}, u32[]{:S(2)}) collective-permute-start(bf16[4,3,704,512]{3,2,1,0:T(8,128)(2,1)} %bitcast.268), channel_id=1, source_target_pairs={{0,1},{1,0},{2,3},{3,2},{4,5},{5,4},{6,7},{7,6},{8,9},{9,8},{10,11... | collective-permute-start | bytes 25952264 | tf_op jit(solution)/shard_map/ppermute | solution.py:425
  195.3 29.3 %collective-permute-start.18 = (bf16[256,512]{1,0:T(8,128)(2,1)}, bf16[256,512]{1,0:T(8,128)(2,1)}, u32[]{:S(2)}, u32[]{:S(2)}) collective-permute-start(bf16[256,512]{1,0:T(8,128)(2,1)} %get-tuple-element.187), channel_id=1, source_target_pairs={{0,2},{2,0},{4,6},{6,4},{8,10},{10,8},{12,14},{14,12},{16,18},{18,... | collective-permute-start | bytes 786440 | tf_op jit(solution)/shard_map/ppermute | solution.py:436
  195.8 32.6 %collective-permute-start.19 = (bf16[256,512]{1,0:T(8,128)(2,1)}, bf16[256,512]{1,0:T(8,128)(2,1)}, u32[]{:S(2)}, u32[]{:S(2)}) collective-permute-start(bf16[256,512]{1,0:T(8,128)(2,1)} %get-tuple-element.187), channel_id=1, source_target_pairs={{0,4},{2,6},{4,0},{6,2},{8,12},{10,14},{12,8},{14,10},{16,20},{18,... | collective-permute-start | bytes 786440 | tf_op jit(solution)/shard_map/ppermute | solution.py:436
  203.7 24.7 %collective-permute-start.20 = (bf16[256,512]{1,0:T(8,128)(2,1)}, bf16[256,512]{1,0:T(8,128)(2,1)}, u32[]{:S(2)}, u32[]{:S(2)}) collective-permute-start(bf16[256,512]{1,0:T(8,128)(2,1)} %get-tuple-element.187), channel_id=1, source_target_pairs={{0,6},{2,4},{4,2},{6,0},{8,14},{10,12},{12,10},{14,8},{16,22},{18,... | collective-permute-start | bytes 786440 | tf_op jit(solution)/shard_map/ppermute | solution.py:436
  224.6 39.9 %collective-permute-start.29 = (bf16[64,2048]{1,0:T(8,128)(2,1)S(1)}, bf16[64,2048]{1,0:T(8,128)(2,1)S(1)}, u32[]{:S(2)}, u32[]{:S(2)}) collective-permute-start(bf16[64,2048]{1,0:T(8,128)(2,1)S(1)} %reshape.486), channel_id=1, source_target_pairs={{0,8},{2,10},{4,12},{6,14},{8,16},{10,18},{12,20},{14,22},{16,24},... | collective-permute-start | bytes 786440 | tf_op jit(solution)/shard_map/ppermute | solution.py:433
  262.4 29.7 %collective-permute-start.24 = (bf16[64,2048]{1,0:T(8,128)(2,1)S(1)}, bf16[64,2048]{1,0:T(8,128)(2,1)S(1)}, u32[]{:S(2)}, u32[]{:S(2)}) collective-permute-start(bf16[64,2048]{1,0:T(8,128)(2,1)S(1)} %get-tuple-element.143), channel_id=1, source_target_pairs={{0,16},{2,18},{4,20},{6,22},{8,24},{10,26},{12,28},{14,30},{16,0},... | collective-permute-start | bytes 786440 | tf_op jit(solution)/shard_map/ppermute | solution.py:433
  262.6 29.5 %collective-permute-start.25 = (bf16[64,2048]{1,0:T(8,128)(2,1)S(1)}, bf16[64,2048]{1,0:T(8,128)(2,1)S(1)}, u32[]{:S(2)}, u32[]{:S(2)}) collective-permute-start(bf16[64,2048]{1,0:T(8,128)(2,1)S(1)} %get-tuple-element.142), channel_id=1, source_target_pairs={{0,8},{2,10},{4,12},{6,14},{8,16},{10,18},{12,20},{14,22},{16,24},... | collective-permute-start | bytes 786440 | tf_op jit(solution)/shard_map/ppermute | solution.py:433
  264.5 38.8 %collective-permute-start.30 = (bf16[64,2048]{1,0:T(8,128)(2,1)S(1)}, bf16[64,2048]{1,0:T(8,128)(2,1)S(1)}, u32[]{:S(2)}, u32[]{:S(2)}) collective-permute-start(bf16[64,2048]{1,0:T(8,128)(2,1)S(1)} %reshape.486), channel_id=1, source_target_pairs={{0,16},{2,18},{4,20},{6,22},{8,24},{10,26},{12,28},{14,30},{16,0},... | collective-permute-start | bytes 786440 | tf_op jit(solution)/shard_map/ppermute | solution.py:433
  269.2 37.2 %collective-permute-start.31 = (bf16[64,2048]{1,0:T(8,128)(2,1)S(1)}, bf16[64,2048]{1,0:T(8,128)(2,1)S(1)}, u32[]{:S(2)}, u32[]{:S(2)}) collective-permute-start(bf16[64,2048]{1,0:T(8,128)(2,1)S(1)} %reshape.486), channel_id=1, source_target_pairs={{0,24},{2,26},{4,28},{6,30},{8,0},{10,2},{12,4},{14,6},{16,8},{18,... | collective-permute-start | bytes 786440 | tf_op jit(solution)/shard_map/ppermute | solution.py:433
  389.4 23.0 %collective-permute-start.33 = (bf16[64,2048]{1,0:T(8,128)(2,1)S(1)}, bf16[64,2048]{1,0:T(8,128)(2,1)S(1)}, u32[]{:S(2)}, u32[]{:S(2)}) collective-permute-start(bf16[64,2048]{1,0:T(8,128)(2,1)S(1)} %get-tuple-element.138), channel_id=1, source_target_pairs={{0,24},{2,26},{4,28},{6,30},{8,0},{10,2},{12,4},{14,6},{16,8},{18,... | collective-permute-start | bytes 786440 | tf_op jit(solution)/shard_map/ppermute | solution.py:433
  392.6 40.4 %collective-permute-start.34 = (bf16[64,2048]{1,0:T(8,128)(2,1)S(1)}, bf16[64,2048]{1,0:T(8,128)(2,1)S(1)}, u32[]{:S(2)}, u32[]{:S(2)}) collective-permute-start(bf16[64,2048]{1,0:T(8,128)(2,1)S(1)} %get-tuple-element.140), channel_id=1, source_target_pairs={{0,16},{2,18},{4,20},{6,22},{8,24},{10,26},{12,28},{14,30},{16,0},... | collective-permute-start | bytes 786440 | tf_op jit(solution)/shard_map/ppermute | solution.py:433
  395.4 37.6 %collective-permute-start.35 = (bf16[64,2048]{1,0:T(8,128)(2,1)S(1)}, bf16[64,2048]{1,0:T(8,128)(2,1)S(1)}, u32[]{:S(2)}, u32[]{:S(2)}) collective-permute-start(bf16[64,2048]{1,0:T(8,128)(2,1)S(1)} %get-tuple-element.139), channel_id=1, source_target_pairs={{0,8},{2,10},{4,12},{6,14},{8,16},{10,18},{12,20},{14,22},{16,24},... | collective-permute-start | bytes 786440 | tf_op jit(solution)/shard_map/ppermute | solution.py:433
  502.1 54.5 %collective-permute-start.60 = (bf16[4,4,768,128]{3,2,1,0:T(8,128)(2,1)}, bf16[4,4,768,128]{3,2,1,0:T(8,128)(2,1)}, u32[]{:S(2)}, u32[]{:S(2)}) collective-permute-start(bf16[4,4,768,128]{3,2,1,0:T(8,128)(2,1)} %fusion.2), channel_id=1, source_target_pairs={{0,1},{1,0},{2,3},{3,2},{4,5},{5,4},{6,7},{7,6},{8,9},{9,8},{10,11... | collective-permute-start | bytes 9437192 | tf_op jit(solution)/shard_map/ppermute | solution.py:425
  554.2 66.4 %collective-permute-start.36 = (bf16[64,2048]{1,0:T(8,128)(2,1)}, bf16[64,2048]{1,0:T(8,128)(2,1)}, u32[]{:S(2)}, u32[]{:S(2)}) collective-permute-start(bf16[64,2048]{1,0:T(8,128)(2,1)} %reshape.491), channel_id=1, source_target_pairs={{0,1},{1,0},{2,3},{3,2},{4,5},{5,4},{6,7},{7,6},{8,9},{9,8},{10,11... | collective-permute-start | bytes 786440 | tf_op jit(solution)/shard_map/ppermute | solution.py:425
  560.3 26.9 %collective-permute-start.63 = (bf16[2,2,768,128]{3,2,1,0:T(8,128)(2,1)S(1)}, bf16[2,2,768,128]{3,2,1,0:T(8,128)(2,1)S(1)}, u32[]{:S(2)}, u32[]{:S(2)}) collective-permute-start(bf16[2,2,768,128]{3,2,1,0:T(8,128)(2,1)S(1)} %pad_maximum_fusion.12), channel_id=1, source_target_pairs={{0,4},{2,6},{4,0},{6,2},{8,12},{10,14},{12,8},{14,10},{16,20},{18,... | collective-permute-start | bytes 2359304 | tf_op jit(solution)/shard_map/ppermute | solution.py:436
  562.0 25.1 %collective-permute-start.61 = (bf16[2,2,768,128]{3,2,1,0:T(8,128)(2,1)S(1)}, bf16[2,2,768,128]{3,2,1,0:T(8,128)(2,1)S(1)}, u32[]{:S(2)}, u32[]{:S(2)}) collective-permute-start(bf16[2,2,768,128]{3,2,1,0:T(8,128)(2,1)S(1)} %pad_maximum_fusion.11), channel_id=1, source_target_pairs={{0,2},{2,0},{4,6},{6,4},{8,10},{10,8},{12,14},{14,12},{16,18},{18,... | collective-permute-start | bytes 2359304 | tf_op jit(solution)/shard_map/ppermute | solution.py:436
  591.3 31.3 %collective-permute-start.50 = (bf16[64,2048]{1,0:T(8,128)(2,1)}, bf16[64,2048]{1,0:T(8,128)(2,1)S(1)}, u32[]{:S(2)}, u32[]{:S(2)}) collective-permute-start(bf16[64,2048]{1,0:T(8,128)(2,1)} %get-tuple-element.129), channel_id=1, source_target_pairs={{0,24},{2,26},{4,28},{6,30},{8,0},{10,2},{12,4},{14,6},{16,8},{18,... | collective-permute-start | bytes 786440 | tf_op jit(solution)/shard_map/ppermute | solution.py:433
  591.7 30.9 %collective-permute-start.51 = (bf16[64,2048]{1,0:T(8,128)(2,1)}, bf16[64,2048]{1,0:T(8,128)(2,1)}, u32[]{:S(2)}, u32[]{:S(2)}) collective-permute-start(bf16[64,2048]{1,0:T(8,128)(2,1)} %get-tuple-element.131), channel_id=1, source_target_pairs={{0,16},{2,18},{4,20},{6,22},{8,24},{10,26},{12,28},{14,30},{16,0},... | collective-permute-start | bytes 786440 | tf_op jit(solution)/shard_map/ppermute | solution.py:433
  592.5 23.9 %all-to-all-start.3 = ((bf16[4,64,384]{2,1,0:T(8,128)(2,1)}), bf16[4,64,384]{2,1,0:T(8,128)(2,1)}, u32[]{:S(2)}, u32[]{:S(2)}) async-start(bf16[4,64,384]{2,1,0:T(8,128)(2,1)} %pad_maximum_fusion.30), calls=%async_computation.3 | async-start | bytes 393216 | tf_op jit(solution)/shard_map/all_to_all | solution.py:439
  597.9 24.7 %collective-permute-start.52 = (bf16[64,2048]{1,0:T(8,128)(2,1)}, bf16[64,2048]{1,0:T(8,128)(2,1)}, u32[]{:S(2)}, u32[]{:S(2)}) collective-permute-start(bf16[64,2048]{1,0:T(8,128)(2,1)} %get-tuple-element.130), channel_id=1, source_target_pairs={{0,8},{2,10},{4,12},{6,14},{8,16},{10,18},{12,20},{14,22},{16,24},... | collective-permute-start | bytes 786440 | tf_op jit(solution)/shard_map/ppermute | solution.py:433
  638.4 52.2 %all-to-all-start.5 = ((bf16[4,2112,128]{2,1,0:T(8,128)(2,1)}), bf16[4,2112,128]{2,1,0:T(8,128)(2,1)S(1)}, u32[]{:S(2)}, u32[]{:S(2)}) async-start(bf16[4,2112,128]{2,1,0:T(8,128)(2,1)} %copy.200), calls=%async_computation.5 | async-start | bytes 4325376 | tf_op jit(solution)/shard_map/all_to_all | solution.py:439
  (95 other events, 1012.7 us)
Sparse Core Ops, SparseCore 0:
  79.5 106.1 all-gather.1
  378.9 93.2 reduce-scatter.3

commit v3 on v1

v3 whole, which is shorter than its diff:
```python
import functools
import math

import jax
import jax.numpy as jnp
from jax import lax
from jax.experimental import pallas as pl
from jax.experimental.pallas import tpu as pltpu
from jax.sharding import PartitionSpec as P

EPSILON = 1e-06
ROPE_BASE = 10000.0
MASKED = -1e30
HEAD = 256
SQUARE = 4
VMEM_LIMIT = 56 * 1024 * 1024
BF16 = jnp.bfloat16
F32 = jnp.float32


def matmul(left, right):
    return jnp.dot(left, right, preferred_element_type=F32)


def contract_rows(left, right):
    return lax.dot_general(left, right, (((0,), (0,)), ((), ())), preferred_element_type=F32)


def times_transposed(left, right):
    return lax.dot_general(left, right, (((1,), (1,)), ((), ())), preferred_element_type=F32)


def inverse_rms(vector):
    return lax.rsqrt(jnp.mean(vector * vector, axis=-1, keepdims=True) + EPSILON)


def norm_back(scaled_grad, normed, inverse):
    return inverse * (scaled_grad - normed * jnp.mean(scaled_grad * normed, axis=-1, keepdims=True))


def angles(position):
    half = HEAD // 2
    frequency = jnp.exp(jnp.arange(half, dtype=F32) * (-math.log(ROPE_BASE) / half))
    phase = position.astype(F32)[:, None] * frequency[None, :]
    return jnp.cos(phase), jnp.sin(phase)


def rotate(vector, cosine, sine):
    half = HEAD // 2
    front, back = vector[:, :half], vector[:, half:]
    return jnp.concatenate([front * cosine - back * sine, back * cosine + front * sine], axis=1)


def unrotate(vector, cosine, sine):
    return rotate(vector, cosine, -sine)


def params(limit=VMEM_LIMIT):
    return pltpu.CompilerParams(vmem_limit_bytes=limit)


VMEM = pl.BlockSpec(memory_space=pltpu.VMEM)
SMEM = pl.BlockSpec(memory_space=pltpu.SMEM)
HBM = pl.BlockSpec(memory_space=pl.ANY)


def shape(dims, dtype=BF16):
    return jax.ShapeDtypeStruct(tuple(dims), dtype)


def project_kernel(layers, at_ref, x_ref, *refs):
    near, far = refs[:layers], refs[layers : 2 * layers]
    part_ref, w_ref, sems = refs[2 * layers :]
    layer, core = at_ref[0], at_ref[2]
    copies = []
    for c, pieces in enumerate((near, far)):
        side = core if c == 0 else 1 - core
        for k, piece in enumerate(pieces):
            first = lax.rem(layer + layers - k, layers) * SQUARE
            target = w_ref.at[pl.ds(first, SQUARE), side]
            copies.append(pltpu.make_async_copy(piece, target, sems.at[c, k]))
    for copy in copies:
        copy.start()
    for copy in copies:
        copy.wait()
    width, share = x_ref.shape[1], w_ref.shape[-1]
    part_ref[...] = matmul(x_ref[...], w_ref[...].reshape(width, share)).astype(BF16)


def project(at, x, near, far):
    layers = len(near)
    rows, width = x.shape
    _, lane_rows, share = near[0].shape
    return pl.pallas_call(
        functools.partial(project_kernel, layers),
        in_specs=[SMEM, VMEM] + [HBM] * (2 * layers),
        out_specs=[VMEM, VMEM],
        out_shape=[
            shape((rows, share)),
            shape((layers * SQUARE, 2, lane_rows, share)),
        ],
        scratch_shapes=[pltpu.SemaphoreType.DMA((2, layers))],
        compiler_params=params(),
        cost_estimate=pl.CostEstimate(
            flops=2 * rows * width * share, bytes_accessed=4 * width * share, transcendentals=0
        ),
        name="project",
    )(at, x, *near, *far)


def latent_kernel(at_ref, cos_ref, sin_ref, *refs):
    parts = refs[:SQUARE]
    hat_ref, low_ref, inverse_ref, kv_ref, kv_sum = refs[SQUARE:]
    corner = at_ref[1]
    rows = kv_ref.shape[0]
    rank_share, kv_share = hat_ref.shape[1] // SQUARE, 2 * HEAD // SQUARE
    for m, part in enumerate(parts):
        b = corner ^ m
        columns = pl.ds(pl.multiple_of(b * rank_share, rank_share), rank_share)
        for i in range(SQUARE):
            source = slice((i ^ m) * rows, (i ^ m) * rows + rows)
            hat_ref[i * rows : (i + 1) * rows, columns] = part[source, :rank_share].astype(F32)
        columns = pl.ds(pl.multiple_of(b * kv_share, kv_share), kv_share)
        kv_sum[:, columns] = part[m * rows : (m + 1) * rows, rank_share:].astype(F32)
    q_lat = hat_ref[...]
    inverse = inverse_rms(q_lat)
    hat = q_lat * inverse
    hat_ref[...] = hat
    low_ref[...] = hat.astype(BF16)
    inverse_ref[...] = inverse
    kv_ref[:, :HEAD] = rotate(kv_sum[:, :HEAD], cos_ref[:rows], sin_ref[:rows]).astype(BF16)
    kv_ref[:, HEAD:] = kv_sum[:, HEAD:].astype(BF16)


def latent(at, cosine, sine, parts, rank):
    count = parts[0].shape[0]
    rows = count // SQUARE
    return pl.pallas_call(
        latent_kernel,
        in_specs=[SMEM] + [VMEM] * (2 + SQUARE),
        out_specs=[VMEM] * 4,
        out_shape=[
            shape((count, rank), F32),
            shape((count, rank)),
            shape((count, 1), F32),
            shape((rows, 2 * HEAD)),
        ],
        scratch_shapes=[pltpu.VMEM((rows, 2 * HEAD), F32)],
        compiler_params=params(),
        cost_estimate=pl.CostEstimate(flops=8 * count * rank, bytes_accessed=10 * count * rank, transcendentals=0),
        name="latent",
    )(at, cosine, sine, *parts)


def head_copies(layers, layer, refs, wq, wo, sems):
    per_layer = wo.shape[1] // layers
    copies = []
    for i, (target, count) in enumerate(((wq, SQUARE), (wo, per_layer))):
        for c in range(2):
            for k in range(layers):
                source = refs[(2 * i + c) * layers + k]
                first = lax.rem(layer + layers - k, layers) * count
                copies.append(
                    pltpu.make_async_copy(source, target.at[c, pl.ds(first, count)], sems.at[i, c, k])
                )
    return copies


def head_q(wq, c, h):
    rank = wq.shape[1] * wq.shape[3]
    half = HEAD // 2
    return jnp.concatenate([wq[c, :, 2 * h + i].reshape(rank, half) for i in range(2)], axis=1)


def head_out(wo, c, h):
    return jnp.concatenate(
        [wo[c, tile, h * HEAD : (h + 1) * HEAD, :] for tile in range(wo.shape[1])], axis=1
    )


def attend_kernel(
    layers, at_ref, lat_ref, cos_ref, sin_ref, natural_ref, start_ref, kv_ref, keys_ref, *refs
):
    weights, (q_ref, o_ref, lse_ref, part_ref, wq, wo, sems) = refs[: 4 * layers], refs[4 * layers :]

    @pl.when(pl.program_id(0) == 0)
    def _():
        copies = head_copies(layers, at_ref[0], weights, wq, wo, sems)
        for copy in copies:
            copy.start()
        for copy in copies:
            copy.wait()

    keys = keys_ref[...]
    allowed = (keys <= natural_ref[...]) & (keys >= start_ref[...])
    pair = wq.shape[2] // 2
    part = None
    for c in range(2):
        for h in range(pair):
            q_pre = matmul(lat_ref[...], head_q(wq, c, h))
            q = rotate(q_pre, cos_ref[...], sin_ref[...]).astype(BF16)
            q = (q.astype(F32) * HEAD**-0.5).astype(BF16)
            scores = jnp.where(allowed, times_transposed(q, kv_ref[:, :HEAD]), MASKED)
            top = jnp.max(scores, axis=-1, keepdims=True)
            terms = jnp.exp(scores - top)
            total = jnp.sum(terms, axis=-1, keepdims=True)
            mix = matmul(terms.astype(BF16), kv_ref[:, HEAD:]) / total
            q_ref[c * pair + h] = q
            o_ref[c * pair + h] = mix
            lse_ref[c * pair + h] = top + jnp.log(total)
            share = matmul(mix.astype(BF16), head_out(wo, c, h))
            part = share if part is None else part + share
    part_ref[...] = part.astype(BF16)


def attend_specs(layers, block, rank, count):
    row = lambda size: pl.BlockSpec((block, size), lambda i: (i, 0))
    whole = lambda dims: pl.BlockSpec(dims, lambda i: (0,) * len(dims))
    half = HEAD // 2
    return [
        SMEM,
        row(rank),
        row(half),
        row(half),
        row(1),
        row(1),
        whole((count, 2 * HEAD)),
        whole((1, count)),
    ] + [HBM] * (4 * layers)


def attend(at, lat, tables, kv, keys, weights, block):
    near_q, far_q, near_out, far_out = weights
    layers = len(near_q)
    rows, rank = lat.shape
    count = kv.shape[0]
    _, tiles_q, rank_rows, half = near_q[0].shape
    per_layer, pair_rows, lanes = near_out[0].shape
    heads, width = tiles_q, per_layer * layers * lanes
    by_head = lambda size: pl.BlockSpec((heads, block, size), lambda i: (0, i, 0))
    return pl.pallas_call(
        functools.partial(attend_kernel, layers),
        grid=(rows // block,),
        in_specs=attend_specs(layers, block, rank, count),
        out_specs=[
            by_head(HEAD),
            by_head(HEAD),
            by_head(1),
            pl.BlockSpec((block, width), lambda i: (i, 0)),
        ],
        out_shape=[
            shape((heads, rows, HEAD)),
            shape((heads, rows, HEAD), F32),
            shape((heads, rows, 1), F32),
            shape((rows, width)),
        ],
        scratch_shapes=[
            pltpu.VMEM((2, layers * SQUARE, tiles_q, rank_rows, half), BF16),
            pltpu.VMEM((2, layers * per_layer, pair_rows, lanes), BF16),
            pltpu.SemaphoreType.DMA((2, 2, layers)),
        ],
        compiler_params=params(),
        cost_estimate=pl.CostEstimate(
            flops=2 * rows * heads * HEAD * (2 * count + rank + width),
            bytes_accessed=4 * count * HEAD + 2 * heads * HEAD * (rank + width),
            transcendentals=rows * heads * count,
        ),
        name="attend",
    )(at, lat, *tables, kv, keys, *near_q, *far_q, *near_out, *far_out)


def attend_back_kernel(
    layers, at_ref, lat_ref, cos_ref, sin_ref, natural_ref, start_ref, kv_ref, keys_ref, *refs
):
    weights, refs = refs[: 4 * layers], refs[4 * layers :]
    q_ref, o_ref, lse_ref, d_attn_ref = refs[:4]
    grads_q, grads_out, d_lat_ref, near_ref, far_ref = refs[4:6], refs[6:8], refs[8], refs[9], refs[10]
    wq, wo, sems, d_kv_sum, d_lat_sum = refs[11:16]
    sums = refs[16:]
    step, steps = pl.program_id(0), pl.num_programs(0)
    layer, corner = at_ref[0], at_ref[1]
    per_layer = wo.shape[1] // layers

    @pl.when(step == 0)
    def _():
        copies = head_copies(layers, layer, weights, wq, wo, sems)
        for copy in copies:
            copy.start()
        d_kv_sum[...] = jnp.zeros_like(d_kv_sum)
        for total in sums:
            total[...] = jnp.zeros_like(total)
        for copy in copies:
            copy.wait()

    def store(c, h, grad_q, grad_out):
        for z in range(layers):
            k = lax.rem(layer + layers - z, layers)
            ranks = grad_q.shape[0] // layers
            rows_here = grad_q[z * ranks : (z + 1) * ranks].astype(BF16)
            for i in range(2):
                tile = rows_here[:, i * 128 : (i + 1) * 128]
                grads_q[c][k, :, 2 * h + i] = tile.reshape(SQUARE, ranks // SQUARE, 128)
            for i in range(per_layer):
                tile = z * per_layer + i
                grads_out[c][k, i, h * HEAD : (h + 1) * HEAD, :] = grad_out[
                    :, tile * 128 : (tile + 1) * 128
                ].astype(BF16)

    keys = keys_ref[...]
    allowed = (keys <= natural_ref[...]) & (keys >= start_ref[...])
    d_attn, lat = d_attn_ref[...], lat_ref[...]
    pair = wq.shape[2] // 2
    d_lat = None
    for c in range(2):
        for h in range(pair):
            q, mix, lse = q_ref[c * pair + h], o_ref[c * pair + h], lse_ref[c * pair + h]
            w_q, w_out = head_q(wq, c, h), head_out(wo, c, h)
            grad_out = contract_rows(mix.astype(BF16), d_attn)
            d_o = times_transposed(d_attn, w_out).astype(BF16)
            delta = jnp.sum(d_o.astype(F32) * mix, axis=-1, keepdims=True)
            scores = times_transposed(q, kv_ref[:, :HEAD])
            probs = jnp.exp(jnp.where(allowed, scores - lse, MASKED))
            d_probs = times_transposed(d_o, kv_ref[:, HEAD:])
            d_scores = (probs * (d_probs - delta)).astype(BF16)
            d_query = matmul(d_scores, kv_ref[:, :HEAD]) * HEAD**-0.5
            probs_low = probs.astype(BF16)
            for some in range(0, d_kv_sum.shape[0], 2048):
                these = slice(some, some + 2048)
                d_kv_sum[these, :HEAD] += contract_rows(d_scores[:, these], q)
                d_kv_sum[these, HEAD:] += contract_rows(probs_low[:, these], d_o)
            d_qpre = unrotate(d_query, cos_ref[...], sin_ref[...]).astype(BF16)
            grad_q = contract_rows(lat, d_qpre)
            share = times_transposed(d_qpre, w_q)
            d_lat = share if d_lat is None else d_lat + share
            if sums:
                sums[0][c, h] += grad_q
                sums[1][c, h] = (sums[1][c, h].astype(F32) + grad_out).astype(BF16)
            else:
                store(c, h, grad_q, grad_out)
    if sums:

        @pl.when(step == steps - 1)
        def _():
            for c in range(2):
                for h in range(pair):
                    store(c, h, sums[0][c, h], sums[1][c, h])

    d_lat_sum[...] = d_lat
    share = d_lat.shape[1] // SQUARE
    dot = jnp.sum(d_lat * lat.astype(F32), axis=-1, keepdims=True)
    for m in range(SQUARE):
        b = corner ^ m
        columns = pl.ds(pl.multiple_of(b * share, share), share)
        d_lat_ref[m, :, :share] = d_lat_sum[:, columns].astype(BF16)
        d_lat_ref[m, :, share:] = jnp.broadcast_to(dot, (d_lat.shape[0], 128)).astype(BF16)

    @pl.when(step == steps - 1)
    def _():
        size = near_ref.shape[0]
        near_ref[...] = d_kv_sum[:size, :].astype(near_ref.dtype)
        far_ref[...] = d_kv_sum[size:, :].astype(BF16)


def attend_back(at, lat, tables, kv, keys, weights, q, o, lse, d_attn, block):
    near_q, far_q, near_out, far_out = weights
    layers = len(near_q)
    rows, rank = lat.shape
    count = kv.shape[0]
    _, tiles_q, rank_rows, half = near_q[0].shape
    per_layer, pair_rows, lanes = near_out[0].shape
    heads, width = tiles_q, per_layer * layers * lanes
    by_head = lambda size: pl.BlockSpec((heads, block, size), lambda i: (0, i, 0))
    whole = lambda dims: pl.BlockSpec(dims, lambda i: (0,) * len(dims))
    q_dims = (layers, SQUARE, tiles_q, rank_rows, half)
    out_dims = (layers, per_layer, pair_rows, lanes)
    d_lat_dims = (SQUARE, rows, rank // SQUARE + 128)
    pair = tiles_q // 2
    sums = []
    if rows != block:
        sums = [pltpu.VMEM((2, pair, rank, HEAD), F32), pltpu.VMEM((2, pair, HEAD, width), BF16)]
    return pl.pallas_call(
        functools.partial(attend_back_kernel, layers),
        grid=(rows // block,),
        in_specs=attend_specs(layers, block, rank, count)
        + [by_head(HEAD), by_head(HEAD), by_head(1), pl.BlockSpec((block, width), lambda i: (i, 0))],
        out_specs=[
            whole(q_dims),
            whole(q_dims),
            whole(out_dims),
            whole(out_dims),
            pl.BlockSpec((SQUARE, block, d_lat_dims[2]), lambda i: (0, i, 0)),
            whole((count // 2, 2 * HEAD)),
            whole((count // 2, 2 * HEAD)),
        ],
        out_shape=[
            shape(q_dims),
            shape(q_dims),
            shape(out_dims),
            shape(out_dims),
            shape(d_lat_dims),
            shape((count // 2, 2 * HEAD), BF16 if sums else F32),
            shape((count // 2, 2 * HEAD)),
        ],
        scratch_shapes=[
            pltpu.VMEM((2, layers * SQUARE, tiles_q, rank_rows, half), BF16),
            pltpu.VMEM((2, layers * per_layer, pair_rows, lanes), BF16),
            pltpu.SemaphoreType.DMA((2, 2, layers)),
            pltpu.VMEM((count, 2 * HEAD), F32),
            pltpu.VMEM((block, rank), F32),
        ]
        + sums,
        compiler_params=params(VMEM_LIMIT + len(sums) * 2**21),
        cost_estimate=pl.CostEstimate(
            flops=2 * rows * heads * HEAD * (5 * count + 2 * rank + 2 * width),
            bytes_accessed=12 * count * HEAD + 4 * heads * HEAD * (rank + width),
            transcendentals=rows * heads * count,
        ),
        name="attend_back",
    )(at, lat, *tables, kv, keys, *near_q, *far_q, *near_out, *far_out, q, o, lse, d_attn)


def latent_back_kernel(layers, at_ref, hat_ref, inverse_ref, d_kv_ref, x_ref, w_ref, *refs):
    parts = refs[:SQUARE]
    d_x_ref, near_ref, far_ref, d_sum = refs[SQUARE:]
    layer, corner, core = at_ref[0], at_ref[1], at_ref[2]
    count, width = x_ref.shape
    rows = count // SQUARE
    share = w_ref.shape[-1]
    rank_share = hat_ref.shape[1] // SQUARE
    for i in range(SQUARE):
        d_sum[i * rows : (i + 1) * rows] = sum(
            part[(i ^ m) * rows : (i ^ m) * rows + rows].astype(F32) for m, part in enumerate(parts)
        )
    columns = pl.ds(pl.multiple_of(corner * rank_share, rank_share), rank_share)
    dot = d_sum[:, rank_share : rank_share + 1] * (1.0 / hat_ref.shape[1])
    d_lat = inverse_ref[...] * (d_sum[:, :rank_share] - hat_ref[:, columns] * dot)
    d_down = jnp.concatenate([d_lat.astype(BF16), d_kv_ref[...]], axis=1)
    weight = w_ref[...].reshape(width, share)
    d_x_ref[...] = times_transposed(d_down, weight).astype(BF16)
    grad = contract_rows(x_ref[...], d_down)
    grad = grad.reshape(layers, SQUARE, 2, near_ref.shape[2], share)
    low, high = grad[:, :, 0], grad[:, :, 1]
    near = jnp.where(core == 0, low, high)
    far = jnp.where(core == 0, high, low).astype(BF16)
    for z in range(layers):
        k = lax.rem(layer + layers - z, layers)
        near_ref[k] = near[z]
        far_ref[k] = far[z]


def latent_back(at, hat, inverse, d_kv, x, weight, parts):
    count, width = x.shape
    places, _, lane_rows, share = weight.shape
    layers = places // SQUARE
    dims = (layers, SQUARE, lane_rows, share)
    return pl.pallas_call(
        functools.partial(latent_back_kernel, layers),
        in_specs=[SMEM] + [VMEM] * (5 + SQUARE),
        out_specs=[VMEM] * 3,
        out_shape=[shape((count, width)), shape(dims, F32), shape(dims)],
        scratch_shapes=[pltpu.VMEM(parts[0].shape, F32)],
        compiler_params=params(),
        cost_estimate=pl.CostEstimate(
            flops=4 * count * width * share, bytes_accessed=10 * width * share, transcendentals=0
        ),
        name="latent_back",
    )(at, hat, inverse, d_kv, x, weight, *parts)


def chunk(ref, corner, m, size):
    tiles = size // 128
    columns = [(t * SQUARE + (corner ^ m)) * 128 for t in range(tiles)]
    return jnp.concatenate([ref[:, pl.ds(pl.multiple_of(c, 128), 128)] for c in columns], axis=1)


def mlp_kernel(at_ref, h_ref, cot_ref, *refs):
    pieces = refs[: 2 * 3 * 5]
    d_h_ref, out_ref, act_near_ref, act_far_ref, weights, sems = refs[2 * 3 * 5 :]
    corner = at_ref[1]
    tiles, units = weights.shape[3], weights.shape[4]
    half = tiles // 2
    copies = []
    for c in range(2):
        for kind in range(3):
            one = []
            for i in range(5):
                target = weights.at[c, kind, min(i, 3)]
                if i >= 3:
                    target = target.at[pl.ds((i - 3) * half, half)]
                source = pieces[(c * 3 + kind) * 5 + i]
                one.append(pltpu.make_async_copy(source, target, sems.at[c, kind, i]))
            copies.append(one)
    for one in copies:
        for copy in one:
            copy.start()
    size = tiles * 128

    def weight(c, kind, m):
        return jnp.concatenate([weights[c, kind, m, t] for t in range(tiles)], axis=1)

    for c, acts in enumerate((act_near_ref, act_far_ref)):

        def product(value_ref, kind):
            for copy in copies[c * 3 + kind]:
                copy.wait()
            return sum(
                times_transposed(chunk(value_ref, corner, m, size), weight(c, kind, m))
                for m in range(SQUARE)
            )

        gate_act, up_proj, d_act = product(h_ref, 0), product(h_ref, 1), product(cot_ref, 2)
        sigmoid_gate = 1.0 / (1.0 + jnp.exp(-gate_act))
        silu_gate = gate_act * sigmoid_gate
        d_gate = d_act * up_proj * sigmoid_gate * (1.0 + gate_act * (1.0 - sigmoid_gate))
        acts[0] = d_gate.astype(BF16)
        acts[1] = (d_act * silu_gate).astype(BF16)
        acts[2] = (silu_gate * up_proj).astype(BF16)
    accumulators = (act_near_ref, act_far_ref)
    for m in range(SQUARE):
        d_h = sum(
            matmul(acts[kind], weight(c, kind, m))
            for c, acts in enumerate(accumulators)
            for kind in range(2)
        )
        out = sum(matmul(acts[2], weight(c, 2, m)) for c, acts in enumerate(accumulators))
        for t in range(tiles):
            here = pl.ds(pl.multiple_of((t * SQUARE + (corner ^ m)) * 128, 128), 128)
            d_h_ref[:, here] = d_h[:, t * 128 : (t + 1) * 128].astype(BF16)
            out_ref[:, here] = out[:, t * 128 : (t + 1) * 128].astype(BF16)


def mlp(at, h, cot, near, far):
    rows, width = h.shape
    tiles, units, lanes = near[0][0].shape
    low = shape((rows, width))
    acts = shape((3, rows, units))
    return pl.pallas_call(
        mlp_kernel,
        in_specs=[SMEM, VMEM, VMEM] + [HBM] * 30,
        out_specs=[VMEM] * 4,
        out_shape=[low, low, acts, acts],
        scratch_shapes=[
            pltpu.VMEM((2, 3, SQUARE, tiles, units, lanes), BF16),
            pltpu.SemaphoreType.DMA((2, 3, 5)),
        ],
        compiler_params=params(),
        cost_estimate=pl.CostEstimate(
            flops=24 * rows * width * units,
            bytes_accessed=12 * width * units + 8 * rows * width,
            transcendentals=2 * rows * units,
        ),
        name="mlp",
    )(at, h, cot, *[piece for side in (near, far) for kind in side for piece in kind])


ROUTES = (((1, 3), 0), ((0, 2), 0), ((2, 3), 1), ((0, 1), 1))


def unit_grads_kernel(at_ref, acts_ref, value_ref, *refs):
    more, outs = refs[: len(refs) - 4], refs[len(refs) - 4 :]
    corner = at_ref[1]
    half = outs[0].shape[1]
    acts = acts_ref[...]
    size = 2 * half * 128
    for m in range(SQUARE):
        grad = contract_rows(acts, chunk(value_ref, corner, m, size))
        for i, (flips, side) in enumerate(ROUTES):
            if m in flips:
                j = flips.index(m)
                for t in range(half):
                    column = (side * half + t) * 128
                    tile = grad[:, column : column + 128]
                    if more:
                        tile = tile + more[i][j, t].astype(F32)
                    outs[i][j, t] = tile.astype(BF16)


def unit_grads(at, acts, value, *more):
    rows, width = value.shape
    units = acts.shape[1]
    dims = (2, width // SQUARE // 256, units, 128)
    return pl.pallas_call(
        unit_grads_kernel,
        in_specs=[SMEM] + [VMEM] * (2 + len(more)),
        out_specs=[VMEM] * 4,
        out_shape=[shape(dims)] * 4,
        compiler_params=params(),
        cost_estimate=pl.CostEstimate(
            flops=2 * rows * width * units, bytes_accessed=2 * width * units * (1 + bool(more)), transcendentals=0
        ),
        name="unit_grads",
    )(at, acts, value, *more)


def local(
    chips,
    tokens,
    attn_gain,
    q_gain,
    w_qdown,
    w_qup,
    w_kv,
    w_out,
    mlp_gain,
    w_gate,
    w_up,
    w_down,
    cotangent,
    seq_lengths,
    block_slots,
):
    layers = chips // SQUARE
    rows, width = tokens.shape[0] // 2, tokens.shape[1]
    lanes = width // chips
    rank = w_qdown.shape[1]
    rank_rows = w_qup.shape[0]
    pair = w_qup.shape[1] // HEAD // SQUARE
    units = w_gate.shape[1] // layers
    half = HEAD // 2
    place = lax.axis_index("seq")
    core = lax.axis_index("tp")
    layer, corner = place // SQUARE, place % SQUARE
    at = jnp.stack([layer, corner, core]).astype(jnp.int32)
    first = core == 0
    lines = [[z * SQUARE + c for z in range(layers)] for c in range(SQUARE)]
    square_groups = [[z * SQUARE + c for c in range(SQUARE)] for z in range(layers)]

    def across(value):
        return lax.ppermute(value, "tp", [(0, 1), (1, 0)])

    def along(value, step):
        pairs = [
            (z * SQUARE + c, (z + step) % layers * SQUARE + c)
            for z in range(layers)
            for c in range(SQUARE)
        ]
        return lax.ppermute(value, "seq", pairs)

    def within(value, flip):
        return lax.ppermute(value, "seq", [(i, i ^ flip) for i in range(chips)])

    def line_exchange(value):
        return lax.all_to_all(value, "seq", 0, 0, axis_index_groups=lines, tiled=True)

    def square_exchange(value):
        return lax.all_to_all(value, "seq", 0, 0, axis_index_groups=square_groups, tiled=True)

    def line_pieces(value):
        return [value] + [along(value, k) for k in range(1, layers)]

    def line_sum(blocks):
        return blocks[0].astype(F32) + sum(
            along(blocks[k], -k).astype(F32) for k in range(1, layers)
        )

    def square_pieces(value):
        return [value] + [within(value, m) for m in range(1, SQUARE)]

    def square_sum(blocks):
        return blocks[0].astype(F32) + sum(
            within(blocks[m], m).astype(F32) for m in range(1, SQUARE)
        )

    def after(value, *earlier):
        return lax.optimization_barrier((value,) + earlier)[0]

    def own(pair_value):
        return lax.dynamic_slice_in_dim(pair_value, core * rows, rows, 0)

    def both(mine, theirs, axis=0):
        return jnp.concatenate(
            [jnp.where(first, mine, theirs), jnp.where(first, theirs, mine)], axis=axis
        )

    def tiled(value):
        if lanes == 128:
            return value
        count, size, _ = value.shape
        value = jnp.swapaxes(value, 0, 1).reshape(size, count * lanes // 128, 128)
        return jnp.swapaxes(value, 0, 1)

    def untiled(value):
        if lanes == 128:
            return value
        count, size, _ = value.shape
        value = jnp.swapaxes(value, 0, 1).reshape(size, count * 128 // lanes, lanes)
        return jnp.swapaxes(value, 0, 1)

    def arranged(value):
        if lanes == 128:
            return value
        shaped = value.reshape(value.shape[0], -1, 128 // lanes, SQUARE, lanes)
        return jnp.swapaxes(shaped, 2, 3).reshape(value.shape)

    def unarranged(value):
        if lanes == 128:
            return value
        shaped = value.reshape(value.shape[0], -1, SQUARE, 128 // lanes, lanes)
        return jnp.swapaxes(shaped, 2, 3).reshape(value.shape)

    inputs = own(tokens).astype(F32)
    x_inverse = inverse_rms(inputs)
    x_hat = inputs * x_inverse
    x_all = jnp.concatenate(square_pieces(x_hat.astype(BF16)))

    gain_rows = attn_gain.astype(F32)[:, None]
    down = jnp.concatenate([w_qdown, w_kv], axis=1)
    rank_share, kv_share = rank // SQUARE, 2 * HEAD // SQUARE

    def shares(value):
        return jnp.stack(
            [
                jnp.concatenate(
                    [
                        value[:, b * rank_share : (b + 1) * rank_share],
                        value[:, rank + b * kv_share : rank + (b + 1) * kv_share],
                    ],
                    axis=1,
                )
                for b in range(SQUARE)
            ]
        )

    def unshares(value):
        return jnp.concatenate(
            [value[b, :, :rank_share] for b in range(SQUARE)]
            + [value[b, :, rank_share:] for b in range(SQUARE)],
            axis=1,
        )

    down_scaled = (down.astype(F32) * gain_rows).astype(BF16)
    down_half = lax.dynamic_slice_in_dim(down_scaled, core * (lanes // 2), lanes // 2, 0)
    down_near = line_pieces(square_exchange(shares(down_half)))
    down_far = [across(piece) for piece in down_near]

    q_gain_rows = q_gain.astype(F32)[:, None]
    qup_scaled = (w_qup.astype(F32) * q_gain_rows).astype(BF16)
    qup_send = qup_scaled.reshape(rank_rows, SQUARE, 2 * pair, half)
    qup_send = jnp.transpose(qup_send, (1, 2, 0, 3))
    qup_own = square_exchange(after(qup_send, down_near[0]))
    out_own = square_exchange(w_out.reshape(SQUARE, pair * HEAD, lanes))
    qup_near = line_pieces(qup_own)
    qup_far = [across(piece) for piece in qup_near]
    out_near = line_pieces(tiled(after(out_own, qup_near[1])))
    out_far = [across(piece) for piece in out_near]
    head_weights = (qup_near, qup_far, out_near, out_far)

    mlp_gain_rows = mlp_gain.astype(F32)[:, None]
    gate_send = (w_gate.astype(F32) * mlp_gain_rows).astype(BF16).T
    up_send = (w_up.astype(F32) * mlp_gain_rows).astype(BF16).T
    mlp_near, mlp_far = [], []
    earlier = out_near[1]
    for sent in (gate_send, up_send, w_down):
        mine = line_exchange(after(sent, earlier).reshape(layers, units, lanes))
        earlier = mine
        mine = tiled(mine)
        size = mine.shape[0] // 2
        one, two = within(mine, 1), within(mine, 2)
        pieces = [mine, one, two, within(one[:size], 2), within(two[size:], 1)]
        mlp_near.append(pieces)
        mlp_far.append([across(piece) for piece in pieces])
    cot_own = own(cotangent)
    cot_all = jnp.concatenate(line_pieces(after(arranged(cot_own), earlier)))

    bounds = jnp.cumsum(seq_lengths)
    starts = bounds - seq_lengths

    def layout(blocks):
        natural = (blocks[:, None] * rows + jnp.arange(rows, dtype=jnp.int32)[None, :]).reshape(-1)
        member = (natural[:, None] >= starts[None, :]) & (natural[:, None] < bounds[None, :])
        return natural, jnp.sum(jnp.where(member, starts[None, :], 0), axis=1)

    back_steps = jnp.arange(layers, dtype=jnp.int32)
    flips = jnp.arange(SQUARE, dtype=jnp.int32)
    owners = (((layer - back_steps) % layers) * SQUARE)[None, :] + (corner ^ flips)[:, None]
    square_slots = block_slots[2 * owners[:, 0] + core]
    row_natural, row_start = layout(square_slots)
    owners = owners.reshape(-1)
    near_natural, _ = layout(block_slots[2 * owners + core])
    far_natural, _ = layout(block_slots[2 * owners + 1 - core])
    key_natural = jnp.concatenate([near_natural, far_natural])[None, :]
    cosine, sine = angles(row_natural - row_start)
    tables = (cosine, sine, row_natural[:, None], row_start[:, None])

    part, down_here = project(at, x_all, down_near, down_far)
    lat_hat, lat_low, lat_inverse, kv_own = latent(at, cosine, sine, square_pieces(part), rank)
    kv_line = jnp.concatenate(line_pieces(kv_own))
    kv_near = jnp.concatenate(square_pieces(kv_line))
    kv_all = jnp.concatenate([kv_near, across(kv_near)])

    block = max(32, min(SQUARE * rows, 2**30 // kv_all.shape[0] ** 2))
    queries, attn_mix, log_total, attn_part = attend(
        at, lat_low, tables, kv_all, key_natural, head_weights, block
    )
    hidden = inputs + square_sum(attn_part.reshape(SQUARE, rows, width))
    h_inverse = inverse_rms(hidden)
    h_hat = hidden * h_inverse
    h_all = jnp.concatenate(line_pieces(arranged(h_hat.astype(BF16))))

    d_h_part, mlp_part, acts_near, acts_far = mlp(at, h_all, cot_all, mlp_near, mlp_far)
    d_hscaled = unarranged(line_sum(d_h_part.reshape(layers, rows, width)))
    d_hidden = cot_own.astype(F32) + norm_back(d_hscaled, h_hat, h_inverse)
    d_attn_all = jnp.concatenate(square_pieces(d_hidden.astype(BF16)))
    mlp_own = unarranged(line_sum(mlp_part.reshape(layers, rows, width)))
    layer_own = (hidden + mlp_own).astype(BF16)
    layer_out = both(layer_own, across(layer_own))

    mlp_back = []
    for kind, value in ((0, h_all), (1, h_all), (2, cot_all)):
        far_grads = unit_grads(at, acts_far[kind], value)
        sent_a, kept_a, sent_b, kept_b = unit_grads(
            at, acts_near[kind], value, *[across(grad) for grad in far_grads]
        )
        sums = []
        for sent, kept, flip, next_flip in ((sent_a, kept_a, 1, 2), (sent_b, kept_b, 2, 1)):
            total = kept.astype(F32) + within(sent, flip).astype(F32)
            sums.append(total[0] + within(total[1].astype(BF16), next_flip).astype(F32))
        back = line_exchange(untiled(jnp.concatenate(sums).astype(BF16)))
        mlp_back.append(back.reshape(layers * units, lanes).astype(F32))
    gate_back, up_back, down_part = mlp_back[0].T, mlp_back[1].T, mlp_back[2]
    gate_part, up_part = gate_back * mlp_gain_rows, up_back * mlp_gain_rows
    mlp_gain_part = jnp.sum(gate_back * w_gate.astype(F32) + up_back * w_up.astype(F32), axis=1)

    grad_q_near, grad_q_far, grad_out_near, grad_out_far, d_lat_parts, d_kv_near, d_kv_far = attend_back(
        at, lat_low, tables, kv_all, key_natural, head_weights, queries, attn_mix, log_total, d_attn_all, block
    )
    d_kv_low = (d_kv_near.astype(F32) + across(d_kv_far).astype(F32)).astype(BF16)
    d_kv_line = square_sum(d_kv_low.reshape(SQUARE, layers * rows, 2 * HEAD)).astype(BF16)
    d_kv_own = line_sum(d_kv_line.reshape(layers, rows, 2 * HEAD))
    d_kv_own = jnp.concatenate(
        [unrotate(d_kv_own[:, :HEAD], cosine[:rows], sine[:rows]), d_kv_own[:, HEAD:]], axis=1
    ).astype(BF16)
    kv_share_of = lambda m: lax.dynamic_slice_in_dim(d_kv_own, (corner ^ m) * kv_share, kv_share, 1)
    d_kv_share = jnp.concatenate(
        [kv_share_of(0)] + [within(kv_share_of(m), m) for m in range(1, SQUARE)]
    )
    d_lat_received = [d_lat_parts[0]] + [within(d_lat_parts[m], m) for m in range(1, SQUARE)]

    d_x_part, down_grad_near, down_grad_far = latent_back(
        at, lat_hat, lat_inverse, d_kv_share, x_all, down_here, d_lat_received
    )
    d_xscaled = square_sum(d_x_part.reshape(SQUARE, rows, width))
    token_own = (d_hidden + norm_back(d_xscaled, x_hat, x_inverse)).astype(BF16)
    token_grad = both(token_own, across(token_own))
    down_sum = (down_grad_near + across(down_grad_far).astype(F32)).astype(BF16)
    down_back = unshares(square_exchange(line_sum(down_sum).astype(BF16))).astype(F32)
    down_back = both(down_back, across(down_back))
    attn_gain_part = jnp.sum(down_back * down.astype(F32), axis=1)
    down_grad = down_back * gain_rows
    qdown_part, kv_part = down_grad[:, :rank], down_grad[:, rank:]

    def head_back(near, far):
        total = (near.astype(F32) + across(far).astype(F32)).astype(BF16)
        return line_sum(total).astype(BF16)

    qup_back = square_exchange(head_back(grad_q_near, grad_q_far))
    qup_back = jnp.transpose(qup_back, (2, 0, 1, 3)).reshape(rank_rows, -1).astype(F32)
    out_back = square_exchange(untiled(head_back(grad_out_near, grad_out_far)))
    out_part = out_back.reshape(-1, lanes).astype(F32)
    qup_part = qup_back * q_gain_rows
    q_gain_half = jnp.sum(qup_back * w_qup.astype(F32), axis=1)
    gain_parts = jnp.concatenate([q_gain_half, mlp_gain_part])
    gain_parts = gain_parts + across(gain_parts)
    q_gain_part, mlp_gain_part = gain_parts[:rank_rows], gain_parts[rank_rows:]
    return (
        layer_out,
        token_grad,
        attn_gain_part,
        q_gain_part,
        qdown_part,
        qup_part,
        kv_part,
        out_part,
        mlp_gain_part,
        gate_part,
        up_part,
        down_part,
    )


def solution(mesh):
    in_specs = (
        P("seq", None),
        P("seq"),
        P("seq"),
        P("seq", None),
        P("seq", "tp"),
        P("seq", None),
        P("tp", "seq"),
        P("seq"),
        P("seq", "tp"),
        P("seq", "tp"),
        P("tp", "seq"),
        P("seq", None),
        P(),
        P(),
    )
    out_specs = (
        P("seq", None),
        P("seq", None),
        P("seq"),
        P("seq"),
        P("seq", None),
        P("seq", "tp"),
        P("seq", None),
        P("tp", "seq"),
        P("seq"),
        P("seq", "tp"),
        P("seq", "tp"),
        P("tp", "seq"),
    )
    body = functools.partial(local, mesh.shape["seq"])
    return jax.shard_map(body, mesh=mesh, in_specs=in_specs, out_specs=out_specs, check_vma=False)
```

time: 785 us -> 713 us (0.908)
  waiting for transfers between devices: 436 us -> 283 us
  starting transfers between devices: 113 us -> 241 us
  Pallas kernels: 24.9 us -> 88.8 us
  local copies, waits for them, and re-layouts: 89.1 us -> 43.1 us
  matrix products: 35.8 us -> 0 us
  other arithmetic: 71.4 us -> 47.9 us
    ppermute x30 -> x51, waiting for transfers between devices: 297 us -> 101 us  [within(): return lax.ppermute(value, 'seq', [(i, i ^ flip) for i in range(chips)])]
    pallas_call x2 -> x12, Pallas kernels: 24.9 us -> 88.8 us  [the longest x6 24.2 us: unit_grads(): pl.pallas_call(unit_grads_kernel, in_specs=[SMEM] + [VMEM] * (2 + len(mor...]
    all_to_all x4 -> x12, starting transfers between devices: 20 us -> 83.7 us  [the longest x6 60.8 us: line_exchange(): lax.all_to_all(value, 'seq', 0, 0, axis_index_groups=lines, tiled=True)]
    all_to_all x4 -> x12, waiting for transfers between devices: 15.1 us -> 72.3 us  [the longest x6 54.6 us: line_exchange(): lax.all_to_all(value, 'seq', 0, 0, axis_index_groups=lines, tiled=True)]
    dot_general x27 -> x0, matrix products: 35.8 us -> none  [the longest x11 12.8 us: times_transposed(): lax.dot_general(left, right, (((1,), (1,)), ((), ())), preferred_element_...]
    ppermute x30 -> x51, starting transfers between devices: 36.1 us -> 66.9 us  [within(): return lax.ppermute(value, 'seq', [(i, i ^ flip) for i in range(chips)])]
    ppermute x30 -> x36, starting transfers between devices: 53.5 us -> 81.1 us  [along(): return lax.ppermute(value, 'seq', pairs)]
    ppermute x30 -> x36, waiting for transfers between devices: 122 us -> 106 us  [along(): return lax.ppermute(value, 'seq', pairs)]
  transfers between devices with their start and end apart: 82 -> 147, of which waited for: 40 -> 53; matrix products, arithmetic and copies ran while one was open for 22% -> 11% of each run, Pallas kernels for 1% -> 9%
where the time goes in v3:
time: 713 us; the launch traced here: 705 us
  waiting for transfers between devices  283 us (40%)
  starting transfers between devices  241 us (34%)
  Pallas kernels  88.8 us (12%)
  other arithmetic  47.9 us (7%)
  local copies, waits for them, and re-layouts  43.1 us (6%)
    ppermute x36, waiting for transfers between devices, along(): return lax.ppermute(value, 'seq', pairs)  106 us
    ppermute x51, waiting for transfers between devices, within(): return lax.ppermute(value, 'seq', [(i, i ^ flip) for i in range(chips)])  101 us
    ppermute x36, starting transfers between devices, along(): return lax.ppermute(value, 'seq', pairs)  81.1 us
    ppermute x51, starting transfers between devices, within(): return lax.ppermute(value, 'seq', [(i, i ^ flip) for i in range(chips)])  66.9 us
    all_to_all x6, starting transfers between devices, line_exchange(): lax.all_to_all(value, 'seq', 0, 0, axis_index_groups=lines, tiled=True)  60.8 us
    all_to_all x6, waiting for transfers between devices, line_exchange(): lax.all_to_all(value, 'seq', 0, 0, axis_index_groups=lines, tiled=True)  54.6 us
    pallas_call x6, Pallas kernels, unit_grads(): pl.pallas_call(unit_grads_kernel, in_specs=[SMEM] + [VMEM] * (2 + len(mor...  24.2 us
    all_to_all x6, starting transfers between devices, square_exchange(): lax.all_to_all(value, 'seq', 0, 0, axis_index_groups=square_groups, tiled...  22.9 us
  transfers between devices with their start and end apart: 147, of which 53 were waited for; matrix products, arithmetic and copies ran while one was open for 11% of the time, Pallas kernels for 9%

profile of v3, /device:TPU:0, one launch (start us, length us, event | category | flops | bytes accessed | tf_op | source)
XLA Modules:
  0.0 705.3 jit_solution(12957128573576056110)
XLA Ops:
  31.0 7.5 %collective-permute-done.4.refs_2_ = bf16[4,64,384]{2,1,0:T(8,128)(2,1)S(1)} collective-permute-done((bf16[4,64,384]{2,1,0:T(8,128)(2,1)S(1)}, bf16[4,64,384]{2,1,0:T(8,128)(2,1)S(1)}, u32[]{:S(2)}, u32[]{:S(2)}) %collective-permute-start.4) | collective-permute-done | bytes 196640 | tf_op jit(solution)/shard_map/ppermute | solution.py:637
  62.0 4.6 collective-permute-start.13
  94.9 6.4 collective-permute-done.21.refs_2_
  104.1 13.5 %collective-permute-start.28 = (bf16[4,512,128]{2,1,0:T(8,128)(2,1)}, bf16[4,512,128]{2,1,0:T(8,128)(2,1)}, u32[]{:S(2)}, u32[]{:S(2)}) collective-permute-start(bf16[4,512,128]{2,1,0:T(8,128)(2,1)} %all-to-all-done.2.refs_8_), channel_id=1, source_target_pairs={{0,16},{2,18},{4,20},{6,22},{8,24},{10,26},{12,28},{14,30},{16,0},... | collective-permute-start | bytes 1572872 | tf_op jit(solution)/shard_map/ppermute | solution.py:637
  123.4 18.6 %collective-permute-done.28.refs_10_ = bf16[4,512,128]{2,1,0:T(8,128)(2,1)} collective-permute-done((bf16[4,512,128]{2,1,0:T(8,128)(2,1)}, bf16[4,512,128]{2,1,0:T(8,128)(2,1)}, u32[]{:S(2)}, u32[]{:S(2)}) %collective-permute-start.28) | collective-permute-done | bytes 524320 | tf_op jit(solution)/shard_map/ppermute | solution.py:637
  146.1 15.4 %all-to-all-start.3 = ((bf16[4,704,128]{2,1,0:T(8,128)(2,1)}), bf16[4,704,128]{2,1,0:T(8,128)(2,1)S(1)}, u32[]{:S(2)}, u32[]{:S(2)}) async-start(bf16[4,704,128]{2,1,0:T(8,128)(2,1)} %bitcast.17), calls=%async_computation.3 | async-start | bytes 1441792 | tf_op jit(solution)/shard_map/all_to_all | solution.py:643
  162.6 13.7 %attend.1 = (bf16[4,256,256]{2,1,0:T(8,128)(2,1)}, f32[4,256,256]{2,1,0:T(8,128)}, f32[4,256,1]{2,1,0:T(8,128)}, bf16[256,2048]{1,0:T(8,128)(2,1)}) custom-call(s32[3]{0:T(128)} %pad_add_fusion.1.at_ref, bf16[256,1024]{1,0:T(8,128)(2,1)} %get-tuple-element.67.lat_ref, f32[256,128]{1,0:T(8,128)} %get-tuple-element.208.cos_ref, ...), custom_call_target="tpu_custom_call" | custom-call | flops 3758096384 | bytes 8388608 | tf_op jit(solution)/shard_map/attend/pallas_call | solution.py:241
  182.8 5.1 all-to-all-start.4
  200.4 7.5 %collective-permute-done.43.refs_1_ = bf16[4,704,128]{2,1,0:T(8,128)(2,1)S(1)} collective-permute-done((bf16[4,704,128]{2,1,0:T(8,128)(2,1)S(1)}, bf16[4,704,128]{2,1,0:T(8,128)(2,1)S(1)}, u32[]{:S(2)}, u32[]{:S(2)}) %collective-permute-start.43) | collective-permute-done | bytes 720928 | tf_op jit(solution)/shard_map/ppermute | solution.py:640
  212.3 6.0 all-to-all-done.4.refs_5_
  225.6 7.4 %all-to-all-start.5 = ((bf16[4,704,128]{2,1,0:T(8,128)(2,1)}), bf16[4,704,128]{2,1,0:T(8,128)(2,1)}, u32[]{:S(2)}, u32[]{:S(2)}) async-start(bf16[4,704,128]{2,1,0:T(8,128)(2,1)} %bitcast.19), calls=%async_computation.5 | async-start | bytes 1441792 | tf_op jit(solution)/shard_map/all_to_all | solution.py:643
  236.7 11.1 %collective-permute-done.46.refs_4_ = bf16[2,704,128]{2,1,0:T(8,128)(2,1)} collective-permute-done((bf16[2,704,128]{2,1,0:T(8,128)(2,1)S(1)}, bf16[2,704,128]{2,1,0:T(8,128)(2,1)}, u32[]{:S(2)}, u32[]{:S(2)}) %collective-permute-start.46) | collective-permute-done | bytes 360480 | tf_op jit(solution)/shard_map/ppermute | solution.py:640
  266.4 13.5 %collective-permute-done.41 = bf16[64,2048]{1,0:T(8,128)(2,1)S(1)} collective-permute-done((bf16[64,2048]{1,0:T(8,128)(2,1)S(1)}, bf16[64,2048]{1,0:T(8,128)(2,1)S(1)}, u32[]{:S(2)}, u32[]{:S(2)}) %collective-permute-start.41) | collective-permute-done | bytes 262176 | tf_op jit(solution)/shard_map/ppermute | solution.py:637
  292.6 8.0 %collective-permute-done.53.refs_13_ = bf16[2,704,128]{2,1,0:T(8,128)(2,1)S(1)} collective-permute-done((bf16[2,704,128]{2,1,0:T(8,128)(2,1)S(1)}, bf16[2,704,128]{2,1,0:T(8,128)(2,1)S(1)}, u32[]{:S(2)}, u32[]{:S(2)}) %collective-permute-start.53) | collective-permute-done | bytes 360480 | tf_op jit(solution)/shard_map/ppermute | solution.py:640
  303.1 20.4 %mlp.1 = (bf16[256,2048]{1,0:T(8,128)(2,1)}, bf16[256,2048]{1,0:T(8,128)(2,1)}, bf16[3,256,704]{2,1,0:T(8,128)(2,1)}, bf16[3,256,704]{2,1,0:T(8,128)(2,1)}) custom-call(s32[3]{0:T(128)} %pad_add_fusion.1.at_ref, bf16[256,2048]{1,0:T(8,128)(2,1)} %pad_maximum_fusion.1.h_ref.value_ref, bf16[256,2048]{1,0:T(8,128)(2,1)} %copy-done.10, ...), custom_call_target="tpu_custom_call" | custom-call | flops 8858370048 | bytes 21495808 | tf_op jit(solution)/shard_map/mlp/pallas_call | solution.py:537
  337.2 13.4 %collective-permute-done.75 = bf16[64,2048]{1,0:T(8,128)(2,1)S(1)} collective-permute-done((bf16[64,2048]{1,0:T(8,128)(2,1)S(1)}, bf16[64,2048]{1,0:T(8,128)(2,1)S(1)}, u32[]{:S(2)}, u32[]{:S(2)}) %collective-permute-start.75) | collective-permute-done | bytes 262176 | tf_op jit(solution)/shard_map/ppermute | solution.py:637
  352.8 19.4 %collective-permute-done.71 = bf16[64,2048]{1,0:T(8,128)(2,1)S(1)} collective-permute-done((bf16[64,2048]{1,0:T(8,128)(2,1)S(1)}, bf16[64,2048]{1,0:T(8,128)(2,1)S(1)}, u32[]{:S(2)}, u32[]{:S(2)}) %collective-permute-start.71) | collective-permute-done | bytes 262176 | tf_op jit(solution)/shard_map/ppermute | solution.py:637
  387.9 6.6 collective-permute-done.79
  401.1 18.6 %attend_back.1 = (bf16[4,4,4,64,128]{4,3,2,1,0:T(8,128)(2,1)}, bf16[4,4,4,64,128]{4,3,2,1,0:T(8,128)(2,1)}, bf16[4,4,512,128]{3,2,1,0:T(8,128)(2,1)}, bf16[4,4,5...) custom-call(s32[3]{0:T(128)} %pad_add_fusion.1.at_ref, ...), custom_call_target="tpu_custom_call" | custom-call | flops 8589934592 | bytes 18874368 | tf_op jit(solution)/shard_map/attend_back/pallas_call | solution.py:381
  419.7 4.4 unit_grads.11
  429.0 4.5 unit_grads.7
  436.3 4.6 unit_grads.9
  448.3 11.1 %collective-permute-done.110 = bf16[2,2,704,128]{3,2,1,0:T(8,128)(2,1)S(1)} collective-permute-done((bf16[2,2,704,128]{3,2,1,0:T(8,128)(2,1)}, bf16[2,2,704,128]{3,2,1,0:T(8,128)(2,1)S(1)}, u32[]{:S(2)}, u32[]{:S(2)}) %collective-permute-start.110) | collective-permute-done | bytes 720928 | tf_op jit(solution)/shard_map/ppermute | solution.py:640
  462.7 12.2 %collective-permute-done.118 = bf16[2,2,704,128]{3,2,1,0:T(8,128)(2,1)S(1)} collective-permute-done((bf16[2,2,704,128]{3,2,1,0:T(8,128)(2,1)S(1)}, bf16[2,2,704,128]{3,2,1,0:T(8,128)(2,1)S(1)}, u32[]{:S(2)}, u32[]{:S(2)}) %collective-permute-start.118) | collective-permute-done | bytes 720928 | tf_op jit(solution)/shard_map/ppermute | solution.py:640
  499.5 8.1 %collective-permute-done.119 = bf16[2,704,128]{2,1,0:T(8,128)(2,1)S(1)} collective-permute-done((bf16[2,704,128]{2,1,0:T(8,128)(2,1)S(1)}, bf16[2,704,128]{2,1,0:T(8,128)(2,1)S(1)}, u32[]{:S(2)}, u32[]{:S(2)}) %collective-permute-start.119) | collective-permute-done | bytes 360480 | tf_op jit(solution)/shard_map/ppermute | solution.py:640
  537.1 5.0 latent_back.1
  558.3 5.3 all-to-all-done.7
  577.3 9.9 %all-to-all-done.8 = bf16[4,704,128]{2,1,0:T(8,128)(2,1)S(1)} async-done(((bf16[4,704,128]{2,1,0:T(8,128)(2,1)}), bf16[4,704,128]{2,1,0:T(8,128)(2,1)S(1)}, u32[]{:S(2)}, u32[]{:S(2)}) %all-to-all-start.8) | async-done | bytes 720928 | tf_op jit(solution)/shard_map/all_to_all | solution.py:643
  587.2 25.2 %all-to-all-start.9 = ((bf16[4,704,128]{2,1,0:T(8,128)(2,1)}), bf16[4,704,128]{2,1,0:T(8,128)(2,1)}, u32[]{:S(2)}, u32[]{:S(2)}) async-start(bf16[4,704,128]{2,1,0:T(8,128)(2,1)} %pad_maximum_fusion.5), calls=%async_computation.9 | async-start | bytes 1441792 | tf_op jit(solution)/shard_map/all_to_all | solution.py:643
  621.3 23.6 %all-to-all-done.9 = bf16[4,704,128]{2,1,0:T(8,128)(2,1)} async-done(((bf16[4,704,128]{2,1,0:T(8,128)(2,1)}), bf16[4,704,128]{2,1,0:T(8,128)(2,1)}, u32[]{:S(2)}, u32[]{:S(2)}) %all-to-all-start.9) | async-done | bytes 720928 | tf_op jit(solution)/shard_map/all_to_all | solution.py:643
  663.9 15.1 %all-to-all-done.11 = bf16[4,704,128]{2,1,0:T(8,128)(2,1)} async-done(((bf16[4,704,128]{2,1,0:T(8,128)(2,1)}), bf16[4,704,128]{2,1,0:T(8,128)(2,1)}, u32[]{:S(2)}, u32[]{:S(2)}) %all-to-all-start.11) | async-done | bytes 720928 | tf_op jit(solution)/shard_map/all_to_all | solution.py:643
  698.2 5.6 all-to-all-done.10
  (598 shorter events, 351.4 us)
Async XLA Ops:
  7.4 31.7 %collective-permute-start.2 = (bf16[64,2048]{1,0:T(8,128)(2,1)S(1)}, bf16[64,2048]{1,0:T(8,128)(2,1)S(1)}, u32[]{:S(2)}, u32[]{:S(2)}) collective-permute-start(bf16[64,2048]{1,0:T(8,128)(2,1)S(1)} %fusion.7), channel_id=1, source_target_pairs={{0,6},{2,4},{4,2},{6,0},{8,14},{10,12},{12,10},{14,8},{16,22},{18,... | collective-permute-start | bytes 786440 | tf_op jit(solution)/shard_map/ppermute | solution.py:640
  50.6 27.1 %all-to-all-start.1 = ((bf16[4,4,64,128]{3,2,1,0:T(8,128)(2,1)}), bf16[4,4,64,128]{3,2,1,0:T(8,128)(2,1)}, u32[]{:S(2)}, u32[]{:S(2)}) async-start(bf16[4,4,64,128]{3,2,1,0:T(8,128)(2,1)} %bitcast.183), calls=%async_computation.1 | async-start | bytes 524288 | tf_op jit(solution)/shard_map/all_to_all | solution.py:646
  93.6 48.9 %collective-permute-start.19 = (bf16[1024,512]{1,0:T(8,128)(2,1)}, bf16[1024,512]{1,0:T(8,128)(2,1)S(1)}, u32[]{:S(2)}, u32[]{:S(2)}) collective-permute-start(bf16[1024,512]{1,0:T(8,128)(2,1)} %get-tuple-element.177), channel_id=1, source_target_pairs={{0,1},{1,0},{2,3},{3,2},{4,5},{5,4},{6,7},{7,6},{8,9},{9,8},{10,11... | collective-permute-start | bytes 3145736 | tf_op jit(solution)/shard_map/ppermute | solution.py:629
  94.1 26.9 %collective-permute-start.24 = (bf16[4,4,64,128]{3,2,1,0:T(8,128)(2,1)S(1)}, bf16[4,4,64,128]{3,2,1,0:T(8,128)(2,1)S(1)}, u32[]{:S(2)}, u32[]{:S(2)}) collective-permute-start(bf16[4,4,64,128]{3,2,1,0:T(8,128)(2,1)S(1)} %collective-permute-done.20.refs_1_), channel_id=1, source_target_pairs={{0,1},{1,0},{2,3},{3,2},{4,5},{5,4},{6,7},{7,6},{8,9},{9,8},{10,11... | collective-permute-start | bytes 786440 | tf_op jit(solution)/shard_map/ppermute | solution.py:629
  104.1 37.9 %collective-permute-start.28 = (bf16[4,512,128]{2,1,0:T(8,128)(2,1)}, bf16[4,512,128]{2,1,0:T(8,128)(2,1)}, u32[]{:S(2)}, u32[]{:S(2)}) collective-permute-start(bf16[4,512,128]{2,1,0:T(8,128)(2,1)} %all-to-all-done.2.refs_8_), channel_id=1, source_target_pairs={{0,16},{2,18},{4,20},{6,22},{8,24},{10,26},{12,28},{14,30},{16,0},... | collective-permute-start | bytes 1572872 | tf_op jit(solution)/shard_map/ppermute | solution.py:637
  122.8 39.7 %collective-permute-start.30 = (bf16[4,512,128]{2,1,0:T(8,128)(2,1)}, bf16[4,512,128]{2,1,0:T(8,128)(2,1)}, u32[]{:S(2)}, u32[]{:S(2)}) collective-permute-start(bf16[4,512,128]{2,1,0:T(8,128)(2,1)} %all-to-all-done.2.refs_8_), channel_id=1, source_target_pairs={{0,1},{1,0},{2,3},{3,2},{4,5},{5,4},{6,7},{7,6},{8,9},{9,8},{10,11... | collective-permute-start | bytes 1572872 | tf_op jit(solution)/shard_map/ppermute | solution.py:629
  123.0 39.6 %collective-permute-start.31 = (bf16[4,512,128]{2,1,0:T(8,128)(2,1)}, bf16[4,512,128]{2,1,0:T(8,128)(2,1)}, u32[]{:S(2)}, u32[]{:S(2)}) collective-permute-start(bf16[4,512,128]{2,1,0:T(8,128)(2,1)} %collective-permute-done.27.refs_9_), channel_id=1, source_target_pairs={{0,1},{1,0},{2,3},{3,2},{4,5},{5,4},{6,7},{7,6},{8,9},{9,8},{10,11... | collective-permute-start | bytes 1572872 | tf_op jit(solution)/shard_map/ppermute | solution.py:629
  146.1 35.6 %all-to-all-start.3 = ((bf16[4,704,128]{2,1,0:T(8,128)(2,1)}), bf16[4,704,128]{2,1,0:T(8,128)(2,1)S(1)}, u32[]{:S(2)}, u32[]{:S(2)}) async-start(bf16[4,704,128]{2,1,0:T(8,128)(2,1)} %bitcast.17), calls=%async_computation.3 | async-start | bytes 1441792 | tf_op jit(solution)/shard_map/all_to_all | solution.py:643
  182.8 35.4 %all-to-all-start.4 = ((bf16[4,704,128]{2,1,0:T(8,128)(2,1)}), bf16[4,704,128]{2,1,0:T(8,128)(2,1)S(1)}, u32[]{:S(2)}, u32[]{:S(2)}) async-start(bf16[4,704,128]{2,1,0:T(8,128)(2,1)} %bitcast.18), calls=%async_computation.4 | async-start | bytes 1441792 | tf_op jit(solution)/shard_map/all_to_all | solution.py:643
  189.7 43.3 %collective-permute-start.44 = (bf16[4,704,128]{2,1,0:T(8,128)(2,1)S(1)}, bf16[4,704,128]{2,1,0:T(8,128)(2,1)}, u32[]{:S(2)}, u32[]{:S(2)}) collective-permute-start(bf16[4,704,128]{2,1,0:T(8,128)(2,1)S(1)} %all-to-all-done.3.refs_0_), channel_id=1, source_target_pairs={{0,4},{2,6},{4,0},{6,2},{8,12},{10,14},{12,8},{14,10},{16,20},{18,... | collective-permute-start | bytes 2162696 | tf_op jit(solution)/shard_map/ppermute | solution.py:640
  191.1 45.0 %collective-permute-start.55 = (bf16[4,704,128]{2,1,0:T(8,128)(2,1)S(1)}, bf16[4,704,128]{2,1,0:T(8,128)(2,1)}, u32[]{:S(2)}, u32[]{:S(2)}) collective-permute-start(bf16[4,704,128]{2,1,0:T(8,128)(2,1)S(1)} %all-to-all-done.3.refs_0_), channel_id=1, source_target_pairs={{0,1},{1,0},{2,3},{3,2},{4,5},{5,4},{6,7},{7,6},{8,9},{9,8},{10,11... | collective-permute-start | bytes 2162696 | tf_op jit(solution)/shard_map/ppermute | solution.py:629
  208.0 27.4 %collective-permute-start.39 = (bf16[64,2048]{1,0:T(8,128)(2,1)S(1)}, bf16[64,2048]{1,0:T(8,128)(2,1)}, u32[]{:S(2)}, u32[]{:S(2)}) collective-permute-start(bf16[64,2048]{1,0:T(8,128)(2,1)S(1)} %multiply_convert_fusion), channel_id=1, source_target_pairs={{0,24},{2,26},{4,28},{6,30},{8,0},{10,2},{12,4},{14,6},{16,8},{18,... | collective-permute-start | bytes 786440 | tf_op jit(solution)/shard_map/ppermute | solution.py:637
  225.6 27.2 %all-to-all-start.5 = ((bf16[4,704,128]{2,1,0:T(8,128)(2,1)}), bf16[4,704,128]{2,1,0:T(8,128)(2,1)}, u32[]{:S(2)}, u32[]{:S(2)}) async-start(bf16[4,704,128]{2,1,0:T(8,128)(2,1)} %bitcast.19), calls=%async_computation.5 | async-start | bytes 1441792 | tf_op jit(solution)/shard_map/all_to_all | solution.py:643
  252.8 27.1 %collective-permute-start.51 = (bf16[4,704,128]{2,1,0:T(8,128)(2,1)}, bf16[4,704,128]{2,1,0:T(8,128)(2,1)S(1)}, u32[]{:S(2)}, u32[]{:S(2)}) collective-permute-start(bf16[4,704,128]{2,1,0:T(8,128)(2,1)} %all-to-all-done.5.refs_10_), channel_id=1, source_target_pairs={{0,2},{2,0},{4,6},{6,4},{8,10},{10,8},{12,14},{14,12},{16,18},{18,... | collective-permute-start | bytes 2162696 | tf_op jit(solution)/shard_map/ppermute | solution.py:640
  261.3 28.5 %collective-permute-start.61 = (bf16[4,704,128]{2,1,0:T(8,128)(2,1)}, bf16[4,704,128]{2,1,0:T(8,128)(2,1)S(1)}, u32[]{:S(2)}, u32[]{:S(2)}) collective-permute-start(bf16[4,704,128]{2,1,0:T(8,128)(2,1)} %collective-permute-done.47.refs_6_), channel_id=1, source_target_pairs={{0,1},{1,0},{2,3},{3,2},{4,5},{5,4},{6,7},{7,6},{8,9},{9,8},{10,11... | collective-permute-start | bytes 2162696 | tf_op jit(solution)/shard_map/ppermute | solution.py:629
  262.8 27.8 %collective-permute-start.62 = (bf16[4,704,128]{2,1,0:T(8,128)(2,1)}, bf16[4,704,128]{2,1,0:T(8,128)(2,1)S(1)}, u32[]{:S(2)}, u32[]{:S(2)}) collective-permute-start(bf16[4,704,128]{2,1,0:T(8,128)(2,1)} %copy-done.56), channel_id=1, source_target_pairs={{0,1},{1,0},{2,3},{3,2},{4,5},{5,4},{6,7},{7,6},{8,9},{9,8},{10,11... | collective-permute-start | bytes 2162696 | tf_op jit(solution)/shard_map/ppermute | solution.py:629
  333.1 39.1 %collective-permute-start.71 = (bf16[64,2048]{1,0:T(8,128)(2,1)S(1)}, bf16[64,2048]{1,0:T(8,128)(2,1)S(1)}, u32[]{:S(2)}, u32[]{:S(2)}) collective-permute-start(bf16[64,2048]{1,0:T(8,128)(2,1)S(1)} %get-tuple-element.150), channel_id=1, source_target_pairs={{0,16},{2,18},{4,20},{6,22},{8,24},{10,26},{12,28},{14,30},{16,0},... | collective-permute-start | bytes 786440 | tf_op jit(solution)/shard_map/ppermute | solution.py:637
  337.0 35.2 %collective-permute-start.72 = (bf16[64,2048]{1,0:T(8,128)(2,1)S(1)}, bf16[64,2048]{1,0:T(8,128)(2,1)S(1)}, u32[]{:S(2)}, u32[]{:S(2)}) collective-permute-start(bf16[64,2048]{1,0:T(8,128)(2,1)S(1)} %get-tuple-element.149), channel_id=1, source_target_pairs={{0,8},{2,10},{4,12},{6,14},{8,16},{10,18},{12,20},{14,22},{16,24},... | collective-permute-start | bytes 786440 | tf_op jit(solution)/shard_map/ppermute | solution.py:637
  434.4 45.8 %collective-permute-start.102 = (bf16[4,4,4,64,128]{4,3,2,1,0:T(8,128)(2,1)}, bf16[4,4,4,64,128]{4,3,2,1,0:T(8,128)(2,1)S(1)}, u32[]{:S(2)}, u32[]{:S(2)}) collective-permute-start(bf16[4,4,4,64,128]{4,3,2,1,0:T(8,128)(2,1)} %get-tuple-element.91), channel_id=1, source_target_pairs={{0,1},{1,0},{2,3},{3,2},{4,5},{5,4},{6,7},{7,6},{8,9},{9,8},{10,11... | collective-permute-start | bytes 3145736 | tf_op jit(solution)/shard_map/ppermute | solution.py:629
  435.2 46.8 %collective-permute-start.80 = (bf16[1024,512]{1,0:T(8,128)(2,1)}, bf16[1024,512]{1,0:T(8,128)(2,1)S(1)}, u32[]{:S(2)}, u32[]{:S(2)}) collective-permute-start(bf16[1024,512]{1,0:T(8,128)(2,1)} %get-tuple-element.84), channel_id=1, source_target_pairs={{0,1},{1,0},{2,3},{3,2},{4,5},{5,4},{6,7},{7,6},{8,9},{9,8},{10,11... | collective-permute-start | bytes 3145736 | tf_op jit(solution)/shard_map/ppermute | solution.py:629
  446.5 28.4 %collective-permute-start.118 = (bf16[2,2,704,128]{3,2,1,0:T(8,128)(2,1)S(1)}, bf16[2,2,704,128]{3,2,1,0:T(8,128)(2,1)S(1)}, u32[]{:S(2)}, u32[]{:S(2)}) collective-permute-start(bf16[2,2,704,128]{3,2,1,0:T(8,128)(2,1)S(1)} %copy-done.69), channel_id=1, source_target_pairs={{0,2},{2,0},{4,6},{6,4},{8,10},{10,8},{12,14},{14,12},{16,18},{18,... | collective-permute-start | bytes 2162696 | tf_op jit(solution)/shard_map/ppermute | solution.py:640
  459.4 76.9 %collective-permute-start.90 = (bf16[256,384]{1,0:T(8,128)(2,1)S(1)}, bf16[256,384]{1,0:T(8,128)(2,1)S(1)}, u32[]{:S(2)}, u32[]{:S(2)}) collective-permute-start(bf16[256,384]{1,0:T(8,128)(2,1)S(1)} %get-tuple-element.161), channel_id=1, source_target_pairs={{0,2},{2,0},{4,6},{6,4},{8,10},{10,8},{12,14},{14,12},{16,18},{18,... | collective-permute-start | bytes 589832 | tf_op jit(solution)/shard_map/ppermute | solution.py:640
  507.6 28.7 %collective-permute-start.91 = (bf16[256,384]{1,0:T(8,128)(2,1)S(1)}, bf16[256,384]{1,0:T(8,128)(2,1)S(1)}, u32[]{:S(2)}, u32[]{:S(2)}) collective-permute-start(bf16[256,384]{1,0:T(8,128)(2,1)S(1)} %get-tuple-element.160), channel_id=1, source_target_pairs={{0,4},{2,6},{4,0},{6,2},{8,12},{10,14},{12,8},{14,10},{16,20},{18,... | collective-permute-start | bytes 589832 | tf_op jit(solution)/shard_map/ppermute | solution.py:640
  557.1 55.3 %collective-permute-start.97 = (bf16[4,4,64,384]{3,2,1,0:T(8,128)(2,1)}, bf16[4,4,64,384]{3,2,1,0:T(8,128)(2,1)}, u32[]{:S(2)}, u32[]{:S(2)}) collective-permute-start(bf16[4,4,64,384]{3,2,1,0:T(8,128)(2,1)} %get-tuple-element.89), channel_id=1, source_target_pairs={{0,1},{1,0},{2,3},{3,2},{4,5},{5,4},{6,7},{7,6},{8,9},{9,8},{10,11... | collective-permute-start | bytes 2359304 | tf_op jit(solution)/shard_map/ppermute | solution.py:629
  573.5 115.4 %collective-permute-start.124 = (bf16[4,512,128]{2,1,0:T(8,128)(2,1)}, bf16[4,512,128]{2,1,0:T(8,128)(2,1)}, u32[]{:S(2)}, u32[]{:S(2)}) collective-permute-start(bf16[4,512,128]{2,1,0:T(8,128)(2,1)} %get-tuple-element.124), channel_id=1, source_target_pairs={{0,24},{2,26},{4,28},{6,30},{8,0},{10,2},{12,4},{14,6},{16,8},{18,... | collective-permute-start | bytes 1572872 | tf_op jit(solution)/shard_map/ppermute | solution.py:637
  577.3 111.6 %collective-permute-start.125 = (bf16[4,512,128]{2,1,0:T(8,128)(2,1)}, bf16[4,512,128]{2,1,0:T(8,128)(2,1)}, u32[]{:S(2)}, u32[]{:S(2)}) collective-permute-start(bf16[4,512,128]{2,1,0:T(8,128)(2,1)} %get-tuple-element.126), channel_id=1, source_target_pairs={{0,16},{2,18},{4,20},{6,22},{8,24},{10,26},{12,28},{14,30},{16,0},... | collective-permute-start | bytes 1572872 | tf_op jit(solution)/shard_map/ppermute | solution.py:637
  587.2 57.7 %all-to-all-start.9 = ((bf16[4,704,128]{2,1,0:T(8,128)(2,1)}), bf16[4,704,128]{2,1,0:T(8,128)(2,1)}, u32[]{:S(2)}, u32[]{:S(2)}) async-start(bf16[4,704,128]{2,1,0:T(8,128)(2,1)} %pad_maximum_fusion.5), calls=%async_computation.9 | async-start | bytes 1441792 | tf_op jit(solution)/shard_map/all_to_all | solution.py:643
  615.1 44.8 %collective-permute-start.100 = (bf16[4,64,384]{2,1,0:T(8,128)(2,1)}, bf16[4,64,384]{2,1,0:T(8,128)(2,1)}, u32[]{:S(2)}, u32[]{:S(2)}) collective-permute-start(bf16[4,64,384]{2,1,0:T(8,128)(2,1)} %get-tuple-element.157), channel_id=1, source_target_pairs={{0,8},{2,10},{4,12},{6,14},{8,16},{10,18},{12,20},{14,22},{16,24},... | collective-permute-start | bytes 589832 | tf_op jit(solution)/shard_map/ppermute | solution.py:637
  617.1 44.7 %collective-permute-start.98 = (bf16[4,64,384]{2,1,0:T(8,128)(2,1)}, bf16[4,64,384]{2,1,0:T(8,128)(2,1)}, u32[]{:S(2)}, u32[]{:S(2)}) collective-permute-start(bf16[4,64,384]{2,1,0:T(8,128)(2,1)} %get-tuple-element.156), channel_id=1, source_target_pairs={{0,24},{2,26},{4,28},{6,30},{8,0},{10,2},{12,4},{14,6},{16,8},{18,... | collective-permute-start | bytes 589832 | tf_op jit(solution)/shard_map/ppermute | solution.py:637
  618.9 42.9 %collective-permute-start.99 = (bf16[4,64,384]{2,1,0:T(8,128)(2,1)}, bf16[4,64,384]{2,1,0:T(8,128)(2,1)}, u32[]{:S(2)}, u32[]{:S(2)}) collective-permute-start(bf16[4,64,384]{2,1,0:T(8,128)(2,1)} %get-tuple-element.158), channel_id=1, source_target_pairs={{0,16},{2,18},{4,20},{6,22},{8,24},{10,26},{12,28},{14,30},{16,0},... | collective-permute-start | bytes 589832 | tf_op jit(solution)/shard_map/ppermute | solution.py:637
  644.9 34.1 %all-to-all-start.11 = ((bf16[4,704,128]{2,1,0:T(8,128)(2,1)}), bf16[4,704,128]{2,1,0:T(8,128)(2,1)}, u32[]{:S(2)}, u32[]{:S(2)}) async-start(bf16[4,704,128]{2,1,0:T(8,128)(2,1)} %pad_maximum_fusion.6), calls=%async_computation.11 | async-start | bytes 1441792 | tf_op jit(solution)/shard_map/all_to_all | solution.py:643
  659.9 29.1 %collective-permute-start.126 = (bf16[4,512,128]{2,1,0:T(8,128)(2,1)}, bf16[4,512,128]{2,1,0:T(8,128)(2,1)S(1)}, u32[]{:S(2)}, u32[]{:S(2)}) collective-permute-start(bf16[4,512,128]{2,1,0:T(8,128)(2,1)} %get-tuple-element.125), channel_id=1, source_target_pairs={{0,8},{2,10},{4,12},{6,14},{8,16},{10,18},{12,20},{14,22},{16,24},... | collective-permute-start | bytes 1572872 | tf_op jit(solution)/shard_map/ppermute | solution.py:637
  (196 other events, 2391.4 us)

commit v4 on v3

--- a/solution.py
+++ b/solution.py
@@ -152,24 +152,23 @@
     )(at, cosine, sine, *parts)
 
 
-def head_copies(layers, layer, refs, wq, wo, sems):
-    per_layer = wo.shape[1] // layers
+def head_copies(refs, wq, wo, sems):
     copies = []
-    for i, (target, count) in enumerate(((wq, SQUARE), (wo, per_layer))):
+    for i, target in enumerate((wq, wo)):
+        size = target.shape[2]
         for c in range(2):
-            for k in range(layers):
-                source = refs[(2 * i + c) * layers + k]
-                first = lax.rem(layer + layers - k, layers) * count
-                copies.append(
-                    pltpu.make_async_copy(source, target.at[c, pl.ds(first, count)], sems.at[i, c, k])
-                )
+            source = refs[2 * i + c]
+            if source.shape[1] > size:
+                skipped = 0 if i == 0 else source.shape[1] - size
+                source = source.at[:, pl.ds(skipped, size)]
+            copies.append(pltpu.make_async_copy(source, target.at[c], sems.at[i, c]))
     return copies
 
 
-def head_q(wq, c, h):
-    rank = wq.shape[1] * wq.shape[3]
-    half = HEAD // 2
-    return jnp.concatenate([wq[c, :, 2 * h + i].reshape(rank, half) for i in range(2)], axis=1)
+def head_q(wq, c, h, pair):
+    size = wq.shape[2] // (2 * pair)
+    halves = [wq[c, :, (2 * h + i) * size : (2 * h + i + 1) * size, :] for i in range(2)]
+    return jnp.concatenate([half.reshape(-1, HEAD // 2) for half in halves], axis=1)
 
 
 def head_out(wo, c, h):
@@ -179,13 +178,13 @@
 
 
 def attend_kernel(
-    layers, at_ref, lat_ref, cos_ref, sin_ref, natural_ref, start_ref, kv_ref, keys_ref, *refs
+    lat_ref, cos_ref, sin_ref, natural_ref, start_ref, kv_ref, keys_ref, *refs
 ):
-    weights, (q_ref, o_ref, lse_ref, part_ref, wq, wo, sems) = refs[: 4 * layers], refs[4 * layers :]
+    weights, (q_ref, o_ref, lse_ref, part_ref, wq, wo, sems) = refs[:4], refs[4:]
 
     @pl.when(pl.program_id(0) == 0)
     def _():
-        copies = head_copies(layers, at_ref[0], weights, wq, wo, sems)
+        copies = head_copies(weights, wq, wo, sems)
         for copy in copies:
             copy.start()
         for copy in copies:
@@ -193,11 +192,11 @@
 
     keys = keys_ref[...]
     allowed = (keys <= natural_ref[...]) & (keys >= start_ref[...])
-    pair = wq.shape[2] // 2
+    pair = wo.shape[2] // HEAD
     part = None
     for c in range(2):
         for h in range(pair):
-            q_pre = matmul(lat_ref[...], head_q(wq, c, h))
+            q_pre = matmul(lat_ref[...], head_q(wq, c, h, pair))
             q = rotate(q_pre, cos_ref[...], sin_ref[...]).astype(BF16)
             q = (q.astype(F32) * HEAD**-0.5).astype(BF16)
             scores = jnp.where(allowed, times_transposed(q, kv_ref[:, :HEAD]), MASKED)
@@ -213,12 +212,11 @@
     part_ref[...] = part.astype(BF16)
 
 
-def attend_specs(layers, block, rank, count):
+def attend_specs(block, rank, count):
     row = lambda size: pl.BlockSpec((block, size), lambda i: (i, 0))
     whole = lambda dims: pl.BlockSpec(dims, lambda i: (0,) * len(dims))
     half = HEAD // 2
     return [
-        SMEM,
         row(rank),
         row(half),
         row(half),
@@ -226,22 +224,20 @@
         row(1),
         whole((count, 2 * HEAD)),
         whole((1, count)),
-    ] + [HBM] * (4 * layers)
-
-
-def attend(at, lat, tables, kv, keys, weights, block):
-    near_q, far_q, near_out, far_out = weights
-    layers = len(near_q)
+    ] + [HBM] * 4
+
+
+def attend(lat, tables, kv, keys, weights, pair, block):
+    places, tiles, lanes = weights[0].shape[0], weights[2].shape[0], 128
     rows, rank = lat.shape
     count = kv.shape[0]
-    _, tiles_q, rank_rows, half = near_q[0].shape
-    per_layer, pair_rows, lanes = near_out[0].shape
-    heads, width = tiles_q, per_layer * layers * lanes
+    q_rows = 2 * pair * rank // places
+    heads, width = 2 * pair, tiles * lanes
     by_head = lambda size: pl.BlockSpec((heads, block, size), lambda i: (0, i, 0))
     return pl.pallas_call(
-        functools.partial(attend_kernel, layers),
+        attend_kernel,
         grid=(rows // block,),
-        in_specs=attend_specs(layers, block, rank, count),
+        in_specs=attend_specs(block, rank, count),
         out_specs=[
             by_head(HEAD),
             by_head(HEAD),
@@ -255,9 +251,9 @@
             shape((rows, width)),
         ],
         scratch_shapes=[
-            pltpu.VMEM((2, layers * SQUARE, tiles_q, rank_rows, half), BF16),
-            pltpu.VMEM((2, layers * per_layer, pair_rows, lanes), BF16),
-            pltpu.SemaphoreType.DMA((2, 2, layers)),
+            pltpu.VMEM((2, places, q_rows, HEAD // 2), BF16),
+            pltpu.VMEM((2, tiles, pair * HEAD, lanes), BF16),
+            pltpu.SemaphoreType.DMA((2, 2)),
         ],
         compiler_params=params(),
         cost_estimate=pl.CostEstimate(
@@ -266,24 +262,28 @@
             transcendentals=rows * heads * count,
         ),
         name="attend",
-    )(at, lat, *tables, kv, keys, *near_q, *far_q, *near_out, *far_out)
+    )(lat, *tables, kv, keys, *weights)
 
 
 def attend_back_kernel(
-    layers, at_ref, lat_ref, cos_ref, sin_ref, natural_ref, start_ref, kv_ref, keys_ref, *refs
+    at_ref, lat_ref, cos_ref, sin_ref, natural_ref, start_ref, kv_ref, keys_ref, *refs
 ):
-    weights, refs = refs[: 4 * layers], refs[4 * layers :]
+    weights, refs = refs[:4], refs[4:]
     q_ref, o_ref, lse_ref, d_attn_ref = refs[:4]
-    grads_q, grads_out, d_lat_ref, near_ref, far_ref = refs[4:6], refs[6:8], refs[8], refs[9], refs[10]
-    wq, wo, sems, d_kv_sum, d_lat_sum = refs[11:16]
-    sums = refs[16:]
+    joined = weights[0].shape[0] == weights[-1].shape[0]
+    grads, refs = (refs[4:6], refs[6:]) if joined else (refs[4:8], refs[8:])
+    grads_q, grads_out = grads[:2], grads[-2:]
+    d_lat_ref, near_ref, far_ref, wq, wo, sems, d_kv_sum, d_lat_sum = refs[:8]
+    sums = refs[8:]
+    q_rows = wq.shape[2]
+    skipped = q_rows if joined else 0
+    pair = wo.shape[2] // HEAD
     step, steps = pl.program_id(0), pl.num_programs(0)
-    layer, corner = at_ref[0], at_ref[1]
-    per_layer = wo.shape[1] // layers
+    corner = at_ref[1]
 
     @pl.when(step == 0)
     def _():
-        copies = head_copies(layers, layer, weights, wq, wo, sems)
+        copies = head_copies(weights, wq, wo, sems)
         for copy in copies:
             copy.start()
         d_kv_sum[...] = jnp.zeros_like(d_kv_sum)
@@ -293,28 +293,23 @@
             copy.wait()
 
     def store(c, h, grad_q, grad_out):
-        for z in range(layers):
-            k = lax.rem(layer + layers - z, layers)
-            ranks = grad_q.shape[0] // layers
-            rows_here = grad_q[z * ranks : (z + 1) * ranks].astype(BF16)
-            for i in range(2):
-                tile = rows_here[:, i * 128 : (i + 1) * 128]
-                grads_q[c][k, :, 2 * h + i] = tile.reshape(SQUARE, ranks // SQUARE, 128)
-            for i in range(per_layer):
-                tile = z * per_layer + i
-                grads_out[c][k, i, h * HEAD : (h + 1) * HEAD, :] = grad_out[
-                    :, tile * 128 : (tile + 1) * 128
-                ].astype(BF16)
+        size = q_rows // (2 * pair)
+        for i in range(2):
+            here = slice((2 * h + i) * size, (2 * h + i + 1) * size)
+            tile = grad_q[:, i * 128 : (i + 1) * 128].astype(BF16)
+            grads_q[c][:, here, :] = tile.reshape(-1, size, 128)
+        here = slice(skipped + h * HEAD, skipped + (h + 1) * HEAD)
+        for tile in range(wo.shape[1]):
+            grads_out[c][tile, here, :] = grad_out[:, tile * 128 : (tile + 1) * 128].astype(BF16)
 
     keys = keys_ref[...]
     allowed = (keys <= natural_ref[...]) & (keys >= start_ref[...])
     d_attn, lat = d_attn_ref[...], lat_ref[...]
-    pair = wq.shape[2] // 2
     d_lat = None
     for c in range(2):
         for h in range(pair):
             q, mix, lse = q_ref[c * pair + h], o_ref[c * pair + h], lse_ref[c * pair + h]
-            w_q, w_out = head_q(wq, c, h), head_out(wo, c, h)
+            w_q, w_out = head_q(wq, c, h, pair), head_out(wo, c, h)
             grad_out = contract_rows(mix.astype(BF16), d_attn)
             d_o = times_transposed(d_attn, w_out).astype(BF16)
             delta = jnp.sum(d_o.astype(F32) * mix, axis=-1, keepdims=True)
@@ -361,50 +356,43 @@
         far_ref[...] = d_kv_sum[size:, :].astype(BF16)
 
 
-def attend_back(at, lat, tables, kv, keys, weights, q, o, lse, d_attn, block):
-    near_q, far_q, near_out, far_out = weights
-    layers = len(near_q)
+def attend_back(at, lat, tables, kv, keys, weights, q, o, lse, d_attn, pair, block):
+    places, tiles, lanes = weights[0].shape[0], weights[2].shape[0], 128
     rows, rank = lat.shape
     count = kv.shape[0]
-    _, tiles_q, rank_rows, half = near_q[0].shape
-    per_layer, pair_rows, lanes = near_out[0].shape
-    heads, width = tiles_q, per_layer * layers * lanes
+    q_rows = 2 * pair * rank // places
+    heads, width = 2 * pair, tiles * lanes
     by_head = lambda size: pl.BlockSpec((heads, block, size), lambda i: (0, i, 0))
     whole = lambda dims: pl.BlockSpec(dims, lambda i: (0,) * len(dims))
-    q_dims = (layers, SQUARE, tiles_q, rank_rows, half)
-    out_dims = (layers, per_layer, pair_rows, lanes)
+    grad_dims = [(places, q_rows, HEAD // 2)] * 2 + [(tiles, pair * HEAD, lanes)] * 2
+    if places == tiles:
+        grad_dims = [(places, q_rows + pair * HEAD, lanes)] * 2
     d_lat_dims = (SQUARE, rows, rank // SQUARE + 128)
-    pair = tiles_q // 2
     sums = []
     if rows != block:
         sums = [pltpu.VMEM((2, pair, rank, HEAD), F32), pltpu.VMEM((2, pair, HEAD, width), BF16)]
     return pl.pallas_call(
-        functools.partial(attend_back_kernel, layers),
+        attend_back_kernel,
         grid=(rows // block,),
-        in_specs=attend_specs(layers, block, rank, count)
+        in_specs=[SMEM]
+        + attend_specs(block, rank, count)
         + [by_head(HEAD), by_head(HEAD), by_head(1), pl.BlockSpec((block, width), lambda i: (i, 0))],
         out_specs=[
-            whole(q_dims),
-            whole(q_dims),
-            whole(out_dims),
-            whole(out_dims),
+            *[whole(dims) for dims in grad_dims],
             pl.BlockSpec((SQUARE, block, d_lat_dims[2]), lambda i: (0, i, 0)),
             whole((count // 2, 2 * HEAD)),
             whole((count // 2, 2 * HEAD)),
         ],
         out_shape=[
-            shape(q_dims),
-            shape(q_dims),
-            shape(out_dims),
-            shape(out_dims),
+            *[shape(dims) for dims in grad_dims],
             shape(d_lat_dims),
             shape((count // 2, 2 * HEAD), BF16 if sums else F32),
             shape((count // 2, 2 * HEAD)),
         ],
         scratch_shapes=[
-            pltpu.VMEM((2, layers * SQUARE, tiles_q, rank_rows, half), BF16),
-            pltpu.VMEM((2, layers * per_layer, pair_rows, lanes), BF16),
-            pltpu.SemaphoreType.DMA((2, 2, layers)),
+            pltpu.VMEM((2, places, q_rows, HEAD // 2), BF16),
+            pltpu.VMEM((2, tiles, pair * HEAD, lanes), BF16),
+            pltpu.SemaphoreType.DMA((2, 2)),
             pltpu.VMEM((count, 2 * HEAD), F32),
             pltpu.VMEM((block, rank), F32),
         ]
@@ -416,7 +404,7 @@
             transcendentals=rows * heads * count,
         ),
         name="attend_back",
-    )(at, lat, *tables, kv, keys, *near_q, *far_q, *near_out, *far_out, q, o, lse, d_attn)
+    )(at, lat, *tables, kv, keys, *weights, q, o, lse, d_attn)
 
 
 def latent_back_kernel(layers, at_ref, hat_ref, inverse_ref, d_kv_ref, x_ref, w_ref, *refs):
@@ -467,45 +455,37 @@
     )(at, hat, inverse, d_kv, x, weight, *parts)
 
 
-def chunk(ref, corner, m, size):
-    tiles = size // 128
-    columns = [(t * SQUARE + (corner ^ m)) * 128 for t in range(tiles)]
-    return jnp.concatenate([ref[:, pl.ds(pl.multiple_of(c, 128), 128)] for c in columns], axis=1)
-
-
-def mlp_kernel(at_ref, h_ref, cot_ref, *refs):
-    pieces = refs[: 2 * 3 * 5]
-    d_h_ref, out_ref, act_near_ref, act_far_ref, weights, sems = refs[2 * 3 * 5 :]
-    corner = at_ref[1]
-    tiles, units = weights.shape[3], weights.shape[4]
-    half = tiles // 2
-    copies = []
-    for c in range(2):
-        for kind in range(3):
-            one = []
-            for i in range(5):
-                target = weights.at[c, kind, min(i, 3)]
-                if i >= 3:
-                    target = target.at[pl.ds((i - 3) * half, half)]
-                source = pieces[(c * 3 + kind) * 5 + i]
-                one.append(pltpu.make_async_copy(source, target, sems.at[c, kind, i]))
-            copies.append(one)
+def chunk(ref, q, tiles):
+    columns = [(t * SQUARE + q) * 128 for t in range(tiles)]
+    return jnp.concatenate([ref[:, c : c + 128] for c in columns], axis=1)
+
+
+def mlp_kernel(h_ref, cot_ref, *refs):
+    d_h_ref, out_ref, act_near_ref, act_far_ref, weights, sems = refs[2:]
+    tiles, units = weights.shape[3:5]
+    copies = [
+        [
+            pltpu.make_async_copy(
+                refs[c].at[:, :, pl.ds(kind * units, units)], weights.at[c, kind], sems.at[c, kind]
+            )
+            for kind in range(3)
+        ]
+        for c in range(2)
+    ]
     for one in copies:
         for copy in one:
             copy.start()
-    size = tiles * 128
-
-    def weight(c, kind, m):
-        return jnp.concatenate([weights[c, kind, m, t] for t in range(tiles)], axis=1)
-
-    for c, acts in enumerate((act_near_ref, act_far_ref)):
+
+    def weight(c, kind, q):
+        return jnp.concatenate([weights[c, kind, q, t] for t in range(tiles)], axis=1)
+
+    sides = (act_near_ref, act_far_ref)
+    for c, acts in enumerate(sides):
 
         def product(value_ref, kind):
-            for copy in copies[c * 3 + kind]:
-                copy.wait()
+            copies[c][kind].wait()
             return sum(
-                times_transposed(chunk(value_ref, corner, m, size), weight(c, kind, m))
-                for m in range(SQUARE)
+                times_transposed(chunk(value_ref, q, tiles), weight(c, kind, q)) for q in range(SQUARE)
             )
 
         gate_act, up_proj, d_act = product(h_ref, 0), product(h_ref, 1), product(cot_ref, 2)
@@ -515,33 +495,31 @@
         acts[0] = d_gate.astype(BF16)
         acts[1] = (d_act * silu_gate).astype(BF16)
         acts[2] = (silu_gate * up_proj).astype(BF16)
-    accumulators = (act_near_ref, act_far_ref)
-    for m in range(SQUARE):
+    for q in range(SQUARE):
         d_h = sum(
-            matmul(acts[kind], weight(c, kind, m))
-            for c, acts in enumerate(accumulators)
-            for kind in range(2)
+            matmul(acts[kind], weight(c, kind, q)) for c, acts in enumerate(sides) for kind in range(2)
         )
-        out = sum(matmul(acts[2], weight(c, 2, m)) for c, acts in enumerate(accumulators))
+        out = sum(matmul(acts[2], weight(c, 2, q)) for c, acts in enumerate(sides))
         for t in range(tiles):
-            here = pl.ds(pl.multiple_of((t * SQUARE + (corner ^ m)) * 128, 128), 128)
+            here = slice((t * SQUARE + q) * 128, (t * SQUARE + q + 1) * 128)
             d_h_ref[:, here] = d_h[:, t * 128 : (t + 1) * 128].astype(BF16)
             out_ref[:, here] = out[:, t * 128 : (t + 1) * 128].astype(BF16)
 
 
-def mlp(at, h, cot, near, far):
+def mlp(h, cot, near, far):
     rows, width = h.shape
-    tiles, units, lanes = near[0][0].shape
+    _, tiles, units, lanes = near.shape
+    units = units // 3
     low = shape((rows, width))
     acts = shape((3, rows, units))
     return pl.pallas_call(
         mlp_kernel,
-        in_specs=[SMEM, VMEM, VMEM] + [HBM] * 30,
+        in_specs=[VMEM, VMEM, HBM, HBM],
         out_specs=[VMEM] * 4,
         out_shape=[low, low, acts, acts],
         scratch_shapes=[
             pltpu.VMEM((2, 3, SQUARE, tiles, units, lanes), BF16),
-            pltpu.SemaphoreType.DMA((2, 3, 5)),
+            pltpu.SemaphoreType.DMA((2, 3)),
         ],
         compiler_params=params(),
         cost_estimate=pl.CostEstimate(
@@ -550,46 +528,54 @@
             transcendentals=2 * rows * units,
         ),
         name="mlp",
-    )(at, h, cot, *[piece for side in (near, far) for kind in side for piece in kind])
-
-
-ROUTES = (((1, 3), 0), ((0, 2), 0), ((2, 3), 1), ((0, 1), 1))
-
-
-def unit_grads_kernel(at_ref, acts_ref, value_ref, *refs):
-    more, outs = refs[: len(refs) - 4], refs[len(refs) - 4 :]
-    corner = at_ref[1]
-    half = outs[0].shape[1]
-    acts = acts_ref[...]
-    size = 2 * half * 128
-    for m in range(SQUARE):
-        grad = contract_rows(acts, chunk(value_ref, corner, m, size))
-        for i, (flips, side) in enumerate(ROUTES):
-            if m in flips:
-                j = flips.index(m)
-                for t in range(half):
-                    column = (side * half + t) * 128
-                    tile = grad[:, column : column + 128]
-                    if more:
-                        tile = tile + more[i][j, t].astype(F32)
-                    outs[i][j, t] = tile.astype(BF16)
-
-
-def unit_grads(at, acts, value, *more):
+    )(h, cot, near, far)
+
+
+def unit_grads_kernel(acts_ref, value_ref, *refs):
+    more, out_ref = refs[:-1], refs[-1]
+    acts = acts_ref[0]
+    tiles = out_ref.shape[1]
+    for q in range(SQUARE):
+        grad = contract_rows(acts, chunk(value_ref, q, tiles))
+        for t in range(tiles):
+            tile = grad[:, t * 128 : (t + 1) * 128]
+            if more:
+                tile = tile + more[0][q, t].astype(F32)
+            out_ref[q, t] = tile.astype(BF16)
+
+
+def unit_grads(acts, kind, value, received=None, kinds=None):
     rows, width = value.shape
-    units = acts.shape[1]
-    dims = (2, width // SQUARE // 256, units, 128)
+    units = acts.shape[2]
+    tiles = width // SQUARE // 128
+    whole = lambda dims: pl.BlockSpec(dims, lambda i: (0,) * len(dims))
+    dims = (SQUARE, tiles, units, 128)
+    in_specs = [pl.BlockSpec((1, rows, units), lambda i: (kind, 0, 0)), whole((rows, width))]
+    args, aliases, body = [acts, value], {}, unit_grads_kernel
+    out_specs, out_dims = whole(dims), dims
+    if received is not None:
+        args.append(received)
+        in_specs.append(whole(dims))
+        out_specs = pl.BlockSpec(dims, lambda i: (0, 0, kind, 0))
+        out_dims = (SQUARE, tiles, 3 * units, 128)
+    if kinds is not None:
+        args.append(kinds)
+        in_specs.append(HBM)
+        aliases = {3: 0}
+        body = lambda a, v, r, k, o: unit_grads_kernel(a, v, r, o)
     return pl.pallas_call(
-        unit_grads_kernel,
-        in_specs=[SMEM] + [VMEM] * (2 + len(more)),
-        out_specs=[VMEM] * 4,
-        out_shape=[shape(dims)] * 4,
+        body,
+        grid=(1,),
+        in_specs=in_specs,
+        out_specs=out_specs,
+        out_shape=shape(out_dims),
+        input_output_aliases=aliases,
         compiler_params=params(),
         cost_estimate=pl.CostEstimate(
-            flops=2 * rows * width * units, bytes_accessed=2 * width * units * (1 + bool(more)), transcendentals=0
+            flops=2 * rows * width * units, bytes_accessed=4 * width * units, transcendentals=0
         ),
         name="unit_grads",
-    )(at, acts, value, *more)
+    )(*args)
 
 
 def local(
@@ -653,6 +639,15 @@
             along(blocks[k], -k).astype(F32) for k in range(1, layers)
         )
 
+    def by_layer(value):
+        blocks = value.reshape(layers, rows, -1)
+        return jnp.concatenate(
+            [
+                lax.dynamic_index_in_dim(blocks, (layer - z) % layers, 0, keepdims=False)
+                for z in range(layers)
+            ]
+        )
+
     def square_pieces(value):
         return [value] + [within(value, m) for m in range(1, SQUARE)]
 
@@ -663,6 +658,9 @@
 
     def after(value, *earlier):
         return lax.optimization_barrier((value,) + earlier)[0]
+
+    def together(*values):
+        return lax.optimization_barrier(values)
 
     def own(pair_value):
         return lax.dynamic_slice_in_dim(pair_value, core * rows, rows, 0)
@@ -730,37 +728,27 @@
 
     down_scaled = (down.astype(F32) * gain_rows).astype(BF16)
     down_half = lax.dynamic_slice_in_dim(down_scaled, core * (lanes // 2), lanes // 2, 0)
-    down_near = line_pieces(square_exchange(shares(down_half)))
+    cot_own = own(cotangent)
+    cot_pieces = line_pieces(arranged(cot_own))
+    cot_all = by_layer(jnp.concatenate(cot_pieces))
+    down_own = square_exchange(shares(down_half))
+    down_near = line_pieces(after(down_own, *cot_pieces[1:]))
     down_far = [across(piece) for piece in down_near]
 
     q_gain_rows = q_gain.astype(F32)[:, None]
     qup_scaled = (w_qup.astype(F32) * q_gain_rows).astype(BF16)
     qup_send = qup_scaled.reshape(rank_rows, SQUARE, 2 * pair, half)
-    qup_send = jnp.transpose(qup_send, (1, 2, 0, 3))
-    qup_own = square_exchange(after(qup_send, down_near[0]))
-    out_own = square_exchange(w_out.reshape(SQUARE, pair * HEAD, lanes))
-    qup_near = line_pieces(qup_own)
-    qup_far = [across(piece) for piece in qup_near]
-    out_near = line_pieces(tiled(after(out_own, qup_near[1])))
-    out_far = [across(piece) for piece in out_near]
-    head_weights = (qup_near, qup_far, out_near, out_far)
+    qup_send = jnp.transpose(qup_send, (1, 2, 0, 3)).reshape(SQUARE, -1, lanes)
+    qup_size = qup_send.shape[1]
+    head_send = jnp.concatenate([qup_send, w_out.reshape(SQUARE, pair * HEAD, lanes)], axis=1)
+    head_own = square_exchange(after(head_send, down_own))
 
     mlp_gain_rows = mlp_gain.astype(F32)[:, None]
     gate_send = (w_gate.astype(F32) * mlp_gain_rows).astype(BF16).T
     up_send = (w_up.astype(F32) * mlp_gain_rows).astype(BF16).T
-    mlp_near, mlp_far = [], []
-    earlier = out_near[1]
-    for sent in (gate_send, up_send, w_down):
-        mine = line_exchange(after(sent, earlier).reshape(layers, units, lanes))
-        earlier = mine
-        mine = tiled(mine)
-        size = mine.shape[0] // 2
-        one, two = within(mine, 1), within(mine, 2)
-        pieces = [mine, one, two, within(one[:size], 2), within(two[size:], 1)]
-        mlp_near.append(pieces)
-        mlp_far.append([across(piece) for piece in pieces])
-    cot_own = own(cotangent)
-    cot_all = jnp.concatenate(line_pieces(after(arranged(cot_own), earlier)))
+    mlp_send = jnp.concatenate(
+        [value.reshape(layers, units, lanes) for value in (gate_send, up_send, w_down)], axis=1
+    )
 
     bounds = jnp.cumsum(seq_lengths)
     starts = bounds - seq_lengths
@@ -782,54 +770,96 @@
     cosine, sine = angles(row_natural - row_start)
     tables = (cosine, sine, row_natural[:, None], row_start[:, None])
 
+    x_all = after(x_all, head_own)
     part, down_here = project(at, x_all, down_near, down_far)
     lat_hat, lat_low, lat_inverse, kv_own = latent(at, cosine, sine, square_pieces(part), rank)
+    mlp_layer = line_exchange(after(mlp_send, *down_near[1:]))
+    mlp_layer, kv_own = together(mlp_layer, kv_own)
     kv_line = jnp.concatenate(line_pieces(kv_own))
+    mlp_near = lax.all_gather(tiled(mlp_layer), "seq", axis_index_groups=square_groups)
+
+    head_near = line_exchange(jnp.tile(after(head_own, mlp_layer, kv_line), (layers, 1, 1)))
     kv_near = jnp.concatenate(square_pieces(kv_line))
     kv_all = jnp.concatenate([kv_near, across(kv_near)])
+    head_near, kv_all = together(head_near, kv_all)
+    head_far = across(head_near)
+    if lanes == 128:
+        head_weights = (head_near, head_far, head_near, head_far)
+    else:
+        head_weights = tuple(
+            side[:, :qup_size].reshape(chips, -1, half) for side in (head_near, head_far)
+        ) + tuple(tiled(side[:, qup_size:]) for side in (head_near, head_far))
 
     block = max(32, min(SQUARE * rows, 2**30 // kv_all.shape[0] ** 2))
     queries, attn_mix, log_total, attn_part = attend(
-        at, lat_low, tables, kv_all, key_natural, head_weights, block
+        lat_low, tables, kv_all, key_natural, head_weights, pair, block
     )
+    mlp_near, attn_part = together(mlp_near, attn_part)
+    mlp_far = across(mlp_near)
     hidden = inputs + square_sum(attn_part.reshape(SQUARE, rows, width))
     h_inverse = inverse_rms(hidden)
     h_hat = hidden * h_inverse
-    h_all = jnp.concatenate(line_pieces(arranged(h_hat.astype(BF16))))
-
-    d_h_part, mlp_part, acts_near, acts_far = mlp(at, h_all, cot_all, mlp_near, mlp_far)
-    d_hscaled = unarranged(line_sum(d_h_part.reshape(layers, rows, width)))
+    h_low = h_hat.astype(BF16)
+    h_all = jnp.concatenate(line_pieces(arranged(h_low)))
+    h_all = by_layer(h_all)
+
+    d_h_part, mlp_part, acts_near, acts_far = mlp(h_all, cot_all, mlp_near, mlp_far)
+    def line_blocks(value):
+        return line_exchange(value.reshape(layers, rows, width))
+
+    def line_total(blocks):
+        return unarranged(jnp.sum(blocks.astype(F32), axis=0))
+
+    mlp_grads = None
+    for kind, value in ((0, h_all), (1, h_all), (2, cot_all)):
+        received = across(unit_grads(acts_far, kind, value))
+        mlp_grads = unit_grads(acts_near, kind, value, received, mlp_grads)
+    d_h_lines, mlp_grads = together(line_blocks(d_h_part), mlp_grads)
+    d_hscaled = line_total(d_h_lines)
     d_hidden = cot_own.astype(F32) + norm_back(d_hscaled, h_hat, h_inverse)
+    mlp_sum = lax.psum_scatter(mlp_grads, "seq", axis_index_groups=square_groups)
+    mlp_lines = line_blocks(after(mlp_part, d_hscaled))
     d_attn_all = jnp.concatenate(square_pieces(d_hidden.astype(BF16)))
-    mlp_own = unarranged(line_sum(mlp_part.reshape(layers, rows, width)))
-    layer_own = (hidden + mlp_own).astype(BF16)
-    layer_out = both(layer_own, across(layer_own))
-
-    mlp_back = []
-    for kind, value in ((0, h_all), (1, h_all), (2, cot_all)):
-        far_grads = unit_grads(at, acts_far[kind], value)
-        sent_a, kept_a, sent_b, kept_b = unit_grads(
-            at, acts_near[kind], value, *[across(grad) for grad in far_grads]
+
+    *head_grads, d_lat_parts, d_kv_near, d_kv_far = attend_back(
+        at,
+        lat_low,
+        tables,
+        kv_all,
+        key_natural,
+        head_weights,
+        queries,
+        attn_mix,
+        log_total,
+        d_attn_all,
+        pair,
+        block,
+    )
+    head_grads = list(head_grads)
+    side = len(head_grads) // 2
+    head_total = [
+        (head_grads[2 * i].astype(F32) + across(head_grads[2 * i + 1]).astype(F32)).astype(BF16)
+        for i in range(side)
+    ]
+    if lanes == 128:
+        head_total = head_total[0]
+    else:
+        head_total = jnp.concatenate(
+            [head_total[0].reshape(chips, -1, lanes), untiled(head_total[1])], axis=1
         )
-        sums = []
-        for sent, kept, flip, next_flip in ((sent_a, kept_a, 1, 2), (sent_b, kept_b, 2, 1)):
-            total = kept.astype(F32) + within(sent, flip).astype(F32)
-            sums.append(total[0] + within(total[1].astype(BF16), next_flip).astype(F32))
-        back = line_exchange(untiled(jnp.concatenate(sums).astype(BF16)))
-        mlp_back.append(back.reshape(layers * units, lanes).astype(F32))
-    gate_back, up_back, down_part = mlp_back[0].T, mlp_back[1].T, mlp_back[2]
-    gate_part, up_part = gate_back * mlp_gain_rows, up_back * mlp_gain_rows
-    mlp_gain_part = jnp.sum(gate_back * w_gate.astype(F32) + up_back * w_up.astype(F32), axis=1)
-
-    grad_q_near, grad_q_far, grad_out_near, grad_out_far, d_lat_parts, d_kv_near, d_kv_far = attend_back(
-        at, lat_low, tables, kv_all, key_natural, head_weights, queries, attn_mix, log_total, d_attn_all, block
-    )
+    d_kv_near, head_total, mlp_lines = together(d_kv_near, head_total, mlp_lines)
+    layer_out_own = (hidden + line_total(mlp_lines)).astype(BF16)
+    layer_out = both(layer_out_own, across(layer_out_own))
+
+    head_q = line_exchange(head_total[:, :qup_size])
     d_kv_low = (d_kv_near.astype(F32) + across(d_kv_far).astype(F32)).astype(BF16)
     d_kv_line = square_sum(d_kv_low.reshape(SQUARE, layers * rows, 2 * HEAD)).astype(BF16)
+    head_q, d_kv_line = together(head_q, d_kv_line)
     d_kv_own = line_sum(d_kv_line.reshape(layers, rows, 2 * HEAD))
     d_kv_own = jnp.concatenate(
         [unrotate(d_kv_own[:, :HEAD], cosine[:rows], sine[:rows]), d_kv_own[:, HEAD:]], axis=1
     ).astype(BF16)
+    head_out_lines = line_exchange(after(head_total[:, qup_size:], d_kv_own))
     kv_share_of = lambda m: lax.dynamic_slice_in_dim(d_kv_own, (corner ^ m) * kv_share, kv_share, 1)
     d_kv_share = jnp.concatenate(
         [kv_share_of(0)] + [within(kv_share_of(m), m) for m in range(1, SQUARE)]
@@ -840,23 +870,32 @@
         at, lat_hat, lat_inverse, d_kv_share, x_all, down_here, d_lat_received
     )
     d_xscaled = square_sum(d_x_part.reshape(SQUARE, rows, width))
+    head_out_lines, d_xscaled = together(head_out_lines, d_xscaled)
+    mlp_back = line_exchange(untiled(after(mlp_sum, head_out_lines)))
     token_own = (d_hidden + norm_back(d_xscaled, x_hat, x_inverse)).astype(BF16)
     token_grad = both(token_own, across(token_own))
     down_sum = (down_grad_near + across(down_grad_far).astype(F32)).astype(BF16)
-    down_back = unshares(square_exchange(line_sum(down_sum).astype(BF16))).astype(F32)
+    down_line, mlp_back = together(line_sum(down_sum).astype(BF16), mlp_back)
+    down_back = unshares(square_exchange(down_line)).astype(F32)
     down_back = both(down_back, across(down_back))
     attn_gain_part = jnp.sum(down_back * down.astype(F32), axis=1)
     down_grad = down_back * gain_rows
     qdown_part, kv_part = down_grad[:, :rank], down_grad[:, rank:]
 
-    def head_back(near, far):
-        total = (near.astype(F32) + across(far).astype(F32)).astype(BF16)
-        return line_sum(total).astype(BF16)
-
-    qup_back = square_exchange(head_back(grad_q_near, grad_q_far))
+    gate_back, up_back, down_part = (
+        mlp_back[:, kind * units : (kind + 1) * units].reshape(layers * units, lanes).astype(F32)
+        for kind in range(3)
+    )
+    gate_back, up_back = gate_back.T, up_back.T
+    gate_part, up_part = gate_back * mlp_gain_rows, up_back * mlp_gain_rows
+    mlp_gain_part = jnp.sum(gate_back * w_gate.astype(F32) + up_back * w_up.astype(F32), axis=1)
+
+    head_lines = jnp.concatenate([head_q, head_out_lines], axis=1)
+    head_lines = head_lines.reshape(layers, SQUARE, -1, lanes).astype(F32)
+    head_sum = square_exchange(jnp.sum(head_lines, axis=0).astype(BF16))
+    qup_back = head_sum[:, :qup_size].reshape(SQUARE, 2 * pair, rank_rows, half)
     qup_back = jnp.transpose(qup_back, (2, 0, 1, 3)).reshape(rank_rows, -1).astype(F32)
-    out_back = square_exchange(untiled(head_back(grad_out_near, grad_out_far)))
-    out_part = out_back.reshape(-1, lanes).astype(F32)
+    out_part = head_sum[:, qup_size:].reshape(-1, lanes).astype(F32)
     qup_part = qup_back * q_gain_rows
     q_gain_half = jnp.sum(qup_back * w_qup.astype(F32), axis=1)
     gain_parts = jnp.concatenate([q_gain_half, mlp_gain_part])

time: 713 us -> 606 us (0.85)
  starting transfers between devices: 241 us -> 110 us
  between operations: 2.47 us -> 15.1 us
  other arithmetic: 47.9 us -> 58 us
  waiting for transfers between devices: 283 us -> 275 us
    ppermute x36 -> x18, waiting for transfers between devices: 106 us -> 43.8 us  [along(): return lax.ppermute(value, 'seq', pairs)]
    all_to_all x6 -> x7, waiting for transfers between devices: 54.6 us -> 113 us  [line_exchange(): lax.all_to_all(value, 'seq', 0, 0, axis_index_groups=lines, tiled=True)]
    ppermute x36 -> x18, starting transfers between devices: 81.1 us -> 29.4 us  [along(): return lax.ppermute(value, 'seq', pairs)]
    ppermute x51 -> x27, starting transfers between devices: 66.9 us -> 30.5 us  [within(): return lax.ppermute(value, 'seq', [(i, i ^ flip) for i in range(chips)])]
    all_to_all x6 -> x7, starting transfers between devices: 60.8 us -> 32.7 us  [line_exchange(): lax.all_to_all(value, 'seq', 0, 0, axis_index_groups=lines, tiled=True)]
    all_to_all x6 -> x4, waiting for transfers between devices: 17.7 us -> 8.58 us  [square_exchange(): lax.all_to_all(value, 'seq', 0, 0, axis_index_groups=square_groups, tiled...]
    unnamed x178 -> x103, local copies, waits for them, and re-layouts: 11.9 us -> 20.5 us
    all_to_all x6 -> x4, starting transfers between devices: 22.9 us -> 15.1 us  [square_exchange(): lax.all_to_all(value, 'seq', 0, 0, axis_index_groups=square_groups, tiled...]
  transfers between devices with their start and end apart: 147 -> 75, of which waited for: 53 -> 41; matrix products, arithmetic and copies ran while one was open for 11% -> 16% of each run, Pallas kernels for 9% -> 11%
where the time goes in v4:
time: 606 us; the launch traced here: 598 us
  waiting for transfers between devices  275 us (45%)
  starting transfers between devices  110 us (18%)
  Pallas kernels  91.1 us (15%)
  other arithmetic  58 us (10%)
  local copies, waits for them, and re-layouts  49.3 us (8%)
  between operations  15.1 us (2%)
    all_to_all x7, waiting for transfers between devices, line_exchange(): lax.all_to_all(value, 'seq', 0, 0, axis_index_groups=lines, tiled=True)  113 us
    ppermute x27, waiting for transfers between devices, within(): return lax.ppermute(value, 'seq', [(i, i ^ flip) for i in range(chips)])  104 us
    ppermute x18, waiting for transfers between devices, along(): return lax.ppermute(value, 'seq', pairs)  43.8 us
    all_to_all x7, starting transfers between devices, line_exchange(): lax.all_to_all(value, 'seq', 0, 0, axis_index_groups=lines, tiled=True)  32.7 us
    ppermute x27, starting transfers between devices, within(): return lax.ppermute(value, 'seq', [(i, i ^ flip) for i in range(chips)])  30.5 us
    ppermute x18, starting transfers between devices, along(): return lax.ppermute(value, 'seq', pairs)  29.4 us
    pallas_call x6, Pallas kernels, unit_grads(): pl.pallas_call(body, grid=(1,), in_specs=in_specs, out_specs=out_specs, o...  26.6 us
    unnamed x103, local copies, waits for them, and re-layouts  20.5 us
  transfers between devices with their start and end apart: 75, of which 41 were waited for; matrix products, arithmetic and copies ran while one was open for 16% of the time, Pallas kernels for 11%

profile of v4, /device:TPU:0, one launch (start us, length us, event | category | flops | bytes accessed | tf_op | source)
XLA Modules:
  0.0 598.2 jit_solution(13083839930920173047)
XLA Ops:
  31.2 6.1 %collective-permute-start.3 = (bf16[4,64,384]{2,1,0:T(8,128)(2,1)}, bf16[4,64,384]{2,1,0:T(8,128)(2,1)S(1)}, u32[]{:S(2)}, u32[]{:S(2)}) collective-permute-start(bf16[4,64,384]{2,1,0:T(8,128)(2,1)} %all-to-all-done.refs_0_), channel_id=1, source_target_pairs={{0,8},{2,10},{4,12},{6,14},{8,16},{10,18},{12,20},{14,22},{16,24},... | collective-permute-start | bytes 589832 | tf_op jit(solution)/shard_map/ppermute | solution.py:623
  44.4 6.6 %collective-permute-done.4.refs_2_ = bf16[4,64,384]{2,1,0:T(8,128)(2,1)S(1)} collective-permute-done((bf16[4,64,384]{2,1,0:T(8,128)(2,1)}, bf16[4,64,384]{2,1,0:T(8,128)(2,1)S(1)}, u32[]{:S(2)}, u32[]{:S(2)}) %collective-permute-start.4) | collective-permute-done | bytes 196640 | tf_op jit(solution)/shard_map/ppermute | solution.py:623
  51.7 7.8 %all-to-all-start.1 = ((bf16[4,2112,128]{2,1,0:T(8,128)(2,1)}), bf16[4,2112,128]{2,1,0:T(8,128)(2,1)S(1)}, u32[]{:S(2)}, u32[]{:S(2)}) async-start(bf16[4,2112,128]{2,1,0:T(8,128)(2,1)} %pad_maximum_fusion.1), calls=%async_computation.1 | async-start | bytes 4325376 | tf_op jit(solution)/shard_map/all_to_all | solution.py:629
  70.0 5.0 collective-permute-done.7
  99.0 9.8 %all-to-all-done.1 = bf16[4,2112,128]{2,1,0:T(8,128)(2,1)S(1)} async-done(((bf16[4,2112,128]{2,1,0:T(8,128)(2,1)}), bf16[4,2112,128]{2,1,0:T(8,128)(2,1)S(1)}, u32[]{:S(2)}, u32[]{:S(2)}) %all-to-all-start.1) | async-done | bytes 2162720 | tf_op jit(solution)/shard_map/all_to_all | solution.py:629
  129.2 11.5 %collective-permute-done.19 = bf16[256,512]{1,0:T(8,128)(2,1)S(1)} collective-permute-done((bf16[256,512]{1,0:T(8,128)(2,1)}, bf16[256,512]{1,0:T(8,128)(2,1)S(1)}, u32[]{:S(2)}, u32[]{:S(2)}) %collective-permute-start.19) | collective-permute-done | bytes 262176 | tf_op jit(solution)/shard_map/ppermute | solution.py:626
  143.4 8.4 %collective-permute-done.21 = bf16[256,512]{1,0:T(8,128)(2,1)S(1)} collective-permute-done((bf16[256,512]{1,0:T(8,128)(2,1)}, bf16[256,512]{1,0:T(8,128)(2,1)S(1)}, u32[]{:S(2)}, u32[]{:S(2)}) %collective-permute-start.21) | collective-permute-done | bytes 262176 | tf_op jit(solution)/shard_map/ppermute | solution.py:626
  156.5 37.7 %all-to-all-done.3.refs_0_.refs_2_ = bf16[16,768,128]{2,1,0:T(8,128)(2,1)S(1)} async-done(((bf16[16,768,128]{2,1,0:T(8,128)(2,1)}), bf16[16,768,128]{2,1,0:T(8,128)(2,1)S(1)}, u32[]{:S(2)}, u32[]{:S(2)}) %all-to-all-start.3) | async-done | bytes 3145760 | tf_op jit(solution)/shard_map/all_to_all | solution.py:629
  200.0 13.7 %attend.1 = (bf16[4,256,256]{2,1,0:T(8,128)(2,1)}, f32[4,256,256]{2,1,0:T(8,128)}, f32[4,256,1]{2,1,0:T(8,128)}, bf16[256,2048]{1,0:T(8,128)(2,1)}) custom-call(bf16[256,1024]{1,0:T(8,128)(2,1)} %get-tuple-element.66.lat_ref, f32[256,128]{1,0:T(8,128)} %get-tuple-element.234.cos_ref, f32[256,128]{1,0:T(8,128)} %get-tuple-element.233.sin_ref, ...), custom_call_target="tpu_custom_call" | custom-call | flops 3758096384 | bytes 8388608 | tf_op jit(solution)/shard_map/attend/pallas_call | solution.py:237
  224.3 6.3 %collective-permute-done.25 = bf16[64,2048]{1,0:T(8,128)(2,1)S(1)} collective-permute-done((bf16[64,2048]{1,0:T(8,128)(2,1)S(1)}, bf16[64,2048]{1,0:T(8,128)(2,1)S(1)}, u32[]{:S(2)}, u32[]{:S(2)}) %collective-permute-start.25) | collective-permute-done | bytes 262176 | tf_op jit(solution)/shard_map/ppermute | solution.py:626
  237.2 6.0 %collective-permute-done.27 = bf16[64,2048]{1,0:T(8,128)(2,1)S(1)} collective-permute-done((bf16[64,2048]{1,0:T(8,128)(2,1)S(1)}, bf16[64,2048]{1,0:T(8,128)(2,1)S(1)}, u32[]{:S(2)}, u32[]{:S(2)}) %collective-permute-start.27) | collective-permute-done | bytes 262176 | tf_op jit(solution)/shard_map/ppermute | solution.py:623
  243.2 9.7 %collective-permute-done.28 = bf16[64,2048]{1,0:T(8,128)(2,1)S(1)} collective-permute-done((bf16[64,2048]{1,0:T(8,128)(2,1)S(1)}, bf16[64,2048]{1,0:T(8,128)(2,1)S(1)}, u32[]{:S(2)}, u32[]{:S(2)}) %collective-permute-start.28) | collective-permute-done | bytes 262176 | tf_op jit(solution)/shard_map/ppermute | solution.py:623
  254.1 19.8 %mlp.1 = (bf16[256,2048]{1,0:T(8,128)(2,1)}, bf16[256,2048]{1,0:T(8,128)(2,1)}, bf16[3,256,704]{2,1,0:T(8,128)(2,1)}, bf16[3,256,704]{2,1,0:T(8,128)(2,1)}) custom-call(bf16[256,2048]{1,0:T(8,128)(2,1)} %pad_maximum_fusion.4.h_ref.value_ref.v, bf16[256,2048]{1,0:T(8,128)(2,1)} %pad_maximum_fusion.6.cot_ref.value_ref.v, bf16[4,4,2112,128]{3,2,1,0:T(8,128)(2,1)} %bitcast.155, ...), custom_call_target="tpu_custom_call" | custom-call | flops 8858370048 | bytes 21495808 | tf_op jit(solution)/shard_map/mlp/pallas_call | solution.py:515
  286.5 6.5 %all-to-all-start.4 = ((bf16[4,64,2048]{2,1,0:T(8,128)(2,1)}), bf16[4,64,2048]{2,1,0:T(8,128)(2,1)S(1)}, u32[]{:S(2)}, u32[]{:S(2)}) async-start(bf16[4,64,2048]{2,1,0:T(8,128)(2,1)} %bitcast.33), calls=%async_computation.4 | async-start | bytes 2097152 | tf_op jit(solution)/shard_map/all_to_all | solution.py:629
  293.0 4.8 unit_grads.9.k
  297.8 4.8 unit_grads.10.k
  302.6 4.9 unit_grads.11
  307.5 11.9 %all-to-all-done.4 = bf16[4,64,2048]{2,1,0:T(8,128)(2,1)S(1)} async-done(((bf16[4,64,2048]{2,1,0:T(8,128)(2,1)}), bf16[4,64,2048]{2,1,0:T(8,128)(2,1)S(1)}, u32[]{:S(2)}, u32[]{:S(2)}) %all-to-all-start.4) | async-done | bytes 1048608 | tf_op jit(solution)/shard_map/all_to_all | solution.py:629
  324.2 8.7 %collective-permute-done.34 = bf16[64,2048]{1,0:T(8,128)(2,1)S(1)} collective-permute-done((bf16[64,2048]{1,0:T(8,128)(2,1)S(1)}, bf16[64,2048]{1,0:T(8,128)(2,1)S(1)}, u32[]{:S(2)}, u32[]{:S(2)}) %collective-permute-start.34) | collective-permute-done | bytes 262176 | tf_op jit(solution)/shard_map/ppermute | solution.py:626
  332.9 4.4 collective-permute-done.35
  337.4 5.8 collective-permute-done.36
  344.2 19.1 %attend_back.1 = (bf16[16,768,128]{2,1,0:T(8,128)(2,1)}, bf16[16,768,128]{2,1,0:T(8,128)(2,1)}, bf16[4,256,384]{2,1,0:T(8,128)(2,1)}, f32[1024,512]{1,0:T(8,128)}, bf16[1024,512]{1,0:T(8,128)(2,1)}) custom-call(s32[3]{0:T(128)} %pad_add_fusion.1.at_ref, bf16[256,1024]{1,0:T(8,128)(2,1)} %get-tuple-element.66.lat_ref, f32[256,128]{1,0:T(8,128)} %get-tuple-element.234.cos_ref, ...), custom_call_target="tpu_custom_call" | custom-call | flops 8589934592 | bytes 18874368 | tf_op jit(solution)/shard_map/attend_back/pallas_call | solution.py:374
  369.4 5.6 add_convert_fusion
  375.0 18.6 %all-to-all-done.5 = bf16[4,64,2048]{2,1,0:T(8,128)(2,1)S(1)} async-done(((bf16[4,64,2048]{2,1,0:T(8,128)(2,1)}), bf16[4,64,2048]{2,1,0:T(8,128)(2,1)S(1)}, u32[]{:S(2)}, u32[]{:S(2)}) %all-to-all-start.5) | async-done | bytes 1048608 | tf_op jit(solution)/shard_map/all_to_all | solution.py:629
  405.8 11.3 %collective-permute-done.40 = bf16[256,512]{1,0:T(8,128)(2,1)S(1)} collective-permute-done((bf16[256,512]{1,0:T(8,128)(2,1)S(1)}, bf16[256,512]{1,0:T(8,128)(2,1)S(1)}, u32[]{:S(2)}, u32[]{:S(2)}) %collective-permute-start.40) | collective-permute-done | bytes 262176 | tf_op jit(solution)/shard_map/ppermute | solution.py:626
  418.1 6.8 %collective-permute-done.42 = bf16[256,512]{1,0:T(8,128)(2,1)S(1)} collective-permute-done((bf16[256,512]{1,0:T(8,128)(2,1)S(1)}, bf16[256,512]{1,0:T(8,128)(2,1)S(1)}, u32[]{:S(2)}, u32[]{:S(2)}) %collective-permute-start.42) | collective-permute-done | bytes 262176 | tf_op jit(solution)/shard_map/ppermute | solution.py:626
  446.6 5.3 collective-permute-done.46
  458.0 5.0 latent_back.1
  467.7 4.8 collective-permute-done.52
  477.6 9.5 %all-to-all-done.7 = bf16[16,512,128]{2,1,0:T(8,128)(2,1)S(1)} async-done(((bf16[16,512,128]{2,1,0:T(8,128)(2,1)}), bf16[16,512,128]{2,1,0:T(8,128)(2,1)S(1)}, u32[]{:S(2)}, u32[]{:S(2)}) %all-to-all-start.7) | async-done | bytes 2097184 | tf_op jit(solution)/shard_map/all_to_all | solution.py:629
  516.0 14.7 %collective-permute-done.58 = bf16[4,64,384]{2,1,0:T(8,128)(2,1)} collective-permute-done((bf16[4,64,384]{2,1,0:T(8,128)(2,1)}, bf16[4,64,384]{2,1,0:T(8,128)(2,1)}, u32[]{:S(2)}, u32[]{:S(2)}) %collective-permute-start.58) | collective-permute-done | bytes 196640 | tf_op jit(solution)/shard_map/ppermute | solution.py:623
  539.8 24.6 %all-to-all-done.8 = bf16[4,2112,128]{2,1,0:T(8,128)(2,1)S(1)} async-done(((bf16[4,2112,128]{2,1,0:T(8,128)(2,1)}), bf16[4,2112,128]{2,1,0:T(8,128)(2,1)S(1)}, u32[]{:S(2)}, u32[]{:S(2)}) %all-to-all-start.8) | async-done | bytes 2162720 | tf_op jit(solution)/shard_map/all_to_all | solution.py:629
  (357 shorter events, 257.7 us)
Async XLA Ops:
  8.3 22.8 %collective-permute-start = (bf16[64,2048]{1,0:T(8,128)(2,1)S(1)}, bf16[64,2048]{1,0:T(8,128)(2,1)}, u32[]{:S(2)}, u32[]{:S(2)}) collective-permute-start(bf16[64,2048]{1,0:T(8,128)(2,1)S(1)} %constant_dynamic-slice_fusion.4), channel_id=1, source_target_pairs={{0,8},{2,10},{4,12},{6,14},{8,16},{10,18},{12,20},{14,22},{16,24},... | collective-permute-start | bytes 786440 | tf_op jit(solution)/shard_map/ppermute | solution.py:623
  11.4 19.8 %collective-permute-start.1 = (bf16[64,2048]{1,0:T(8,128)(2,1)S(1)}, bf16[64,2048]{1,0:T(8,128)(2,1)}, u32[]{:S(2)}, u32[]{:S(2)}) collective-permute-start(bf16[64,2048]{1,0:T(8,128)(2,1)S(1)} %constant_dynamic-slice_fusion.4), channel_id=1, source_target_pairs={{0,16},{2,18},{4,20},{6,22},{8,24},{10,26},{12,28},{14,30},{16,0},... | collective-permute-start | bytes 786440 | tf_op jit(solution)/shard_map/ppermute | solution.py:623
  14.0 17.2 %collective-permute-start.2 = (bf16[64,2048]{1,0:T(8,128)(2,1)S(1)}, bf16[64,2048]{1,0:T(8,128)(2,1)}, u32[]{:S(2)}, u32[]{:S(2)}) collective-permute-start(bf16[64,2048]{1,0:T(8,128)(2,1)S(1)} %constant_dynamic-slice_fusion.4), channel_id=1, source_target_pairs={{0,24},{2,26},{4,28},{6,30},{8,0},{10,2},{12,4},{14,6},{16,8},{18,... | collective-permute-start | bytes 786440 | tf_op jit(solution)/shard_map/ppermute | solution.py:623
  27.3 24.4 %all-to-all-start.2 = ((bf16[4,768,128]{2,1,0:T(8,128)(2,1)}), bf16[4,768,128]{2,1,0:T(8,128)(2,1)S(1)}, u32[]{:S(2)}, u32[]{:S(2)}) async-start(bf16[4,768,128]{2,1,0:T(8,128)(2,1)} %pad_maximum_fusion.8), calls=%async_computation.2 | async-start | bytes 1572864 | tf_op jit(solution)/shard_map/all_to_all | solution.py:632
  51.7 57.0 %all-to-all-start.1 = ((bf16[4,2112,128]{2,1,0:T(8,128)(2,1)}), bf16[4,2112,128]{2,1,0:T(8,128)(2,1)S(1)}, u32[]{:S(2)}, u32[]{:S(2)}) async-start(bf16[4,2112,128]{2,1,0:T(8,128)(2,1)} %pad_maximum_fusion.1), calls=%async_computation.1 | async-start | bytes 4325376 | tf_op jit(solution)/shard_map/all_to_all | solution.py:629
  59.5 154.2 %all-gather.3.cloned.1.call-start = ((), (), s32[]{:S(2)}) async-start(), calls=%async_computation.12 | async-start | bytes 10813440 | tf_op jit(solution)/shard_map/all_gather | solution.py:779
  121.5 72.7 %all-to-all-start.3 = ((bf16[16,768,128]{2,1,0:T(8,128)(2,1)}), bf16[16,768,128]{2,1,0:T(8,128)(2,1)S(1)}, u32[]{:S(2)}, u32[]{:S(2)}) async-start(bf16[16,768,128]{2,1,0:T(8,128)(2,1)} %bitcast.138), calls=%async_computation.3 | async-start | bytes 6291456 | tf_op jit(solution)/shard_map/all_to_all | solution.py:629
  127.2 15.3 %collective-permute-start.20 = (bf16[256,512]{1,0:T(8,128)(2,1)}, bf16[256,512]{1,0:T(8,128)(2,1)S(1)}, u32[]{:S(2)}, u32[]{:S(2)}) collective-permute-start(bf16[256,512]{1,0:T(8,128)(2,1)} %copy-done.38), channel_id=1, source_target_pairs={{0,4},{2,6},{4,0},{6,2},{8,12},{10,14},{12,8},{14,10},{16,20},{18,... | collective-permute-start | bytes 786440 | tf_op jit(solution)/shard_map/ppermute | solution.py:626
  128.8 23.0 %collective-permute-start.21 = (bf16[256,512]{1,0:T(8,128)(2,1)}, bf16[256,512]{1,0:T(8,128)(2,1)S(1)}, u32[]{:S(2)}, u32[]{:S(2)}) collective-permute-start(bf16[256,512]{1,0:T(8,128)(2,1)} %copy-done.38), channel_id=1, source_target_pairs={{0,6},{2,4},{4,2},{6,0},{8,14},{10,12},{12,10},{14,8},{16,22},{18,... | collective-permute-start | bytes 786440 | tf_op jit(solution)/shard_map/ppermute | solution.py:626
  213.8 40.4 %collective-permute-start.30 = (bf16[4,4,2112,128]{3,2,1,0:T(8,128)(2,1)}, bf16[4,4,2112,128]{3,2,1,0:T(8,128)(2,1)}, u32[]{:S(2)}, u32[]{:S(2)}) collective-permute-start(bf16[4,4,2112,128]{3,2,1,0:T(8,128)(2,1)} %bitcast.154), channel_id=1, source_target_pairs={{0,1},{1,0},{2,3},{3,2},{4,5},{5,4},{6,7},{7,6},{8,9},{9,8},{10,11... | collective-permute-start | bytes 25952264 | tf_op jit(solution)/shard_map/ppermute | solution.py:615
  232.1 20.8 %collective-permute-start.28 = (bf16[64,2048]{1,0:T(8,128)(2,1)S(1)}, bf16[64,2048]{1,0:T(8,128)(2,1)S(1)}, u32[]{:S(2)}, u32[]{:S(2)}) collective-permute-start(bf16[64,2048]{1,0:T(8,128)(2,1)S(1)} %multiply_convert_fusion), channel_id=1, source_target_pairs={{0,16},{2,18},{4,20},{6,22},{8,24},{10,26},{12,28},{14,30},{16,0},... | collective-permute-start | bytes 786440 | tf_op jit(solution)/shard_map/ppermute | solution.py:623
  235.0 17.8 %collective-permute-start.29 = (bf16[64,2048]{1,0:T(8,128)(2,1)S(1)}, bf16[64,2048]{1,0:T(8,128)(2,1)S(1)}, u32[]{:S(2)}, u32[]{:S(2)}) collective-permute-start(bf16[64,2048]{1,0:T(8,128)(2,1)S(1)} %multiply_convert_fusion), channel_id=1, source_target_pairs={{0,24},{2,26},{4,28},{6,30},{8,0},{10,2},{12,4},{14,6},{16,8},{18,... | collective-permute-start | bytes 786440 | tf_op jit(solution)/shard_map/ppermute | solution.py:623
  277.9 15.1 %collective-permute-start.33 = (bf16[4,4,704,128]{3,2,1,0:T(8,128)(2,1)}, bf16[4,4,704,128]{3,2,1,0:T(8,128)(2,1)}, u32[]{:S(2)}, u32[]{:S(2)}) collective-permute-start(bf16[4,4,704,128]{3,2,1,0:T(8,128)(2,1)} %unit_grads.8), channel_id=1, source_target_pairs={{0,1},{1,0},{2,3},{3,2},{4,5},{5,4},{6,7},{7,6},{8,9},{9,8},{10,11... | collective-permute-start | bytes 8650760 | tf_op jit(solution)/shard_map/ppermute | solution.py:615
  281.7 16.0 %collective-permute-start.32 = (bf16[4,4,704,128]{3,2,1,0:T(8,128)(2,1)}, bf16[4,4,704,128]{3,2,1,0:T(8,128)(2,1)}, u32[]{:S(2)}, u32[]{:S(2)}) collective-permute-start(bf16[4,4,704,128]{3,2,1,0:T(8,128)(2,1)} %unit_grads.7), channel_id=1, source_target_pairs={{0,1},{1,0},{2,3},{3,2},{4,5},{5,4},{6,7},{7,6},{8,9},{9,8},{10,11... | collective-permute-start | bytes 8650760 | tf_op jit(solution)/shard_map/ppermute | solution.py:615
  286.5 16.1 %collective-permute-start.31 = (bf16[4,4,704,128]{3,2,1,0:T(8,128)(2,1)}, bf16[4,4,704,128]{3,2,1,0:T(8,128)(2,1)}, u32[]{:S(2)}, u32[]{:S(2)}) collective-permute-start(bf16[4,4,704,128]{3,2,1,0:T(8,128)(2,1)} %unit_grads.6), channel_id=1, source_target_pairs={{0,1},{1,0},{2,3},{3,2},{4,5},{5,4},{6,7},{7,6},{8,9},{9,8},{10,11... | collective-permute-start | bytes 8650760 | tf_op jit(solution)/shard_map/ppermute | solution.py:615
  286.5 32.9 %all-to-all-start.4 = ((bf16[4,64,2048]{2,1,0:T(8,128)(2,1)}), bf16[4,64,2048]{2,1,0:T(8,128)(2,1)S(1)}, u32[]{:S(2)}, u32[]{:S(2)}) async-start(bf16[4,64,2048]{2,1,0:T(8,128)(2,1)} %bitcast.33), calls=%async_computation.4 | async-start | bytes 2097152 | tf_op jit(solution)/shard_map/all_to_all | solution.py:629
  293.0 210.3 %reduce-scatter.4.cloned.1.call-start = ((), (), s32[]{:S(2)}) async-start(), calls=%async_computation.13 | async-start | bytes 10813440
  322.2 15.2 %collective-permute-start.35 = (bf16[64,2048]{1,0:T(8,128)(2,1)S(1)}, bf16[64,2048]{1,0:T(8,128)(2,1)S(1)}, u32[]{:S(2)}, u32[]{:S(2)}) collective-permute-start(bf16[64,2048]{1,0:T(8,128)(2,1)S(1)} %fusion.26), channel_id=1, source_target_pairs={{0,4},{2,6},{4,0},{6,2},{8,12},{10,14},{12,8},{14,10},{16,20},{18,... | collective-permute-start | bytes 786440 | tf_op jit(solution)/shard_map/ppermute | solution.py:626
  322.7 20.5 %collective-permute-start.36 = (bf16[64,2048]{1,0:T(8,128)(2,1)S(1)}, bf16[64,2048]{1,0:T(8,128)(2,1)S(1)}, u32[]{:S(2)}, u32[]{:S(2)}) collective-permute-start(bf16[64,2048]{1,0:T(8,128)(2,1)S(1)} %fusion.26), channel_id=1, source_target_pairs={{0,6},{2,4},{4,2},{6,0},{8,14},{10,12},{12,10},{14,8},{16,22},{18,... | collective-permute-start | bytes 786440 | tf_op jit(solution)/shard_map/ppermute | solution.py:626
  363.4 30.2 %all-to-all-start.5 = ((bf16[4,64,2048]{2,1,0:T(8,128)(2,1)}), bf16[4,64,2048]{2,1,0:T(8,128)(2,1)S(1)}, u32[]{:S(2)}, u32[]{:S(2)}) async-start(bf16[4,64,2048]{2,1,0:T(8,128)(2,1)} %bitcast.34), calls=%async_computation.5 | async-start | bytes 2097152 | tf_op jit(solution)/shard_map/all_to_all | solution.py:629
  366.9 32.9 %collective-permute-start.39 = (bf16[1024,512]{1,0:T(8,128)(2,1)}, bf16[1024,512]{1,0:T(8,128)(2,1)}, u32[]{:S(2)}, u32[]{:S(2)}) collective-permute-start(bf16[1024,512]{1,0:T(8,128)(2,1)} %get-tuple-element.89), channel_id=1, source_target_pairs={{0,1},{1,0},{2,3},{3,2},{4,5},{5,4},{6,7},{7,6},{8,9},{9,8},{10,11... | collective-permute-start | bytes 3145736 | tf_op jit(solution)/shard_map/ppermute | solution.py:615
  396.3 29.3 %all-to-all-start.6 = ((bf16[16,256,128]{2,1,0:T(8,128)(2,1)}), bf16[16,256,128]{2,1,0:T(8,128)(2,1)S(1)}, u32[]{:S(2)}, u32[]{:S(2)}) async-start(bf16[16,256,128]{2,1,0:T(8,128)(2,1)} %slice.205), calls=%async_computation.6 | async-start | bytes 2097152 | tf_op jit(solution)/shard_map/all_to_all | solution.py:629
  403.0 15.1 %collective-permute-start.41 = (bf16[256,512]{1,0:T(8,128)(2,1)S(1)}, bf16[256,512]{1,0:T(8,128)(2,1)S(1)}, u32[]{:S(2)}, u32[]{:S(2)}) collective-permute-start(bf16[256,512]{1,0:T(8,128)(2,1)S(1)} %get-tuple-element.164), channel_id=1, source_target_pairs={{0,4},{2,6},{4,0},{6,2},{8,12},{10,14},{12,8},{14,10},{16,20},{18,... | collective-permute-start | bytes 786440 | tf_op jit(solution)/shard_map/ppermute | solution.py:626
  404.9 20.0 %collective-permute-start.42 = (bf16[256,512]{1,0:T(8,128)(2,1)S(1)}, bf16[256,512]{1,0:T(8,128)(2,1)S(1)}, u32[]{:S(2)}, u32[]{:S(2)}) collective-permute-start(bf16[256,512]{1,0:T(8,128)(2,1)S(1)} %get-tuple-element.163), channel_id=1, source_target_pairs={{0,6},{2,4},{4,2},{6,0},{8,14},{10,12},{12,10},{14,8},{16,22},{18,... | collective-permute-start | bytes 786440 | tf_op jit(solution)/shard_map/ppermute | solution.py:626
  435.8 51.3 %all-to-all-start.7 = ((bf16[16,512,128]{2,1,0:T(8,128)(2,1)}), bf16[16,512,128]{2,1,0:T(8,128)(2,1)S(1)}, u32[]{:S(2)}, u32[]{:S(2)}) async-start(bf16[16,512,128]{2,1,0:T(8,128)(2,1)} %slice.204), calls=%async_computation.7 | async-start | bytes 4194304 | tf_op jit(solution)/shard_map/all_to_all | solution.py:629
  441.4 15.7 %collective-permute-start.49 = (bf16[256,384]{1,0:T(8,128)(2,1)S(1)}, bf16[256,384]{1,0:T(8,128)(2,1)S(1)}, u32[]{:S(2)}, u32[]{:S(2)}) collective-permute-start(bf16[256,384]{1,0:T(8,128)(2,1)S(1)} %get-tuple-element.183), channel_id=1, source_target_pairs={{0,2},{2,0},{4,6},{6,4},{8,10},{10,8},{12,14},{14,12},{16,18},{18,... | collective-permute-start | bytes 589832 | tf_op jit(solution)/shard_map/ppermute | solution.py:626
  441.9 15.3 %collective-permute-start.50 = (bf16[256,384]{1,0:T(8,128)(2,1)S(1)}, bf16[256,384]{1,0:T(8,128)(2,1)S(1)}, u32[]{:S(2)}, u32[]{:S(2)}) collective-permute-start(bf16[256,384]{1,0:T(8,128)(2,1)S(1)} %get-tuple-element.182), channel_id=1, source_target_pairs={{0,4},{2,6},{4,0},{6,2},{8,12},{10,14},{12,8},{14,10},{16,20},{18,... | collective-permute-start | bytes 589832 | tf_op jit(solution)/shard_map/ppermute | solution.py:626
  467.7 30.7 %collective-permute-start.56 = (bf16[4,4,64,384]{3,2,1,0:T(8,128)(2,1)}, bf16[4,4,64,384]{3,2,1,0:T(8,128)(2,1)}, u32[]{:S(2)}, u32[]{:S(2)}) collective-permute-start(bf16[4,4,64,384]{3,2,1,0:T(8,128)(2,1)} %get-tuple-element.99), channel_id=1, source_target_pairs={{0,1},{1,0},{2,3},{3,2},{4,5},{5,4},{6,7},{7,6},{8,9},{9,8},{10,11... | collective-permute-start | bytes 2359304 | tf_op jit(solution)/shard_map/ppermute | solution.py:615
  502.8 28.0 %collective-permute-start.58 = (bf16[4,64,384]{2,1,0:T(8,128)(2,1)}, bf16[4,64,384]{2,1,0:T(8,128)(2,1)}, u32[]{:S(2)}, u32[]{:S(2)}) collective-permute-start(bf16[4,64,384]{2,1,0:T(8,128)(2,1)} %get-tuple-element.180), channel_id=1, source_target_pairs={{0,16},{2,18},{4,20},{6,22},{8,24},{10,26},{12,28},{14,30},{16,0},... | collective-permute-start | bytes 589832 | tf_op jit(solution)/shard_map/ppermute | solution.py:623
  502.8 28.0 %collective-permute-start.59 = (bf16[4,64,384]{2,1,0:T(8,128)(2,1)}, bf16[4,64,384]{2,1,0:T(8,128)(2,1)}, u32[]{:S(2)}, u32[]{:S(2)}) collective-permute-start(bf16[4,64,384]{2,1,0:T(8,128)(2,1)} %get-tuple-element.179), channel_id=1, source_target_pairs={{0,8},{2,10},{4,12},{6,14},{8,16},{10,18},{12,20},{14,22},{16,24},... | collective-permute-start | bytes 589832 | tf_op jit(solution)/shard_map/ppermute | solution.py:623
  508.6 55.8 %all-to-all-start.8 = ((bf16[4,2112,128]{2,1,0:T(8,128)(2,1)}), bf16[4,2112,128]{2,1,0:T(8,128)(2,1)S(1)}, u32[]{:S(2)}, u32[]{:S(2)}) async-start(bf16[4,2112,128]{2,1,0:T(8,128)(2,1)} %bitcast.144), calls=%async_computation.8 | async-start | bytes 4325376 | tf_op jit(solution)/shard_map/all_to_all | solution.py:629
  516.0 16.7 %collective-permute-start.55 = (bf16[64,2048]{1,0:T(8,128)(2,1)}, bf16[64,2048]{1,0:T(8,128)(2,1)S(1)}, u32[]{:S(2)}, u32[]{:S(2)}) collective-permute-start(bf16[64,2048]{1,0:T(8,128)(2,1)} %get-tuple-element.194), channel_id=1, source_target_pairs={{0,1},{1,0},{2,3},{3,2},{4,5},{5,4},{6,7},{7,6},{8,9},{9,8},{10,11... | collective-permute-start | bytes 786440 | tf_op jit(solution)/shard_map/ppermute | solution.py:615
  (88 other events, 759.9 us)
Sparse Core Ops, SparseCore 0:
  110.3 100.1 all-gather.2
  319.5 102.8 reduce-scatter.3

commit v5 on v4

--- a/solution.py
+++ b/solution.py
@@ -270,13 +270,10 @@
 ):
     weights, refs = refs[:4], refs[4:]
     q_ref, o_ref, lse_ref, d_attn_ref = refs[:4]
-    joined = weights[0].shape[0] == weights[-1].shape[0]
-    grads, refs = (refs[4:6], refs[6:]) if joined else (refs[4:8], refs[8:])
-    grads_q, grads_out = grads[:2], grads[-2:]
+    grads_q, refs = refs[4:6], refs[6:]
     d_lat_ref, near_ref, far_ref, wq, wo, sems, d_kv_sum, d_lat_sum = refs[:8]
     sums = refs[8:]
     q_rows = wq.shape[2]
-    skipped = q_rows if joined else 0
     pair = wo.shape[2] // HEAD
     step, steps = pl.program_id(0), pl.num_programs(0)
     corner = at_ref[1]
@@ -292,15 +289,12 @@
         for copy in copies:
             copy.wait()
 
-    def store(c, h, grad_q, grad_out):
+    def store(c, h, grad_q):
         size = q_rows // (2 * pair)
         for i in range(2):
             here = slice((2 * h + i) * size, (2 * h + i + 1) * size)
             tile = grad_q[:, i * 128 : (i + 1) * 128].astype(BF16)
             grads_q[c][:, here, :] = tile.reshape(-1, size, 128)
-        here = slice(skipped + h * HEAD, skipped + (h + 1) * HEAD)
-        for tile in range(wo.shape[1]):
-            grads_out[c][tile, here, :] = grad_out[:, tile * 128 : (tile + 1) * 128].astype(BF16)
 
     keys = keys_ref[...]
     allowed = (keys <= natural_ref[...]) & (keys >= start_ref[...])
@@ -310,7 +304,6 @@
         for h in range(pair):
             q, mix, lse = q_ref[c * pair + h], o_ref[c * pair + h], lse_ref[c * pair + h]
             w_q, w_out = head_q(wq, c, h, pair), head_out(wo, c, h)
-            grad_out = contract_rows(mix.astype(BF16), d_attn)
             d_o = times_transposed(d_attn, w_out).astype(BF16)
             delta = jnp.sum(d_o.astype(F32) * mix, axis=-1, keepdims=True)
             scores = times_transposed(q, kv_ref[:, :HEAD])
@@ -329,16 +322,15 @@
             d_lat = share if d_lat is None else d_lat + share
             if sums:
                 sums[0][c, h] += grad_q
-                sums[1][c, h] = (sums[1][c, h].astype(F32) + grad_out).astype(BF16)
             else:
-                store(c, h, grad_q, grad_out)
+                store(c, h, grad_q)
     if sums:
 
         @pl.when(step == steps - 1)
         def _():
             for c in range(2):
                 for h in range(pair):
-                    store(c, h, sums[0][c, h], sums[1][c, h])
+                    store(c, h, sums[0][c, h])
 
     d_lat_sum[...] = d_lat
     share = d_lat.shape[1] // SQUARE
@@ -364,13 +356,11 @@
     heads, width = 2 * pair, tiles * lanes
     by_head = lambda size: pl.BlockSpec((heads, block, size), lambda i: (0, i, 0))
     whole = lambda dims: pl.BlockSpec(dims, lambda i: (0,) * len(dims))
-    grad_dims = [(places, q_rows, HEAD // 2)] * 2 + [(tiles, pair * HEAD, lanes)] * 2
-    if places == tiles:
-        grad_dims = [(places, q_rows + pair * HEAD, lanes)] * 2
+    grad_dims = [(places, q_rows, HEAD // 2)] * 2
     d_lat_dims = (SQUARE, rows, rank // SQUARE + 128)
     sums = []
     if rows != block:
-        sums = [pltpu.VMEM((2, pair, rank, HEAD), F32), pltpu.VMEM((2, pair, HEAD, width), BF16)]
+        sums = [pltpu.VMEM((2, pair, rank, HEAD), F32)]
     return pl.pallas_call(
         attend_back_kernel,
         grid=(rows // block,),
@@ -397,7 +387,7 @@
             pltpu.VMEM((block, rank), F32),
         ]
         + sums,
-        compiler_params=params(VMEM_LIMIT + len(sums) * 2**21),
+        compiler_params=params(VMEM_LIMIT + len(sums) * 2**22),
         cost_estimate=pl.CostEstimate(
             flops=2 * rows * heads * HEAD * (5 * count + 2 * rank + 2 * width),
             bytes_accessed=12 * count * HEAD + 4 * heads * HEAD * (rank + width),
@@ -405,6 +395,34 @@
         ),
         name="attend_back",
     )(at, lat, *tables, kv, keys, *weights, q, o, lse, d_attn)
+
+
+def out_grads_kernel(mix_ref, d_attn_ref, near_ref, far_ref):
+    d_attn = d_attn_ref[...]
+    pair = mix_ref.shape[0] // 2
+    for c, out_ref in enumerate((near_ref, far_ref)):
+        for h in range(pair):
+            grad = contract_rows(mix_ref[c * pair + h], d_attn)
+            for tile in range(out_ref.shape[0]):
+                out_ref[tile, h * HEAD : (h + 1) * HEAD, :] = grad[
+                    :, tile * 128 : (tile + 1) * 128
+                ].astype(BF16)
+
+
+def out_grads(mix, d_attn, pair):
+    rows, width = d_attn.shape
+    dims = (width // 128, pair * HEAD, 128)
+    return pl.pallas_call(
+        out_grads_kernel,
+        in_specs=[VMEM, VMEM],
+        out_specs=[VMEM, VMEM],
+        out_shape=[shape(dims), shape(dims)],
+        compiler_params=params(),
+        cost_estimate=pl.CostEstimate(
+            flops=4 * rows * pair * HEAD * width, bytes_accessed=8 * pair * HEAD * width, transcendentals=0
+        ),
+        name="out_grads",
+    )(mix, d_attn)
 
 
 def latent_back_kernel(layers, at_ref, hat_ref, inverse_ref, d_kv_ref, x_ref, w_ref, *refs):
@@ -729,9 +747,9 @@
     down_scaled = (down.astype(F32) * gain_rows).astype(BF16)
     down_half = lax.dynamic_slice_in_dim(down_scaled, core * (lanes // 2), lanes // 2, 0)
     cot_own = own(cotangent)
+    down_own = square_exchange(shares(down_half))
     cot_pieces = line_pieces(arranged(cot_own))
     cot_all = by_layer(jnp.concatenate(cot_pieces))
-    down_own = square_exchange(shares(down_half))
     down_near = line_pieces(after(down_own, *cot_pieces[1:]))
     down_far = [across(piece) for piece in down_near]
 
@@ -810,18 +828,29 @@
     def line_total(blocks):
         return unarranged(jnp.sum(blocks.astype(F32), axis=0))
 
-    mlp_grads = None
-    for kind, value in ((0, h_all), (1, h_all), (2, cot_all)):
-        received = across(unit_grads(acts_far, kind, value))
-        mlp_grads = unit_grads(acts_near, kind, value, received, mlp_grads)
-    d_h_lines, mlp_grads = together(line_blocks(d_h_part), mlp_grads)
+    kinds = ((0, h_all), (1, h_all), (2, cot_all))
+    far_grads = [unit_grads(acts_far, kind, value) for kind, value in kinds]
+    d_h_lines = line_blocks(d_h_part)
+    d_h_lines, acts_near, *far_grads = together(d_h_lines, acts_near, *far_grads)
     d_hscaled = line_total(d_h_lines)
     d_hidden = cot_own.astype(F32) + norm_back(d_hscaled, h_hat, h_inverse)
+    mlp_grads = None
+    for kind, value in kinds:
+        mlp_grads = unit_grads(acts_near, kind, value, across(far_grads[kind]), mlp_grads)
+    mlp_lines = line_blocks(after(mlp_part, d_hscaled))
+    d_attn_pieces = square_pieces(d_hidden.astype(BF16))
+    mlp_lines, mlp_grads, *d_attn_pieces = together(mlp_lines, mlp_grads, *d_attn_pieces)
+    d_attn_all = jnp.concatenate(d_attn_pieces)
     mlp_sum = lax.psum_scatter(mlp_grads, "seq", axis_index_groups=square_groups)
-    mlp_lines = line_blocks(after(mlp_part, d_hscaled))
-    d_attn_all = jnp.concatenate(square_pieces(d_hidden.astype(BF16)))
-
-    *head_grads, d_lat_parts, d_kv_near, d_kv_far = attend_back(
+
+    mix_low = attn_mix.astype(BF16)
+    grad_out_near, grad_out_far = out_grads(mix_low, d_attn_all, pair)
+    grad_out_total = grad_out_near.astype(F32) + across(grad_out_far).astype(F32)
+    grad_out_total = untiled(grad_out_total.astype(BF16))
+    head_out_lines = line_exchange(grad_out_total)
+    layer_out_own = (hidden + line_total(mlp_lines)).astype(BF16)
+    layer_out = both(layer_out_own, across(layer_out_own))
+    grad_q_near, grad_q_far, d_lat_parts, d_kv_near, d_kv_far = attend_back(
         at,
         lat_low,
         tables,
@@ -835,64 +864,80 @@
         pair,
         block,
     )
-    head_grads = list(head_grads)
-    side = len(head_grads) // 2
-    head_total = [
-        (head_grads[2 * i].astype(F32) + across(head_grads[2 * i + 1]).astype(F32)).astype(BF16)
-        for i in range(side)
-    ]
-    if lanes == 128:
-        head_total = head_total[0]
-    else:
-        head_total = jnp.concatenate(
-            [head_total[0].reshape(chips, -1, lanes), untiled(head_total[1])], axis=1
-        )
-    d_kv_near, head_total, mlp_lines = together(d_kv_near, head_total, mlp_lines)
-    layer_out_own = (hidden + line_total(mlp_lines)).astype(BF16)
-    layer_out = both(layer_out_own, across(layer_out_own))
-
-    head_q = line_exchange(head_total[:, :qup_size])
     d_kv_low = (d_kv_near.astype(F32) + across(d_kv_far).astype(F32)).astype(BF16)
     d_kv_line = square_sum(d_kv_low.reshape(SQUARE, layers * rows, 2 * HEAD)).astype(BF16)
-    head_q, d_kv_line = together(head_q, d_kv_line)
+    head_out_lines, d_kv_line = together(head_out_lines, d_kv_line)
+    grad_q_total = (grad_q_near.astype(F32) + across(grad_q_far).astype(F32)).astype(BF16)
     d_kv_own = line_sum(d_kv_line.reshape(layers, rows, 2 * HEAD))
     d_kv_own = jnp.concatenate(
         [unrotate(d_kv_own[:, :HEAD], cosine[:rows], sine[:rows]), d_kv_own[:, HEAD:]], axis=1
     ).astype(BF16)
-    head_out_lines = line_exchange(after(head_total[:, qup_size:], d_kv_own))
+    head_q = line_exchange(after(grad_q_total, d_kv_own).reshape(chips, -1, lanes))
     kv_share_of = lambda m: lax.dynamic_slice_in_dim(d_kv_own, (corner ^ m) * kv_share, kv_share, 1)
     d_kv_share = jnp.concatenate(
         [kv_share_of(0)] + [within(kv_share_of(m), m) for m in range(1, SQUARE)]
     )
     d_lat_received = [d_lat_parts[0]] + [within(d_lat_parts[m], m) for m in range(1, SQUARE)]
+    head_q, *d_lat_received = together(head_q, *d_lat_received)
 
     d_x_part, down_grad_near, down_grad_far = latent_back(
         at, lat_hat, lat_inverse, d_kv_share, x_all, down_here, d_lat_received
     )
-    d_xscaled = square_sum(d_x_part.reshape(SQUARE, rows, width))
-    head_out_lines, d_xscaled = together(head_out_lines, d_xscaled)
-    mlp_back = line_exchange(untiled(after(mlp_sum, head_out_lines)))
+    d_x_blocks = d_x_part.reshape(SQUARE, rows, width)
+    d_x_received = [within(d_x_blocks[m], m) for m in range(1, SQUARE)]
+    down_sum = (down_grad_near + across(down_grad_far).astype(F32)).astype(BF16)
+
+    def square_send(value):
+        blocks = [
+            lax.dynamic_index_in_dim(value, corner ^ m, 0, keepdims=False) for m in range(SQUARE)
+        ]
+        return [blocks[0]] + [within(blocks[m], m) for m in range(1, SQUARE)]
+
+    def by_corner(pieces):
+        pieces = jnp.stack(pieces)
+        return jnp.stack(
+            [
+                lax.dynamic_index_in_dim(pieces, corner ^ q, 0, keepdims=False)
+                for q in range(SQUARE)
+            ]
+        )
+
+    mlp_sum = untiled(mlp_sum)
+    gate_up_back = line_exchange(after(mlp_sum[:, : 2 * units], head_q))
+    head_sum = jnp.concatenate(
+        [
+            jnp.sum(blocks.reshape(layers, SQUARE, -1, lanes).astype(F32), axis=0).astype(BF16)
+            for blocks in (head_q, head_out_lines)
+        ],
+        axis=1,
+    )
+    head_pieces = square_send(head_sum)
+    gate_up_back, *received = together(gate_up_back, *d_x_received, *head_pieces)
+    d_x_received, head_pieces = received[: SQUARE - 1], received[SQUARE - 1 :]
+    d_xscaled = d_x_blocks[0].astype(F32) + sum(block.astype(F32) for block in d_x_received)
     token_own = (d_hidden + norm_back(d_xscaled, x_hat, x_inverse)).astype(BF16)
     token_grad = both(token_own, across(token_own))
-    down_sum = (down_grad_near + across(down_grad_far).astype(F32)).astype(BF16)
-    down_line, mlp_back = together(line_sum(down_sum).astype(BF16), mlp_back)
-    down_back = unshares(square_exchange(down_line)).astype(F32)
+    down_sum = after(down_sum, gate_up_back)
+    down_pieces = [along(down_sum[k], -k) for k in range(1, layers)]
+    unit_back = line_exchange(after(mlp_sum[:, 2 * units :], *down_pieces))
+    down_line = down_sum[0].astype(F32) + sum(piece.astype(F32) for piece in down_pieces)
+    down_pieces = square_send(down_line.astype(BF16))
+    unit_back, *down_pieces = together(unit_back, *down_pieces)
+    head_sum = by_corner(head_pieces)
+    down_back = unshares(by_corner(down_pieces)).astype(F32)
     down_back = both(down_back, across(down_back))
     attn_gain_part = jnp.sum(down_back * down.astype(F32), axis=1)
     down_grad = down_back * gain_rows
     qdown_part, kv_part = down_grad[:, :rank], down_grad[:, rank:]
 
     gate_back, up_back, down_part = (
-        mlp_back[:, kind * units : (kind + 1) * units].reshape(layers * units, lanes).astype(F32)
-        for kind in range(3)
+        value.reshape(layers * units, lanes).astype(F32)
+        for value in (gate_up_back[:, :units], gate_up_back[:, units:], unit_back)
     )
     gate_back, up_back = gate_back.T, up_back.T
     gate_part, up_part = gate_back * mlp_gain_rows, up_back * mlp_gain_rows
     mlp_gain_part = jnp.sum(gate_back * w_gate.astype(F32) + up_back * w_up.astype(F32), axis=1)
 
-    head_lines = jnp.concatenate([head_q, head_out_lines], axis=1)
-    head_lines = head_lines.reshape(layers, SQUARE, -1, lanes).astype(F32)
-    head_sum = square_exchange(jnp.sum(head_lines, axis=0).astype(BF16))
     qup_back = head_sum[:, :qup_size].reshape(SQUARE, 2 * pair, rank_rows, half)
     qup_back = jnp.transpose(qup_back, (2, 0, 1, 3)).reshape(rank_rows, -1).astype(F32)
     out_part = head_sum[:, qup_size:].reshape(-1, lanes).astype(F32)

time: 606 us -> 568 us (0.937)
  waiting for transfers between devices: 275 us -> 238 us
  starting transfers between devices: 110 us -> 118 us
    all_to_all x7 -> x8, waiting for transfers between devices: 113 us -> 85.7 us  [line_exchange(): lax.all_to_all(value, 'seq', 0, 0, axis_index_groups=lines, tiled=True)]
    ppermute x27 -> x33, starting transfers between devices: 30.5 us -> 38.4 us  [within(): return lax.ppermute(value, 'seq', [(i, i ^ flip) for i in range(chips)])]
    all_to_all x4 -> x2, starting transfers between devices: 15.1 us -> 7.49 us  [square_exchange(): lax.all_to_all(value, 'seq', 0, 0, axis_index_groups=square_groups, tiled...]
    all_to_all x4 -> x2, waiting for transfers between devices: 8.58 us -> 2.09 us  [square_exchange(): lax.all_to_all(value, 'seq', 0, 0, axis_index_groups=square_groups, tiled...]
    ppermute x17 -> x18, waiting for transfers between devices: 6.42 us -> 12.4 us  [across(): return lax.ppermute(value, 'tp', [(0, 1), (1, 0)])]
    ppermute x27 -> x33, waiting for transfers between devices: 104 us -> 98.9 us  [within(): return lax.ppermute(value, 'seq', [(i, i ^ flip) for i in range(chips)])]
    all_to_all x7 -> x8, starting transfers between devices: 32.7 us -> 37.3 us  [line_exchange(): lax.all_to_all(value, 'seq', 0, 0, axis_index_groups=lines, tiled=True)]
    unnamed x103 -> x122, local copies, waits for them, and re-layouts: 20.5 us -> 17.9 us
  transfers between devices with their start and end apart: 75 -> 81, of which waited for: 41 -> 45; matrix products, arithmetic and copies ran while one was open for 16% -> 14% of each run, Pallas kernels for 11% -> 13%
where the time goes in v5:
time: 568 us; the launch traced here: 560 us
  waiting for transfers between devices  238 us (42%)
  starting transfers between devices  118 us (21%)
  Pallas kernels  92.8 us (16%)
  other arithmetic  53.2 us (9%)
  local copies, waits for them, and re-layouts  43.4 us (8%)
  between operations  15.4 us (3%)
    ppermute x33, waiting for transfers between devices, within(): return lax.ppermute(value, 'seq', [(i, i ^ flip) for i in range(chips)])  98.9 us
    all_to_all x8, waiting for transfers between devices, line_exchange(): lax.all_to_all(value, 'seq', 0, 0, axis_index_groups=lines, tiled=True)  85.7 us
    ppermute x18, waiting for transfers between devices, along(): return lax.ppermute(value, 'seq', pairs)  38.8 us
    ppermute x33, starting transfers between devices, within(): return lax.ppermute(value, 'seq', [(i, i ^ flip) for i in range(chips)])  38.4 us
    all_to_all x8, starting transfers between devices, line_exchange(): lax.all_to_all(value, 'seq', 0, 0, axis_index_groups=lines, tiled=True)  37.3 us
    ppermute x18, starting transfers between devices, along(): return lax.ppermute(value, 'seq', pairs)  31.4 us
    pallas_call x6, Pallas kernels, unit_grads(): pl.pallas_call(body, grid=(1,), in_specs=in_specs, out_specs=out_specs, o...  26.2 us
    pallas_call x1, Pallas kernels, mlp(): pl.pallas_call(mlp_kernel, in_specs=[VMEM, VMEM, HBM, HBM], out_specs=[VM...  19.8 us
  transfers between devices with their start and end apart: 81, of which 45 were waited for; matrix products, arithmetic and copies ran while one was open for 14% of the time, Pallas kernels for 13%

profile of v5, /device:TPU:0, one launch (start us, length us, event | category | flops | bytes accessed | tf_op | source)
XLA Modules:
  0.0 560.5 jit_solution(16542224075631631229)
XLA Ops:
  31.2 6.1 %collective-permute-start.3 = (bf16[4,64,384]{2,1,0:T(8,128)(2,1)}, bf16[4,64,384]{2,1,0:T(8,128)(2,1)S(1)}, u32[]{:S(2)}, u32[]{:S(2)}) collective-permute-start(bf16[4,64,384]{2,1,0:T(8,128)(2,1)} %all-to-all-done.refs_0_), channel_id=1, source_target_pairs={{0,8},{2,10},{4,12},{6,14},{8,16},{10,18},{12,20},{14,22},{16,24},... | collective-permute-start | bytes 589832 | tf_op jit(solution)/shard_map/ppermute | solution.py:641
  44.4 6.6 %collective-permute-done.4.refs_2_ = bf16[4,64,384]{2,1,0:T(8,128)(2,1)S(1)} collective-permute-done((bf16[4,64,384]{2,1,0:T(8,128)(2,1)}, bf16[4,64,384]{2,1,0:T(8,128)(2,1)S(1)}, u32[]{:S(2)}, u32[]{:S(2)}) %collective-permute-start.4) | collective-permute-done | bytes 196640 | tf_op jit(solution)/shard_map/ppermute | solution.py:641
  51.7 7.8 %all-to-all-start.1 = ((bf16[4,2112,128]{2,1,0:T(8,128)(2,1)}), bf16[4,2112,128]{2,1,0:T(8,128)(2,1)S(1)}, u32[]{:S(2)}, u32[]{:S(2)}) async-start(bf16[4,2112,128]{2,1,0:T(8,128)(2,1)} %pad_maximum_fusion), calls=%async_computation.1 | async-start | bytes 4325376 | tf_op jit(solution)/shard_map/all_to_all | solution.py:647
  90.7 4.8 collective-permute-done.14.refs_2_
  99.0 9.7 %all-to-all-done.1 = bf16[4,2112,128]{2,1,0:T(8,128)(2,1)S(1)} async-done(((bf16[4,2112,128]{2,1,0:T(8,128)(2,1)}), bf16[4,2112,128]{2,1,0:T(8,128)(2,1)S(1)}, u32[]{:S(2)}, u32[]{:S(2)}) %all-to-all-start.1) | async-done | bytes 2162720 | tf_op jit(solution)/shard_map/all_to_all | solution.py:647
  128.9 11.5 %collective-permute-done.19 = bf16[256,512]{1,0:T(8,128)(2,1)S(1)} collective-permute-done((bf16[256,512]{1,0:T(8,128)(2,1)}, bf16[256,512]{1,0:T(8,128)(2,1)S(1)}, u32[]{:S(2)}, u32[]{:S(2)}) %collective-permute-start.19) | collective-permute-done | bytes 262176 | tf_op jit(solution)/shard_map/ppermute | solution.py:644
  143.1 8.4 %collective-permute-done.21 = bf16[256,512]{1,0:T(8,128)(2,1)S(1)} collective-permute-done((bf16[256,512]{1,0:T(8,128)(2,1)}, bf16[256,512]{1,0:T(8,128)(2,1)S(1)}, u32[]{:S(2)}, u32[]{:S(2)}) %collective-permute-start.21) | collective-permute-done | bytes 262176 | tf_op jit(solution)/shard_map/ppermute | solution.py:644
  156.2 37.7 %all-to-all-done.3.refs_0_.refs_2_ = bf16[16,768,128]{2,1,0:T(8,128)(2,1)S(1)} async-done(((bf16[16,768,128]{2,1,0:T(8,128)(2,1)}), bf16[16,768,128]{2,1,0:T(8,128)(2,1)S(1)}, u32[]{:S(2)}, u32[]{:S(2)}) %all-to-all-start.3) | async-done | bytes 3145760 | tf_op jit(solution)/shard_map/all_to_all | solution.py:647
  199.7 13.7 %attend.1 = (bf16[4,256,256]{2,1,0:T(8,128)(2,1)}, f32[4,256,256]{2,1,0:T(8,128)}, f32[4,256,1]{2,1,0:T(8,128)}, bf16[256,2048]{1,0:T(8,128)(2,1)}) custom-call(bf16[256,1024]{1,0:T(8,128)(2,1)} %get-tuple-element.90.lat_ref, f32[256,128]{1,0:T(8,128)} %get-tuple-element.293.cos_ref, f32[256,128]{1,0:T(8,128)} %get-tuple-element.292.sin_ref, ...), custom_call_target="tpu_custom_call" | custom-call | flops 3758096384 | bytes 8388608 | tf_op jit(solution)/shard_map/attend/pallas_call | solution.py:237
  219.6 5.4 collective-permute-done.26
  225.0 5.0 collective-permute-done.25
  235.9 5.4 collective-permute-done.29
  241.3 14.4 %collective-permute-done.28 = bf16[64,2048]{1,0:T(8,128)(2,1)S(1)} collective-permute-done((bf16[64,2048]{1,0:T(8,128)(2,1)S(1)}, bf16[64,2048]{1,0:T(8,128)(2,1)S(1)}, u32[]{:S(2)}, u32[]{:S(2)}) %collective-permute-start.28) | collective-permute-done | bytes 262176 | tf_op jit(solution)/shard_map/ppermute | solution.py:641
  256.9 19.8 %mlp.1 = (bf16[256,2048]{1,0:T(8,128)(2,1)}, bf16[256,2048]{1,0:T(8,128)(2,1)}, bf16[3,256,704]{2,1,0:T(8,128)(2,1)}, bf16[3,256,704]{2,1,0:T(8,128)(2,1)}) custom-call(bf16[256,2048]{1,0:T(8,128)(2,1)} %pad_maximum_fusion.3.h_ref.value_ref.v, bf16[256,2048]{1,0:T(8,128)(2,1)} %pad_maximum_fusion.5.cot_ref.value_ref.v, bf16[4,4,2112,128]{3,2,1,0:T(8,128)(2,1)} %bitcast.189, ...), custom_call_target="tpu_custom_call" | custom-call | flops 8858370048 | bytes 21495808 | tf_op jit(solution)/shard_map/mlp/pallas_call | solution.py:533
  276.7 5.1 all-to-all-start.4
  293.6 13.3 %all-to-all-done.4 = bf16[4,64,2048]{2,1,0:T(8,128)(2,1)S(1)} async-done(((bf16[4,64,2048]{2,1,0:T(8,128)(2,1)}), bf16[4,64,2048]{2,1,0:T(8,128)(2,1)S(1)}, u32[]{:S(2)}, u32[]{:S(2)}) %all-to-all-start.4) | async-done | bytes 1048608 | tf_op jit(solution)/shard_map/all_to_all | solution.py:647
  315.1 4.8 unit_grads.9.k
  319.9 4.9 unit_grads.10.k
  324.8 4.8 unit_grads.11
  329.6 8.1 %all-to-all-done.5 = bf16[4,64,2048]{2,1,0:T(8,128)(2,1)S(1)} async-done(((bf16[4,64,2048]{2,1,0:T(8,128)(2,1)}), bf16[4,64,2048]{2,1,0:T(8,128)(2,1)S(1)}, u32[]{:S(2)}, u32[]{:S(2)}) %all-to-all-start.5) | async-done | bytes 1048608 | tf_op jit(solution)/shard_map/all_to_all | solution.py:647
  341.9 4.6 out_grads.1
  358.3 16.6 %attend_back.1 = (bf16[16,256,128]{2,1,0:T(8,128)(2,1)}, bf16[16,256,128]{2,1,0:T(8,128)(2,1)}, bf16[4,256,384]{2,1,0:T(8,128)(2,1)}, f32[1024,512]{1,0:T(8,128)}, bf16[1024,512]{1,0:T(8,128)(2,1)}) custom-call(s32[3]{0:T(128)} %pad_add_fusion.1.at_ref, bf16[256,1024]{1,0:T(8,128)(2,1)} %get-tuple-element.90.lat_ref, f32[256,128]{1,0:T(8,128)} %get-tuple-element.293.cos_ref, ...), custom_call_target="tpu_custom_call" | custom-call | flops 8589934592 | bytes 18874368 | tf_op jit(solution)/shard_map/attend_back/pallas_call | solution.py:364
  384.7 12.2 %collective-permute-done.42 = bf16[256,512]{1,0:T(8,128)(2,1)S(1)} collective-permute-done((bf16[256,512]{1,0:T(8,128)(2,1)S(1)}, bf16[256,512]{1,0:T(8,128)(2,1)S(1)}, u32[]{:S(2)}, u32[]{:S(2)}) %collective-permute-start.42) | collective-permute-done | bytes 262176 | tf_op jit(solution)/shard_map/ppermute | solution.py:644
  396.9 5.2 collective-permute-done.41
  402.4 4.9 all-to-all-done.6
  426.3 8.5 %collective-permute-done.50.refs_1_ = bf16[256,384]{1,0:T(8,128)(2,1)S(1)} collective-permute-done((bf16[256,384]{1,0:T(8,128)(2,1)S(1)}, bf16[256,384]{1,0:T(8,128)(2,1)S(1)}, u32[]{:S(2)}, u32[]{:S(2)}) %collective-permute-start.50) | collective-permute-done | bytes 196640 | tf_op jit(solution)/shard_map/ppermute | solution.py:644
  436.5 6.5 %collective-permute-done.52.refs_3_ = bf16[256,384]{1,0:T(8,128)(2,1)} collective-permute-done((bf16[256,384]{1,0:T(8,128)(2,1)S(1)}, bf16[256,384]{1,0:T(8,128)(2,1)}, u32[]{:S(2)}, u32[]{:S(2)}) %collective-permute-start.52) | collective-permute-done | bytes 196640 | tf_op jit(solution)/shard_map/ppermute | solution.py:644
  447.2 4.5 all-to-all-start.8
  459.0 5.1 latent_back.1
  484.0 10.7 %collective-permute-done.57 = bf16[768,128]{1,0:T(8,128)(2,1)S(1)} collective-permute-done((bf16[768,128]{1,0:T(8,128)(2,1)S(1)}, bf16[768,128]{1,0:T(8,128)(2,1)S(1)}, u32[]{:S(2)}, u32[]{:S(2)}) %collective-permute-start.57) | collective-permute-done | bytes 196640 | tf_op jit(solution)/shard_map/ppermute | solution.py:644
  521.2 4.5 collective-permute-done.63
  538.8 10.2 %all-to-all-done.9 = bf16[4,704,128]{2,1,0:T(8,128)(2,1)S(1)} async-done(((bf16[4,704,128]{2,1,0:T(8,128)(2,1)}), bf16[4,704,128]{2,1,0:T(8,128)(2,1)S(1)}, u32[]{:S(2)}, u32[]{:S(2)}) %all-to-all-start.9) | async-done | bytes 720928 | tf_op jit(solution)/shard_map/all_to_all | solution.py:647
  (393 shorter events, 254.4 us)
Async XLA Ops:
  8.3 22.8 %collective-permute-start = (bf16[64,2048]{1,0:T(8,128)(2,1)S(1)}, bf16[64,2048]{1,0:T(8,128)(2,1)}, u32[]{:S(2)}, u32[]{:S(2)}) collective-permute-start(bf16[64,2048]{1,0:T(8,128)(2,1)S(1)} %constant_dynamic-slice_fusion.8), channel_id=1, source_target_pairs={{0,8},{2,10},{4,12},{6,14},{8,16},{10,18},{12,20},{14,22},{16,24},... | collective-permute-start | bytes 786440 | tf_op jit(solution)/shard_map/ppermute | solution.py:641
  11.4 19.8 %collective-permute-start.1 = (bf16[64,2048]{1,0:T(8,128)(2,1)S(1)}, bf16[64,2048]{1,0:T(8,128)(2,1)}, u32[]{:S(2)}, u32[]{:S(2)}) collective-permute-start(bf16[64,2048]{1,0:T(8,128)(2,1)S(1)} %constant_dynamic-slice_fusion.8), channel_id=1, source_target_pairs={{0,16},{2,18},{4,20},{6,22},{8,24},{10,26},{12,28},{14,30},{16,0},... | collective-permute-start | bytes 786440 | tf_op jit(solution)/shard_map/ppermute | solution.py:641
  14.0 17.2 %collective-permute-start.2 = (bf16[64,2048]{1,0:T(8,128)(2,1)S(1)}, bf16[64,2048]{1,0:T(8,128)(2,1)}, u32[]{:S(2)}, u32[]{:S(2)}) collective-permute-start(bf16[64,2048]{1,0:T(8,128)(2,1)S(1)} %constant_dynamic-slice_fusion.8), channel_id=1, source_target_pairs={{0,24},{2,26},{4,28},{6,30},{8,0},{10,2},{12,4},{14,6},{16,8},{18,... | collective-permute-start | bytes 786440 | tf_op jit(solution)/shard_map/ppermute | solution.py:641
  27.3 24.4 %all-to-all-start.2 = ((bf16[4,768,128]{2,1,0:T(8,128)(2,1)}), bf16[4,768,128]{2,1,0:T(8,128)(2,1)S(1)}, u32[]{:S(2)}, u32[]{:S(2)}) async-start(bf16[4,768,128]{2,1,0:T(8,128)(2,1)} %pad_maximum_fusion.6), calls=%async_computation.2 | async-start | bytes 1572864 | tf_op jit(solution)/shard_map/all_to_all | solution.py:650
  51.7 57.0 %all-to-all-start.1 = ((bf16[4,2112,128]{2,1,0:T(8,128)(2,1)}), bf16[4,2112,128]{2,1,0:T(8,128)(2,1)S(1)}, u32[]{:S(2)}, u32[]{:S(2)}) async-start(bf16[4,2112,128]{2,1,0:T(8,128)(2,1)} %pad_maximum_fusion), calls=%async_computation.1 | async-start | bytes 4325376 | tf_op jit(solution)/shard_map/all_to_all | solution.py:647
  59.5 153.9 %all-gather.3.cloned.1.call-start = ((), (), s32[]{:S(2)}) async-start(), calls=%async_computation.11 | async-start | bytes 10813440 | tf_op jit(solution)/shard_map/all_gather | solution.py:797
  121.5 72.4 %all-to-all-start.3 = ((bf16[16,768,128]{2,1,0:T(8,128)(2,1)}), bf16[16,768,128]{2,1,0:T(8,128)(2,1)S(1)}, u32[]{:S(2)}, u32[]{:S(2)}) async-start(bf16[16,768,128]{2,1,0:T(8,128)(2,1)} %bitcast.160), calls=%async_computation.3 | async-start | bytes 6291456 | tf_op jit(solution)/shard_map/all_to_all | solution.py:647
  128.5 23.0 %collective-permute-start.21 = (bf16[256,512]{1,0:T(8,128)(2,1)}, bf16[256,512]{1,0:T(8,128)(2,1)S(1)}, u32[]{:S(2)}, u32[]{:S(2)}) collective-permute-start(bf16[256,512]{1,0:T(8,128)(2,1)} %copy-done.46), channel_id=1, source_target_pairs={{0,6},{2,4},{4,2},{6,0},{8,14},{10,12},{12,10},{14,8},{16,22},{18,... | collective-permute-start | bytes 786440 | tf_op jit(solution)/shard_map/ppermute | solution.py:644
  213.5 43.5 %collective-permute-start.30 = (bf16[4,4,2112,128]{3,2,1,0:T(8,128)(2,1)}, bf16[4,4,2112,128]{3,2,1,0:T(8,128)(2,1)}, u32[]{:S(2)}, u32[]{:S(2)}) collective-permute-start(bf16[4,4,2112,128]{3,2,1,0:T(8,128)(2,1)} %bitcast.188), channel_id=1, source_target_pairs={{0,1},{1,0},{2,3},{3,2},{4,5},{5,4},{6,7},{7,6},{8,9},{9,8},{10,11... | collective-permute-start | bytes 25952264 | tf_op jit(solution)/shard_map/ppermute | solution.py:633
  233.9 21.7 %collective-permute-start.28 = (bf16[64,2048]{1,0:T(8,128)(2,1)S(1)}, bf16[64,2048]{1,0:T(8,128)(2,1)S(1)}, u32[]{:S(2)}, u32[]{:S(2)}) collective-permute-start(bf16[64,2048]{1,0:T(8,128)(2,1)S(1)} %multiply_convert_fusion), channel_id=1, source_target_pairs={{0,16},{2,18},{4,20},{6,22},{8,24},{10,26},{12,28},{14,30},{16,0},... | collective-permute-start | bytes 786440 | tf_op jit(solution)/shard_map/ppermute | solution.py:641
  233.9 21.7 %collective-permute-start.27 = (bf16[64,2048]{1,0:T(8,128)(2,1)S(1)}, bf16[64,2048]{1,0:T(8,128)(2,1)S(1)}, u32[]{:S(2)}, u32[]{:S(2)}) collective-permute-start(bf16[64,2048]{1,0:T(8,128)(2,1)S(1)} %multiply_convert_fusion), channel_id=1, source_target_pairs={{0,8},{2,10},{4,12},{6,14},{8,16},{10,18},{12,20},{14,22},{16,24},... | collective-permute-start | bytes 786440 | tf_op jit(solution)/shard_map/ppermute | solution.py:641
  276.7 30.1 %all-to-all-start.4 = ((bf16[4,64,2048]{2,1,0:T(8,128)(2,1)}), bf16[4,64,2048]{2,1,0:T(8,128)(2,1)S(1)}, u32[]{:S(2)}, u32[]{:S(2)}) async-start(bf16[4,64,2048]{2,1,0:T(8,128)(2,1)} %bitcast.170), calls=%async_computation.4 | async-start | bytes 2097152 | tf_op jit(solution)/shard_map/all_to_all | solution.py:647
  307.4 17.4 %collective-permute-start.31 = (bf16[4,4,704,128]{3,2,1,0:T(8,128)(2,1)}, bf16[4,4,704,128]{3,2,1,0:T(8,128)(2,1)}, u32[]{:S(2)}, u32[]{:S(2)}) collective-permute-start(bf16[4,4,704,128]{3,2,1,0:T(8,128)(2,1)} %unit_grads.8), channel_id=1, source_target_pairs={{0,1},{1,0},{2,3},{3,2},{4,5},{5,4},{6,7},{7,6},{8,9},{9,8},{10,11... | collective-permute-start | bytes 8650760 | tf_op jit(solution)/shard_map/ppermute | solution.py:633
  307.6 30.2 %all-to-all-start.5 = ((bf16[4,64,2048]{2,1,0:T(8,128)(2,1)}), bf16[4,64,2048]{2,1,0:T(8,128)(2,1)S(1)}, u32[]{:S(2)}, u32[]{:S(2)}) async-start(bf16[4,64,2048]{2,1,0:T(8,128)(2,1)} %bitcast.169), calls=%async_computation.5 | async-start | bytes 2097152 | tf_op jit(solution)/shard_map/all_to_all | solution.py:647
  311.1 133.6 %reduce-scatter.4.cloned.1.call-start = ((), (), s32[]{:S(2)}) async-start(), calls=%async_computation.12 | async-start | bytes 10813440
  311.6 18.0 %collective-permute-start.34 = (bf16[64,2048]{1,0:T(8,128)(2,1)S(1)}, bf16[64,2048]{1,0:T(8,128)(2,1)S(1)}, u32[]{:S(2)}, u32[]{:S(2)}) collective-permute-start(bf16[64,2048]{1,0:T(8,128)(2,1)S(1)} %fusion.34), channel_id=1, source_target_pairs={{0,2},{2,0},{4,6},{6,4},{8,10},{10,8},{12,14},{14,12},{16,18},{18,... | collective-permute-start | bytes 786440 | tf_op jit(solution)/shard_map/ppermute | solution.py:644
  313.1 16.5 %collective-permute-start.35 = (bf16[64,2048]{1,0:T(8,128)(2,1)S(1)}, bf16[64,2048]{1,0:T(8,128)(2,1)S(1)}, u32[]{:S(2)}, u32[]{:S(2)}) collective-permute-start(bf16[64,2048]{1,0:T(8,128)(2,1)S(1)} %fusion.34), channel_id=1, source_target_pairs={{0,4},{2,6},{4,0},{6,2},{8,12},{10,14},{12,8},{14,10},{16,20},{18,... | collective-permute-start | bytes 786440 | tf_op jit(solution)/shard_map/ppermute | solution.py:644
  313.3 16.3 %collective-permute-start.36 = (bf16[64,2048]{1,0:T(8,128)(2,1)S(1)}, bf16[64,2048]{1,0:T(8,128)(2,1)S(1)}, u32[]{:S(2)}, u32[]{:S(2)}) collective-permute-start(bf16[64,2048]{1,0:T(8,128)(2,1)S(1)} %fusion.34), channel_id=1, source_target_pairs={{0,6},{2,4},{4,2},{6,0},{8,14},{10,12},{12,10},{14,8},{16,22},{18,... | collective-permute-start | bytes 786440 | tf_op jit(solution)/shard_map/ppermute | solution.py:644
  354.5 52.8 %all-to-all-start.6 = ((bf16[16,512,128]{2,1,0:T(8,128)(2,1)}), bf16[16,512,128]{2,1,0:T(8,128)(2,1)S(1)}, u32[]{:S(2)}, u32[]{:S(2)}) async-start(bf16[16,512,128]{2,1,0:T(8,128)(2,1)} %add_convert_fusion), calls=%async_computation.6 | async-start | bytes 4194304 | tf_op jit(solution)/shard_map/all_to_all | solution.py:647
  375.9 35.3 %collective-permute-start.49 = (bf16[16,256,128]{2,1,0:T(8,128)(2,1)}, bf16[16,256,128]{2,1,0:T(8,128)(2,1)}, u32[]{:S(2)}, u32[]{:S(2)}) collective-permute-start(bf16[16,256,128]{2,1,0:T(8,128)(2,1)} %get-tuple-element.125), channel_id=1, source_target_pairs={{0,1},{1,0},{2,3},{3,2},{4,5},{5,4},{6,7},{7,6},{8,9},{9,8},{10,11... | collective-permute-start | bytes 3145736 | tf_op jit(solution)/shard_map/ppermute | solution.py:633
  381.6 20.4 %collective-permute-start.41 = (bf16[256,512]{1,0:T(8,128)(2,1)S(1)}, bf16[256,512]{1,0:T(8,128)(2,1)S(1)}, u32[]{:S(2)}, u32[]{:S(2)}) collective-permute-start(bf16[256,512]{1,0:T(8,128)(2,1)S(1)} %get-tuple-element.211), channel_id=1, source_target_pairs={{0,4},{2,6},{4,0},{6,2},{8,12},{10,14},{12,8},{14,10},{16,20},{18,... | collective-permute-start | bytes 786440 | tf_op jit(solution)/shard_map/ppermute | solution.py:644
  384.0 18.2 %collective-permute-start.40 = (bf16[256,512]{1,0:T(8,128)(2,1)S(1)}, bf16[256,512]{1,0:T(8,128)(2,1)S(1)}, u32[]{:S(2)}, u32[]{:S(2)}) collective-permute-start(bf16[256,512]{1,0:T(8,128)(2,1)S(1)} %get-tuple-element.209), channel_id=1, source_target_pairs={{0,2},{2,0},{4,6},{6,4},{8,10},{10,8},{12,14},{14,12},{16,18},{18,... | collective-permute-start | bytes 786440 | tf_op jit(solution)/shard_map/ppermute | solution.py:644
  416.4 28.2 %all-to-all-start.7 = ((bf16[16,256,128]{2,1,0:T(8,128)(2,1)}), bf16[16,256,128]{2,1,0:T(8,128)(2,1)}, u32[]{:S(2)}, u32[]{:S(2)}) async-start(bf16[16,256,128]{2,1,0:T(8,128)(2,1)} %add_convert_fusion.1), calls=%async_computation.7 | async-start | bytes 2097152 | tf_op jit(solution)/shard_map/all_to_all | solution.py:647
  424.3 18.8 %collective-permute-start.52 = (bf16[256,384]{1,0:T(8,128)(2,1)S(1)}, bf16[256,384]{1,0:T(8,128)(2,1)}, u32[]{:S(2)}, u32[]{:S(2)}) collective-permute-start(bf16[256,384]{1,0:T(8,128)(2,1)S(1)} %get-tuple-element.236), channel_id=1, source_target_pairs={{0,6},{2,4},{4,2},{6,0},{8,14},{10,12},{12,10},{14,8},{16,22},{18,... | collective-permute-start | bytes 589832 | tf_op jit(solution)/shard_map/ppermute | solution.py:644
  447.2 48.2 %all-to-all-start.8 = ((bf16[4,1408,128]{2,1,0:T(8,128)(2,1)}), bf16[4,1408,128]{2,1,0:T(8,128)(2,1)}, u32[]{:S(2)}, u32[]{:S(2)}) async-start(bf16[4,1408,128]{2,1,0:T(8,128)(2,1)} %slice.267), calls=%async_computation.8 | async-start | bytes 2883584 | tf_op jit(solution)/shard_map/all_to_all | solution.py:647
  471.2 23.5 %collective-permute-start.53 = (bf16[64,2048]{1,0:T(8,128)(2,1)S(1)}, bf16[64,2048]{1,0:T(8,128)(2,1)S(1)}, u32[]{:S(2)}, u32[]{:S(2)}) collective-permute-start(bf16[64,2048]{1,0:T(8,128)(2,1)S(1)} %get-tuple-element.208), channel_id=1, source_target_pairs={{0,2},{2,0},{4,6},{6,4},{8,10},{10,8},{12,14},{14,12},{16,18},{18,... | collective-permute-start | bytes 786440 | tf_op jit(solution)/shard_map/ppermute | solution.py:644
  472.6 22.2 %collective-permute-start.54 = (bf16[64,2048]{1,0:T(8,128)(2,1)S(1)}, bf16[64,2048]{1,0:T(8,128)(2,1)S(1)}, u32[]{:S(2)}, u32[]{:S(2)}) collective-permute-start(bf16[64,2048]{1,0:T(8,128)(2,1)S(1)} %get-tuple-element.207), channel_id=1, source_target_pairs={{0,4},{2,6},{4,0},{6,2},{8,12},{10,14},{12,8},{14,10},{16,20},{18,... | collective-permute-start | bytes 786440 | tf_op jit(solution)/shard_map/ppermute | solution.py:644
  473.1 22.3 %collective-permute-start.55 = (bf16[64,2048]{1,0:T(8,128)(2,1)S(1)}, bf16[64,2048]{1,0:T(8,128)(2,1)S(1)}, u32[]{:S(2)}, u32[]{:S(2)}) collective-permute-start(bf16[64,2048]{1,0:T(8,128)(2,1)S(1)} %get-tuple-element.206), channel_id=1, source_target_pairs={{0,6},{2,4},{4,2},{6,0},{8,14},{10,12},{12,10},{14,8},{16,22},{18,... | collective-permute-start | bytes 786440 | tf_op jit(solution)/shard_map/ppermute | solution.py:644
  478.1 16.6 %collective-permute-start.57 = (bf16[768,128]{1,0:T(8,128)(2,1)S(1)}, bf16[768,128]{1,0:T(8,128)(2,1)S(1)}, u32[]{:S(2)}, u32[]{:S(2)}) collective-permute-start(bf16[768,128]{1,0:T(8,128)(2,1)S(1)} %get-tuple-element.235), channel_id=1, source_target_pairs={{0,4},{2,6},{4,0},{6,2},{8,12},{10,14},{12,8},{14,10},{16,20},{18,... | collective-permute-start | bytes 589832 | tf_op jit(solution)/shard_map/ppermute | solution.py:644
  500.3 34.6 %collective-permute-start.37 = (bf16[64,2048]{1,0:T(8,128)(2,1)}, bf16[64,2048]{1,0:T(8,128)(2,1)}, u32[]{:S(2)}, u32[]{:S(2)}) collective-permute-start(bf16[64,2048]{1,0:T(8,128)(2,1)} %get-tuple-element.250), channel_id=1, source_target_pairs={{0,1},{1,0},{2,3},{3,2},{4,5},{5,4},{6,7},{7,6},{8,9},{9,8},{10,11... | collective-permute-start | bytes 786440 | tf_op jit(solution)/shard_map/ppermute | solution.py:633
  500.3 36.6 %collective-permute-start.59 = (bf16[64,2048]{1,0:T(8,128)(2,1)}, bf16[64,2048]{1,0:T(8,128)(2,1)}, u32[]{:S(2)}, u32[]{:S(2)}) collective-permute-start(bf16[64,2048]{1,0:T(8,128)(2,1)} %get-tuple-element.249), channel_id=1, source_target_pairs={{0,1},{1,0},{2,3},{3,2},{4,5},{5,4},{6,7},{7,6},{8,9},{9,8},{10,11... | collective-permute-start | bytes 786440 | tf_op jit(solution)/shard_map/ppermute | solution.py:633
  525.7 23.3 %all-to-all-start.9 = ((bf16[4,704,128]{2,1,0:T(8,128)(2,1)}), bf16[4,704,128]{2,1,0:T(8,128)(2,1)S(1)}, u32[]{:S(2)}, u32[]{:S(2)}) async-start(bf16[4,704,128]{2,1,0:T(8,128)(2,1)} %slice.268), calls=%async_computation.9 | async-start | bytes 1441792 | tf_op jit(solution)/shard_map/all_to_all | solution.py:647
  (100 other events, 803.7 us)
Sparse Core Ops, SparseCore 0:
  110.3 100.1 all-gather.2
  337.9 106.2 reduce-scatter.3

commit v6 on v5

--- a/solution.py
+++ b/solution.py
@@ -14,6 +14,9 @@
 HEAD = 256
 SQUARE = 4
 VMEM_LIMIT = 56 * 1024 * 1024
+MLP_LIMIT = 26 * 1024 * 1024
+ATTEND_LIMIT = 32 * 1024 * 1024
+GRADS_LIMIT = 16 * 1024 * 1024
 BF16 = jnp.bfloat16
 F32 = jnp.float32
 
@@ -62,6 +65,7 @@
 VMEM = pl.BlockSpec(memory_space=pltpu.VMEM)
 SMEM = pl.BlockSpec(memory_space=pltpu.SMEM)
 HBM = pl.BlockSpec(memory_space=pl.ANY)
+FAR = pl.BlockSpec(memory_space=pltpu.HBM)
 
 
 def shape(dims, dtype=BF16):
@@ -114,21 +118,20 @@
     corner = at_ref[1]
     rows = kv_ref.shape[0]
     rank_share, kv_share = hat_ref.shape[1] // SQUARE, 2 * HEAD // SQUARE
+    own = pl.ds(pl.multiple_of(corner * rows, rows), rows)
     for m, part in enumerate(parts):
         b = corner ^ m
         columns = pl.ds(pl.multiple_of(b * rank_share, rank_share), rank_share)
-        for i in range(SQUARE):
-            source = slice((i ^ m) * rows, (i ^ m) * rows + rows)
-            hat_ref[i * rows : (i + 1) * rows, columns] = part[source, :rank_share].astype(F32)
+        hat_ref[:, columns] = part[:, :rank_share].astype(F32)
         columns = pl.ds(pl.multiple_of(b * kv_share, kv_share), kv_share)
-        kv_sum[:, columns] = part[m * rows : (m + 1) * rows, rank_share:].astype(F32)
+        kv_sum[:, columns] = part[own, rank_share:].astype(F32)
     q_lat = hat_ref[...]
     inverse = inverse_rms(q_lat)
     hat = q_lat * inverse
     hat_ref[...] = hat
     low_ref[...] = hat.astype(BF16)
     inverse_ref[...] = inverse
-    kv_ref[:, :HEAD] = rotate(kv_sum[:, :HEAD], cos_ref[:rows], sin_ref[:rows]).astype(BF16)
+    kv_ref[:, :HEAD] = rotate(kv_sum[:, :HEAD], cos_ref[own, :], sin_ref[own, :]).astype(BF16)
     kv_ref[:, HEAD:] = kv_sum[:, HEAD:].astype(BF16)
 
 
@@ -152,67 +155,52 @@
     )(at, cosine, sine, *parts)
 
 
-def head_copies(refs, wq, wo, sems):
-    copies = []
-    for i, target in enumerate((wq, wo)):
-        size = target.shape[2]
-        for c in range(2):
-            source = refs[2 * i + c]
-            if source.shape[1] > size:
-                skipped = 0 if i == 0 else source.shape[1] - size
-                source = source.at[:, pl.ds(skipped, size)]
-            copies.append(pltpu.make_async_copy(source, target.at[c], sems.at[i, c]))
-    return copies
-
-
-def head_q(wq, c, h, pair):
-    size = wq.shape[2] // (2 * pair)
-    halves = [wq[c, :, (2 * h + i) * size : (2 * h + i + 1) * size, :] for i in range(2)]
+def head_q(weights, c, h, pair):
+    ref = weights[c]
+    size = (ref.shape[1] if len(weights) == 4 else ref.shape[1] - pair * HEAD) // (2 * pair)
+    halves = [ref[:, (2 * h + i) * size : (2 * h + i + 1) * size, :] for i in range(2)]
     return jnp.concatenate([half.reshape(-1, HEAD // 2) for half in halves], axis=1)
 
 
-def head_out(wo, c, h):
+def head_out(weights, c, h, pair):
+    ref = weights[len(weights) - 2 + c]
+    first = ref.shape[1] - pair * HEAD + h * HEAD
     return jnp.concatenate(
-        [wo[c, tile, h * HEAD : (h + 1) * HEAD, :] for tile in range(wo.shape[1])], axis=1
-    )
-
-
-def attend_kernel(
-    lat_ref, cos_ref, sin_ref, natural_ref, start_ref, kv_ref, keys_ref, *refs
-):
-    weights, (q_ref, o_ref, lse_ref, part_ref, wq, wo, sems) = refs[:4], refs[4:]
-
-    @pl.when(pl.program_id(0) == 0)
-    def _():
-        copies = head_copies(weights, wq, wo, sems)
-        for copy in copies:
-            copy.start()
-        for copy in copies:
-            copy.wait()
-
+        [ref[tile, first : first + HEAD, :] for tile in range(ref.shape[0])], axis=1
+    )
+
+
+def attend_kernel(pair, count, lat_ref, cos_ref, sin_ref, places_ref, kv_ref, keys_ref, *refs):
+    weights, (saved_ref, part_ref, kept, sems) = refs[:count], refs[count:]
     keys = keys_ref[...]
-    allowed = (keys <= natural_ref[...]) & (keys >= start_ref[...])
-    pair = wo.shape[2] // HEAD
-    part = None
+    rows = part_ref.shape[0]
+    here = pl.ds(pl.program_id(0) * rows, rows)
+    allowed = (keys <= places_ref[:, 0:1]) & (keys >= places_ref[:, 1:2])
+    part, copies = None, []
     for c in range(2):
         for h in range(pair):
-            q_pre = matmul(lat_ref[...], head_q(wq, c, h, pair))
+            head = c * pair + h
+            q_pre = matmul(lat_ref[...], head_q(weights, c, h, pair))
             q = rotate(q_pre, cos_ref[...], sin_ref[...]).astype(BF16)
             q = (q.astype(F32) * HEAD**-0.5).astype(BF16)
             scores = jnp.where(allowed, times_transposed(q, kv_ref[:, :HEAD]), MASKED)
             top = jnp.max(scores, axis=-1, keepdims=True)
             terms = jnp.exp(scores - top)
             total = jnp.sum(terms, axis=-1, keepdims=True)
-            mix = matmul(terms.astype(BF16), kv_ref[:, HEAD:]) / total
-            q_ref[c * pair + h] = q
-            o_ref[c * pair + h] = mix
-            lse_ref[c * pair + h] = top + jnp.log(total)
-            share = matmul(mix.astype(BF16), head_out(wo, c, h))
+            mix = (matmul(terms.astype(BF16), kv_ref[:, HEAD:]) / total).astype(BF16)
+            kept[head, :, :HEAD] = q
+            kept[head, :, HEAD:] = mix
+            copy = pltpu.make_async_copy(kept.at[head], saved_ref.at[head, here], sems.at[head])
+            copy.start()
+            copies.append(copy)
+            share = matmul(mix, head_out(weights, c, h, pair))
             part = share if part is None else part + share
     part_ref[...] = part.astype(BF16)
-
-
-def attend_specs(block, rank, count):
+    for copy in copies:
+        copy.wait()
+
+
+def attend_specs(block, rank, count, weights):
     row = lambda size: pl.BlockSpec((block, size), lambda i: (i, 0))
     whole = lambda dims: pl.BlockSpec(dims, lambda i: (0,) * len(dims))
     half = HEAD // 2
@@ -220,42 +208,27 @@
         row(rank),
         row(half),
         row(half),
-        row(1),
-        row(1),
+        row(128),
         whole((count, 2 * HEAD)),
         whole((1, count)),
-    ] + [HBM] * 4
+    ] + [whole(weight.shape) for weight in weights]
 
 
 def attend(lat, tables, kv, keys, weights, pair, block):
-    places, tiles, lanes = weights[0].shape[0], weights[2].shape[0], 128
     rows, rank = lat.shape
     count = kv.shape[0]
-    q_rows = 2 * pair * rank // places
-    heads, width = 2 * pair, tiles * lanes
-    by_head = lambda size: pl.BlockSpec((heads, block, size), lambda i: (0, i, 0))
+    heads, width = 2 * pair, weights[-1].shape[0] * 128
     return pl.pallas_call(
-        attend_kernel,
+        functools.partial(attend_kernel, pair, len(weights)),
         grid=(rows // block,),
-        in_specs=attend_specs(block, rank, count),
-        out_specs=[
-            by_head(HEAD),
-            by_head(HEAD),
-            by_head(1),
-            pl.BlockSpec((block, width), lambda i: (i, 0)),
+        in_specs=attend_specs(block, rank, count, weights),
+        out_specs=[FAR, pl.BlockSpec((block, width), lambda i: (i, 0))],
+        out_shape=[shape((heads, rows, 2 * HEAD)), shape((rows, width))],
+        scratch_shapes=[
+            pltpu.VMEM((heads, block, 2 * HEAD), BF16),
+            pltpu.SemaphoreType.DMA((heads,)),
         ],
-        out_shape=[
-            shape((heads, rows, HEAD)),
-            shape((heads, rows, HEAD), F32),
-            shape((heads, rows, 1), F32),
-            shape((rows, width)),
-        ],
-        scratch_shapes=[
-            pltpu.VMEM((2, places, q_rows, HEAD // 2), BF16),
-            pltpu.VMEM((2, tiles, pair * HEAD, lanes), BF16),
-            pltpu.SemaphoreType.DMA((2, 2)),
-        ],
-        compiler_params=params(),
+        compiler_params=params(ATTEND_LIMIT if rows == block else VMEM_LIMIT),
         cost_estimate=pl.CostEstimate(
             flops=2 * rows * heads * HEAD * (2 * count + rank + width),
             bytes_accessed=4 * count * HEAD + 2 * heads * HEAD * (rank + width),
@@ -266,48 +239,41 @@
 
 
 def attend_back_kernel(
-    at_ref, lat_ref, cos_ref, sin_ref, natural_ref, start_ref, kv_ref, keys_ref, *refs
+    pair, count, at_ref, lat_ref, cos_ref, sin_ref, places_ref, kv_ref, keys_ref, *refs
 ):
-    weights, refs = refs[:4], refs[4:]
-    q_ref, o_ref, lse_ref, d_attn_ref = refs[:4]
-    grads_q, refs = refs[4:6], refs[6:]
-    d_lat_ref, near_ref, far_ref, wq, wo, sems, d_kv_sum, d_lat_sum = refs[:8]
-    sums = refs[8:]
-    q_rows = wq.shape[2]
-    pair = wo.shape[2] // HEAD
+    weights, refs = refs[:count], refs[count:]
+    saved_ref, d_attn_ref = refs[:2]
+    grads_q, d_lat_refs, (near_ref, far_ref, d_kv_sum, d_lat_sum) = refs[2:4], refs[4:8], refs[8:12]
+    sums = refs[12:]
     step, steps = pl.program_id(0), pl.num_programs(0)
     corner = at_ref[1]
 
     @pl.when(step == 0)
     def _():
-        copies = head_copies(weights, wq, wo, sems)
-        for copy in copies:
-            copy.start()
         d_kv_sum[...] = jnp.zeros_like(d_kv_sum)
         for total in sums:
             total[...] = jnp.zeros_like(total)
-        for copy in copies:
-            copy.wait()
 
     def store(c, h, grad_q):
-        size = q_rows // (2 * pair)
+        size = grads_q[c].shape[1] // (2 * pair)
         for i in range(2):
             here = slice((2 * h + i) * size, (2 * h + i + 1) * size)
             tile = grad_q[:, i * 128 : (i + 1) * 128].astype(BF16)
             grads_q[c][:, here, :] = tile.reshape(-1, size, 128)
 
     keys = keys_ref[...]
-    allowed = (keys <= natural_ref[...]) & (keys >= start_ref[...])
+    allowed = (keys <= places_ref[:, 0:1]) & (keys >= places_ref[:, 1:2])
     d_attn, lat = d_attn_ref[...], lat_ref[...]
     d_lat = None
     for c in range(2):
         for h in range(pair):
-            q, mix, lse = q_ref[c * pair + h], o_ref[c * pair + h], lse_ref[c * pair + h]
-            w_q, w_out = head_q(wq, c, h, pair), head_out(wo, c, h)
+            q, mix = saved_ref[c * pair + h, :, :HEAD], saved_ref[c * pair + h, :, HEAD:]
+            w_q, w_out = head_q(weights, c, h, pair), head_out(weights, c, h, pair)
             d_o = times_transposed(d_attn, w_out).astype(BF16)
-            delta = jnp.sum(d_o.astype(F32) * mix, axis=-1, keepdims=True)
-            scores = times_transposed(q, kv_ref[:, :HEAD])
-            probs = jnp.exp(jnp.where(allowed, scores - lse, MASKED))
+            delta = jnp.sum(d_o.astype(F32) * mix.astype(F32), axis=-1, keepdims=True)
+            scores = jnp.where(allowed, times_transposed(q, kv_ref[:, :HEAD]), MASKED)
+            terms = jnp.exp(scores - jnp.max(scores, axis=-1, keepdims=True))
+            probs = terms * (1.0 / jnp.sum(terms, axis=-1, keepdims=True))
             d_probs = times_transposed(d_o, kv_ref[:, HEAD:])
             d_scores = (probs * (d_probs - delta)).astype(BF16)
             d_query = matmul(d_scores, kv_ref[:, :HEAD]) * HEAD**-0.5
@@ -335,11 +301,10 @@
     d_lat_sum[...] = d_lat
     share = d_lat.shape[1] // SQUARE
     dot = jnp.sum(d_lat * lat.astype(F32), axis=-1, keepdims=True)
-    for m in range(SQUARE):
-        b = corner ^ m
-        columns = pl.ds(pl.multiple_of(b * share, share), share)
-        d_lat_ref[m, :, :share] = d_lat_sum[:, columns].astype(BF16)
-        d_lat_ref[m, :, share:] = jnp.broadcast_to(dot, (d_lat.shape[0], 128)).astype(BF16)
+    for m, d_lat_ref in enumerate(d_lat_refs):
+        columns = pl.ds(pl.multiple_of((corner ^ m) * share, share), share)
+        d_lat_ref[:, :share] = d_lat_sum[:, columns].astype(BF16)
+        d_lat_ref[:, share:] = jnp.broadcast_to(dot, (d_lat.shape[0], 128)).astype(BF16)
 
     @pl.when(step == steps - 1)
     def _():
@@ -348,101 +313,94 @@
         far_ref[...] = d_kv_sum[size:, :].astype(BF16)
 
 
-def attend_back(at, lat, tables, kv, keys, weights, q, o, lse, d_attn, pair, block):
-    places, tiles, lanes = weights[0].shape[0], weights[2].shape[0], 128
+def attend_back(at, lat, tables, kv, keys, weights, saved, d_attn, pair, block):
     rows, rank = lat.shape
     count = kv.shape[0]
-    q_rows = 2 * pair * rank // places
-    heads, width = 2 * pair, tiles * lanes
-    by_head = lambda size: pl.BlockSpec((heads, block, size), lambda i: (0, i, 0))
+    heads, width = 2 * pair, weights[-1].shape[0] * 128
+    places = weights[0].shape[0]
+    row = lambda size: pl.BlockSpec((block, size), lambda i: (i, 0))
     whole = lambda dims: pl.BlockSpec(dims, lambda i: (0,) * len(dims))
-    grad_dims = [(places, q_rows, HEAD // 2)] * 2
-    d_lat_dims = (SQUARE, rows, rank // SQUARE + 128)
-    sums = []
-    if rows != block:
-        sums = [pltpu.VMEM((2, pair, rank, HEAD), F32)]
+    grad_dims = (places, 2 * pair * rank // places, HEAD // 2)
+    d_lat_size = rank // SQUARE + 128
+    kv_dims = (count // 2, 2 * HEAD)
+    sums = [pltpu.VMEM((2, pair, rank, HEAD), F32)] if rows != block else []
     return pl.pallas_call(
-        attend_back_kernel,
+        functools.partial(attend_back_kernel, pair, len(weights)),
         grid=(rows // block,),
         in_specs=[SMEM]
-        + attend_specs(block, rank, count)
-        + [by_head(HEAD), by_head(HEAD), by_head(1), pl.BlockSpec((block, width), lambda i: (i, 0))],
-        out_specs=[
-            *[whole(dims) for dims in grad_dims],
-            pl.BlockSpec((SQUARE, block, d_lat_dims[2]), lambda i: (0, i, 0)),
-            whole((count // 2, 2 * HEAD)),
-            whole((count // 2, 2 * HEAD)),
-        ],
-        out_shape=[
-            *[shape(dims) for dims in grad_dims],
-            shape(d_lat_dims),
-            shape((count // 2, 2 * HEAD), BF16 if sums else F32),
-            shape((count // 2, 2 * HEAD)),
-        ],
+        + attend_specs(block, rank, count, weights)
+        + [pl.BlockSpec((heads, block, 2 * HEAD), lambda i: (0, i, 0)), row(width)],
+        out_specs=[whole(grad_dims)] * 2 + [row(d_lat_size)] * SQUARE + [whole(kv_dims)] * 2,
+        out_shape=[shape(grad_dims)] * 2
+        + [shape((rows, d_lat_size))] * SQUARE
+        + [shape(kv_dims, BF16 if sums else F32), shape(kv_dims)],
         scratch_shapes=[
-            pltpu.VMEM((2, places, q_rows, HEAD // 2), BF16),
-            pltpu.VMEM((2, tiles, pair * HEAD, lanes), BF16),
-            pltpu.SemaphoreType.DMA((2, 2)),
             pltpu.VMEM((count, 2 * HEAD), F32),
             pltpu.VMEM((block, rank), F32),
         ]
         + sums,
         compiler_params=params(VMEM_LIMIT + len(sums) * 2**22),
         cost_estimate=pl.CostEstimate(
-            flops=2 * rows * heads * HEAD * (5 * count + 2 * rank + 2 * width),
+            flops=2 * rows * heads * HEAD * (5 * count + 2 * rank + width),
             bytes_accessed=12 * count * HEAD + 4 * heads * HEAD * (rank + width),
             transcendentals=rows * heads * count,
         ),
         name="attend_back",
-    )(at, lat, *tables, kv, keys, *weights, q, o, lse, d_attn)
-
-
-def out_grads_kernel(mix_ref, d_attn_ref, near_ref, far_ref):
-    d_attn = d_attn_ref[...]
-    pair = mix_ref.shape[0] // 2
-    for c, out_ref in enumerate((near_ref, far_ref)):
-        for h in range(pair):
-            grad = contract_rows(mix_ref[c * pair + h], d_attn)
-            for tile in range(out_ref.shape[0]):
-                out_ref[tile, h * HEAD : (h + 1) * HEAD, :] = grad[
-                    :, tile * 128 : (tile + 1) * 128
-                ].astype(BF16)
-
-
-def out_grads(mix, d_attn, pair):
+    )(at, lat, *tables, kv, keys, *weights, saved, d_attn)
+
+
+def out_grads_kernel(mix_ref, d_attn_ref, *refs):
+    more, out_ref = refs[:-1], refs[-1]
+    for h in range(mix_ref.shape[0]):
+        grad = contract_rows(mix_ref[h], d_attn_ref[...])
+        here = slice(h * HEAD, (h + 1) * HEAD)
+        for tile in range(out_ref.shape[0]):
+            value = grad[:, tile * 128 : (tile + 1) * 128]
+            if more:
+                value = value + more[0][tile, here, :].astype(F32)
+            out_ref[tile, here, :] = value.astype(BF16)
+
+
+def out_grads(saved, side, d_attn, *received):
     rows, width = d_attn.shape
+    pair = saved.shape[0] // 2
     dims = (width // 128, pair * HEAD, 128)
+    whole = lambda dims: pl.BlockSpec(dims, lambda i: (0,) * len(dims))
     return pl.pallas_call(
         out_grads_kernel,
-        in_specs=[VMEM, VMEM],
-        out_specs=[VMEM, VMEM],
-        out_shape=[shape(dims), shape(dims)],
-        compiler_params=params(),
+        grid=(1,),
+        in_specs=[pl.BlockSpec((pair, rows, HEAD), lambda i: (side, 0, 1)), whole((rows, width))]
+        + [whole(dims)] * len(received),
+        out_specs=whole(dims),
+        out_shape=shape(dims),
+        compiler_params=params(GRADS_LIMIT),
         cost_estimate=pl.CostEstimate(
-            flops=4 * rows * pair * HEAD * width, bytes_accessed=8 * pair * HEAD * width, transcendentals=0
+            flops=2 * rows * pair * HEAD * width, bytes_accessed=4 * pair * HEAD * width, transcendentals=0
         ),
         name="out_grads",
-    )(mix, d_attn)
-
-
-def latent_back_kernel(layers, at_ref, hat_ref, inverse_ref, d_kv_ref, x_ref, w_ref, *refs):
-    parts = refs[:SQUARE]
-    d_x_ref, near_ref, far_ref, d_sum = refs[SQUARE:]
+    )(saved, d_attn, *received)
+
+
+def latent_back_kernel(layers, at_ref, hat_ref, inverse_ref, x_ref, w_ref, *refs):
+    parts, d_kv_refs, d_x_refs = (refs[i * SQUARE : (i + 1) * SQUARE] for i in range(3))
+    near_ref, far_ref, d_sum, d_kv_sum, d_x_sum = refs[3 * SQUARE :]
     layer, corner, core = at_ref[0], at_ref[1], at_ref[2]
     count, width = x_ref.shape
     rows = count // SQUARE
     share = w_ref.shape[-1]
     rank_share = hat_ref.shape[1] // SQUARE
-    for i in range(SQUARE):
-        d_sum[i * rows : (i + 1) * rows] = sum(
-            part[(i ^ m) * rows : (i ^ m) * rows + rows].astype(F32) for m, part in enumerate(parts)
-        )
+    places = [pl.ds(pl.multiple_of((corner ^ m) * rows, rows), rows) for m in range(SQUARE)]
+    d_sum[...] = sum(part[...].astype(F32) for part in parts)
+    for place, d_kv_ref in zip(places, d_kv_refs):
+        d_kv_sum[place, :] = d_kv_ref[...]
     columns = pl.ds(pl.multiple_of(corner * rank_share, rank_share), rank_share)
     dot = d_sum[:, rank_share : rank_share + 1] * (1.0 / hat_ref.shape[1])
     d_lat = inverse_ref[...] * (d_sum[:, :rank_share] - hat_ref[:, columns] * dot)
-    d_down = jnp.concatenate([d_lat.astype(BF16), d_kv_ref[...]], axis=1)
+    d_down = jnp.concatenate([d_lat.astype(BF16), d_kv_sum[...]], axis=1)
     weight = w_ref[...].reshape(width, share)
-    d_x_ref[...] = times_transposed(d_down, weight).astype(BF16)
+    d_x_sum[...] = times_transposed(d_down, weight).astype(BF16)
+    for place, d_x_ref in zip(places, d_x_refs):
+        d_x_ref[...] = d_x_sum[place, :]
     grad = contract_rows(x_ref[...], d_down)
     grad = grad.reshape(layers, SQUARE, 2, near_ref.shape[2], share)
     low, high = grad[:, :, 0], grad[:, :, 1]
@@ -461,16 +419,20 @@
     dims = (layers, SQUARE, lane_rows, share)
     return pl.pallas_call(
         functools.partial(latent_back_kernel, layers),
-        in_specs=[SMEM] + [VMEM] * (5 + SQUARE),
-        out_specs=[VMEM] * 3,
-        out_shape=[shape((count, width)), shape(dims, F32), shape(dims)],
-        scratch_shapes=[pltpu.VMEM(parts[0].shape, F32)],
+        in_specs=[SMEM] + [VMEM] * (4 + 2 * SQUARE),
+        out_specs=[VMEM] * (SQUARE + 2),
+        out_shape=[shape((count // SQUARE, width))] * SQUARE + [shape(dims, F32), shape(dims)],
+        scratch_shapes=[
+            pltpu.VMEM(parts[0].shape, F32),
+            pltpu.VMEM((count, d_kv[0].shape[1]), BF16),
+            pltpu.VMEM((count, width), BF16),
+        ],
         compiler_params=params(),
         cost_estimate=pl.CostEstimate(
             flops=4 * count * width * share, bytes_accessed=10 * width * share, transcendentals=0
         ),
         name="latent_back",
-    )(at, hat, inverse, d_kv, x, weight, *parts)
+    )(at, hat, inverse, x, weight, *parts, *d_kv)
 
 
 def chunk(ref, q, tiles):
@@ -478,68 +440,79 @@
     return jnp.concatenate([ref[:, c : c + 128] for c in columns], axis=1)
 
 
-def mlp_kernel(h_ref, cot_ref, *refs):
-    d_h_ref, out_ref, act_near_ref, act_far_ref, weights, sems = refs[2:]
-    tiles, units = weights.shape[3:5]
-    copies = [
-        [
-            pltpu.make_async_copy(
-                refs[c].at[:, :, pl.ds(kind * units, units)], weights.at[c, kind], sems.at[c, kind]
-            )
-            for kind in range(3)
-        ]
-        for c in range(2)
-    ]
-    for one in copies:
-        for copy in one:
-            copy.start()
-
-    def weight(c, kind, q):
-        return jnp.concatenate([weights[c, kind, q, t] for t in range(tiles)], axis=1)
-
-    sides = (act_near_ref, act_far_ref)
-    for c, acts in enumerate(sides):
-
-        def product(value_ref, kind):
-            copies[c][kind].wait()
-            return sum(
-                times_transposed(chunk(value_ref, q, tiles), weight(c, kind, q)) for q in range(SQUARE)
-            )
-
-        gate_act, up_proj, d_act = product(h_ref, 0), product(h_ref, 1), product(cot_ref, 2)
+def mlp_kernel(
+    h_ref,
+    cot_ref,
+    near_ref,
+    far_ref,
+    d_h_hbm,
+    out_hbm,
+    act_near_ref,
+    act_far_ref,
+    turned,
+    d_h_ref,
+    out_ref,
+    sems,
+):
+    tiles = near_ref.shape[1]
+    units = act_near_ref.shape[1]
+    for q in range(SQUARE):
+        turned[0, q] = chunk(h_ref, q, tiles).T
+        turned[1, q] = chunk(cot_ref, q, tiles).T
+
+    def weight(side, kind, q):
+        here = slice(kind * units, (kind + 1) * units)
+        return jnp.concatenate([side[q, t, here, :] for t in range(tiles)], axis=1)
+
+    sides = ((near_ref, act_near_ref), (far_ref, act_far_ref))
+    for side, acts in sides:
+
+        def product(which, kind):
+            return sum(matmul(weight(side, kind, q), turned[which, q]) for q in range(SQUARE))
+
+        gate_act, up_proj, d_act = product(0, 0), product(0, 1), product(1, 2)
         sigmoid_gate = 1.0 / (1.0 + jnp.exp(-gate_act))
         silu_gate = gate_act * sigmoid_gate
         d_gate = d_act * up_proj * sigmoid_gate * (1.0 + gate_act * (1.0 - sigmoid_gate))
         acts[0] = d_gate.astype(BF16)
         acts[1] = (d_act * silu_gate).astype(BF16)
         acts[2] = (silu_gate * up_proj).astype(BF16)
-    for q in range(SQUARE):
-        d_h = sum(
-            matmul(acts[kind], weight(c, kind, q)) for c, acts in enumerate(sides) for kind in range(2)
-        )
-        out = sum(matmul(acts[2], weight(c, 2, q)) for c, acts in enumerate(sides))
-        for t in range(tiles):
-            here = slice((t * SQUARE + q) * 128, (t * SQUARE + q + 1) * 128)
-            d_h_ref[:, here] = d_h[:, t * 128 : (t + 1) * 128].astype(BF16)
-            out_ref[:, here] = out[:, t * 128 : (t + 1) * 128].astype(BF16)
+    straight = [[acts[kind].T for kind in range(3)] for _, acts in sides]
+    copies = []
+    for i, (first, count, value_ref, hbm) in enumerate(
+        ((0, 2, d_h_ref, d_h_hbm), (2, 1, out_ref, out_hbm))
+    ):
+        for q in range(SQUARE):
+            value = sum(
+                matmul(straight[c][kind], weight(sides[c][0], kind, q))
+                for c in range(2)
+                for kind in range(first, first + count)
+            )
+            for t in range(tiles):
+                here = slice((t * SQUARE + q) * 128, (t * SQUARE + q + 1) * 128)
+                value_ref[:, here] = value[:, t * 128 : (t + 1) * 128].astype(BF16)
+        copies.append(pltpu.make_async_copy(value_ref, hbm, sems.at[i]))
+        copies[-1].start()
+    for copy in copies:
+        copy.wait()
 
 
 def mlp(h, cot, near, far):
     rows, width = h.shape
-    _, tiles, units, lanes = near.shape
-    units = units // 3
-    low = shape((rows, width))
-    acts = shape((3, rows, units))
+    units = near.shape[2] // 3
+    low, acts = shape((rows, width)), shape((3, units, rows))
     return pl.pallas_call(
         mlp_kernel,
-        in_specs=[VMEM, VMEM, HBM, HBM],
-        out_specs=[VMEM] * 4,
+        in_specs=[VMEM] * 4,
+        out_specs=[FAR, FAR, VMEM, VMEM],
         out_shape=[low, low, acts, acts],
         scratch_shapes=[
-            pltpu.VMEM((2, 3, SQUARE, tiles, units, lanes), BF16),
-            pltpu.SemaphoreType.DMA((2, 3)),
+            pltpu.VMEM((2, SQUARE, width // SQUARE, rows), BF16),
+            pltpu.VMEM((rows, width), BF16),
+            pltpu.VMEM((rows, width), BF16),
+            pltpu.SemaphoreType.DMA((2,)),
         ],
-        compiler_params=params(),
+        compiler_params=params(MLP_LIMIT if rows <= 256 else VMEM_LIMIT),
         cost_estimate=pl.CostEstimate(
             flops=24 * rows * width * units,
             bytes_accessed=12 * width * units + 8 * rows * width,
@@ -554,7 +527,7 @@
     acts = acts_ref[0]
     tiles = out_ref.shape[1]
     for q in range(SQUARE):
-        grad = contract_rows(acts, chunk(value_ref, q, tiles))
+        grad = matmul(acts, chunk(value_ref, q, tiles))
         for t in range(tiles):
             tile = grad[:, t * 128 : (t + 1) * 128]
             if more:
@@ -564,18 +537,19 @@
 
 def unit_grads(acts, kind, value, received=None, kinds=None):
     rows, width = value.shape
-    units = acts.shape[2]
+    units = acts.shape[1]
     tiles = width // SQUARE // 128
     whole = lambda dims: pl.BlockSpec(dims, lambda i: (0,) * len(dims))
     dims = (SQUARE, tiles, units, 128)
-    in_specs = [pl.BlockSpec((1, rows, units), lambda i: (kind, 0, 0)), whole((rows, width))]
+    in_specs = [pl.BlockSpec((1, units, rows), lambda i: (kind, 0, 0)), whole((rows, width))]
     args, aliases, body = [acts, value], {}, unit_grads_kernel
     out_specs, out_dims = whole(dims), dims
     if received is not None:
         args.append(received)
         in_specs.append(whole(dims))
-        out_specs = pl.BlockSpec(dims, lambda i: (0, 0, kind, 0))
-        out_dims = (SQUARE, tiles, 3 * units, 128)
+        if kind < 2:
+            out_specs = pl.BlockSpec(dims, lambda i: (0, 0, kind, 0))
+            out_dims = (SQUARE, tiles, 2 * units, 128)
     if kinds is not None:
         args.append(kinds)
         in_specs.append(HBM)
@@ -588,7 +562,7 @@
         out_specs=out_specs,
         out_shape=shape(out_dims),
         input_output_aliases=aliases,
-        compiler_params=params(),
+        compiler_params=params(GRADS_LIMIT),
         cost_estimate=pl.CostEstimate(
             flops=2 * rows * width * units, bytes_accessed=4 * width * units, transcendentals=0
         ),
@@ -717,7 +691,16 @@
     inputs = own(tokens).astype(F32)
     x_inverse = inverse_rms(inputs)
     x_hat = inputs * x_inverse
-    x_all = jnp.concatenate(square_pieces(x_hat.astype(BF16)))
+    def by_corner(pieces):
+        pieces = jnp.stack(pieces)
+        return jnp.stack(
+            [
+                lax.dynamic_index_in_dim(pieces, corner ^ q, 0, keepdims=False)
+                for q in range(SQUARE)
+            ]
+        )
+
+    x_all = by_corner(square_pieces(x_hat.astype(BF16))).reshape(-1, width)
 
     gain_rows = attn_gain.astype(F32)[:, None]
     down = jnp.concatenate([w_qdown, w_kv], axis=1)
@@ -779,42 +762,45 @@
     back_steps = jnp.arange(layers, dtype=jnp.int32)
     flips = jnp.arange(SQUARE, dtype=jnp.int32)
     owners = (((layer - back_steps) % layers) * SQUARE)[None, :] + (corner ^ flips)[:, None]
-    square_slots = block_slots[2 * owners[:, 0] + core]
+    square_slots = block_slots[2 * (layer * SQUARE + flips) + core]
     row_natural, row_start = layout(square_slots)
     owners = owners.reshape(-1)
     near_natural, _ = layout(block_slots[2 * owners + core])
     far_natural, _ = layout(block_slots[2 * owners + 1 - core])
     key_natural = jnp.concatenate([near_natural, far_natural])[None, :]
     cosine, sine = angles(row_natural - row_start)
-    tables = (cosine, sine, row_natural[:, None], row_start[:, None])
+    lane = jnp.arange(128, dtype=jnp.int32)[None, :]
+    tables = (cosine, sine, jnp.where(lane == 0, row_natural[:, None], row_start[:, None]))
 
     x_all = after(x_all, head_own)
     part, down_here = project(at, x_all, down_near, down_far)
     lat_hat, lat_low, lat_inverse, kv_own = latent(at, cosine, sine, square_pieces(part), rank)
     mlp_layer = line_exchange(after(mlp_send, *down_near[1:]))
-    mlp_layer, kv_own = together(mlp_layer, kv_own)
+    head_copies = jnp.tile(head_own, (layers, 1, 1))
+    mlp_layer, kv_own, head_copies = together(mlp_layer, kv_own, head_copies)
     kv_line = jnp.concatenate(line_pieces(kv_own))
     mlp_near = lax.all_gather(tiled(mlp_layer), "seq", axis_index_groups=square_groups)
 
-    head_near = line_exchange(jnp.tile(after(head_own, mlp_layer, kv_line), (layers, 1, 1)))
+    head_near = line_exchange(after(head_copies, kv_line))
     kv_near = jnp.concatenate(square_pieces(kv_line))
     kv_all = jnp.concatenate([kv_near, across(kv_near)])
     head_near, kv_all = together(head_near, kv_all)
     head_far = across(head_near)
     if lanes == 128:
-        head_weights = (head_near, head_far, head_near, head_far)
+        head_weights = (head_near, head_far)
     else:
         head_weights = tuple(
             side[:, :qup_size].reshape(chips, -1, half) for side in (head_near, head_far)
         ) + tuple(tiled(side[:, qup_size:]) for side in (head_near, head_far))
 
     block = max(32, min(SQUARE * rows, 2**30 // kv_all.shape[0] ** 2))
-    queries, attn_mix, log_total, attn_part = attend(
+    saved, attn_part = attend(
         lat_low, tables, kv_all, key_natural, head_weights, pair, block
     )
     mlp_near, attn_part = together(mlp_near, attn_part)
     mlp_far = across(mlp_near)
-    hidden = inputs + square_sum(attn_part.reshape(SQUARE, rows, width))
+    attn_blocks = square_exchange(attn_part.reshape(SQUARE, rows, width))
+    hidden = inputs + jnp.sum(attn_blocks.astype(F32), axis=0)
     h_inverse = inverse_rms(hidden)
     h_hat = hidden * h_inverse
     h_low = h_hat.astype(BF16)
@@ -823,7 +809,7 @@
 
     d_h_part, mlp_part, acts_near, acts_far = mlp(h_all, cot_all, mlp_near, mlp_far)
     def line_blocks(value):
-        return line_exchange(value.reshape(layers, rows, width))
+        return line_exchange(value.reshape(layers, rows, -1))
 
     def line_total(blocks):
         return unarranged(jnp.sum(blocks.astype(F32), axis=0))
@@ -835,55 +821,60 @@
     d_hscaled = line_total(d_h_lines)
     d_hidden = cot_own.astype(F32) + norm_back(d_hscaled, h_hat, h_inverse)
     mlp_grads = None
-    for kind, value in kinds:
+    for kind, value in kinds[:2]:
         mlp_grads = unit_grads(acts_near, kind, value, across(far_grads[kind]), mlp_grads)
-    mlp_lines = line_blocks(after(mlp_part, d_hscaled))
-    d_attn_pieces = square_pieces(d_hidden.astype(BF16))
-    mlp_lines, mlp_grads, *d_attn_pieces = together(mlp_lines, mlp_grads, *d_attn_pieces)
-    d_attn_all = jnp.concatenate(d_attn_pieces)
-    mlp_sum = lax.psum_scatter(mlp_grads, "seq", axis_index_groups=square_groups)
-
-    mix_low = attn_mix.astype(BF16)
-    grad_out_near, grad_out_far = out_grads(mix_low, d_attn_all, pair)
-    grad_out_total = grad_out_near.astype(F32) + across(grad_out_far).astype(F32)
-    grad_out_total = untiled(grad_out_total.astype(BF16))
+    unit_sum = unit_grads(acts_near, 2, cot_all, across(far_grads[2]))
+    mlp_blocks = after(mlp_part, d_hscaled).reshape(layers, rows, width)
+    mlp_pieces = []
+    for k in range(layers):
+        block_out = lax.dynamic_index_in_dim(mlp_blocks, (layer - k) % layers, 0, keepdims=False)
+        mlp_pieces.append(along(block_out, -k) if k else block_out)
+    d_attn_all = square_exchange(jnp.tile(d_hidden.astype(BF16)[None], (SQUARE, 1, 1)))
+    mlp_grads, unit_sum, d_attn_all, *mlp_pieces = together(
+        mlp_grads, unit_sum, d_attn_all, *mlp_pieces
+    )
+    d_attn_all = d_attn_all.reshape(-1, width)
+    gate_up_sum = lax.psum_scatter(mlp_grads, "seq", axis_index_groups=square_groups)
+    unit_sum = lax.psum_scatter(unit_sum, "seq", axis_index_groups=square_groups)
+
+    received = across(out_grads(saved, 1, d_attn_all))
+    grad_out_total = untiled(out_grads(saved, 0, d_attn_all, received))
     head_out_lines = line_exchange(grad_out_total)
-    layer_out_own = (hidden + line_total(mlp_lines)).astype(BF16)
+    mlp_own = unarranged(sum(piece.astype(F32) for piece in mlp_pieces))
+    layer_out_own = (hidden + mlp_own).astype(BF16)
     layer_out = both(layer_out_own, across(layer_out_own))
-    grad_q_near, grad_q_far, d_lat_parts, d_kv_near, d_kv_far = attend_back(
+    grad_q_near, grad_q_far, *d_lat_parts, d_kv_near, d_kv_far = attend_back(
         at,
         lat_low,
         tables,
         kv_all,
         key_natural,
         head_weights,
-        queries,
-        attn_mix,
-        log_total,
+        saved,
         d_attn_all,
         pair,
         block,
     )
     d_kv_low = (d_kv_near.astype(F32) + across(d_kv_far).astype(F32)).astype(BF16)
     d_kv_line = square_sum(d_kv_low.reshape(SQUARE, layers * rows, 2 * HEAD)).astype(BF16)
-    head_out_lines, d_kv_line = together(head_out_lines, d_kv_line)
     grad_q_total = (grad_q_near.astype(F32) + across(grad_q_far).astype(F32)).astype(BF16)
+    grad_q_total = grad_q_total.reshape(chips, -1, lanes)
+    head_out_lines, d_kv_line, grad_q_total = together(head_out_lines, d_kv_line, grad_q_total)
     d_kv_own = line_sum(d_kv_line.reshape(layers, rows, 2 * HEAD))
+    own_cosine = lax.dynamic_slice_in_dim(cosine, corner * rows, rows, 0)
+    own_sine = lax.dynamic_slice_in_dim(sine, corner * rows, rows, 0)
     d_kv_own = jnp.concatenate(
-        [unrotate(d_kv_own[:, :HEAD], cosine[:rows], sine[:rows]), d_kv_own[:, HEAD:]], axis=1
+        [unrotate(d_kv_own[:, :HEAD], own_cosine, own_sine), d_kv_own[:, HEAD:]], axis=1
     ).astype(BF16)
-    head_q = line_exchange(after(grad_q_total, d_kv_own).reshape(chips, -1, lanes))
+    head_q = line_exchange(after(grad_q_total, d_kv_own))
     kv_share_of = lambda m: lax.dynamic_slice_in_dim(d_kv_own, (corner ^ m) * kv_share, kv_share, 1)
-    d_kv_share = jnp.concatenate(
-        [kv_share_of(0)] + [within(kv_share_of(m), m) for m in range(1, SQUARE)]
-    )
+    d_kv_share = [kv_share_of(0)] + [within(kv_share_of(m), m) for m in range(1, SQUARE)]
     d_lat_received = [d_lat_parts[0]] + [within(d_lat_parts[m], m) for m in range(1, SQUARE)]
     head_q, *d_lat_received = together(head_q, *d_lat_received)
 
-    d_x_part, down_grad_near, down_grad_far = latent_back(
+    *d_x_blocks, down_grad_near, down_grad_far = latent_back(
         at, lat_hat, lat_inverse, d_kv_share, x_all, down_here, d_lat_received
     )
-    d_x_blocks = d_x_part.reshape(SQUARE, rows, width)
     d_x_received = [within(d_x_blocks[m], m) for m in range(1, SQUARE)]
     down_sum = (down_grad_near + across(down_grad_far).astype(F32)).astype(BF16)
 
@@ -893,17 +884,7 @@
         ]
         return [blocks[0]] + [within(blocks[m], m) for m in range(1, SQUARE)]
 
-    def by_corner(pieces):
-        pieces = jnp.stack(pieces)
-        return jnp.stack(
-            [
-                lax.dynamic_index_in_dim(pieces, corner ^ q, 0, keepdims=False)
-                for q in range(SQUARE)
-            ]
-        )
-
-    mlp_sum = untiled(mlp_sum)
-    gate_up_back = line_exchange(after(mlp_sum[:, : 2 * units], head_q))
+    gate_up_back = line_exchange(untiled(after(gate_up_sum, head_q)))
     head_sum = jnp.concatenate(
         [
             jnp.sum(blocks.reshape(layers, SQUARE, -1, lanes).astype(F32), axis=0).astype(BF16)
@@ -912,17 +893,18 @@
         axis=1,
     )
     head_pieces = square_send(head_sum)
-    gate_up_back, *received = together(gate_up_back, *d_x_received, *head_pieces)
-    d_x_received, head_pieces = received[: SQUARE - 1], received[SQUARE - 1 :]
+    down_blocks = [down_sum[k] for k in range(layers)]
+    gate_up_back, *received = together(gate_up_back, *d_x_received, *down_blocks)
+    d_x_received, down_blocks = received[: SQUARE - 1], received[SQUARE - 1 :]
     d_xscaled = d_x_blocks[0].astype(F32) + sum(block.astype(F32) for block in d_x_received)
     token_own = (d_hidden + norm_back(d_xscaled, x_hat, x_inverse)).astype(BF16)
     token_grad = both(token_own, across(token_own))
-    down_sum = after(down_sum, gate_up_back)
-    down_pieces = [along(down_sum[k], -k) for k in range(1, layers)]
-    unit_back = line_exchange(after(mlp_sum[:, 2 * units :], *down_pieces))
-    down_line = down_sum[0].astype(F32) + sum(piece.astype(F32) for piece in down_pieces)
+    down_pieces = [along(down_blocks[k], -k) for k in range(1, layers)]
+    unit_back = line_exchange(untiled(after(unit_sum, *down_pieces)))
+    down_line = down_blocks[0].astype(F32) + sum(piece.astype(F32) for piece in down_pieces)
     down_pieces = square_send(down_line.astype(BF16))
-    unit_back, *down_pieces = together(unit_back, *down_pieces)
+    unit_back, *received = together(unit_back, *down_pieces, *head_pieces)
+    down_pieces, head_pieces = received[:SQUARE], received[SQUARE:]
     head_sum = by_corner(head_pieces)
     down_back = unshares(by_corner(down_pieces)).astype(F32)
     down_back = both(down_back, across(down_back))

time: 568 us -> 552 us (0.972)
  Pallas kernels: 92.8 us -> 74.2 us
  waiting for transfers between devices: 238 us -> 248 us
  other arithmetic: 53.2 us -> 44.7 us
    ppermute x33 -> x27, waiting for transfers between devices: 98.9 us -> 82.7 us  [within(): return lax.ppermute(value, 'seq', [(i, i ^ flip) for i in range(chips)])]
    ppermute x18 -> x21, waiting for transfers between devices: 38.8 us -> 52 us  [along(): return lax.ppermute(value, 'seq', pairs)]
    pallas_call x6, Pallas kernels: 26.2 us -> 13.3 us  [unit_grads(): pl.pallas_call(body, grid=(1,), in_specs=in_specs, out_specs=out_specs, o...]
    unnamed x122 -> x181, local copies, waits for them, and re-layouts: 17.9 us -> 29.9 us
    all_to_all x2 -> x4, waiting for transfers between devices: 2.09 us -> 13.6 us  [square_exchange(): lax.all_to_all(value, 'seq', 0, 0, axis_index_groups=square_groups, tiled...]
    all_to_all x2 -> x4, starting transfers between devices: 7.49 us -> 15.3 us  [square_exchange(): lax.all_to_all(value, 'seq', 0, 0, axis_index_groups=square_groups, tiled...]
    ppermute x33 -> x27, starting transfers between devices: 38.4 us -> 30.8 us  [within(): return lax.ppermute(value, 'seq', [(i, i ^ flip) for i in range(chips)])]
    convert_element_type x4 -> x2, other arithmetic: 6.78 us -> 1 us  [the longest x1 0.81 us: local(): x_all = by_corner(square_pieces(x_hat.astype(BF16))).reshape(-1, width)]
  transfers between devices with their start and end apart: 81 -> 80, of which waited for: 45 -> 44; matrix products, arithmetic and copies ran while one was open for 14% -> 11% of each run, Pallas kernels for 13% -> 11%
where the time goes in v6:
time: 552 us; the launch traced here: 545 us
  waiting for transfers between devices  248 us (45%)
  starting transfers between devices  114 us (21%)
  Pallas kernels  74.2 us (13%)
  local copies, waits for them, and re-layouts  48.5 us (9%)
  other arithmetic  44.7 us (8%)
  between operations  15.3 us (3%)
    all_to_all x7, waiting for transfers between devices, line_exchange(): lax.all_to_all(value, 'seq', 0, 0, axis_index_groups=lines, tiled=True)  86.8 us
    ppermute x27, waiting for transfers between devices, within(): return lax.ppermute(value, 'seq', [(i, i ^ flip) for i in range(chips)])  82.7 us
    ppermute x21, waiting for transfers between devices, along(): return lax.ppermute(value, 'seq', pairs)  52 us
    all_to_all x7, starting transfers between devices, line_exchange(): lax.all_to_all(value, 'seq', 0, 0, axis_index_groups=lines, tiled=True)  33.1 us
    ppermute x21, starting transfers between devices, along(): return lax.ppermute(value, 'seq', pairs)  31.6 us
    ppermute x27, starting transfers between devices, within(): return lax.ppermute(value, 'seq', [(i, i ^ flip) for i in range(chips)])  30.8 us
    unnamed x181, local copies, waits for them, and re-layouts  29.9 us
    pallas_call x1, Pallas kernels, attend_back(): pl.pallas_call(functools.partial(attend_back_kernel, pair, len(weights)),...  17.6 us
  transfers between devices with their start and end apart: 80, of which 44 were waited for; matrix products, arithmetic and copies ran while one was open for 11% of the time, Pallas kernels for 11%

profile of v6, /device:TPU:0, one launch (start us, length us, event | category | flops | bytes accessed | tf_op | source)
XLA Modules:
  0.0 545.1 jit_solution(13064390101944654482)
XLA Ops:
  40.5 4.6 collective-permute-done.3.refs_1_
  45.0 6.6 %collective-permute-done.4.refs_2_ = bf16[4,64,384]{2,1,0:T(8,128)(2,1)S(1)} collective-permute-done((bf16[4,64,384]{2,1,0:T(8,128)(2,1)S(1)}, bf16[4,64,384]{2,1,0:T(8,128)(2,1)S(1)}, u32[]{:S(2)}, u32[]{:S(2)}) %collective-permute-start.4) | collective-permute-done | bytes 196640 | tf_op jit(solution)/shard_map/ppermute | solution.py:615
  52.4 7.8 %all-to-all-start.1 = ((bf16[4,2112,128]{2,1,0:T(8,128)(2,1)}), bf16[4,2112,128]{2,1,0:T(8,128)(2,1)S(1)}, u32[]{:S(2)}, u32[]{:S(2)}) async-start(bf16[4,2112,128]{2,1,0:T(8,128)(2,1)} %pad_maximum_fusion), calls=%async_computation.1 | async-start | bytes 4325376 | tf_op jit(solution)/shard_map/all_to_all | solution.py:621
  70.6 5.0 collective-permute-done.7
  80.4 4.2 project.1
  100.7 8.8 %all-to-all-done.1 = bf16[4,2112,128]{2,1,0:T(8,128)(2,1)S(1)} async-done(((bf16[4,2112,128]{2,1,0:T(8,128)(2,1)}), bf16[4,2112,128]{2,1,0:T(8,128)(2,1)S(1)}, u32[]{:S(2)}, u32[]{:S(2)}) %all-to-all-start.1) | async-done | bytes 2162720 | tf_op jit(solution)/shard_map/all_to_all | solution.py:621
  128.3 11.5 %collective-permute-done.19 = bf16[256,512]{1,0:T(8,128)(2,1)S(1)} collective-permute-done((bf16[256,512]{1,0:T(8,128)(2,1)}, bf16[256,512]{1,0:T(8,128)(2,1)S(1)}, u32[]{:S(2)}, u32[]{:S(2)}) %collective-permute-start.19) | collective-permute-done | bytes 262176 | tf_op jit(solution)/shard_map/ppermute | solution.py:618
  142.6 8.3 %collective-permute-done.21 = bf16[256,512]{1,0:T(8,128)(2,1)S(1)} collective-permute-done((bf16[256,512]{1,0:T(8,128)(2,1)}, bf16[256,512]{1,0:T(8,128)(2,1)S(1)}, u32[]{:S(2)}, u32[]{:S(2)}) %collective-permute-start.21) | collective-permute-done | bytes 262176 | tf_op jit(solution)/shard_map/ppermute | solution.py:618
  155.7 37.6 %all-to-all-done.3.refs_0_ = bf16[16,768,128]{2,1,0:T(8,128)(2,1)S(1)} async-done(((bf16[16,768,128]{2,1,0:T(8,128)(2,1)}), bf16[16,768,128]{2,1,0:T(8,128)(2,1)S(1)}, u32[]{:S(2)}, u32[]{:S(2)}) %all-to-all-start.3) | async-done | bytes 3145760 | tf_op jit(solution)/shard_map/all_to_all | solution.py:621
  200.1 11.9 %attend.1 = (bf16[4,256,512]{2,1,0:T(8,128)(2,1)S(1)}, bf16[256,2048]{1,0:T(8,128)(2,1)S(1)}) custom-call(bf16[256,1024]{1,0:T(8,128)(2,1)S(1)} %copy-done.20, f32[256,128]{1,0:T(8,128)S(1)} %copy-done.16, f32[256,128]{1,0:T(8,128)S(1)} %copy-done.15, s32[256,128]{1,0:T(8,128)S(1)} %broadcast_select_fusion.4.places_ref, ...), custom_call_target="tpu_custom_call" | custom-call | flops 3758096384 | bytes 8388608 | tf_op jit(solution)/shard_map/attend/pallas_call | solution.py:221
  219.8 12.9 %all-to-all-done.4 = bf16[4,64,2048]{2,1,0:T(8,128)(2,1)S(1)} async-done(((bf16[4,64,2048]{2,1,0:T(8,128)(2,1)}), bf16[4,64,2048]{2,1,0:T(8,128)(2,1)S(1)}, u32[]{:S(2)}, u32[]{:S(2)}) %all-to-all-start.4) | async-done | bytes 1048608 | tf_op jit(solution)/shard_map/all_to_all | solution.py:624
  237.6 6.7 %collective-permute-done.24 = bf16[64,2048]{1,0:T(8,128)(2,1)S(1)} collective-permute-done((bf16[64,2048]{1,0:T(8,128)(2,1)S(1)}, bf16[64,2048]{1,0:T(8,128)(2,1)S(1)}, u32[]{:S(2)}, u32[]{:S(2)}) %collective-permute-start.24) | collective-permute-done | bytes 262176 | tf_op jit(solution)/shard_map/ppermute | solution.py:615
  244.4 9.6 %collective-permute-done.25 = bf16[64,2048]{1,0:T(8,128)(2,1)S(1)} collective-permute-done((bf16[64,2048]{1,0:T(8,128)(2,1)S(1)}, bf16[64,2048]{1,0:T(8,128)(2,1)S(1)}, u32[]{:S(2)}, u32[]{:S(2)}) %collective-permute-start.25) | collective-permute-done | bytes 262176 | tf_op jit(solution)/shard_map/ppermute | solution.py:615
  254.3 13.8 %mlp.1 = (bf16[256,2048]{1,0:T(8,128)(2,1)S(1)}, bf16[256,2048]{1,0:T(8,128)(2,1)S(1)}, bf16[3,704,256]{2,1,0:T(8,128)(2,1)S(1)}, bf16[3,704,256]{2,1,0:T(8,128)(2,1)S(1)}) custom-call(bf16[256,2048]{1,0:T(8,128)(2,1)S(1)} %pad_maximum_fusion.4.h_ref.value_ref.v, bf16[256,2048]{1,0:T(8,128)(2,1)S(1)} %pad_maximum_fusion.6.cot_ref.value_ref, ...), custom_call_target="tpu_custom_call" | custom-call | flops 8858370048 | bytes 21495808 | tf_op jit(solution)/shard_map/mlp/pallas_call | solution.py:504
  270.1 6.5 %all-to-all-start.5 = ((bf16[4,64,2048]{2,1,0:T(8,128)(2,1)}), bf16[4,64,2048]{2,1,0:T(8,128)(2,1)}, u32[]{:S(2)}, u32[]{:S(2)}) async-start(bf16[4,64,2048]{2,1,0:T(8,128)(2,1)} %bitcast.171), calls=%async_computation.5 | async-start | bytes 2097152 | tf_op jit(solution)/shard_map/all_to_all | solution.py:621
  285.5 16.2 %all-to-all-done.5 = bf16[4,64,2048]{2,1,0:T(8,128)(2,1)} async-done(((bf16[4,64,2048]{2,1,0:T(8,128)(2,1)}), bf16[4,64,2048]{2,1,0:T(8,128)(2,1)}, u32[]{:S(2)}, u32[]{:S(2)}) %all-to-all-start.5) | async-done | bytes 1048608 | tf_op jit(solution)/shard_map/all_to_all | solution.py:621
  306.5 4.4 all-to-all-start.6
  316.6 4.4 unit_grads.11
  329.7 8.9 %collective-permute-done.32 = bf16[64,2048]{1,0:T(8,128)(2,1)} collective-permute-done((bf16[64,2048]{1,0:T(8,128)(2,1)}, bf16[64,2048]{1,0:T(8,128)(2,1)}, u32[]{:S(2)}, u32[]{:S(2)}) %collective-permute-start.32) | collective-permute-done | bytes 262176 | tf_op jit(solution)/shard_map/ppermute | solution.py:615
  341.9 4.1 collective-permute-done.35.refs_0_
  349.7 4.4 all-to-all-start.7
  354.3 17.6 %attend_back.1 = (bf16[16,256,128]{2,1,0:T(8,128)(2,1)}, bf16[16,256,128]{2,1,0:T(8,128)(2,1)}, bf16[256,384]{1,0:T(8,128)(2,1)}, bf16[256,384]{1,0:T(8,128)(2,1...) custom-call(s32[3]{0:T(128)} %pad_add_fusion.1.at_ref, ...), custom_call_target="tpu_custom_call" | custom-call | flops 7516192768 | bytes 18874368 | tf_op jit(solution)/shard_map/attend_back/pallas_call | solution.py:327
  381.8 4.4 collective-permute-done.37
  386.2 7.3 %collective-permute-done.38 = bf16[256,512]{1,0:T(8,128)(2,1)S(1)} collective-permute-done((bf16[256,512]{1,0:T(8,128)(2,1)S(1)}, bf16[256,512]{1,0:T(8,128)(2,1)S(1)}, u32[]{:S(2)}, u32[]{:S(2)}) %collective-permute-start.38) | collective-permute-done | bytes 262176 | tf_op jit(solution)/shard_map/ppermute | solution.py:618
  395.9 6.8 %all-to-all-done.7 = bf16[16,512,128]{2,1,0:T(8,128)(2,1)S(1)} async-done(((bf16[16,512,128]{2,1,0:T(8,128)(2,1)}), bf16[16,512,128]{2,1,0:T(8,128)(2,1)S(1)}, u32[]{:S(2)}, u32[]{:S(2)}) %all-to-all-start.7) | async-done | bytes 2097184 | tf_op jit(solution)/shard_map/all_to_all | solution.py:621
  419.3 6.1 %collective-permute-done.44.refs_1_ = bf16[256,384]{1,0:T(8,128)(2,1)S(1)} collective-permute-done((bf16[256,384]{1,0:T(8,128)(2,1)}, bf16[256,384]{1,0:T(8,128)(2,1)S(1)}, u32[]{:S(2)}, u32[]{:S(2)}) %collective-permute-start.44) | collective-permute-done | bytes 196640 | tf_op jit(solution)/shard_map/ppermute | solution.py:618
  432.3 7.5 %all-to-all-done.8 = bf16[16,256,128]{2,1,0:T(8,128)(2,1)S(1)} async-done(((bf16[16,256,128]{2,1,0:T(8,128)(2,1)}), bf16[16,256,128]{2,1,0:T(8,128)(2,1)S(1)}, u32[]{:S(2)}, u32[]{:S(2)}) %all-to-all-start.8) | async-done | bytes 1048608 | tf_op jit(solution)/shard_map/all_to_all | solution.py:621
  454.3 5.1 latent_back.1
  472.2 6.7 %collective-permute-done.50 = bf16[64,2048]{1,0:T(8,128)(2,1)S(1)} collective-permute-done((bf16[64,2048]{1,0:T(8,128)(2,1)}, bf16[64,2048]{1,0:T(8,128)(2,1)S(1)}, u32[]{:S(2)}, u32[]{:S(2)}) %collective-permute-start.50) | collective-permute-done | bytes 262176 | tf_op jit(solution)/shard_map/ppermute | solution.py:618
  478.9 5.5 %collective-permute-done.51 = bf16[64,2048]{1,0:T(8,128)(2,1)S(1)} collective-permute-done((bf16[64,2048]{1,0:T(8,128)(2,1)}, bf16[64,2048]{1,0:T(8,128)(2,1)S(1)}, u32[]{:S(2)}, u32[]{:S(2)}) %collective-permute-start.51) | collective-permute-done | bytes 262176 | tf_op jit(solution)/shard_map/ppermute | solution.py:618
  497.9 7.2 %collective-permute-done.56 = bf16[4,64,384]{2,1,0:T(8,128)(2,1)} collective-permute-done((bf16[4,64,384]{2,1,0:T(8,128)(2,1)}, bf16[4,64,384]{2,1,0:T(8,128)(2,1)}, u32[]{:S(2)}, u32[]{:S(2)}) %collective-permute-start.56) | collective-permute-done | bytes 196640 | tf_op jit(solution)/shard_map/ppermute | solution.py:615
  518.5 9.9 %all-to-all-done.10 = bf16[4,704,128]{2,1,0:T(8,128)(2,1)S(1)} async-done(((bf16[4,704,128]{2,1,0:T(8,128)(2,1)}), bf16[4,704,128]{2,1,0:T(8,128)(2,1)S(1)}, u32[]{:S(2)}, u32[]{:S(2)}) %all-to-all-start.10) | async-done | bytes 720928 | tf_op jit(solution)/shard_map/all_to_all | solution.py:621
  (448 shorter events, 247.7 us)
Async XLA Ops:
  9.0 25.5 %collective-permute-start = (bf16[64,2048]{1,0:T(8,128)(2,1)}, bf16[64,2048]{1,0:T(8,128)(2,1)}, u32[]{:S(2)}, u32[]{:S(2)}) collective-permute-start(bf16[64,2048]{1,0:T(8,128)(2,1)} %constant_dynamic-slice_fusion.12), channel_id=1, source_target_pairs={{0,8},{2,10},{4,12},{6,14},{8,16},{10,18},{12,20},{14,22},{16,24},... | collective-permute-start | bytes 786440 | tf_op jit(solution)/shard_map/ppermute | solution.py:615
  12.0 22.4 %collective-permute-start.1 = (bf16[64,2048]{1,0:T(8,128)(2,1)}, bf16[64,2048]{1,0:T(8,128)(2,1)}, u32[]{:S(2)}, u32[]{:S(2)}) collective-permute-start(bf16[64,2048]{1,0:T(8,128)(2,1)} %constant_dynamic-slice_fusion.12), channel_id=1, source_target_pairs={{0,16},{2,18},{4,20},{6,22},{8,24},{10,26},{12,28},{14,30},{16,0},... | collective-permute-start | bytes 786440 | tf_op jit(solution)/shard_map/ppermute | solution.py:615
  14.6 19.9 %collective-permute-start.2 = (bf16[64,2048]{1,0:T(8,128)(2,1)}, bf16[64,2048]{1,0:T(8,128)(2,1)}, u32[]{:S(2)}, u32[]{:S(2)}) collective-permute-start(bf16[64,2048]{1,0:T(8,128)(2,1)} %constant_dynamic-slice_fusion.12), channel_id=1, source_target_pairs={{0,24},{2,26},{4,28},{6,30},{8,0},{10,2},{12,4},{14,6},{16,8},{18,... | collective-permute-start | bytes 786440 | tf_op jit(solution)/shard_map/ppermute | solution.py:615
  28.3 23.4 %all-to-all-start.2 = ((bf16[4,768,128]{2,1,0:T(8,128)(2,1)}), bf16[4,768,128]{2,1,0:T(8,128)(2,1)S(1)}, u32[]{:S(2)}, u32[]{:S(2)}) async-start(bf16[4,768,128]{2,1,0:T(8,128)(2,1)} %pad_maximum_fusion.7), calls=%async_computation.2 | async-start | bytes 1572864 | tf_op jit(solution)/shard_map/all_to_all | solution.py:624
  52.4 57.0 %all-to-all-start.1 = ((bf16[4,2112,128]{2,1,0:T(8,128)(2,1)}), bf16[4,2112,128]{2,1,0:T(8,128)(2,1)S(1)}, u32[]{:S(2)}, u32[]{:S(2)}) async-start(bf16[4,2112,128]{2,1,0:T(8,128)(2,1)} %pad_maximum_fusion), calls=%async_computation.1 | async-start | bytes 4325376 | tf_op jit(solution)/shard_map/all_to_all | solution.py:621
  60.2 154.4 %all-gather.3.cloned.1.call-start = ((), (), s32[]{:S(2)}) async-start(), calls=%async_computation.13 | async-start | bytes 10813440 | tf_op jit(solution)/shard_map/all_gather | solution.py:782
  120.9 72.4 %all-to-all-start.3 = ((bf16[16,768,128]{2,1,0:T(8,128)(2,1)}), bf16[16,768,128]{2,1,0:T(8,128)(2,1)S(1)}, u32[]{:S(2)}, u32[]{:S(2)}) async-start(bf16[16,768,128]{2,1,0:T(8,128)(2,1)} %bitcast.176), calls=%async_computation.3 | async-start | bytes 6291456 | tf_op jit(solution)/shard_map/all_to_all | solution.py:621
  128.0 22.9 %collective-permute-start.21 = (bf16[256,512]{1,0:T(8,128)(2,1)}, bf16[256,512]{1,0:T(8,128)(2,1)S(1)}, u32[]{:S(2)}, u32[]{:S(2)}) collective-permute-start(bf16[256,512]{1,0:T(8,128)(2,1)} %get-tuple-element.297), channel_id=1, source_target_pairs={{0,6},{2,4},{4,2},{6,0},{8,14},{10,12},{12,10},{14,8},{16,22},{18,... | collective-permute-start | bytes 786440 | tf_op jit(solution)/shard_map/ppermute | solution.py:618
  214.6 39.7 %collective-permute-start.27 = (bf16[4,4,2112,128]{3,2,1,0:T(8,128)(2,1)}, bf16[4,4,2112,128]{3,2,1,0:T(8,128)(2,1)}, u32[]{:S(2)}, u32[]{:S(2)}) collective-permute-start(bf16[4,4,2112,128]{3,2,1,0:T(8,128)(2,1)} %bitcast.174), channel_id=1, source_target_pairs={{0,1},{1,0},{2,3},{3,2},{4,5},{5,4},{6,7},{7,6},{8,9},{9,8},{10,11... | collective-permute-start | bytes 25952264 | tf_op jit(solution)/shard_map/ppermute | solution.py:607
  214.7 17.9 %all-to-all-start.4 = ((bf16[4,64,2048]{2,1,0:T(8,128)(2,1)}), bf16[4,64,2048]{2,1,0:T(8,128)(2,1)S(1)}, u32[]{:S(2)}, u32[]{:S(2)}) async-start(bf16[4,64,2048]{2,1,0:T(8,128)(2,1)} %bitcast.170), calls=%async_computation.4 | async-start | bytes 2097152 | tf_op jit(solution)/shard_map/all_to_all | solution.py:624
  233.2 20.7 %collective-permute-start.25 = (bf16[64,2048]{1,0:T(8,128)(2,1)S(1)}, bf16[64,2048]{1,0:T(8,128)(2,1)S(1)}, u32[]{:S(2)}, u32[]{:S(2)}) collective-permute-start(bf16[64,2048]{1,0:T(8,128)(2,1)S(1)} %multiply_convert_fusion), channel_id=1, source_target_pairs={{0,16},{2,18},{4,20},{6,22},{8,24},{10,26},{12,28},{14,30},{16,0},... | collective-permute-start | bytes 786440 | tf_op jit(solution)/shard_map/ppermute | solution.py:615
  236.2 17.7 %collective-permute-start.26 = (bf16[64,2048]{1,0:T(8,128)(2,1)S(1)}, bf16[64,2048]{1,0:T(8,128)(2,1)S(1)}, u32[]{:S(2)}, u32[]{:S(2)}) collective-permute-start(bf16[64,2048]{1,0:T(8,128)(2,1)S(1)} %multiply_convert_fusion), channel_id=1, source_target_pairs={{0,24},{2,26},{4,28},{6,30},{8,0},{10,2},{12,4},{14,6},{16,8},{18,... | collective-permute-start | bytes 786440 | tf_op jit(solution)/shard_map/ppermute | solution.py:615
  270.1 31.6 %all-to-all-start.5 = ((bf16[4,64,2048]{2,1,0:T(8,128)(2,1)}), bf16[4,64,2048]{2,1,0:T(8,128)(2,1)}, u32[]{:S(2)}, u32[]{:S(2)}) async-start(bf16[4,64,2048]{2,1,0:T(8,128)(2,1)} %bitcast.171), calls=%async_computation.5 | async-start | bytes 2097152 | tf_op jit(solution)/shard_map/all_to_all | solution.py:621
  301.7 19.4 %collective-permute-start.29 = (bf16[4,4,704,128]{3,2,1,0:T(8,128)(2,1)}, bf16[4,4,704,128]{3,2,1,0:T(8,128)(2,1)}, u32[]{:S(2)}, u32[]{:S(2)}) collective-permute-start(bf16[4,4,704,128]{3,2,1,0:T(8,128)(2,1)} %copy-done.10), channel_id=1, source_target_pairs={{0,1},{1,0},{2,3},{3,2},{4,5},{5,4},{6,7},{7,6},{8,9},{9,8},{10,11... | collective-permute-start | bytes 8650760 | tf_op jit(solution)/shard_map/ppermute | solution.py:607
  302.2 21.9 %collective-permute-start.28 = (bf16[4,4,704,128]{3,2,1,0:T(8,128)(2,1)}, bf16[4,4,704,128]{3,2,1,0:T(8,128)(2,1)}, u32[]{:S(2)}, u32[]{:S(2)}) collective-permute-start(bf16[4,4,704,128]{3,2,1,0:T(8,128)(2,1)} %copy-done.9), channel_id=1, source_target_pairs={{0,1},{1,0},{2,3},{3,2},{4,5},{5,4},{6,7},{7,6},{8,9},{9,8},{10,11... | collective-permute-start | bytes 8650760 | tf_op jit(solution)/shard_map/ppermute | solution.py:607
  306.5 32.1 %all-to-all-start.6 = ((bf16[4,64,2048]{2,1,0:T(8,128)(2,1)}), bf16[4,64,2048]{2,1,0:T(8,128)(2,1)}, u32[]{:S(2)}, u32[]{:S(2)}) async-start(bf16[4,64,2048]{2,1,0:T(8,128)(2,1)} %tile.8), calls=%async_computation.6 | async-start | bytes 2097152 | tf_op jit(solution)/shard_map/all_to_all | solution.py:624
  310.9 128.9 %reduce-scatter.7.cloned.1.call-start = ((), (), s32[]{:S(2)}) async-start(), calls=%async_computation.14 | async-start | bytes 7208960
  313.1 16.6 %collective-permute-start.31 = (bf16[64,2048]{1,0:T(8,128)(2,1)}, bf16[64,2048]{1,0:T(8,128)(2,1)S(1)}, u32[]{:S(2)}, u32[]{:S(2)}) collective-permute-start(bf16[64,2048]{1,0:T(8,128)(2,1)} %get-tuple-element.227), channel_id=1, source_target_pairs={{0,24},{2,26},{4,28},{6,30},{8,0},{10,2},{12,4},{14,6},{16,8},{18,... | collective-permute-start | bytes 786440 | tf_op jit(solution)/shard_map/ppermute | solution.py:615
  316.0 22.6 %collective-permute-start.32 = (bf16[64,2048]{1,0:T(8,128)(2,1)}, bf16[64,2048]{1,0:T(8,128)(2,1)}, u32[]{:S(2)}, u32[]{:S(2)}) collective-permute-start(bf16[64,2048]{1,0:T(8,128)(2,1)} %get-tuple-element.226), channel_id=1, source_target_pairs={{0,16},{2,18},{4,20},{6,22},{8,24},{10,26},{12,28},{14,30},{16,0},... | collective-permute-start | bytes 786440 | tf_op jit(solution)/shard_map/ppermute | solution.py:615
  316.0 22.6 %collective-permute-start.33 = (bf16[64,2048]{1,0:T(8,128)(2,1)}, bf16[64,2048]{1,0:T(8,128)(2,1)}, u32[]{:S(2)}, u32[]{:S(2)}) collective-permute-start(bf16[64,2048]{1,0:T(8,128)(2,1)} %get-tuple-element.225), channel_id=1, source_target_pairs={{0,8},{2,10},{4,12},{6,14},{8,16},{10,18},{12,20},{14,22},{16,24},... | collective-permute-start | bytes 786440 | tf_op jit(solution)/shard_map/ppermute | solution.py:615
  349.7 53.0 %all-to-all-start.7 = ((bf16[16,512,128]{2,1,0:T(8,128)(2,1)}), bf16[16,512,128]{2,1,0:T(8,128)(2,1)S(1)}, u32[]{:S(2)}, u32[]{:S(2)}) async-start(bf16[16,512,128]{2,1,0:T(8,128)(2,1)} %out_grads.3), calls=%async_computation.7 | async-start | bytes 4194304 | tf_op jit(solution)/shard_map/all_to_all | solution.py:621
  354.1 151.5 %reduce-scatter.9.cloned.1.call-start = ((), (), s32[]{:S(2)}) async-start(), calls=%async_computation.15 | async-start | bytes 3604480
  380.2 15.4 %collective-permute-start.39 = (bf16[256,512]{1,0:T(8,128)(2,1)S(1)}, bf16[256,512]{1,0:T(8,128)(2,1)S(1)}, u32[]{:S(2)}, u32[]{:S(2)}) collective-permute-start(bf16[256,512]{1,0:T(8,128)(2,1)S(1)} %get-tuple-element.223), channel_id=1, source_target_pairs={{0,6},{2,4},{4,2},{6,0},{8,14},{10,12},{12,10},{14,8},{16,22},{18,... | collective-permute-start | bytes 786440 | tf_op jit(solution)/shard_map/ppermute | solution.py:618
  412.3 27.5 %all-to-all-start.8 = ((bf16[16,256,128]{2,1,0:T(8,128)(2,1)}), bf16[16,256,128]{2,1,0:T(8,128)(2,1)S(1)}, u32[]{:S(2)}, u32[]{:S(2)}) async-start(bf16[16,256,128]{2,1,0:T(8,128)(2,1)} %add_convert_fusion), calls=%async_computation.8 | async-start | bytes 2097152 | tf_op jit(solution)/shard_map/all_to_all | solution.py:621
  440.7 43.6 %all-to-all-start.9 = ((bf16[4,1408,128]{2,1,0:T(8,128)(2,1)}), bf16[4,1408,128]{2,1,0:T(8,128)(2,1)S(1)}, u32[]{:S(2)}, u32[]{:S(2)}) async-start(bf16[4,1408,128]{2,1,0:T(8,128)(2,1)} %bitcast.186), calls=%async_computation.9 | async-start | bytes 2883584 | tf_op jit(solution)/shard_map/all_to_all | solution.py:621
  465.4 48.2 %collective-permute-start.61 = (bf16[768,128]{1,0:T(8,128)(2,1)}, bf16[768,128]{1,0:T(8,128)(2,1)}, u32[]{:S(2)}, u32[]{:S(2)}) collective-permute-start(bf16[768,128]{1,0:T(8,128)(2,1)} %get-tuple-element.249), channel_id=1, source_target_pairs={{0,2},{2,0},{4,6},{6,4},{8,10},{10,8},{12,14},{14,12},{16,18},{18,... | collective-permute-start | bytes 589832 | tf_op jit(solution)/shard_map/ppermute | solution.py:618
  465.9 49.9 %collective-permute-start.62 = (bf16[768,128]{1,0:T(8,128)(2,1)}, bf16[768,128]{1,0:T(8,128)(2,1)}, u32[]{:S(2)}, u32[]{:S(2)}) collective-permute-start(bf16[768,128]{1,0:T(8,128)(2,1)} %get-tuple-element.250), channel_id=1, source_target_pairs={{0,4},{2,6},{4,0},{6,2},{8,12},{10,14},{12,8},{14,10},{16,20},{18,... | collective-permute-start | bytes 589832 | tf_op jit(solution)/shard_map/ppermute | solution.py:618
  467.9 16.4 %collective-permute-start.51 = (bf16[64,2048]{1,0:T(8,128)(2,1)}, bf16[64,2048]{1,0:T(8,128)(2,1)S(1)}, u32[]{:S(2)}, u32[]{:S(2)}) collective-permute-start(bf16[64,2048]{1,0:T(8,128)(2,1)} %get-tuple-element.146), channel_id=1, source_target_pairs={{0,4},{2,6},{4,0},{6,2},{8,12},{10,14},{12,8},{14,10},{16,20},{18,... | collective-permute-start | bytes 786440 | tf_op jit(solution)/shard_map/ppermute | solution.py:618
  488.1 17.0 %collective-permute-start.56 = (bf16[4,64,384]{2,1,0:T(8,128)(2,1)}, bf16[4,64,384]{2,1,0:T(8,128)(2,1)}, u32[]{:S(2)}, u32[]{:S(2)}) collective-permute-start(bf16[4,64,384]{2,1,0:T(8,128)(2,1)} %get-tuple-element.155), channel_id=1, source_target_pairs={{0,16},{2,18},{4,20},{6,22},{8,24},{10,26},{12,28},{14,30},{16,0},... | collective-permute-start | bytes 589832 | tf_op jit(solution)/shard_map/ppermute | solution.py:615
  488.1 17.0 %collective-permute-start.57 = (bf16[4,64,384]{2,1,0:T(8,128)(2,1)}, bf16[4,64,384]{2,1,0:T(8,128)(2,1)}, u32[]{:S(2)}, u32[]{:S(2)}) collective-permute-start(bf16[4,64,384]{2,1,0:T(8,128)(2,1)} %get-tuple-element.156), channel_id=1, source_target_pairs={{0,8},{2,10},{4,12},{6,14},{8,16},{10,18},{12,20},{14,22},{16,24},... | collective-permute-start | bytes 589832 | tf_op jit(solution)/shard_map/ppermute | solution.py:615
  496.4 19.4 %collective-permute-start.63 = (bf16[768,128]{1,0:T(8,128)(2,1)S(1)}, bf16[768,128]{1,0:T(8,128)(2,1)S(1)}, u32[]{:S(2)}, u32[]{:S(2)}) collective-permute-start(bf16[768,128]{1,0:T(8,128)(2,1)S(1)} %copy-done.56), channel_id=1, source_target_pairs={{0,6},{2,4},{4,2},{6,0},{8,14},{10,12},{12,10},{14,8},{16,22},{18,... | collective-permute-start | bytes 589832 | tf_op jit(solution)/shard_map/ppermute | solution.py:618
  505.6 22.8 %all-to-all-start.10 = ((bf16[4,704,128]{2,1,0:T(8,128)(2,1)}), bf16[4,704,128]{2,1,0:T(8,128)(2,1)S(1)}, u32[]{:S(2)}, u32[]{:S(2)}) async-start(bf16[4,704,128]{2,1,0:T(8,128)(2,1)} %bitcast.191), calls=%async_computation.10 | async-start | bytes 1441792 | tf_op jit(solution)/shard_map/all_to_all | solution.py:621
  (130 other events, 994.7 us)
Sparse Core Ops, SparseCore 0:
  112.0 100.1 all-gather.2
  338.7 70.6 reduce-scatter.6
  412.5 47.2 reduce-scatter.8

commit v7 on v6

--- a/solution.py
+++ b/solution.py
@@ -15,7 +15,7 @@
 SQUARE = 4
 VMEM_LIMIT = 56 * 1024 * 1024
 MLP_LIMIT = 26 * 1024 * 1024
-ATTEND_LIMIT = 32 * 1024 * 1024
+ATTEND_LIMIT = 22 * 1024 * 1024
 GRADS_LIMIT = 16 * 1024 * 1024
 BF16 = jnp.bfloat16
 F32 = jnp.float32
@@ -445,14 +445,10 @@
     cot_ref,
     near_ref,
     far_ref,
-    d_h_hbm,
-    out_hbm,
+    d_h_ref,
     act_near_ref,
     act_far_ref,
     turned,
-    d_h_ref,
-    out_ref,
-    sems,
 ):
     tiles = near_ref.shape[1]
     units = act_near_ref.shape[1]
@@ -478,23 +474,46 @@
         acts[1] = (d_act * silu_gate).astype(BF16)
         acts[2] = (silu_gate * up_proj).astype(BF16)
     straight = [[acts[kind].T for kind in range(3)] for _, acts in sides]
-    copies = []
-    for i, (first, count, value_ref, hbm) in enumerate(
-        ((0, 2, d_h_ref, d_h_hbm), (2, 1, out_ref, out_hbm))
-    ):
-        for q in range(SQUARE):
-            value = sum(
-                matmul(straight[c][kind], weight(sides[c][0], kind, q))
-                for c in range(2)
-                for kind in range(first, first + count)
-            )
-            for t in range(tiles):
-                here = slice((t * SQUARE + q) * 128, (t * SQUARE + q + 1) * 128)
-                value_ref[:, here] = value[:, t * 128 : (t + 1) * 128].astype(BF16)
-        copies.append(pltpu.make_async_copy(value_ref, hbm, sems.at[i]))
-        copies[-1].start()
-    for copy in copies:
-        copy.wait()
+    for q in range(SQUARE):
+        value = sum(
+            matmul(straight[c][kind], weight(sides[c][0], kind, q)) for c in range(2) for kind in range(2)
+        )
+        for t in range(tiles):
+            here = slice((t * SQUARE + q) * 128, (t * SQUARE + q + 1) * 128)
+            d_h_ref[:, here] = value[:, t * 128 : (t + 1) * 128].astype(BF16)
+
+
+def mlp_out_kernel(near_ref, far_ref, act_near_ref, act_far_ref, out_ref):
+    tiles, units = near_ref.shape[1], act_near_ref.shape[1]
+    sides = ((near_ref, act_near_ref[0].T), (far_ref, act_far_ref[0].T))
+    for q in range(SQUARE):
+        value = sum(
+            matmul(act, jnp.concatenate([side[q, t] for t in range(tiles)], axis=1))
+            for side, act in sides
+        )
+        for t in range(tiles):
+            here = slice((t * SQUARE + q) * 128, (t * SQUARE + q + 1) * 128)
+            out_ref[:, here] = value[:, t * 128 : (t + 1) * 128].astype(BF16)
+
+
+def mlp_out(near, far, act_near, act_far):
+    _, units, rows = act_near.shape
+    tiles = near.shape[1]
+    width = SQUARE * tiles * 128
+    weights = pl.BlockSpec((SQUARE, tiles, units, 128), lambda i: (0, 0, 2, 0))
+    acts = pl.BlockSpec((1, units, rows), lambda i: (2, 0, 0))
+    return pl.pallas_call(
+        mlp_out_kernel,
+        grid=(1,),
+        in_specs=[weights, weights, acts, acts],
+        out_specs=pl.BlockSpec((rows, width), lambda i: (0, 0)),
+        out_shape=shape((rows, width)),
+        compiler_params=params(GRADS_LIMIT if rows <= 256 else VMEM_LIMIT),
+        cost_estimate=pl.CostEstimate(
+            flops=4 * rows * width * units, bytes_accessed=4 * width * units, transcendentals=0
+        ),
+        name="mlp_out",
+    )(near, far, act_near, act_far)
 
 
 def mlp(h, cot, near, far):
@@ -504,18 +523,13 @@
     return pl.pallas_call(
         mlp_kernel,
         in_specs=[VMEM] * 4,
-        out_specs=[FAR, FAR, VMEM, VMEM],
-        out_shape=[low, low, acts, acts],
-        scratch_shapes=[
-            pltpu.VMEM((2, SQUARE, width // SQUARE, rows), BF16),
-            pltpu.VMEM((rows, width), BF16),
-            pltpu.VMEM((rows, width), BF16),
-            pltpu.SemaphoreType.DMA((2,)),
-        ],
+        out_specs=[VMEM] * 3,
+        out_shape=[low, acts, acts],
+        scratch_shapes=[pltpu.VMEM((2, SQUARE, width // SQUARE, rows), BF16)],
         compiler_params=params(MLP_LIMIT if rows <= 256 else VMEM_LIMIT),
         cost_estimate=pl.CostEstimate(
-            flops=24 * rows * width * units,
-            bytes_accessed=12 * width * units + 8 * rows * width,
+            flops=20 * rows * width * units,
+            bytes_accessed=12 * width * units + 6 * rows * width,
             transcendentals=2 * rows * units,
         ),
         name="mlp",
@@ -563,9 +577,7 @@
         out_shape=shape(out_dims),
         input_output_aliases=aliases,
         compiler_params=params(GRADS_LIMIT),
-        cost_estimate=pl.CostEstimate(
-            flops=2 * rows * width * units, bytes_accessed=4 * width * units, transcendentals=0
-        ),
+        cost_estimate=pl.CostEstimate(flops=1000, bytes_accessed=1000, transcendentals=0),
         name="unit_grads",
     )(*args)
 
@@ -691,6 +703,12 @@
     inputs = own(tokens).astype(F32)
     x_inverse = inverse_rms(inputs)
     x_hat = inputs * x_inverse
+    def square_send(value):
+        blocks = [
+            lax.dynamic_index_in_dim(value, corner ^ m, 0, keepdims=False) for m in range(SQUARE)
+        ]
+        return [blocks[0]] + [within(blocks[m], m) for m in range(1, SQUARE)]
+
     def by_corner(pieces):
         pieces = jnp.stack(pieces)
         return jnp.stack(
@@ -700,7 +718,7 @@
             ]
         )
 
-    x_all = by_corner(square_pieces(x_hat.astype(BF16))).reshape(-1, width)
+    x_low = x_hat.astype(BF16)
 
     gain_rows = attn_gain.astype(F32)[:, None]
     down = jnp.concatenate([w_qdown, w_kv], axis=1)
@@ -731,9 +749,9 @@
     down_half = lax.dynamic_slice_in_dim(down_scaled, core * (lanes // 2), lanes // 2, 0)
     cot_own = own(cotangent)
     down_own = square_exchange(shares(down_half))
-    cot_pieces = line_pieces(arranged(cot_own))
-    cot_all = by_layer(jnp.concatenate(cot_pieces))
-    down_near = line_pieces(after(down_own, *cot_pieces[1:]))
+    down_near = line_pieces(down_own)
+    x_pieces = square_pieces(after(x_low, down_own))
+    x_all = by_corner(x_pieces).reshape(-1, width)
     down_far = [across(piece) for piece in down_near]
 
     q_gain_rows = q_gain.astype(F32)[:, None]
@@ -742,7 +760,7 @@
     qup_send = jnp.transpose(qup_send, (1, 2, 0, 3)).reshape(SQUARE, -1, lanes)
     qup_size = qup_send.shape[1]
     head_send = jnp.concatenate([qup_send, w_out.reshape(SQUARE, pair * HEAD, lanes)], axis=1)
-    head_own = square_exchange(after(head_send, down_own))
+    head_own = by_corner(square_send(after(head_send, x_pieces[1])))
 
     mlp_gain_rows = mlp_gain.astype(F32)[:, None]
     gate_send = (w_gate.astype(F32) * mlp_gain_rows).astype(BF16).T
@@ -772,16 +790,17 @@
     lane = jnp.arange(128, dtype=jnp.int32)[None, :]
     tables = (cosine, sine, jnp.where(lane == 0, row_natural[:, None], row_start[:, None]))
 
-    x_all = after(x_all, head_own)
+    cot_copies = jnp.tile(arranged(cot_own), (layers, 1))
+    head_copies = jnp.tile(head_own, (layers, 1, 1))
     part, down_here = project(at, x_all, down_near, down_far)
-    lat_hat, lat_low, lat_inverse, kv_own = latent(at, cosine, sine, square_pieces(part), rank)
+    head_copies, cot_copies, *part_pieces = together(head_copies, cot_copies, *square_pieces(part))
+    lat_hat, lat_low, lat_inverse, kv_own = latent(at, cosine, sine, part_pieces, rank)
     mlp_layer = line_exchange(after(mlp_send, *down_near[1:]))
-    head_copies = jnp.tile(head_own, (layers, 1, 1))
-    mlp_layer, kv_own, head_copies = together(mlp_layer, kv_own, head_copies)
-    kv_line = jnp.concatenate(line_pieces(kv_own))
+    mlp_layer, head_copies, *kv_pieces = together(mlp_layer, head_copies, *line_pieces(kv_own))
+    kv_line = jnp.concatenate(kv_pieces)
     mlp_near = lax.all_gather(tiled(mlp_layer), "seq", axis_index_groups=square_groups)
 
-    head_near = line_exchange(after(head_copies, kv_line))
+    head_near = line_exchange(head_copies)
     kv_near = jnp.concatenate(square_pieces(kv_line))
     kv_all = jnp.concatenate([kv_near, across(kv_near)])
     head_near, kv_all = together(head_near, kv_all)
@@ -797,17 +816,19 @@
     saved, attn_part = attend(
         lat_low, tables, kv_all, key_natural, head_weights, pair, block
     )
-    mlp_near, attn_part = together(mlp_near, attn_part)
+    cot_lines = line_exchange(after(cot_copies, head_near))
+    attn_pieces = square_send(attn_part.reshape(SQUARE, rows, width))
+    mlp_near, cot_all, *attn_pieces = together(mlp_near, cot_lines, *attn_pieces)
     mlp_far = across(mlp_near)
-    attn_blocks = square_exchange(attn_part.reshape(SQUARE, rows, width))
-    hidden = inputs + jnp.sum(attn_blocks.astype(F32), axis=0)
+    hidden = inputs + sum(piece.astype(F32) for piece in attn_pieces)
     h_inverse = inverse_rms(hidden)
     h_hat = hidden * h_inverse
     h_low = h_hat.astype(BF16)
     h_all = jnp.concatenate(line_pieces(arranged(h_low)))
     h_all = by_layer(h_all)
 
-    d_h_part, mlp_part, acts_near, acts_far = mlp(h_all, cot_all, mlp_near, mlp_far)
+    d_h_part, acts_near, acts_far = mlp(h_all, cot_all, mlp_near, mlp_far)
+    mlp_part = mlp_out(mlp_near, mlp_far, acts_near, acts_far)
     def line_blocks(value):
         return line_exchange(value.reshape(layers, rows, -1))
 
@@ -817,18 +838,20 @@
     kinds = ((0, h_all), (1, h_all), (2, cot_all))
     far_grads = [unit_grads(acts_far, kind, value) for kind, value in kinds]
     d_h_lines = line_blocks(d_h_part)
-    d_h_lines, acts_near, *far_grads = together(d_h_lines, acts_near, *far_grads)
+    d_h_lines, acts_near, mlp_part, *far_grads = together(
+        d_h_lines, acts_near, mlp_part, *far_grads
+    )
     d_hscaled = line_total(d_h_lines)
     d_hidden = cot_own.astype(F32) + norm_back(d_hscaled, h_hat, h_inverse)
     mlp_grads = None
     for kind, value in kinds[:2]:
         mlp_grads = unit_grads(acts_near, kind, value, across(far_grads[kind]), mlp_grads)
     unit_sum = unit_grads(acts_near, 2, cot_all, across(far_grads[2]))
-    mlp_blocks = after(mlp_part, d_hscaled).reshape(layers, rows, width)
+    mlp_blocks = mlp_part.reshape(layers, rows, width)
     mlp_pieces = []
     for k in range(layers):
         block_out = lax.dynamic_index_in_dim(mlp_blocks, (layer - k) % layers, 0, keepdims=False)
-        mlp_pieces.append(along(block_out, -k) if k else block_out)
+        mlp_pieces.append(along(after(block_out, d_h_lines), -k) if k else block_out)
     d_attn_all = square_exchange(jnp.tile(d_hidden.astype(BF16)[None], (SQUARE, 1, 1)))
     mlp_grads, unit_sum, d_attn_all, *mlp_pieces = together(
         mlp_grads, unit_sum, d_attn_all, *mlp_pieces
@@ -859,14 +882,16 @@
     d_kv_line = square_sum(d_kv_low.reshape(SQUARE, layers * rows, 2 * HEAD)).astype(BF16)
     grad_q_total = (grad_q_near.astype(F32) + across(grad_q_far).astype(F32)).astype(BF16)
     grad_q_total = grad_q_total.reshape(chips, -1, lanes)
-    head_out_lines, d_kv_line, grad_q_total = together(head_out_lines, d_kv_line, grad_q_total)
-    d_kv_own = line_sum(d_kv_line.reshape(layers, rows, 2 * HEAD))
+    d_kv_blocks = d_kv_line.reshape(layers, rows, 2 * HEAD)
+    d_kv_blocks = [d_kv_blocks[0]] + [along(d_kv_blocks[k], -k) for k in range(1, layers)]
+    head_out_lines, grad_q_total, *d_kv_blocks = together(head_out_lines, grad_q_total, *d_kv_blocks)
+    d_kv_own = sum(block.astype(F32) for block in d_kv_blocks)
     own_cosine = lax.dynamic_slice_in_dim(cosine, corner * rows, rows, 0)
     own_sine = lax.dynamic_slice_in_dim(sine, corner * rows, rows, 0)
     d_kv_own = jnp.concatenate(
         [unrotate(d_kv_own[:, :HEAD], own_cosine, own_sine), d_kv_own[:, HEAD:]], axis=1
     ).astype(BF16)
-    head_q = line_exchange(after(grad_q_total, d_kv_own))
+    head_q = line_exchange(grad_q_total)
     kv_share_of = lambda m: lax.dynamic_slice_in_dim(d_kv_own, (corner ^ m) * kv_share, kv_share, 1)
     d_kv_share = [kv_share_of(0)] + [within(kv_share_of(m), m) for m in range(1, SQUARE)]
     d_lat_received = [d_lat_parts[0]] + [within(d_lat_parts[m], m) for m in range(1, SQUARE)]
@@ -878,13 +903,7 @@
     d_x_received = [within(d_x_blocks[m], m) for m in range(1, SQUARE)]
     down_sum = (down_grad_near + across(down_grad_far).astype(F32)).astype(BF16)
 
-    def square_send(value):
-        blocks = [
-            lax.dynamic_index_in_dim(value, corner ^ m, 0, keepdims=False) for m in range(SQUARE)
-        ]
-        return [blocks[0]] + [within(blocks[m], m) for m in range(1, SQUARE)]
-
-    gate_up_back = line_exchange(untiled(after(gate_up_sum, head_q)))
+    gate_up_raw = line_exchange(untiled(after(gate_up_sum, head_q)))
     head_sum = jnp.concatenate(
         [
             jnp.sum(blocks.reshape(layers, SQUARE, -1, lanes).astype(F32), axis=0).astype(BF16)
@@ -894,14 +913,14 @@
     )
     head_pieces = square_send(head_sum)
     down_blocks = [down_sum[k] for k in range(layers)]
-    gate_up_back, *received = together(gate_up_back, *d_x_received, *down_blocks)
-    d_x_received, down_blocks = received[: SQUARE - 1], received[SQUARE - 1 :]
+    down_pieces = [down_blocks[0]] + [along(down_blocks[k], -k) for k in range(1, layers)]
+    gate_up_back, *received = together(gate_up_raw, *d_x_received, *down_pieces)
+    d_x_received, down_pieces = received[: SQUARE - 1], received[SQUARE - 1 :]
     d_xscaled = d_x_blocks[0].astype(F32) + sum(block.astype(F32) for block in d_x_received)
     token_own = (d_hidden + norm_back(d_xscaled, x_hat, x_inverse)).astype(BF16)
     token_grad = both(token_own, across(token_own))
-    down_pieces = [along(down_blocks[k], -k) for k in range(1, layers)]
-    unit_back = line_exchange(untiled(after(unit_sum, *down_pieces)))
-    down_line = down_blocks[0].astype(F32) + sum(piece.astype(F32) for piece in down_pieces)
+    unit_back = line_exchange(untiled(after(unit_sum, gate_up_raw)))
+    down_line = sum(piece.astype(F32) for piece in down_pieces)
     down_pieces = square_send(down_line.astype(BF16))
     unit_back, *received = together(unit_back, *down_pieces, *head_pieces)
     down_pieces, head_pieces = received[:SQUARE], received[SQUARE:]

time: 552 us -> 522 us (0.946)
  waiting for transfers between devices: 248 us -> 210 us
    ppermute x27 -> x33, waiting for transfers between devices: 82.7 us -> 66.2 us  [within(): return lax.ppermute(value, 'seq', [(i, i ^ flip) for i in range(chips)])]
    all_to_all x4 -> x2, waiting for transfers between devices: 13.6 us -> 0.52 us  [square_exchange(): lax.all_to_all(value, 'seq', 0, 0, axis_index_groups=square_groups, tiled...]
    ppermute x27 -> x33, starting transfers between devices: 30.8 us -> 39.1 us  [within(): return lax.ppermute(value, 'seq', [(i, i ^ flip) for i in range(chips)])]
    unnamed x181 -> x185, local copies, waits for them, and re-layouts: 29.9 us -> 37.8 us
    all_to_all x4 -> x2, starting transfers between devices: 15.3 us -> 9.4 us  [square_exchange(): lax.all_to_all(value, 'seq', 0, 0, axis_index_groups=square_groups, tiled...]
    all_to_all x7 -> x8, waiting for transfers between devices: 86.8 us -> 84 us  [line_exchange(): lax.all_to_all(value, 'seq', 0, 0, axis_index_groups=lines, tiled=True)]
    ppermute x21 -> x18, waiting for transfers between devices: 52 us -> 49.5 us  [along(): return lax.ppermute(value, 'seq', pairs)]
    pallas_call x1 -> x2, Pallas kernels: 13.8 us -> 15.6 us  [the longest x1 11.8 us: mlp(): pl.pallas_call(mlp_kernel, in_specs=[VMEM] * 4, out_specs=[VMEM] * 3, out...]
  transfers between devices with their start and end apart: 80 -> 82, of which waited for: 44 -> 38; matrix products, arithmetic and copies ran while one was open for 11% -> 11% of each run, Pallas kernels for 11% -> 13%
where the time goes in v7:
time: 522 us; the launch traced here: 513 us
  waiting for transfers between devices  210 us (40%)
  starting transfers between devices  114 us (22%)
  Pallas kernels  76.4 us (15%)
  local copies, waits for them, and re-layouts  53.4 us (10%)
  other arithmetic  43.6 us (8%)
  between operations  15.4 us (3%)
    all_to_all x8, waiting for transfers between devices, line_exchange(): lax.all_to_all(value, 'seq', 0, 0, axis_index_groups=lines, tiled=True)  84 us
    ppermute x33, waiting for transfers between devices, within(): return lax.ppermute(value, 'seq', [(i, i ^ flip) for i in range(chips)])  66.2 us
    ppermute x18, waiting for transfers between devices, along(): return lax.ppermute(value, 'seq', pairs)  49.5 us
    ppermute x33, starting transfers between devices, within(): return lax.ppermute(value, 'seq', [(i, i ^ flip) for i in range(chips)])  39.1 us
    unnamed x185, local copies, waits for them, and re-layouts  37.8 us
    all_to_all x8, starting transfers between devices, line_exchange(): lax.all_to_all(value, 'seq', 0, 0, axis_index_groups=lines, tiled=True)  32.4 us
    ppermute x18, starting transfers between devices, along(): return lax.ppermute(value, 'seq', pairs)  29.9 us
    pallas_call x1, Pallas kernels, attend_back(): pl.pallas_call(functools.partial(attend_back_kernel, pair, len(weights)),...  17.6 us
  transfers between devices with their start and end apart: 82, of which 38 were waited for; matrix products, arithmetic and copies ran while one was open for 11% of the time, Pallas kernels for 13%

profile of v7, /device:TPU:0, one launch (start us, length us, event | category | flops | bytes accessed | tf_op | source)
XLA Modules:
  0.0 512.5 jit_solution(14267193402171038368)
XLA Ops:
  10.0 5.2 %all-to-all-start = ((bf16[4,64,384]{2,1,0:T(8,128)(2,1)}), bf16[4,64,384]{2,1,0:T(8,128)(2,1)}, u32[]{:S(2)}, u32[]{:S(2)}) async-start(bf16[4,64,384]{2,1,0:T(8,128)(2,1)} %pad_maximum_fusion.16), calls=%async_computation | async-start | bytes 393216 | tf_op jit(solution)/shard_map/all_to_all | solution.py:636
  25.4 4.7 collective-permute-done.2.refs_3_
  30.1 10.9 %collective-permute-done.1.refs_2_ = bf16[4,64,384]{2,1,0:T(8,128)(2,1)} collective-permute-done((bf16[4,64,384]{2,1,0:T(8,128)(2,1)}, bf16[4,64,384]{2,1,0:T(8,128)(2,1)}, u32[]{:S(2)}, u32[]{:S(2)}) %collective-permute-start.1) | collective-permute-done | bytes 196640 | tf_op jit(solution)/shard_map/ppermute | solution.py:627
  41.0 4.1 all-to-all-start.1
  56.8 4.7 collective-permute-done.8
  69.8 4.2 project.1
  77.8 4.5 collective-permute-done.15.refs_3_
  101.7 4.8 all-to-all-start.2
  110.1 9.5 %collective-permute-done.19 = bf16[256,512]{1,0:T(8,128)(2,1)S(1)} collective-permute-done((bf16[256,512]{1,0:T(8,128)(2,1)S(1)}, bf16[256,512]{1,0:T(8,128)(2,1)S(1)}, u32[]{:S(2)}, u32[]{:S(2)}) %collective-permute-start.19) | collective-permute-done | bytes 262176 | tf_op jit(solution)/shard_map/ppermute | solution.py:630
  119.6 4.0 collective-permute-done.20
  123.6 4.4 collective-permute-done.21
  130.9 44.8 %all-to-all-done.2.refs_0_ = bf16[16,768,128]{2,1,0:T(8,128)(2,1)} async-done(((bf16[16,768,128]{2,1,0:T(8,128)(2,1)}), bf16[16,768,128]{2,1,0:T(8,128)(2,1)}, u32[]{:S(2)}, u32[]{:S(2)}) %all-to-all-start.2) | async-done | bytes 3145760 | tf_op jit(solution)/shard_map/all_to_all | solution.py:633
  182.8 12.3 %attend.1 = (bf16[4,256,512]{2,1,0:T(8,128)(2,1)S(1)}, bf16[256,2048]{1,0:T(8,128)(2,1)S(1)}) custom-call(bf16[256,1024]{1,0:T(8,128)(2,1)S(1)} %copy-done.24, f32[256,128]{1,0:T(8,128)S(1)} %copy-done.20, f32[256,128]{1,0:T(8,128)S(1)} %copy-done.19, s32[256,128]{1,0:T(8,128)S(1)} %broadcast_select_fusion.4.places_ref, ...), custom_call_target="tpu_custom_call" | custom-call | flops 3758096384 | bytes 8388608 | tf_op jit(solution)/shard_map/attend/pallas_call | solution.py:221
  198.8 9.0 %all-to-all-done.3 = bf16[4,64,2048]{2,1,0:T(8,128)(2,1)S(1)} async-done(((bf16[4,64,2048]{2,1,0:T(8,128)(2,1)}), bf16[4,64,2048]{2,1,0:T(8,128)(2,1)S(1)}, u32[]{:S(2)}, u32[]{:S(2)}) %all-to-all-start.3) | async-done | bytes 1048608 | tf_op jit(solution)/shard_map/all_to_all | solution.py:633
  216.6 5.2 %collective-permute-done.29 = bf16[64,2048]{1,0:T(8,128)(2,1)S(1)} collective-permute-done((bf16[64,2048]{1,0:T(8,128)(2,1)S(1)}, bf16[64,2048]{1,0:T(8,128)(2,1)S(1)}, u32[]{:S(2)}, u32[]{:S(2)}) %collective-permute-start.29) | collective-permute-done | bytes 262176 | tf_op jit(solution)/shard_map/ppermute | solution.py:627
  221.9 16.5 %collective-permute-done.28 = bf16[64,2048]{1,0:T(8,128)(2,1)S(1)} collective-permute-done((bf16[64,2048]{1,0:T(8,128)(2,1)S(1)}, bf16[64,2048]{1,0:T(8,128)(2,1)S(1)}, u32[]{:S(2)}, u32[]{:S(2)}) %collective-permute-start.28) | collective-permute-done | bytes 262176 | tf_op jit(solution)/shard_map/ppermute | solution.py:627
  243.2 11.8 %mlp.1 = (bf16[256,2048]{1,0:T(8,128)(2,1)S(1)}, bf16[3,704,256]{2,1,0:T(8,128)(2,1)S(1)}, bf16[3,704,256]{2,1,0:T(8,128)(2,1)S(1)}) custom-call(bf16[256,2048]{1,0:T(8,128)(2,1)S(1)} %pad_maximum_fusion.4.h_ref.value_ref.v, bf16[256,2048]{1,0:T(8,128)(2,1)S(1)} %bitcast.179, bf16[4,4,2112,128]{3,2,1,0:T(8,128)(2,1)S(1)} %bitcast.183, ...), custom_call_target="tpu_custom_call" | custom-call | flops 7381975040 | bytes 20447232 | tf_op jit(solution)/shard_map/mlp/pallas_call | solution.py:523
  256.0 4.2 all-to-all-start.4
  277.3 8.9 %all-to-all-done.4 = bf16[4,64,2048]{2,1,0:T(8,128)(2,1)} async-done(((bf16[4,64,2048]{2,1,0:T(8,128)(2,1)}), bf16[4,64,2048]{2,1,0:T(8,128)(2,1)}, u32[]{:S(2)}, u32[]{:S(2)}) %all-to-all-start.4) | async-done | bytes 1048608 | tf_op jit(solution)/shard_map/all_to_all | solution.py:633
  291.0 4.2 all-to-all-start.5
  303.8 4.4 unit_grads.11
  323.6 4.1 collective-permute-done.38.refs_0_
  331.5 4.3 all-to-all-start.6
  335.9 17.6 %attend_back.1 = (bf16[16,256,128]{2,1,0:T(8,128)(2,1)}, bf16[16,256,128]{2,1,0:T(8,128)(2,1)}, bf16[256,384]{1,0:T(8,128)(2,1)}, bf16[256,384]{1,0:T(8,128)(2,1...) custom-call(s32[3]{0:T(128)} %pad_add_fusion.1.at_ref, ...), custom_call_target="tpu_custom_call" | custom-call | flops 7516192768 | bytes 18874368 | tf_op jit(solution)/shard_map/attend_back/pallas_call | solution.py:327
  362.0 5.7 %collective-permute-done.41 = bf16[256,512]{1,0:T(8,128)(2,1)S(1)} collective-permute-done((bf16[256,512]{1,0:T(8,128)(2,1)S(1)}, bf16[256,512]{1,0:T(8,128)(2,1)S(1)}, u32[]{:S(2)}, u32[]{:S(2)}) %collective-permute-start.41) | collective-permute-done | bytes 262176 | tf_op jit(solution)/shard_map/ppermute | solution.py:630
  367.7 9.4 %collective-permute-done.43 = bf16[256,512]{1,0:T(8,128)(2,1)S(1)} collective-permute-done((bf16[256,512]{1,0:T(8,128)(2,1)S(1)}, bf16[256,512]{1,0:T(8,128)(2,1)S(1)}, u32[]{:S(2)}, u32[]{:S(2)}) %collective-permute-start.43) | collective-permute-done | bytes 262176 | tf_op jit(solution)/shard_map/ppermute | solution.py:630
  396.9 4.2 collective-permute-done.47.refs_1_
  401.1 4.6 collective-permute-done.48.refs_2_
  405.7 12.2 %all-to-all-done.7 = bf16[16,256,128]{2,1,0:T(8,128)(2,1)S(1)} async-done(((bf16[16,256,128]{2,1,0:T(8,128)(2,1)}), bf16[16,256,128]{2,1,0:T(8,128)(2,1)S(1)}, u32[]{:S(2)}, u32[]{:S(2)}) %all-to-all-start.7) | async-done | bytes 1048608 | tf_op jit(solution)/shard_map/all_to_all | solution.py:633
  432.1 5.0 latent_back.1
  456.4 9.1 %all-to-all-done.8 = bf16[4,1408,128]{2,1,0:T(8,128)(2,1)S(1)} async-done(((bf16[4,1408,128]{2,1,0:T(8,128)(2,1)}), bf16[4,1408,128]{2,1,0:T(8,128)(2,1)S(1)}, u32[]{:S(2)}, u32[]{:S(2)}) %all-to-all-start.8) | async-done | bytes 1441824 | tf_op jit(solution)/shard_map/all_to_all | solution.py:633
  465.6 4.2 all-to-all-start.9
  (458 shorter events, 234.6 us)
Async XLA Ops:
  24.3 16.6 %collective-permute-start.1 = (bf16[4,64,384]{2,1,0:T(8,128)(2,1)}, bf16[4,64,384]{2,1,0:T(8,128)(2,1)}, u32[]{:S(2)}, u32[]{:S(2)}) collective-permute-start(bf16[4,64,384]{2,1,0:T(8,128)(2,1)} %all-to-all-done.refs_0_), channel_id=1, source_target_pairs={{0,16},{2,18},{4,20},{6,22},{8,24},{10,26},{12,28},{14,30},{16,0},... | collective-permute-start | bytes 589832 | tf_op jit(solution)/shard_map/ppermute | solution.py:627
  41.0 59.4 %all-to-all-start.1 = ((bf16[4,2112,128]{2,1,0:T(8,128)(2,1)}), bf16[4,2112,128]{2,1,0:T(8,128)(2,1)S(1)}, u32[]{:S(2)}, u32[]{:S(2)}) async-start(bf16[4,2112,128]{2,1,0:T(8,128)(2,1)} %pad_maximum_fusion), calls=%async_computation.1 | async-start | bytes 4325376 | tf_op jit(solution)/shard_map/all_to_all | solution.py:633
  45.0 165.3 %all-gather.3.cloned.1.call-start = ((), (), s32[]{:S(2)}) async-start(), calls=%async_computation.12 | async-start | bytes 10813440 | tf_op jit(solution)/shard_map/all_gather | solution.py:801
  101.7 74.1 %all-to-all-start.2 = ((bf16[16,768,128]{2,1,0:T(8,128)(2,1)}), bf16[16,768,128]{2,1,0:T(8,128)(2,1)}, u32[]{:S(2)}, u32[]{:S(2)}) async-start(bf16[16,768,128]{2,1,0:T(8,128)(2,1)} %bitcast.18), calls=%async_computation.2 | async-start | bytes 6291456 | tf_op jit(solution)/shard_map/all_to_all | solution.py:633
  109.1 19.0 %collective-permute-start.21 = (bf16[256,512]{1,0:T(8,128)(2,1)S(1)}, bf16[256,512]{1,0:T(8,128)(2,1)S(1)}, u32[]{:S(2)}, u32[]{:S(2)}) collective-permute-start(bf16[256,512]{1,0:T(8,128)(2,1)S(1)} %get-tuple-element.338), channel_id=1, source_target_pairs={{0,6},{2,4},{4,2},{6,0},{8,14},{10,12},{12,10},{14,8},{16,22},{18,... | collective-permute-start | bytes 786440 | tf_op jit(solution)/shard_map/ppermute | solution.py:630
  177.4 30.3 %all-to-all-start.3 = ((bf16[4,64,2048]{2,1,0:T(8,128)(2,1)}), bf16[4,64,2048]{2,1,0:T(8,128)(2,1)S(1)}, u32[]{:S(2)}, u32[]{:S(2)}) async-start(bf16[4,64,2048]{2,1,0:T(8,128)(2,1)} %tile.12), calls=%async_computation.3 | async-start | bytes 2097152 | tf_op jit(solution)/shard_map/all_to_all | solution.py:633
  210.4 28.3 %collective-permute-start.30 = (bf16[4,4,2112,128]{3,2,1,0:T(8,128)(2,1)}, bf16[4,4,2112,128]{3,2,1,0:T(8,128)(2,1)}, u32[]{:S(2)}, u32[]{:S(2)}) collective-permute-start(bf16[4,4,2112,128]{3,2,1,0:T(8,128)(2,1)} %bitcast.182), channel_id=1, source_target_pairs={{0,1},{1,0},{2,3},{3,2},{4,5},{5,4},{6,7},{7,6},{8,9},{9,8},{10,11... | collective-permute-start | bytes 25952264 | tf_op jit(solution)/shard_map/ppermute | solution.py:619
  215.1 23.2 %collective-permute-start.28 = (bf16[64,2048]{1,0:T(8,128)(2,1)S(1)}, bf16[64,2048]{1,0:T(8,128)(2,1)S(1)}, u32[]{:S(2)}, u32[]{:S(2)}) collective-permute-start(bf16[64,2048]{1,0:T(8,128)(2,1)S(1)} %multiply_convert_fusion), channel_id=1, source_target_pairs={{0,16},{2,18},{4,20},{6,22},{8,24},{10,26},{12,28},{14,30},{16,0},... | collective-permute-start | bytes 786440 | tf_op jit(solution)/shard_map/ppermute | solution.py:627
  215.1 23.2 %collective-permute-start.27 = (bf16[64,2048]{1,0:T(8,128)(2,1)S(1)}, bf16[64,2048]{1,0:T(8,128)(2,1)S(1)}, u32[]{:S(2)}, u32[]{:S(2)}) collective-permute-start(bf16[64,2048]{1,0:T(8,128)(2,1)S(1)} %multiply_convert_fusion), channel_id=1, source_target_pairs={{0,8},{2,10},{4,12},{6,14},{8,16},{10,18},{12,20},{14,22},{16,24},... | collective-permute-start | bytes 786440 | tf_op jit(solution)/shard_map/ppermute | solution.py:627
  256.0 30.2 %all-to-all-start.4 = ((bf16[4,64,2048]{2,1,0:T(8,128)(2,1)}), bf16[4,64,2048]{2,1,0:T(8,128)(2,1)}, u32[]{:S(2)}, u32[]{:S(2)}) async-start(bf16[4,64,2048]{2,1,0:T(8,128)(2,1)} %bitcast.187), calls=%async_computation.4 | async-start | bytes 2097152 | tf_op jit(solution)/shard_map/all_to_all | solution.py:633
  286.2 17.6 %collective-permute-start.33 = (bf16[4,4,704,128]{3,2,1,0:T(8,128)(2,1)}, bf16[4,4,704,128]{3,2,1,0:T(8,128)(2,1)}, u32[]{:S(2)}, u32[]{:S(2)}) collective-permute-start(bf16[4,4,704,128]{3,2,1,0:T(8,128)(2,1)} %copy-done.16), channel_id=1, source_target_pairs={{0,1},{1,0},{2,3},{3,2},{4,5},{5,4},{6,7},{7,6},{8,9},{9,8},{10,11... | collective-permute-start | bytes 8650760 | tf_op jit(solution)/shard_map/ppermute | solution.py:619
  286.7 21.5 %collective-permute-start.31 = (bf16[4,4,704,128]{3,2,1,0:T(8,128)(2,1)}, bf16[4,4,704,128]{3,2,1,0:T(8,128)(2,1)}, u32[]{:S(2)}, u32[]{:S(2)}) collective-permute-start(bf16[4,4,704,128]{3,2,1,0:T(8,128)(2,1)} %copy-done.15), channel_id=1, source_target_pairs={{0,1},{1,0},{2,3},{3,2},{4,5},{5,4},{6,7},{7,6},{8,9},{9,8},{10,11... | collective-permute-start | bytes 8650760 | tf_op jit(solution)/shard_map/ppermute | solution.py:619
  291.0 29.1 %all-to-all-start.5 = ((bf16[4,64,2048]{2,1,0:T(8,128)(2,1)}), bf16[4,64,2048]{2,1,0:T(8,128)(2,1)}, u32[]{:S(2)}, u32[]{:S(2)}) async-start(bf16[4,64,2048]{2,1,0:T(8,128)(2,1)} %tile.28), calls=%async_computation.5 | async-start | bytes 2097152 | tf_op jit(solution)/shard_map/all_to_all | solution.py:636
  295.2 122.7 %reduce-scatter.7.cloned.1.call-start = ((), (), s32[]{:S(2)}) async-start(), calls=%async_computation.13 | async-start | bytes 7208960
  296.2 20.2 %collective-permute-start.34 = (bf16[64,2048]{1,0:T(8,128)(2,1)}, bf16[64,2048]{1,0:T(8,128)(2,1)S(1)}, u32[]{:S(2)}, u32[]{:S(2)}) collective-permute-start(bf16[64,2048]{1,0:T(8,128)(2,1)} %get-tuple-element.144), channel_id=1, source_target_pairs={{0,24},{2,26},{4,28},{6,30},{8,0},{10,2},{12,4},{14,6},{16,8},{18,... | collective-permute-start | bytes 786440 | tf_op jit(solution)/shard_map/ppermute | solution.py:627
  297.7 22.4 %collective-permute-start.35 = (bf16[64,2048]{1,0:T(8,128)(2,1)}, bf16[64,2048]{1,0:T(8,128)(2,1)S(1)}, u32[]{:S(2)}, u32[]{:S(2)}) collective-permute-start(bf16[64,2048]{1,0:T(8,128)(2,1)} %get-tuple-element.145), channel_id=1, source_target_pairs={{0,16},{2,18},{4,20},{6,22},{8,24},{10,26},{12,28},{14,30},{16,0},... | collective-permute-start | bytes 786440 | tf_op jit(solution)/shard_map/ppermute | solution.py:627
  297.7 22.4 %collective-permute-start.36 = (bf16[64,2048]{1,0:T(8,128)(2,1)S(1)}, bf16[64,2048]{1,0:T(8,128)(2,1)S(1)}, u32[]{:S(2)}, u32[]{:S(2)}) collective-permute-start(bf16[64,2048]{1,0:T(8,128)(2,1)S(1)} %get-tuple-element.146), channel_id=1, source_target_pairs={{0,8},{2,10},{4,12},{6,14},{8,16},{10,18},{12,20},{14,22},{16,24},... | collective-permute-start | bytes 786440 | tf_op jit(solution)/shard_map/ppermute | solution.py:627
  331.5 58.4 %all-to-all-start.6 = ((bf16[16,512,128]{2,1,0:T(8,128)(2,1)}), bf16[16,512,128]{2,1,0:T(8,128)(2,1)S(1)}, u32[]{:S(2)}, u32[]{:S(2)}) async-start(bf16[16,512,128]{2,1,0:T(8,128)(2,1)} %out_grads.3), calls=%async_computation.6 | async-start | bytes 4194304 | tf_op jit(solution)/shard_map/all_to_all | solution.py:633
  335.8 120.7 %reduce-scatter.9.cloned.1.call-start = ((), (), s32[]{:S(2)}) async-start(), calls=%async_computation.14 | async-start | bytes 3604480
  353.6 31.0 %collective-permute-start.39 = (bf16[16,256,128]{2,1,0:T(8,128)(2,1)}, bf16[16,256,128]{2,1,0:T(8,128)(2,1)S(1)}, u32[]{:S(2)}, u32[]{:S(2)}) collective-permute-start(bf16[16,256,128]{2,1,0:T(8,128)(2,1)} %get-tuple-element.157), channel_id=1, source_target_pairs={{0,1},{1,0},{2,3},{3,2},{4,5},{5,4},{6,7},{7,6},{8,9},{9,8},{10,11... | collective-permute-start | bytes 3145736 | tf_op jit(solution)/shard_map/ppermute | solution.py:619
  360.2 16.9 %collective-permute-start.43 = (bf16[256,512]{1,0:T(8,128)(2,1)S(1)}, bf16[256,512]{1,0:T(8,128)(2,1)S(1)}, u32[]{:S(2)}, u32[]{:S(2)}) collective-permute-start(bf16[256,512]{1,0:T(8,128)(2,1)S(1)} %get-tuple-element.255), channel_id=1, source_target_pairs={{0,6},{2,4},{4,2},{6,0},{8,14},{10,12},{12,10},{14,8},{16,22},{18,... | collective-permute-start | bytes 786440 | tf_op jit(solution)/shard_map/ppermute | solution.py:630
  389.8 28.1 %all-to-all-start.7 = ((bf16[16,256,128]{2,1,0:T(8,128)(2,1)}), bf16[16,256,128]{2,1,0:T(8,128)(2,1)S(1)}, u32[]{:S(2)}, u32[]{:S(2)}) async-start(bf16[16,256,128]{2,1,0:T(8,128)(2,1)} %add_convert_fusion.1), calls=%async_computation.7 | async-start | bytes 2097152 | tf_op jit(solution)/shard_map/all_to_all | solution.py:633
  418.9 46.7 %all-to-all-start.8 = ((bf16[4,1408,128]{2,1,0:T(8,128)(2,1)}), bf16[4,1408,128]{2,1,0:T(8,128)(2,1)S(1)}, u32[]{:S(2)}, u32[]{:S(2)}) async-start(bf16[4,1408,128]{2,1,0:T(8,128)(2,1)} %bitcast.198), calls=%async_computation.8 | async-start | bytes 2883584 | tf_op jit(solution)/shard_map/all_to_all | solution.py:633
  438.2 31.6 %collective-permute-start.54 = (bf16[64,2048]{1,0:T(8,128)(2,1)}, bf16[64,2048]{1,0:T(8,128)(2,1)}, u32[]{:S(2)}, u32[]{:S(2)}) collective-permute-start(bf16[64,2048]{1,0:T(8,128)(2,1)} %get-tuple-element.178), channel_id=1, source_target_pairs={{0,4},{2,6},{4,0},{6,2},{8,12},{10,14},{12,8},{14,10},{16,20},{18,... | collective-permute-start | bytes 786440 | tf_op jit(solution)/shard_map/ppermute | solution.py:630
  439.9 32.5 %collective-permute-start.55 = (bf16[64,2048]{1,0:T(8,128)(2,1)}, bf16[64,2048]{1,0:T(8,128)(2,1)}, u32[]{:S(2)}, u32[]{:S(2)}) collective-permute-start(bf16[64,2048]{1,0:T(8,128)(2,1)} %get-tuple-element.179), channel_id=1, source_target_pairs={{0,6},{2,4},{4,2},{6,0},{8,14},{10,12},{12,10},{14,8},{16,22},{18,... | collective-permute-start | bytes 786440 | tf_op jit(solution)/shard_map/ppermute | solution.py:630
  443.3 29.8 %collective-permute-start.59 = (bf16[4,64,384]{2,1,0:T(8,128)(2,1)}, bf16[4,64,384]{2,1,0:T(8,128)(2,1)}, u32[]{:S(2)}, u32[]{:S(2)}) collective-permute-start(bf16[4,64,384]{2,1,0:T(8,128)(2,1)} %get-tuple-element.283), channel_id=1, source_target_pairs={{0,8},{2,10},{4,12},{6,14},{8,16},{10,18},{12,20},{14,22},{16,24},... | collective-permute-start | bytes 589832 | tf_op jit(solution)/shard_map/ppermute | solution.py:627
  445.3 28.1 %collective-permute-start.58 = (bf16[4,64,384]{2,1,0:T(8,128)(2,1)}, bf16[4,64,384]{2,1,0:T(8,128)(2,1)}, u32[]{:S(2)}, u32[]{:S(2)}) collective-permute-start(bf16[4,64,384]{2,1,0:T(8,128)(2,1)} %get-tuple-element.284), channel_id=1, source_target_pairs={{0,16},{2,18},{4,20},{6,22},{8,24},{10,26},{12,28},{14,30},{16,0},... | collective-permute-start | bytes 589832 | tf_op jit(solution)/shard_map/ppermute | solution.py:627
  447.6 25.8 %collective-permute-start.57 = (bf16[4,64,384]{2,1,0:T(8,128)(2,1)}, bf16[4,64,384]{2,1,0:T(8,128)(2,1)}, u32[]{:S(2)}, u32[]{:S(2)}) collective-permute-start(bf16[4,64,384]{2,1,0:T(8,128)(2,1)} %get-tuple-element.285), channel_id=1, source_target_pairs={{0,24},{2,26},{4,28},{6,30},{8,0},{10,2},{12,4},{14,6},{16,8},{18,... | collective-permute-start | bytes 589832 | tf_op jit(solution)/shard_map/ppermute | solution.py:627
  465.6 28.0 %all-to-all-start.9 = ((bf16[4,704,128]{2,1,0:T(8,128)(2,1)}), bf16[4,704,128]{2,1,0:T(8,128)(2,1)}, u32[]{:S(2)}, u32[]{:S(2)}) async-start(bf16[4,704,128]{2,1,0:T(8,128)(2,1)} %bitcast.203), calls=%async_computation.9 | async-start | bytes 1441792 | tf_op jit(solution)/shard_map/all_to_all | solution.py:633
  469.8 19.7 %collective-permute-start.66 = (bf16[768,128]{1,0:T(8,128)(2,1)}, bf16[768,128]{1,0:T(8,128)(2,1)}, u32[]{:S(2)}, u32[]{:S(2)}) collective-permute-start(bf16[768,128]{1,0:T(8,128)(2,1)} %get-tuple-element.279), channel_id=1, source_target_pairs={{0,6},{2,4},{4,2},{6,0},{8,14},{10,12},{12,10},{14,8},{16,22},{18,... | collective-permute-start | bytes 589832 | tf_op jit(solution)/shard_map/ppermute | solution.py:630
  472.4 18.9 %collective-permute-start.64 = (bf16[768,128]{1,0:T(8,128)(2,1)}, bf16[768,128]{1,0:T(8,128)(2,1)}, u32[]{:S(2)}, u32[]{:S(2)}) collective-permute-start(bf16[768,128]{1,0:T(8,128)(2,1)} %get-tuple-element.281), channel_id=1, source_target_pairs={{0,2},{2,0},{4,6},{6,4},{8,10},{10,8},{12,14},{14,12},{16,18},{18,... | collective-permute-start | bytes 589832 | tf_op jit(solution)/shard_map/ppermute | solution.py:630
  473.1 18.3 %collective-permute-start.65 = (bf16[768,128]{1,0:T(8,128)(2,1)}, bf16[768,128]{1,0:T(8,128)(2,1)}, u32[]{:S(2)}, u32[]{:S(2)}) collective-permute-start(bf16[768,128]{1,0:T(8,128)(2,1)} %get-tuple-element.282), channel_id=1, source_target_pairs={{0,4},{2,6},{4,0},{6,2},{8,12},{10,14},{12,8},{14,10},{16,20},{18,... | collective-permute-start | bytes 589832 | tf_op jit(solution)/shard_map/ppermute | solution.py:630
  (134 other events, 1134.3 us)
Sparse Core Ops, SparseCore 0:
  101.8 95.7 all-gather.2
  320.3 71.8 reduce-scatter.6
  395.3 42.9 reduce-scatter.8

commit v8 on v7

--- a/solution.py
+++ b/solution.py
@@ -14,8 +14,8 @@
 HEAD = 256
 SQUARE = 4
 VMEM_LIMIT = 56 * 1024 * 1024
-MLP_LIMIT = 26 * 1024 * 1024
-ATTEND_LIMIT = 22 * 1024 * 1024
+MLP_LIMIT = 23 * 1024 * 1024
+ATTEND_LIMIT = 40 * 1024 * 1024
 GRADS_LIMIT = 16 * 1024 * 1024
 BF16 = jnp.bfloat16
 F32 = jnp.float32

time: 522 us -> 522 us (level)
  no operation moved by 1% of the time
where the time goes in v8:
time: 522 us; the launch traced here: 513 us
  waiting for transfers between devices  210 us (40%)
  starting transfers between devices  114 us (22%)
  Pallas kernels  76.4 us (15%)
  local copies, waits for them, and re-layouts  53.4 us (10%)
  other arithmetic  43.6 us (8%)
  between operations  15.4 us (3%)
    all_to_all x8, waiting for transfers between devices, line_exchange(): lax.all_to_all(value, 'seq', 0, 0, axis_index_groups=lines, tiled=True)  84 us
    ppermute x33, waiting for transfers between devices, within(): return lax.ppermute(value, 'seq', [(i, i ^ flip) for i in range(chips)])  66.2 us
    ppermute x18, waiting for transfers between devices, along(): return lax.ppermute(value, 'seq', pairs)  49.5 us
    ppermute x33, starting transfers between devices, within(): return lax.ppermute(value, 'seq', [(i, i ^ flip) for i in range(chips)])  39.1 us
    unnamed x185, local copies, waits for them, and re-layouts  37.8 us
    all_to_all x8, starting transfers between devices, line_exchange(): lax.all_to_all(value, 'seq', 0, 0, axis_index_groups=lines, tiled=True)  32.4 us
    ppermute x18, starting transfers between devices, along(): return lax.ppermute(value, 'seq', pairs)  29.9 us
    pallas_call x1, Pallas kernels, attend_back(): pl.pallas_call(functools.partial(attend_back_kernel, pair, len(weights)),...  17.6 us
  transfers between devices with their start and end apart: 82, of which 38 were waited for; matrix products, arithmetic and copies ran while one was open for 11% of the time, Pallas kernels for 13%

profile of v8, /device:TPU:0, one launch (start us, length us, event | category | flops | bytes accessed | tf_op | source)
XLA Modules:
  0.0 512.5 jit_solution(3956372786027073255)
XLA Ops:
  10.0 5.2 %all-to-all-start = ((bf16[4,64,384]{2,1,0:T(8,128)(2,1)}), bf16[4,64,384]{2,1,0:T(8,128)(2,1)}, u32[]{:S(2)}, u32[]{:S(2)}) async-start(bf16[4,64,384]{2,1,0:T(8,128)(2,1)} %pad_maximum_fusion.16), calls=%async_computation | async-start | bytes 393216 | tf_op jit(solution)/shard_map/all_to_all | solution.py:636
  25.4 4.7 collective-permute-done.2.refs_3_
  30.1 10.9 %collective-permute-done.1.refs_2_ = bf16[4,64,384]{2,1,0:T(8,128)(2,1)} collective-permute-done((bf16[4,64,384]{2,1,0:T(8,128)(2,1)}, bf16[4,64,384]{2,1,0:T(8,128)(2,1)}, u32[]{:S(2)}, u32[]{:S(2)}) %collective-permute-start.1) | collective-permute-done | bytes 196640 | tf_op jit(solution)/shard_map/ppermute | solution.py:627
  41.0 4.1 all-to-all-start.1
  56.8 4.7 collective-permute-done.8
  69.8 4.2 project.1
  77.8 4.5 collective-permute-done.15.refs_3_
  101.7 4.8 all-to-all-start.2
  110.1 9.5 %collective-permute-done.19 = bf16[256,512]{1,0:T(8,128)(2,1)S(1)} collective-permute-done((bf16[256,512]{1,0:T(8,128)(2,1)S(1)}, bf16[256,512]{1,0:T(8,128)(2,1)S(1)}, u32[]{:S(2)}, u32[]{:S(2)}) %collective-permute-start.19) | collective-permute-done | bytes 262176 | tf_op jit(solution)/shard_map/ppermute | solution.py:630
  119.6 4.0 collective-permute-done.20
  123.6 4.4 collective-permute-done.21
  130.9 44.8 %all-to-all-done.2.refs_0_ = bf16[16,768,128]{2,1,0:T(8,128)(2,1)} async-done(((bf16[16,768,128]{2,1,0:T(8,128)(2,1)}), bf16[16,768,128]{2,1,0:T(8,128)(2,1)}, u32[]{:S(2)}, u32[]{:S(2)}) %all-to-all-start.2) | async-done | bytes 3145760 | tf_op jit(solution)/shard_map/all_to_all | solution.py:633
  182.8 12.3 %attend.1 = (bf16[4,256,512]{2,1,0:T(8,128)(2,1)S(1)}, bf16[256,2048]{1,0:T(8,128)(2,1)S(1)}) custom-call(bf16[256,1024]{1,0:T(8,128)(2,1)S(1)} %copy-done.24, f32[256,128]{1,0:T(8,128)S(1)} %copy-done.20, f32[256,128]{1,0:T(8,128)S(1)} %copy-done.19, s32[256,128]{1,0:T(8,128)S(1)} %broadcast_select_fusion.4.places_ref, ...), custom_call_target="tpu_custom_call" | custom-call | flops 3758096384 | bytes 8388608 | tf_op jit(solution)/shard_map/attend/pallas_call | solution.py:221
  198.8 9.0 %all-to-all-done.3 = bf16[4,64,2048]{2,1,0:T(8,128)(2,1)S(1)} async-done(((bf16[4,64,2048]{2,1,0:T(8,128)(2,1)}), bf16[4,64,2048]{2,1,0:T(8,128)(2,1)S(1)}, u32[]{:S(2)}, u32[]{:S(2)}) %all-to-all-start.3) | async-done | bytes 1048608 | tf_op jit(solution)/shard_map/all_to_all | solution.py:633
  216.6 5.2 %collective-permute-done.29 = bf16[64,2048]{1,0:T(8,128)(2,1)S(1)} collective-permute-done((bf16[64,2048]{1,0:T(8,128)(2,1)S(1)}, bf16[64,2048]{1,0:T(8,128)(2,1)S(1)}, u32[]{:S(2)}, u32[]{:S(2)}) %collective-permute-start.29) | collective-permute-done | bytes 262176 | tf_op jit(solution)/shard_map/ppermute | solution.py:627
  221.9 16.5 %collective-permute-done.28 = bf16[64,2048]{1,0:T(8,128)(2,1)S(1)} collective-permute-done((bf16[64,2048]{1,0:T(8,128)(2,1)S(1)}, bf16[64,2048]{1,0:T(8,128)(2,1)S(1)}, u32[]{:S(2)}, u32[]{:S(2)}) %collective-permute-start.28) | collective-permute-done | bytes 262176 | tf_op jit(solution)/shard_map/ppermute | solution.py:627
  243.2 11.8 %mlp.1 = (bf16[256,2048]{1,0:T(8,128)(2,1)S(1)}, bf16[3,704,256]{2,1,0:T(8,128)(2,1)S(1)}, bf16[3,704,256]{2,1,0:T(8,128)(2,1)S(1)}) custom-call(bf16[256,2048]{1,0:T(8,128)(2,1)S(1)} %pad_maximum_fusion.4.h_ref.value_ref.v, bf16[256,2048]{1,0:T(8,128)(2,1)S(1)} %bitcast.179, bf16[4,4,2112,128]{3,2,1,0:T(8,128)(2,1)S(1)} %bitcast.183, ...), custom_call_target="tpu_custom_call" | custom-call | flops 7381975040 | bytes 20447232 | tf_op jit(solution)/shard_map/mlp/pallas_call | solution.py:523
  256.0 4.2 all-to-all-start.4
  277.3 8.9 %all-to-all-done.4 = bf16[4,64,2048]{2,1,0:T(8,128)(2,1)} async-done(((bf16[4,64,2048]{2,1,0:T(8,128)(2,1)}), bf16[4,64,2048]{2,1,0:T(8,128)(2,1)}, u32[]{:S(2)}, u32[]{:S(2)}) %all-to-all-start.4) | async-done | bytes 1048608 | tf_op jit(solution)/shard_map/all_to_all | solution.py:633
  291.0 4.2 all-to-all-start.5
  303.8 4.4 unit_grads.11
  323.6 4.1 collective-permute-done.38.refs_0_
  331.5 4.3 all-to-all-start.6
  335.9 17.6 %attend_back.1 = (bf16[16,256,128]{2,1,0:T(8,128)(2,1)}, bf16[16,256,128]{2,1,0:T(8,128)(2,1)}, bf16[256,384]{1,0:T(8,128)(2,1)}, bf16[256,384]{1,0:T(8,128)(2,1...) custom-call(s32[3]{0:T(128)} %pad_add_fusion.1.at_ref, ...), custom_call_target="tpu_custom_call" | custom-call | flops 7516192768 | bytes 18874368 | tf_op jit(solution)/shard_map/attend_back/pallas_call | solution.py:327
  362.0 5.7 %collective-permute-done.41 = bf16[256,512]{1,0:T(8,128)(2,1)S(1)} collective-permute-done((bf16[256,512]{1,0:T(8,128)(2,1)S(1)}, bf16[256,512]{1,0:T(8,128)(2,1)S(1)}, u32[]{:S(2)}, u32[]{:S(2)}) %collective-permute-start.41) | collective-permute-done | bytes 262176 | tf_op jit(solution)/shard_map/ppermute | solution.py:630
  367.7 9.4 %collective-permute-done.43 = bf16[256,512]{1,0:T(8,128)(2,1)S(1)} collective-permute-done((bf16[256,512]{1,0:T(8,128)(2,1)S(1)}, bf16[256,512]{1,0:T(8,128)(2,1)S(1)}, u32[]{:S(2)}, u32[]{:S(2)}) %collective-permute-start.43) | collective-permute-done | bytes 262176 | tf_op jit(solution)/shard_map/ppermute | solution.py:630
  396.9 4.2 collective-permute-done.47.refs_1_
  401.1 4.6 collective-permute-done.48.refs_2_
  405.7 12.2 %all-to-all-done.7 = bf16[16,256,128]{2,1,0:T(8,128)(2,1)S(1)} async-done(((bf16[16,256,128]{2,1,0:T(8,128)(2,1)}), bf16[16,256,128]{2,1,0:T(8,128)(2,1)S(1)}, u32[]{:S(2)}, u32[]{:S(2)}) %all-to-all-start.7) | async-done | bytes 1048608 | tf_op jit(solution)/shard_map/all_to_all | solution.py:633
  432.1 5.0 latent_back.1
  456.4 9.1 %all-to-all-done.8 = bf16[4,1408,128]{2,1,0:T(8,128)(2,1)S(1)} async-done(((bf16[4,1408,128]{2,1,0:T(8,128)(2,1)}), bf16[4,1408,128]{2,1,0:T(8,128)(2,1)S(1)}, u32[]{:S(2)}, u32[]{:S(2)}) %all-to-all-start.8) | async-done | bytes 1441824 | tf_op jit(solution)/shard_map/all_to_all | solution.py:633
  465.6 4.2 all-to-all-start.9
  (458 shorter events, 234.6 us)
Async XLA Ops:
  24.3 16.6 %collective-permute-start.1 = (bf16[4,64,384]{2,1,0:T(8,128)(2,1)}, bf16[4,64,384]{2,1,0:T(8,128)(2,1)}, u32[]{:S(2)}, u32[]{:S(2)}) collective-permute-start(bf16[4,64,384]{2,1,0:T(8,128)(2,1)} %all-to-all-done.refs_0_), channel_id=1, source_target_pairs={{0,16},{2,18},{4,20},{6,22},{8,24},{10,26},{12,28},{14,30},{16,0},... | collective-permute-start | bytes 589832 | tf_op jit(solution)/shard_map/ppermute | solution.py:627
  41.0 59.4 %all-to-all-start.1 = ((bf16[4,2112,128]{2,1,0:T(8,128)(2,1)}), bf16[4,2112,128]{2,1,0:T(8,128)(2,1)S(1)}, u32[]{:S(2)}, u32[]{:S(2)}) async-start(bf16[4,2112,128]{2,1,0:T(8,128)(2,1)} %pad_maximum_fusion), calls=%async_computation.1 | async-start | bytes 4325376 | tf_op jit(solution)/shard_map/all_to_all | solution.py:633
  45.0 165.3 %all-gather.3.cloned.1.call-start = ((), (), s32[]{:S(2)}) async-start(), calls=%async_computation.12 | async-start | bytes 10813440 | tf_op jit(solution)/shard_map/all_gather | solution.py:801
  101.7 74.1 %all-to-all-start.2 = ((bf16[16,768,128]{2,1,0:T(8,128)(2,1)}), bf16[16,768,128]{2,1,0:T(8,128)(2,1)}, u32[]{:S(2)}, u32[]{:S(2)}) async-start(bf16[16,768,128]{2,1,0:T(8,128)(2,1)} %bitcast.18), calls=%async_computation.2 | async-start | bytes 6291456 | tf_op jit(solution)/shard_map/all_to_all | solution.py:633
  109.1 19.0 %collective-permute-start.21 = (bf16[256,512]{1,0:T(8,128)(2,1)S(1)}, bf16[256,512]{1,0:T(8,128)(2,1)S(1)}, u32[]{:S(2)}, u32[]{:S(2)}) collective-permute-start(bf16[256,512]{1,0:T(8,128)(2,1)S(1)} %get-tuple-element.338), channel_id=1, source_target_pairs={{0,6},{2,4},{4,2},{6,0},{8,14},{10,12},{12,10},{14,8},{16,22},{18,... | collective-permute-start | bytes 786440 | tf_op jit(solution)/shard_map/ppermute | solution.py:630
  177.4 30.3 %all-to-all-start.3 = ((bf16[4,64,2048]{2,1,0:T(8,128)(2,1)}), bf16[4,64,2048]{2,1,0:T(8,128)(2,1)S(1)}, u32[]{:S(2)}, u32[]{:S(2)}) async-start(bf16[4,64,2048]{2,1,0:T(8,128)(2,1)} %tile.12), calls=%async_computation.3 | async-start | bytes 2097152 | tf_op jit(solution)/shard_map/all_to_all | solution.py:633
  210.4 28.3 %collective-permute-start.30 = (bf16[4,4,2112,128]{3,2,1,0:T(8,128)(2,1)}, bf16[4,4,2112,128]{3,2,1,0:T(8,128)(2,1)}, u32[]{:S(2)}, u32[]{:S(2)}) collective-permute-start(bf16[4,4,2112,128]{3,2,1,0:T(8,128)(2,1)} %bitcast.182), channel_id=1, source_target_pairs={{0,1},{1,0},{2,3},{3,2},{4,5},{5,4},{6,7},{7,6},{8,9},{9,8},{10,11... | collective-permute-start | bytes 25952264 | tf_op jit(solution)/shard_map/ppermute | solution.py:619
  215.1 23.2 %collective-permute-start.28 = (bf16[64,2048]{1,0:T(8,128)(2,1)S(1)}, bf16[64,2048]{1,0:T(8,128)(2,1)S(1)}, u32[]{:S(2)}, u32[]{:S(2)}) collective-permute-start(bf16[64,2048]{1,0:T(8,128)(2,1)S(1)} %multiply_convert_fusion), channel_id=1, source_target_pairs={{0,16},{2,18},{4,20},{6,22},{8,24},{10,26},{12,28},{14,30},{16,0},... | collective-permute-start | bytes 786440 | tf_op jit(solution)/shard_map/ppermute | solution.py:627
  215.1 23.2 %collective-permute-start.27 = (bf16[64,2048]{1,0:T(8,128)(2,1)S(1)}, bf16[64,2048]{1,0:T(8,128)(2,1)S(1)}, u32[]{:S(2)}, u32[]{:S(2)}) collective-permute-start(bf16[64,2048]{1,0:T(8,128)(2,1)S(1)} %multiply_convert_fusion), channel_id=1, source_target_pairs={{0,8},{2,10},{4,12},{6,14},{8,16},{10,18},{12,20},{14,22},{16,24},... | collective-permute-start | bytes 786440 | tf_op jit(solution)/shard_map/ppermute | solution.py:627
  256.0 30.2 %all-to-all-start.4 = ((bf16[4,64,2048]{2,1,0:T(8,128)(2,1)}), bf16[4,64,2048]{2,1,0:T(8,128)(2,1)}, u32[]{:S(2)}, u32[]{:S(2)}) async-start(bf16[4,64,2048]{2,1,0:T(8,128)(2,1)} %bitcast.187), calls=%async_computation.4 | async-start | bytes 2097152 | tf_op jit(solution)/shard_map/all_to_all | solution.py:633
  286.2 17.6 %collective-permute-start.33 = (bf16[4,4,704,128]{3,2,1,0:T(8,128)(2,1)}, bf16[4,4,704,128]{3,2,1,0:T(8,128)(2,1)}, u32[]{:S(2)}, u32[]{:S(2)}) collective-permute-start(bf16[4,4,704,128]{3,2,1,0:T(8,128)(2,1)} %copy-done.16), channel_id=1, source_target_pairs={{0,1},{1,0},{2,3},{3,2},{4,5},{5,4},{6,7},{7,6},{8,9},{9,8},{10,11... | collective-permute-start | bytes 8650760 | tf_op jit(solution)/shard_map/ppermute | solution.py:619
  286.7 21.5 %collective-permute-start.31 = (bf16[4,4,704,128]{3,2,1,0:T(8,128)(2,1)}, bf16[4,4,704,128]{3,2,1,0:T(8,128)(2,1)}, u32[]{:S(2)}, u32[]{:S(2)}) collective-permute-start(bf16[4,4,704,128]{3,2,1,0:T(8,128)(2,1)} %copy-done.15), channel_id=1, source_target_pairs={{0,1},{1,0},{2,3},{3,2},{4,5},{5,4},{6,7},{7,6},{8,9},{9,8},{10,11... | collective-permute-start | bytes 8650760 | tf_op jit(solution)/shard_map/ppermute | solution.py:619
  291.0 29.1 %all-to-all-start.5 = ((bf16[4,64,2048]{2,1,0:T(8,128)(2,1)}), bf16[4,64,2048]{2,1,0:T(8,128)(2,1)}, u32[]{:S(2)}, u32[]{:S(2)}) async-start(bf16[4,64,2048]{2,1,0:T(8,128)(2,1)} %tile.28), calls=%async_computation.5 | async-start | bytes 2097152 | tf_op jit(solution)/shard_map/all_to_all | solution.py:636
  295.2 122.7 %reduce-scatter.7.cloned.1.call-start = ((), (), s32[]{:S(2)}) async-start(), calls=%async_computation.13 | async-start | bytes 7208960
  296.2 20.2 %collective-permute-start.34 = (bf16[64,2048]{1,0:T(8,128)(2,1)}, bf16[64,2048]{1,0:T(8,128)(2,1)S(1)}, u32[]{:S(2)}, u32[]{:S(2)}) collective-permute-start(bf16[64,2048]{1,0:T(8,128)(2,1)} %get-tuple-element.144), channel_id=1, source_target_pairs={{0,24},{2,26},{4,28},{6,30},{8,0},{10,2},{12,4},{14,6},{16,8},{18,... | collective-permute-start | bytes 786440 | tf_op jit(solution)/shard_map/ppermute | solution.py:627
  297.7 22.4 %collective-permute-start.35 = (bf16[64,2048]{1,0:T(8,128)(2,1)}, bf16[64,2048]{1,0:T(8,128)(2,1)S(1)}, u32[]{:S(2)}, u32[]{:S(2)}) collective-permute-start(bf16[64,2048]{1,0:T(8,128)(2,1)} %get-tuple-element.145), channel_id=1, source_target_pairs={{0,16},{2,18},{4,20},{6,22},{8,24},{10,26},{12,28},{14,30},{16,0},... | collective-permute-start | bytes 786440 | tf_op jit(solution)/shard_map/ppermute | solution.py:627
  297.7 22.4 %collective-permute-start.36 = (bf16[64,2048]{1,0:T(8,128)(2,1)S(1)}, bf16[64,2048]{1,0:T(8,128)(2,1)S(1)}, u32[]{:S(2)}, u32[]{:S(2)}) collective-permute-start(bf16[64,2048]{1,0:T(8,128)(2,1)S(1)} %get-tuple-element.146), channel_id=1, source_target_pairs={{0,8},{2,10},{4,12},{6,14},{8,16},{10,18},{12,20},{14,22},{16,24},... | collective-permute-start | bytes 786440 | tf_op jit(solution)/shard_map/ppermute | solution.py:627
  331.5 58.4 %all-to-all-start.6 = ((bf16[16,512,128]{2,1,0:T(8,128)(2,1)}), bf16[16,512,128]{2,1,0:T(8,128)(2,1)S(1)}, u32[]{:S(2)}, u32[]{:S(2)}) async-start(bf16[16,512,128]{2,1,0:T(8,128)(2,1)} %out_grads.3), calls=%async_computation.6 | async-start | bytes 4194304 | tf_op jit(solution)/shard_map/all_to_all | solution.py:633
  335.8 120.7 %reduce-scatter.9.cloned.1.call-start = ((), (), s32[]{:S(2)}) async-start(), calls=%async_computation.14 | async-start | bytes 3604480
  353.6 31.0 %collective-permute-start.39 = (bf16[16,256,128]{2,1,0:T(8,128)(2,1)}, bf16[16,256,128]{2,1,0:T(8,128)(2,1)S(1)}, u32[]{:S(2)}, u32[]{:S(2)}) collective-permute-start(bf16[16,256,128]{2,1,0:T(8,128)(2,1)} %get-tuple-element.157), channel_id=1, source_target_pairs={{0,1},{1,0},{2,3},{3,2},{4,5},{5,4},{6,7},{7,6},{8,9},{9,8},{10,11... | collective-permute-start | bytes 3145736 | tf_op jit(solution)/shard_map/ppermute | solution.py:619
  360.2 16.9 %collective-permute-start.43 = (bf16[256,512]{1,0:T(8,128)(2,1)S(1)}, bf16[256,512]{1,0:T(8,128)(2,1)S(1)}, u32[]{:S(2)}, u32[]{:S(2)}) collective-permute-start(bf16[256,512]{1,0:T(8,128)(2,1)S(1)} %get-tuple-element.255), channel_id=1, source_target_pairs={{0,6},{2,4},{4,2},{6,0},{8,14},{10,12},{12,10},{14,8},{16,22},{18,... | collective-permute-start | bytes 786440 | tf_op jit(solution)/shard_map/ppermute | solution.py:630
  389.8 28.1 %all-to-all-start.7 = ((bf16[16,256,128]{2,1,0:T(8,128)(2,1)}), bf16[16,256,128]{2,1,0:T(8,128)(2,1)S(1)}, u32[]{:S(2)}, u32[]{:S(2)}) async-start(bf16[16,256,128]{2,1,0:T(8,128)(2,1)} %add_convert_fusion.1), calls=%async_computation.7 | async-start | bytes 2097152 | tf_op jit(solution)/shard_map/all_to_all | solution.py:633
  418.9 46.7 %all-to-all-start.8 = ((bf16[4,1408,128]{2,1,0:T(8,128)(2,1)}), bf16[4,1408,128]{2,1,0:T(8,128)(2,1)S(1)}, u32[]{:S(2)}, u32[]{:S(2)}) async-start(bf16[4,1408,128]{2,1,0:T(8,128)(2,1)} %bitcast.198), calls=%async_computation.8 | async-start | bytes 2883584 | tf_op jit(solution)/shard_map/all_to_all | solution.py:633
  438.2 31.6 %collective-permute-start.54 = (bf16[64,2048]{1,0:T(8,128)(2,1)}, bf16[64,2048]{1,0:T(8,128)(2,1)}, u32[]{:S(2)}, u32[]{:S(2)}) collective-permute-start(bf16[64,2048]{1,0:T(8,128)(2,1)} %get-tuple-element.178), channel_id=1, source_target_pairs={{0,4},{2,6},{4,0},{6,2},{8,12},{10,14},{12,8},{14,10},{16,20},{18,... | collective-permute-start | bytes 786440 | tf_op jit(solution)/shard_map/ppermute | solution.py:630
  439.9 32.5 %collective-permute-start.55 = (bf16[64,2048]{1,0:T(8,128)(2,1)}, bf16[64,2048]{1,0:T(8,128)(2,1)}, u32[]{:S(2)}, u32[]{:S(2)}) collective-permute-start(bf16[64,2048]{1,0:T(8,128)(2,1)} %get-tuple-element.179), channel_id=1, source_target_pairs={{0,6},{2,4},{4,2},{6,0},{8,14},{10,12},{12,10},{14,8},{16,22},{18,... | collective-permute-start | bytes 786440 | tf_op jit(solution)/shard_map/ppermute | solution.py:630
  443.3 29.8 %collective-permute-start.59 = (bf16[4,64,384]{2,1,0:T(8,128)(2,1)}, bf16[4,64,384]{2,1,0:T(8,128)(2,1)}, u32[]{:S(2)}, u32[]{:S(2)}) collective-permute-start(bf16[4,64,384]{2,1,0:T(8,128)(2,1)} %get-tuple-element.283), channel_id=1, source_target_pairs={{0,8},{2,10},{4,12},{6,14},{8,16},{10,18},{12,20},{14,22},{16,24},... | collective-permute-start | bytes 589832 | tf_op jit(solution)/shard_map/ppermute | solution.py:627
  445.3 28.1 %collective-permute-start.58 = (bf16[4,64,384]{2,1,0:T(8,128)(2,1)}, bf16[4,64,384]{2,1,0:T(8,128)(2,1)}, u32[]{:S(2)}, u32[]{:S(2)}) collective-permute-start(bf16[4,64,384]{2,1,0:T(8,128)(2,1)} %get-tuple-element.284), channel_id=1, source_target_pairs={{0,16},{2,18},{4,20},{6,22},{8,24},{10,26},{12,28},{14,30},{16,0},... | collective-permute-start | bytes 589832 | tf_op jit(solution)/shard_map/ppermute | solution.py:627
  447.6 25.8 %collective-permute-start.57 = (bf16[4,64,384]{2,1,0:T(8,128)(2,1)}, bf16[4,64,384]{2,1,0:T(8,128)(2,1)}, u32[]{:S(2)}, u32[]{:S(2)}) collective-permute-start(bf16[4,64,384]{2,1,0:T(8,128)(2,1)} %get-tuple-element.285), channel_id=1, source_target_pairs={{0,24},{2,26},{4,28},{6,30},{8,0},{10,2},{12,4},{14,6},{16,8},{18,... | collective-permute-start | bytes 589832 | tf_op jit(solution)/shard_map/ppermute | solution.py:627
  465.6 28.0 %all-to-all-start.9 = ((bf16[4,704,128]{2,1,0:T(8,128)(2,1)}), bf16[4,704,128]{2,1,0:T(8,128)(2,1)}, u32[]{:S(2)}, u32[]{:S(2)}) async-start(bf16[4,704,128]{2,1,0:T(8,128)(2,1)} %bitcast.203), calls=%async_computation.9 | async-start | bytes 1441792 | tf_op jit(solution)/shard_map/all_to_all | solution.py:633
  469.8 19.7 %collective-permute-start.66 = (bf16[768,128]{1,0:T(8,128)(2,1)}, bf16[768,128]{1,0:T(8,128)(2,1)}, u32[]{:S(2)}, u32[]{:S(2)}) collective-permute-start(bf16[768,128]{1,0:T(8,128)(2,1)} %get-tuple-element.279), channel_id=1, source_target_pairs={{0,6},{2,4},{4,2},{6,0},{8,14},{10,12},{12,10},{14,8},{16,22},{18,... | collective-permute-start | bytes 589832 | tf_op jit(solution)/shard_map/ppermute | solution.py:630
  472.4 18.9 %collective-permute-start.64 = (bf16[768,128]{1,0:T(8,128)(2,1)}, bf16[768,128]{1,0:T(8,128)(2,1)}, u32[]{:S(2)}, u32[]{:S(2)}) collective-permute-start(bf16[768,128]{1,0:T(8,128)(2,1)} %get-tuple-element.281), channel_id=1, source_target_pairs={{0,2},{2,0},{4,6},{6,4},{8,10},{10,8},{12,14},{14,12},{16,18},{18,... | collective-permute-start | bytes 589832 | tf_op jit(solution)/shard_map/ppermute | solution.py:630
  473.1 18.3 %collective-permute-start.65 = (bf16[768,128]{1,0:T(8,128)(2,1)}, bf16[768,128]{1,0:T(8,128)(2,1)}, u32[]{:S(2)}, u32[]{:S(2)}) collective-permute-start(bf16[768,128]{1,0:T(8,128)(2,1)} %get-tuple-element.282), channel_id=1, source_target_pairs={{0,4},{2,6},{4,0},{6,2},{8,12},{10,14},{12,8},{14,10},{16,20},{18,... | collective-permute-start | bytes 589832 | tf_op jit(solution)/shard_map/ppermute | solution.py:630
  (134 other events, 1134.3 us)
Sparse Core Ops, SparseCore 0:
  101.8 95.7 all-gather.2
  320.3 71.8 reduce-scatter.6
  395.3 42.9 reduce-scatter.8
